TPU v7x, 128 devices: a whole 4x4x4 slice. The times are simulated.
128 devices in a mesh: crow: 8 (over y, core), ccol: 16 (over x, z).
Axes of the slice: x: 4, y: 4, z: 4, core: 2. Of those that a mesh axis runs over, the one named last changes fastest.
Arguments:
- modes: bfloat16 [262144, 512], P(('crow', 'ccol')), may hold values from -6 to 6
- col_basis: bfloat16 [64, 262144], P(None, ('crow', 'ccol')), may hold values from -0.375 to 0.375
- row_basis: bfloat16 [64, 262144], P(None, ('crow', 'ccol')), may hold values from -0.1875 to 0.1875
- near_blocks: bfloat16 [262144, 2304], P(('crow', 'ccol')), may hold values from -0.125 to 0.125
- block_rows: int32 [16384], P(('crow', 'ccol')), may hold values from 0 to 127
- block_owner: int32 [16384, 1], P(('crow', 'ccol')), may hold values from 0 to 127; in each aligned block of 128 rows (0 to 127, 128 to 255, ...) at most 2 rows name the same one
- block_slot: int32 [16384], P(('crow', 'ccol')), may hold values from 0 to 7
- cores: bfloat16 [16384, 4096], P(('crow', 'ccol')), may hold values from -0.75 to 0.75
Outputs:
- pressure: bfloat16 [262144, 512], P(('crow', 'ccol'))
Inputs may be any that keep to these rules, and one draw needn't show every extreme that they name: `block_owner`: among the blocks of one device (rows b * 128 to (b + 1) * 128 - 1), at most 2 name the same device; some device reaches 2 for some owner in every draw.
All inputs are finite; a program needn't handle non-finite values.
Results may differ from a plain program's by a relative error of at most 0.0049.
Values may be sent and summed in bfloat16 or wider, within the bound.
No kernel may reach another device: no remote copies, remote signals or barrier semaphores. Data moves between devices by JAX's collectives and lax.ppermute only.
A program may use at most 192 MiB of HBM per device.

v0:
```python
import jax
import jax.numpy as jnp
from jax import lax
from jax.sharding import PartitionSpec as P

CS = 256
NH = 4
NEAR = 9


def extended(value, sides, width):
    for axis, dim in sides:
        size, length = (lax.axis_size(axis), value.shape[dim])
        up = [(i, (i + 1) % size) for i in range(size - 1)]
        down = [(j, i) for i, j in up]
        last = lax.slice_in_dim(value, length - width, length, axis=dim)
        first = lax.slice_in_dim(value, 0, width, axis=dim)
        before = lax.ppermute(last, axis, up)
        after = lax.ppermute(first, axis, down)
        value = jnp.concatenate([before, value, after], axis=dim)
    return value


def per_device(
    modes, col_basis, row_basis, near_blocks, block_rows, block_owner, block_slot, cores
):
    devices = lax.axis_size(("crow", "ccol"))
    col_devices = lax.axis_size("ccol")
    cluster_count = modes.shape[0] // CS
    block_count = cores.shape[0]
    capacity = (block_count + devices - 1) // devices + 1
    mode_cols = modes.shape[1]
    rank_width = col_basis.shape[0]
    mode_tiles = modes.reshape(cluster_count, CS, mode_cols)
    basis_v = col_basis.reshape(rank_width, cluster_count, CS)
    compressed = jnp.einsum(
        "kcs,csm->ckm", basis_v, mode_tiles, preferred_element_type=jnp.float32
    ).astype(jnp.bfloat16)
    owners = block_owner[:, 0]
    positions = jnp.arange(block_count, dtype=jnp.int32)
    earlier = (owners[None, :] == owners[:, None]) & (positions[None, :] < positions[:, None])
    arrival = jnp.sum(earlier.astype(jnp.int32), axis=1)
    slot_index = owners * capacity + arrival
    places = jnp.arange(devices * capacity, dtype=jnp.int32)
    chosen = slot_index[:, None] == places[None, :]
    wanted = jnp.sum(jnp.where(chosen, block_slot[:, None] + 1, 0), axis=0) - 1
    requested = lax.all_to_all(
        wanted.reshape(devices, capacity), ("crow", "ccol"), split_axis=0, concat_axis=0, tiled=True
    )
    selector = (
        requested.reshape(-1)[:, None] == jnp.arange(cluster_count, dtype=jnp.int32)[None, :]
    ).astype(jnp.bfloat16)
    outgoing = jnp.dot(
        selector,
        compressed.reshape(cluster_count, rank_width * mode_cols),
        preferred_element_type=jnp.float32,
    ).astype(jnp.bfloat16)
    outgoing = outgoing.reshape(devices, capacity, rank_width * mode_cols)
    incoming = lax.all_to_all(outgoing, ("crow", "ccol"), split_axis=0, concat_axis=0, tiled=True)
    fetched = jnp.take(
        incoming.reshape(devices * capacity, rank_width, mode_cols), slot_index, axis=0
    )
    core_mats = cores.reshape(block_count, rank_width, rank_width)
    block_terms = jnp.einsum("bkj,bjm->bkm", core_mats, fetched, preferred_element_type=jnp.float32)
    partial_value = jax.ops.segment_sum(
        block_terms, block_rows, num_segments=col_devices * cluster_count
    )
    far_rounded = lax.psum_scatter(partial_value, "ccol", scatter_dimension=0, tiled=True).astype(
        jnp.bfloat16
    )
    padded = extended(modes, ((("crow", "ccol"), 0),), NH * CS)
    padded_tiles = padded.reshape(cluster_count + 2 * NH, CS, mode_cols)
    near_view = near_blocks.reshape(cluster_count, CS, NEAR, CS)
    near_sum = jnp.zeros((cluster_count, CS, mode_cols), jnp.float32)
    for offset in range(NEAR):
        near_sum = near_sum + jnp.einsum(
            "rpq,rqm->rpm",
            near_view[:, :, offset, :],
            padded_tiles[offset : offset + cluster_count],
            preferred_element_type=jnp.float32,
        )
    basis_u = row_basis.reshape(rank_width, cluster_count, CS)
    far_part = jnp.einsum("krp,rkm->rpm", basis_u, far_rounded, preferred_element_type=jnp.float32)
    return (near_sum + far_part).astype(jnp.bfloat16).reshape(cluster_count * CS, mode_cols)


def solution(mesh):
    in_specs = (
        P(("crow", "ccol"), None),
        P(None, ("crow", "ccol")),
        P(None, ("crow", "ccol")),
        P(("crow", "ccol"), None),
        P(("crow", "ccol")),
        P(("crow", "ccol"), None),
        P(("crow", "ccol")),
        P(("crow", "ccol"), None),
    )
    out_specs = P(("crow", "ccol"), None)
    return jax.shard_map(
        per_device, mesh=mesh, in_specs=in_specs, out_specs=out_specs, check_vma=False
    )
```

profile of v0, /device:TPU:0, one launch (start us, length us, event | category | flops | bytes accessed | tf_op | source)
XLA Modules:
  0.0 565.5 jit_solution(1631018769772477049)
XLA Ops:
  9.7 11.1 %all-to-all-start = ((s32[128,1,2]{2,1,0:T(1,128)}), s32[128,1,2]{2,1,0:T(1,128)S(1)}, u32[]{:S(2)}, u32[]{:S(2)}) async-start(s32[128,1,2]{2,1,0:T(1,128)} %bitcast.27), calls=%async_computation | async-start | bytes 131072 | tf_op jit(solution)/shard_map/all_to_all | solution.py:47
  23.3 6.9 %all-to-all-done = s32[128,1,2]{2,1,0:T(1,128)S(1)} async-done(((s32[128,1,2]{2,1,0:T(1,128)}), s32[128,1,2]{2,1,0:T(1,128)S(1)}, u32[]{:S(2)}, u32[]{:S(2)}) %all-to-all-start) | async-done | bytes 1056 | tf_op jit(solution)/shard_map/all_to_all | solution.py:47
  31.7 8.1 %convolution_convert_fusion = bf16[256,32768]{1,0:T(8,128)(2,1)} fusion(bf16[8,32768]{1,0:T(8,128)(2,1)S(1)} %bitcast.114, s32[256]{0:T(256)S(1)} %eq.53), kind=kOutput, calls=%fused_computation.2 | convolution fusion | flops 142608384 | bytes 17302528 | tf_op jit(solution)/shard_map/dot_general | solution.py:53
  39.8 27.0 %reshape.66 = bf16[128,2,32768]{2,1,0:T(2,128)(2,1)} reshape(bf16[256,32768]{1,0:T(8,128)(2,1)} %convolution_convert_fusion) | data formatting | bytes 33554432 | tf_op jit(solution)/shard_map/reshape | solution.py:58
  66.8 6.2 %all-to-all-start.1 = ((bf16[128,2,32768]{2,1,0:T(2,128)(2,1)}), bf16[128,2,32768]{2,1,0:T(2,128)(2,1)}, u32[]{:S(2)}, u32[]{:S(2)}) async-start(bf16[128,2,32768]{2,1,0:T(2,128)(2,1)} %reshape.66), calls=%async_computation.1 | async-start | bytes 33554432 | tf_op jit(solution)/shard_map/all_to_all | solution.py:59
  73.9 3.0 copy.52
  76.9 233.0 %all-to-all-done.1 = bf16[128,2,32768]{2,1,0:T(2,128)(2,1)} async-done(((bf16[128,2,32768]{2,1,0:T(2,128)(2,1)}), bf16[128,2,32768]{2,1,0:T(2,128)(2,1)}, u32[]{:S(2)}, u32[]{:S(2)}) %all-to-all-start.1) | async-done | bytes 16777248 | tf_op jit(solution)/shard_map/all_to_all | solution.py:59
  309.9 27.4 %reshape.67 = bf16[256,64,512]{2,1,0:T(8,128)(2,1)} reshape(bf16[128,2,32768]{2,1,0:T(2,128)(2,1)} %all-to-all-done.1) | data formatting | bytes 33554432 | tf_op jit(solution)/shard_map/reshape | solution.py:61
  337.3 12.3 %gather_fusion = bf16[128,64,512]{2,1,0:T(8,128)(2,1)} fusion(bf16[256,64,512]{2,1,0:T(8,128)(2,1)} %reshape.67, s32[1024]{0:T(1024)S(1)} %pad_clamp_fusion), kind=kCustom, calls=%fused_computation | custom fusion | bytes 16777728 | tf_op jit(solution)/shard_map/jit(_take)/gather | solution.py:60
  349.7 11.5 %convolution_bitcast_fusion = f32[128,64,512]{2,1,0:T(8,128)} fusion(bf16[128,64,64]{2,1,0:T(8,128)(2,1)S(1)} %copy.52, bf16[128,64,512]{2,1,0:T(8,128)(2,1)} %gather_fusion, pred[128]{0:T(512)(128)(4,1)S(1)} %and_bitcast_fusion), kind=kOutput, calls=%fused_computation.3 | convolution fusion | flops 541065216 | bytes 26214528 | tf_op jit(solution)/shard_map/bkj,bjm->bkm/dot_general | solution.py:64
  361.2 7.9 %broadcast_in_dim.34 = f32[128,64,512]{2,1,0:T(8,128)} broadcast(f32[]{:T(128)} %constant.8.clone.1), dimensions={} | broadcast | bytes 16777220 | tf_op jit(solution)/shard_map/broadcast_in_dim | solution.py:65
  369.1 38.8 %scatter_fusion = f32[128,64,512]{2,1,0:T(8,128)} fusion(f32[128,64,512]{2,1,0:T(8,128)} %broadcast_in_dim.34, s32[128]{0:T(128)S(1)} %copy-done.12, f32[128,64,512]{2,1,0:T(8,128)} %convolution_bitcast_fusion), kind=kCustom, calls=%fused_computation.1 | custom fusion | flops 4194304 | bytes 50332160 | tf_op jit(solution)/shard_map/scatter-add | solution.py:65
  414.6 19.3 %reshape.88 = bf16[8,256,9,256]{3,2,1,0:T(8,128)(2,1)} reshape(bf16[2048,2304]{1,0:T(8,128)(2,1)} %param.11) | data formatting | bytes 18874368 | tf_op jit(solution)/shard_map/reshape | solution.py:73
  434.0 35.0 %fusion.24 = (bf16[8,256,1,256]{3,2,1,0:T(2,128)(2,1)}, bf16[8,256,1,256]{3,2,1,0:T(2,128)(2,1)}, bf16[8,256,1,256]{3,2,1,0:T(2,128)(2,1)}, bf16[8,256,1,256]{3,...) fusion(bf16[8,256,9,256]{3,2,1,0:T(8,128)(2,1)} %reshape.88), kind=kLoop, calls=%fused_computation.59 | loop fusion | bytes 18874368 | tf_op jit(solution)/shard_map/slice | solution.py:78
  469.0 4.3 fusion.8
  477.1 2.7 fusion.5
  479.8 2.7 fusion.6
  482.5 2.6 fusion.7
  486.8 2.8 fusion.9
  489.5 2.7 fusion.10
  492.2 2.7 fusion.12
  497.5 41.6 %reduce-scatter.2.cloned.1.call-done = f32[8,64,512]{2,1,0:T(8,128)} async-done(((f32[128,64,512]{2,1,0:T(8,128)}), f32[8,64,512]{2,1,0:T(8,128)}) %reduce-scatter.2.cloned.1.call-update) | async-done | bytes 1048592 | tf_op jit(solution)/shard_map/reduce_scatter | solution.py:68
  539.1 4.1 fusion.13
  543.2 15.4 %fusion.2 = bf16[8,256,512]{2,1,0:T(8,128)(2,1)} fusion(f32[8,512,256]{1,2,0:T(8,128)} %fusion.13, f32[8,512,256]{1,2,0:T(8,128)} %fusion.5, f32[8,512,256]{1,2,0:T(8,128)} %fusion.6, f32[8,512,256]{1,2,0:T(8,128)} %fusion.7, f32[8,256,512]{2,1,0:T(8,128)S(1)} %copy-done.1, f32[8,512,256]{1,2,0:T(8,128)} %fusion.9, f32[8,512,256]{1,2,0:T(8,128)} %fusion.10, ...), kind=kOutput, calls=%fused_computation.7 | convolution fusion | flops 547356672 | bytes 42991616 | tf_op jit(solution)/shard_map/rpq,rqm->rpm/dot_general | solution.py:76
  (53 shorter events, 22.7 us)
Async XLA Ops:
  9.7 20.6 %all-to-all-start = ((s32[128,1,2]{2,1,0:T(1,128)}), s32[128,1,2]{2,1,0:T(1,128)S(1)}, u32[]{:S(2)}, u32[]{:S(2)}) async-start(s32[128,1,2]{2,1,0:T(1,128)} %bitcast.27), calls=%async_computation | async-start | bytes 131072 | tf_op jit(solution)/shard_map/all_to_all | solution.py:47
  66.8 6.4 %copy-start.9 = (bf16[128,4096]{1,0:T(8,128)(2,1)S(1)}, bf16[128,4096]{1,0:T(8,128)(2,1)}, u32[]{:S(2)}) copy-start(bf16[128,4096]{1,0:T(8,128)(2,1)} %param.15) | copy-start | bytes 3145732
  66.8 243.1 %all-to-all-start.1 = ((bf16[128,2,32768]{2,1,0:T(2,128)(2,1)}), bf16[128,2,32768]{2,1,0:T(2,128)(2,1)}, u32[]{:S(2)}, u32[]{:S(2)}) async-start(bf16[128,2,32768]{2,1,0:T(2,128)(2,1)} %reshape.66), calls=%async_computation.1 | async-start | bytes 33554432 | tf_op jit(solution)/shard_map/all_to_all | solution.py:59
  72.9 466.2 %reduce-scatter.2.cloned.1.call-start = ((), (), s32[]{:S(2)}) async-start(), calls=%async_computation.3 | async-start | bytes 17825792 | tf_op jit(solution)/shard_map/reduce_scatter | solution.py:68
  73.9 3.0 copy-start.11
  361.2 7.9 %copy-start.12 = (s32[128]{0:T(128)S(1)}, s32[128]{0:T(128)}, u32[]{:S(2)}) copy-start(s32[128]{0:T(128)} %param.12) | copy-start | bytes 1540
  407.8 1.6 copy-start
  410.9 62.4 %collective-permute-start = (bf16[1024,512]{1,0:T(8,128)(2,1)}, bf16[1024,512]{1,0:T(8,128)(2,1)}, u32[]{:S(2)}, u32[]{:S(2)}) collective-permute-start(bf16[1024,512]{1,0:T(8,128)(2,1)} %get-tuple-element.24), channel_id=1, source_target_pairs={{0,1},{1,2},{2,3},{3,4},{4,5},{5,6},{6,7},{7,8},{8,9},{9,10},{10,1... | collective-permute-start | bytes 3145736 | tf_op jit(solution)/shard_map/ppermute | solution.py:18
  413.1 61.9 %collective-permute-start.1 = (bf16[1024,512]{1,0:T(8,128)(2,1)}, bf16[1024,512]{1,0:T(8,128)(2,1)S(1)}, u32[]{:S(2)}, u32[]{:S(2)}) collective-permute-start(bf16[1024,512]{1,0:T(8,128)(2,1)} %get-tuple-element.25), channel_id=1, source_target_pairs={{1,0},{2,1},{3,2},{4,3},{5,4},{6,5},{7,6},{8,7},{9,8},{10,9},{11,1... | collective-permute-start | bytes 3145736 | tf_op jit(solution)/shard_map/ppermute | solution.py:19
  475.1 2.1 copy-start.8
  477.1 2.7 copy-start.7
  479.8 2.7 copy-start.6
  485.2 1.6 copy-start.5
  486.8 2.8 copy-start.4
  489.5 2.7 copy-start.3
  492.2 2.7 copy-start.2
  494.9 44.3 %copy-start.10 = (bf16[64,2048]{1,0:T(8,128)(2,1)S(1)}, bf16[64,2048]{1,0:T(8,128)(2,1)}, u32[]{:S(2)}) copy-start(bf16[64,2048]{1,0:T(8,128)(2,1)} %param.10) | copy-start | bytes 786436
  539.1 4.1 copy-start.1
Sparse Core Ops, SparseCore 0:
  408.0 131.0 reduce-scatter.1
where the time goes:
time: 568 us; the launch traced here: 566 us
  waiting for transfers between devices  282 us (50%)
  local copies, waits for them, and re-layouts  143 us (25%)
  matrix products  64.4 us (11%)
  other arithmetic  41.9 us (7%)
  starting transfers between devices  21.3 us (4%)
  between operations  13.6 us (2%)
    all_to_all x1, waiting for transfers between devices, per_device(): lax.all_to_all(outgoing, ('crow', 'ccol'), split_axis=0, concat_axis=0, t...  233 us
    reduce_scatter x1, waiting for transfers between devices, per_device(): lax.psum_scatter(partial_value, 'ccol', scatter_dimension=0, tiled=True)  41.6 us
    scatter-add x1, other arithmetic, per_device(): jax.ops.segment_sum(block_terms, block_rows, num_segments=col_devices * c...  38.8 us
    dot_general x9, matrix products, per_device(): jnp.einsum('rpq,rqm->rpm', near_view[:, :, offset, :], padded_tiles[offse...  38.5 us
    slice x1, local copies, waits for them, and re-layouts, per_device(): near_view[:, :, offset, :]  35 us
    reshape x1, local copies, waits for them, and re-layouts, per_device(): incoming.reshape(devices * capacity, rank_width, mode_cols)  27.4 us
    reshape x1, local copies, waits for them, and re-layouts, per_device(): outgoing = outgoing.reshape(devices, capacity, rank_width * mode_cols)  27 us
    reshape x1, local copies, waits for them, and re-layouts, per_device(): near_view = near_blocks.reshape(cluster_count, CS, NEAR, CS)  19.3 us
  transfers between devices with their start and end apart: 5, of which 3 were waited for; matrix products, arithmetic and copies ran while one was open for 16% of the time, Pallas kernels for 0%

commit v1 on v0

v1 whole, which is shorter than its diff:
```python
import functools

import jax
import jax.numpy as jnp
from jax import lax
from jax.experimental import pallas as pl
from jax.experimental.pallas import tpu as pltpu
from jax.sharding import PartitionSpec as P

CS = 256
NH = 4
NEAR = 9
CAP = 2
MIB = 1 << 20
VMEM = pltpu.VMEM
SMEM = pltpu.SMEM


def whole(space=VMEM):
    return pl.BlockSpec(memory_space=space)


def compress_kernel(basis_ref, modes_ref, out_ref):
    out_ref[0] = jnp.dot(
        basis_ref[...], modes_ref[...], preferred_element_type=jnp.float32
    ).astype(jnp.bfloat16)


def compress(col_basis, modes):
    rank, panels = col_basis.shape
    cols = modes.shape[1]
    count = panels // CS
    return pl.pallas_call(
        compress_kernel,
        grid=(count,),
        in_specs=[
            pl.BlockSpec((rank, CS), lambda r: (0, r)),
            pl.BlockSpec((CS, cols), lambda r: (r, 0)),
        ],
        out_specs=pl.BlockSpec((1, rank, cols), lambda r: (r, 0, 0)),
        out_shape=jax.ShapeDtypeStruct((count, rank, cols), jnp.bfloat16),
        cost_estimate=pl.CostEstimate(
            flops=2 * rank * panels * cols, bytes_accessed=3 * MIB, transcendentals=0
        ),
        name="compress",
    )(col_basis, modes)


def dispatch_kernel(
    cols, slots, cl_dev, rows_ref, owners_ref, slot_ref, cores_ref, out_ref, count_ref, meta_ref
):
    blocks, rows, _ = cores_ref.shape
    out_ref[...] = jnp.zeros_like(out_ref)
    meta_ref[...] = jnp.zeros_like(meta_ref)
    lane = lax.broadcasted_iota(jnp.int32, (1, 128), 1)
    for j in range(cols):
        count_ref[j] = 0

    def place(b, carry):
        owner = owners_ref[b]
        column = owner % cols
        at = count_ref[column]
        count_ref[column] = at + 1
        out_ref[column, pl.ds(pl.multiple_of(at * rows, rows), rows), :] = cores_ref[b]
        cluster = (owner // cols) * cl_dev + slot_ref[b]
        entry = (
            jnp.where(lane == at, cluster, 0)
            + jnp.where(lane == slots + at, rows_ref[b], 0)
            + jnp.where(lane == 2 * slots, 1, 0)
        )
        meta_ref[pl.ds(column, 1), :] += entry.astype(jnp.float32)
        return carry

    lax.fori_loop(0, blocks, place, 0)
    for j in range(cols):
        out_ref[j, slots * rows :, :] = jnp.broadcast_to(
            meta_ref[j : j + 1, :], (16, 128)
        ).astype(jnp.bfloat16)


def dispatch(block_rows, owners, block_slot, cores, cols, slots, cl_dev):
    blocks, rows, _ = cores.shape
    return pl.pallas_call(
        functools.partial(dispatch_kernel, cols, slots, cl_dev),
        in_specs=[whole(SMEM), whole(SMEM), whole(SMEM), whole()],
        out_specs=whole(),
        out_shape=jax.ShapeDtypeStruct((cols, slots * rows + 16, 128), jnp.bfloat16),
        scratch_shapes=[SMEM((cols,), jnp.int32), VMEM((cols, 128), jnp.float32)],
        compiler_params=pltpu.CompilerParams(vmem_limit_bytes=16 * MIB),
        cost_estimate=pl.CostEstimate(flops=4 * MIB, bytes_accessed=3 * MIB, transcendentals=0),
        name="dispatch",
    )(block_rows, owners, block_slot, cores)


UNROLL = 4


def far_kernel(slots, rows, comp_ref, sent_ref, out_ref, meta_ref, smem_ref, list_ref, total_ref, sem):
    sources = sent_ref.shape[0]

    @pl.when(pl.program_id(0) == 0)
    def _():
        meta = sent_ref[:, slots * rows : slots * rows + 16, :].astype(jnp.float32)
        meta_ref[...] = jnp.max(meta, axis=1).astype(jnp.int32)
        copy = pltpu.make_async_copy(meta_ref, smem_ref, sem)
        copy.start()
        copy.wait()

        def source(i, total):
            def entry(p, total):
                list_ref[total] = ((i * slots + p) << 16) + (smem_ref[i, p] << 8) + smem_ref[i, slots + p]
                return total + 1

            return lax.fori_loop(0, smem_ref[i, 2 * slots], entry, total)

        total = lax.fori_loop(0, sources, source, 0)
        total_ref[0] = total
        for i in range(UNROLL):
            list_ref[total + i] = 0

    out_ref[...] = jnp.zeros_like(out_ref)
    total = total_ref[0]

    def group(g, carry):
        terms = []
        for i in range(UNROLL):
            at = g * UNROLL + i
            entry = list_ref[at]
            place = entry >> 16
            core = sent_ref[place // slots, pl.ds(pl.multiple_of((place % slots) * rows, rows), rows), :]
            core = jnp.where(at < total, core, jnp.zeros_like(core))
            half = core.shape[1] // 2
            core = jnp.concatenate([core[:, :half], core[:, half:]], axis=0)
            comp = comp_ref[(entry >> 8) & 255]
            terms.append((entry & 255, jnp.dot(core, comp, preferred_element_type=jnp.float32)))
        for row, term in terms:
            out_ref[row] += term
        return carry

    lax.fori_loop(0, (total + UNROLL - 1) // UNROLL, group, 0)


def far_field(comp, sent, slots, rows, group_rows):
    clusters, rank, cols = comp.shape
    sources = sent.shape[0]
    width = cols // 2
    return pl.pallas_call(
        functools.partial(far_kernel, slots, rows),
        grid=(cols // width,),
        in_specs=[
            pl.BlockSpec((clusters, rank, width), lambda m: (0, 0, m)),
            pl.BlockSpec(sent.shape, lambda m: (0, 0, 0)),
        ],
        out_specs=pl.BlockSpec((group_rows, rank, width), lambda m: (0, 0, m)),
        out_shape=jax.ShapeDtypeStruct((group_rows, rank, cols), jnp.float32),
        scratch_shapes=[
            VMEM((sources, 128), jnp.int32),
            SMEM((sources, 128), jnp.int32),
            SMEM((sources * slots + UNROLL,), jnp.int32),
            SMEM((1,), jnp.int32),
            pltpu.SemaphoreType.DMA,
        ],
        compiler_params=pltpu.CompilerParams(vmem_limit_bytes=40 * MIB),
        cost_estimate=pl.CostEstimate(
            flops=2 * 128 * rank * rank * cols * 8, bytes_accessed=24 * MIB, transcendentals=0
        ),
        name="far_field",
    )(comp, sent)


def near_kernel(near_ref, before_ref, modes_ref, after_ref, out_ref, ext_ref):
    r = pl.program_id(0)
    halo, panels = before_ref.shape[0], modes_ref.shape[0]

    @pl.when(r == 0)
    def _():
        ext_ref[:halo] = before_ref[...]
        ext_ref[halo : halo + panels] = modes_ref[...]
        ext_ref[halo + panels :] = after_ref[...]

    window = ext_ref[pl.ds(pl.multiple_of(r * CS, CS), NEAR * CS), :]
    out_ref[...] = jnp.dot(near_ref[...], window, preferred_element_type=jnp.float32)


def near_field(near_blocks, before, modes, after):
    panels, band = near_blocks.shape
    cols = modes.shape[1]
    halo = before.shape[0]
    return pl.pallas_call(
        near_kernel,
        grid=(panels // CS,),
        in_specs=[pl.BlockSpec((CS, band), lambda r: (r, 0))] + [whole()] * 3,
        out_specs=pl.BlockSpec((CS, cols), lambda r: (r, 0)),
        out_shape=jax.ShapeDtypeStruct((panels, cols), jnp.float32),
        scratch_shapes=[VMEM((panels + 2 * halo, cols), jnp.bfloat16)],
        compiler_params=pltpu.CompilerParams(vmem_limit_bytes=32 * MIB),
        cost_estimate=pl.CostEstimate(
            flops=2 * panels * band * cols, bytes_accessed=18 * MIB, transcendentals=0
        ),
        name="near_field",
    )(near_blocks, before, modes, after)


def expand_kernel(near_ref, basis_ref, far_ref, out_ref):
    rank = basis_ref.shape[0]
    half = rank // 2
    want = lax.broadcasted_iota(jnp.int32, (rank, rank), 0)
    have = lax.broadcasted_iota(jnp.int32, (rank, rank), 1)
    order = jnp.where(want < half, 2 * want, 2 * (want - half) + 1)
    select = jnp.where(order == have, 1.0, 0.0).astype(jnp.bfloat16)
    basis = jnp.dot(select, basis_ref[...], preferred_element_type=jnp.float32).astype(jnp.bfloat16)
    far = lax.dot_general(
        basis, far_ref[0], (((0,), (0,)), ((), ())), preferred_element_type=jnp.float32
    )
    out_ref[...] = (near_ref[...] + far).astype(jnp.bfloat16)


def expand(near, row_basis, far):
    panels, cols = near.shape
    rank = row_basis.shape[0]
    return pl.pallas_call(
        expand_kernel,
        grid=(panels // CS,),
        in_specs=[
            pl.BlockSpec((CS, cols), lambda r: (r, 0)),
            pl.BlockSpec((rank, CS), lambda r: (0, r)),
            pl.BlockSpec((1, rank, cols), lambda r: (r, 0, 0)),
        ],
        out_specs=pl.BlockSpec((CS, cols), lambda r: (r, 0)),
        out_shape=jax.ShapeDtypeStruct((panels, cols), jnp.bfloat16),
        cost_estimate=pl.CostEstimate(
            flops=2 * panels * rank * cols, bytes_accessed=7 * MIB, transcendentals=0
        ),
        name="expand",
    )(near, row_basis, far)


def per_device(modes, col_basis, row_basis, near_blocks, block_rows, block_owner, block_slot, cores):
    row_devices, col_devices = lax.axis_size("crow"), lax.axis_size("ccol")
    devices = row_devices * col_devices
    cluster_count = modes.shape[0] // CS
    rank = col_basis.shape[0]
    blocks = cores.shape[0]
    slots = CAP * row_devices

    up = [(i, i + 1) for i in range(devices - 1)]
    down = [(j, i) for i, j in up]
    before = lax.ppermute(modes[-NH * CS :], ("crow", "ccol"), up)
    after = lax.ppermute(modes[: NH * CS], ("crow", "ccol"), down)

    compressed = compress(col_basis, modes)
    gathered = lax.all_gather(compressed, "crow", axis=0, tiled=True)

    lines = rank * rank // 128
    sent = dispatch(
        block_rows, block_owner[:, 0], block_slot, cores.reshape(blocks, lines, 128),
        col_devices, slots, cluster_count,
    )
    sent = lax.all_to_all(sent, "ccol", split_axis=0, concat_axis=0, tiled=True)
    partial = far_field(gathered, sent, slots, lines, col_devices * cluster_count)
    far = lax.psum_scatter(partial, "ccol", scatter_dimension=0, tiled=True).astype(jnp.bfloat16)
    near = near_field(near_blocks, before, modes, after)
    return expand(near, row_basis, far)


def solution(mesh):
    both = ("crow", "ccol")
    in_specs = (
        P(both, None),
        P(None, both),
        P(None, both),
        P(both, None),
        P(both),
        P(both, None),
        P(both),
        P(both, None),
    )
    return jax.shard_map(
        per_device, mesh=mesh, in_specs=in_specs, out_specs=P(both, None), check_vma=False
    )
```

time: 568 us -> 227 us (0.40)
  waiting for transfers between devices: 282 us -> 109 us
  local copies, waits for them, and re-layouts: 143 us -> 9.86 us
  matrix products: 64.4 us -> 0 us
  Pallas kernels: 0 us -> 48.8 us
  other arithmetic: 41.9 us -> 2.08 us
  blocking collectives: 0 us -> 37.1 us
  starting transfers between devices: 21.3 us -> 5.98 us
    all_to_all x2 -> x0, waiting for transfers between devices: 240 us -> none  [the longest x1 233 us: per_device(): lax.all_to_all(outgoing, ('crow', 'ccol'), split_axis=0, concat_axis=0, t...]
    reshape x4 -> x0, local copies, waits for them, and re-layouts: 76.7 us -> none  [the longest x1 27.4 us: per_device(): incoming.reshape(devices * capacity, rank_width, mode_cols)]
    dot_general x13 -> x0, matrix products: 64.4 us -> none  [the longest x9 38.5 us: per_device(): jnp.einsum('rpq,rqm->rpm', near_view[:, :, offset, :], padded_tiles[offse...]
    pallas_call x0 -> x5, Pallas kernels: none -> 48.8 us  [the longest x1 25.6 us: far_field(): pl.pallas_call(functools.partial(far_kernel, slots, rows), grid=(cols //...]
    ppermute x2, waiting for transfers between devices: 0.01 us -> 43.7 us  [the longest x1 39.5 us: per_device(): after = lax.ppermute(modes[:NH * CS], ('crow', 'ccol'), down)]
    slice x4 -> x1, local copies, waits for them, and re-layouts: 39.5 us -> 0.14 us  [per_device(): after = lax.ppermute(modes[:NH * CS], ('crow', 'ccol'), down)]
    scatter-add x1 -> x0, other arithmetic: 38.8 us -> none  [per_device(): jax.ops.segment_sum(block_terms, block_rows, num_segments=col_devices * c...]
    all_to_all x0 -> x1, blocking collectives: none -> 37.1 us  [per_device(): sent = lax.all_to_all(sent, 'ccol', split_axis=0, concat_axis=0, tiled=True)]
  transfers between devices with their start and end apart: 5 -> 4, of which waited for: 3 -> 3; matrix products, arithmetic and copies ran while one was open for 16% -> 0% of each run, Pallas kernels for 0% -> 4%
where the time goes in v1:
time: 227 us
  waiting for transfers between devices  109 us (48%)
  Pallas kernels  48.8 us (21%)
  blocking collectives  37.1 us (16%)
  between operations  13.5 us (6%)
  local copies, waits for them, and re-layouts  9.86 us (4%)
  starting transfers between devices  5.98 us (3%)
    reduce_scatter x1, waiting for transfers between devices, per_device(): lax.psum_scatter(partial, 'ccol', scatter_dimension=0, tiled=True)  65.6 us
    ppermute x1, waiting for transfers between devices, per_device(): after = lax.ppermute(modes[:NH * CS], ('crow', 'ccol'), down)  39.5 us
    all_to_all x1, blocking collectives, per_device(): sent = lax.all_to_all(sent, 'ccol', split_axis=0, concat_axis=0, tiled=True)  37.1 us
    pallas_call x1, Pallas kernels, far_field(): pl.pallas_call(functools.partial(far_kernel, slots, rows), grid=(cols //...  25.6 us
    unnamed x17, local copies, waits for them, and re-layouts  9.73 us
    pallas_call x1, Pallas kernels, expand(): pl.pallas_call(expand_kernel, grid=(panels // CS,), in_specs=[pl.BlockSpe...  7.51 us
    pallas_call x1, Pallas kernels, near_field(): pl.pallas_call(near_kernel, grid=(panels // CS,), in_specs=[pl.BlockSpec(...  6.5 us
    pallas_call x1, Pallas kernels, compress(): pl.pallas_call(compress_kernel, grid=(count,), in_specs=[pl.BlockSpec((ra...  6.02 us
  transfers between devices with their start and end apart: 4, of which 3 were waited for; matrix products, arithmetic and copies ran while one was open for 0% of the time, Pallas kernels for 4%

profile of v1, /device:TPU:0, one launch (start us, length us, event | category | flops | bytes accessed | tf_op | source)
XLA Modules:
  0.0 226.6 jit_solution(10729406001974108901)
XLA Ops:
  6.5 0.0 all-gather.2.cloned.1.call-start
  6.6 6.0 %compress.1 = bf16[8,64,512]{2,1,0:T(8,128)(2,1)} custom-call(bf16[64,2048]{1,0:T(8,128)(2,1)} %basis_ref.2, bf16[2048,512]{1,0:T(8,128)(2,1)} %modes_ref.3), custom_call_target="tpu_custom_call" | custom-call | flops 134217728 | bytes 3145728 | tf_op jit(solution)/shard_map/compress/pallas_call | solution.py:33
  12.6 0.0 all-gather.2.cloned.1.call-update
  12.6 0.0 reduce-scatter.2.cloned.1.call-start
  12.7 0.0 copy-done.7
  12.7 0.2 copy.9
  13.0 3.2 %dispatch.1 = bf16[16,528,128]{2,1,0:T(8,128)(2,1)S(1)} custom-call(s32[128]{0:T(128)S(1)} %copy-done.3, s32[128]{0:T(128)S(1)} %bitcast.4, s32[128]{0:T(128)S(1)} %copy-done.5, bf16[128,32,128]{2,1,0:T(8,128)(2,1)S(1)} %bitcast.3), custom_call_target="tpu_custom_call" | custom-call | flops 4194304 | bytes 3145728 | tf_op jit(solution)/shard_map/dispatch/pallas_call | solution.py:83
  16.2 37.1 %all_to_all.5.sent_ref = bf16[16,528,128]{2,1,0:T(8,128)(2,1)S(1)} all-to-all(bf16[16,528,128]{2,1,0:T(8,128)(2,1)S(1)} %dispatch.1), channel_id=1, replica_groups=mesh['crow'=8,'ccol'=16] {'ccol'}, dimensions={0} | all-to-all | bytes 4325376 | tf_op jit(solution)/shard_map/all_to_all | solution.py:259
  53.3 2.2 copy-done.2
  55.5 25.6 %far_field.1 = f32[128,64,512]{2,1,0:T(8,128)} custom-call(bf16[64,64,512]{2,1,0:T(8,128)(2,1)S(1)} %copy-done.2, bf16[16,528,128]{2,1,0:T(8,128)(2,1)S(1)} %all_to_all.5.sent_ref), custom_call_target="tpu_custom_call" | custom-call | flops 4294967296 | bytes 25165824 | tf_op jit(solution)/shard_map/far_field/pallas_call | solution.py:147
  81.1 0.0 copy-start
  81.1 0.0 reduce-scatter.2.cloned.1.call-update
  81.1 1.6 copy-done
  82.7 0.1 fusion
  82.8 1.3 collective-permute-start.1
  84.1 4.6 %collective-permute-start = (bf16[1024,512]{1,0:T(8,128)(2,1)S(1)}, bf16[1024,512]{1,0:T(8,128)(2,1)S(1)}, u32[]{:S(2)}, u32[]{:S(2)}) collective-permute-start(bf16[1024,512]{1,0:T(8,128)(2,1)S(1)} %get-tuple-element.6), channel_id=1, source_target_pairs={{0,1},{1,2},{2,3},{3,4},{4,5},{5,6},{6,7},{7,8},{8,9},{9,10},{10,1... | collective-permute-start | bytes 3145736 | tf_op jit(solution)/shard_map/ppermute | solution.py:248
  88.7 39.5 %collective-permute-done.1.after_ref = bf16[1024,512]{1,0:T(8,128)(2,1)S(1)} collective-permute-done((bf16[1024,512]{1,0:T(8,128)(2,1)S(1)}, bf16[1024,512]{1,0:T(8,128)(2,1)S(1)}, u32[]{:S(2)}, u32[]{:S(2)}) %collective-permute-start.1) | collective-permute-done | bytes 1048608 | tf_op jit(solution)/shard_map/ppermute | solution.py:249
  128.2 4.2 %collective-permute-done.before_ref = bf16[1024,512]{1,0:T(8,128)(2,1)S(1)} collective-permute-done((bf16[1024,512]{1,0:T(8,128)(2,1)S(1)}, bf16[1024,512]{1,0:T(8,128)(2,1)S(1)}, u32[]{:S(2)}, u32[]{:S(2)}) %collective-permute-start) | collective-permute-done | bytes 1048608 | tf_op jit(solution)/shard_map/ppermute | solution.py:248
  132.4 3.8 %copy-done.6 = bf16[2048,2304]{1,0:T(8,128)(2,1)S(1)} copy-done((bf16[2048,2304]{1,0:T(8,128)(2,1)S(1)}, bf16[2048,2304]{1,0:T(8,128)(2,1)}, u32[]{:S(2)}) %copy-start.6) | copy-done | bytes 9437208
  136.2 6.5 %near_field.1.near_ref = f32[2048,512]{1,0:T(8,128)S(1)} custom-call(bf16[2048,2304]{1,0:T(8,128)(2,1)S(1)} %copy-done.6, bf16[1024,512]{1,0:T(8,128)(2,1)S(1)} %collective-permute-done.before_ref, bf16[2048,512]{1,0:T(8,128)(2,1)S(1)} %copy-done, bf16[1024,512]{1,0:T(8,128)(2,1)S(1)} %collective-permute-done.1.after_ref), custom_call_target="tpu_custom_call" | custom-call | flops 4831838208 | bytes 18874368 | tf_op jit(solution)/shard_map/near_field/pallas_call | solution.py:189
  142.7 1.9 copy-done.1
  144.6 65.6 %reduce-scatter.2.cloned.1.call-done = f32[8,64,512]{2,1,0:T(8,128)} async-done(((f32[128,64,512]{2,1,0:T(8,128)}), f32[8,64,512]{2,1,0:T(8,128)}) %reduce-scatter.2.cloned.1.call-update) | async-done | bytes 1048592 | tf_op jit(solution)/shard_map/reduce_scatter | solution.py:261
  210.2 2.1 convert_element_type.3.far_ref
  212.3 7.5 %expand.1 = bf16[2048,512]{1,0:T(8,128)(2,1)} custom-call(f32[2048,512]{1,0:T(8,128)} %copy-done.1, bf16[64,2048]{1,0:T(8,128)(2,1)} %basis_ref.3, bf16[8,64,512]{2,1,0:T(8,128)(2,1)} %convert_element_type.3.far_ref), custom_call_target="tpu_custom_call" | custom-call | flops 134217728 | bytes 7340032 | tf_op jit(solution)/shard_map/expand/pallas_call | solution.py:221
  (11 shorter events, 0.0 us)
Async XLA Ops:
  6.5 6.1 %copy-start.7 = (bf16[128,4096]{1,0:T(8,128)(2,1)S(1)}, bf16[128,4096]{1,0:T(8,128)(2,1)}, u32[]{:S(2)}) copy-start(bf16[128,4096]{1,0:T(8,128)(2,1)} %param.15) | copy-start | bytes 3145732
  6.5 6.4 %copy-start.5 = (s32[128]{0:T(128)S(1)}, s32[128]{0:T(128)}, u32[]{:S(2)}) copy-start(s32[128]{0:T(128)} %slot_ref.1) | copy-start | bytes 1540
  6.5 6.4 %copy-start.4 = (s32[128,1]{0,1:T(1,128)S(1)}, s32[128,1]{0,1:T(1,128)}, u32[]{:S(2)}) copy-start(s32[128,1]{0,1:T(1,128)} %param.13) | copy-start | bytes 1540
  6.5 6.4 %copy-start.3 = (s32[128]{0:T(128)S(1)}, s32[128]{0:T(128)}, u32[]{:S(2)}) copy-start(s32[128]{0:T(128)} %rows_ref.1) | copy-start | bytes 1540
  6.5 46.7 %all-gather.2.cloned.1.call-start = ((), (), s32[]{:S(2)}) async-start(), calls=%async_computation.2 | async-start | bytes 4718592 | tf_op jit(solution)/shard_map/all_gather | solution.py:252
  12.6 197.6 %reduce-scatter.2.cloned.1.call-start = ((), (), s32[]{:S(2)}) async-start(), calls=%async_computation.3 | async-start | bytes 17825792 | tf_op jit(solution)/shard_map/reduce_scatter | solution.py:261
  53.3 2.2 copy-start.2
  81.1 1.6 copy-start
  82.8 45.4 %collective-permute-start.1 = (bf16[1024,512]{1,0:T(8,128)(2,1)S(1)}, bf16[1024,512]{1,0:T(8,128)(2,1)S(1)}, u32[]{:S(2)}, u32[]{:S(2)}) collective-permute-start(bf16[1024,512]{1,0:T(8,128)(2,1)S(1)} %get-tuple-element.5), channel_id=1, source_target_pairs={{1,0},{2,1},{3,2},{4,3},{5,4},{6,5},{7,6},{8,7},{9,8},{10,9},{11,1... | collective-permute-start | bytes 3145736 | tf_op jit(solution)/shard_map/ppermute | solution.py:249
  84.1 48.3 %collective-permute-start = (bf16[1024,512]{1,0:T(8,128)(2,1)S(1)}, bf16[1024,512]{1,0:T(8,128)(2,1)S(1)}, u32[]{:S(2)}, u32[]{:S(2)}) collective-permute-start(bf16[1024,512]{1,0:T(8,128)(2,1)S(1)} %get-tuple-element.6), channel_id=1, source_target_pairs={{0,1},{1,2},{2,3},{3,4},{4,5},{5,6},{6,7},{7,8},{8,9},{9,10},{10,1... | collective-permute-start | bytes 3145736 | tf_op jit(solution)/shard_map/ppermute | solution.py:248
  132.4 3.8 %copy-start.6 = (bf16[2048,2304]{1,0:T(8,128)(2,1)S(1)}, bf16[2048,2304]{1,0:T(8,128)(2,1)}, u32[]{:S(2)}) copy-start(bf16[2048,2304]{1,0:T(8,128)(2,1)} %near_ref.1) | copy-start | bytes 28311556
  142.7 1.9 copy-start.1
Sparse Core Ops, SparseCore 0:
  12.7 34.5 all-gather.1
  81.2 128.9 reduce-scatter.1

commit v2 on v1

v2 whole, which is shorter than its diff:
```python
import functools

import jax
import jax.numpy as jnp
from jax import lax
from jax.experimental import pallas as pl
from jax.experimental.pallas import tpu as pltpu
from jax.sharding import PartitionSpec as P

CS = 256
NH = 4
NEAR = 9
CAP = 2
MIB = 1 << 20
VMEM = pltpu.VMEM
SMEM = pltpu.SMEM


def whole(space=VMEM):
    return pl.BlockSpec(memory_space=space)


COMPRESS = 4


def compress_kernel(basis_ref, modes_ref, out_ref):
    for i in range(COMPRESS):
        out_ref[i] = jnp.dot(
            basis_ref[:, i * CS : (i + 1) * CS],
            modes_ref[i * CS : (i + 1) * CS, :],
            preferred_element_type=jnp.float32,
        ).astype(jnp.bfloat16)


def compress(col_basis, modes):
    rank, panels = col_basis.shape
    cols = modes.shape[1]
    count = panels // CS
    return pl.pallas_call(
        compress_kernel,
        grid=(count // COMPRESS,),
        in_specs=[
            pl.BlockSpec((rank, COMPRESS * CS), lambda r: (0, r)),
            pl.BlockSpec((COMPRESS * CS, cols), lambda r: (r, 0)),
        ],
        out_specs=pl.BlockSpec((COMPRESS, rank, cols), lambda r: (r, 0, 0)),
        out_shape=jax.ShapeDtypeStruct((count, rank, cols), jnp.bfloat16),
        cost_estimate=pl.CostEstimate(
            flops=2 * rank * panels * cols, bytes_accessed=3 * MIB, transcendentals=0
        ),
        name="compress",
    )(col_basis, modes)


def dispatch_kernel(
    cols, slots, cl_dev, rows_ref, owners_ref, slot_ref, cores_ref, out_ref, count_ref, meta_ref
):
    blocks, rows, _ = cores_ref.shape
    out_ref[...] = jnp.zeros_like(out_ref)
    meta_ref[...] = jnp.zeros_like(meta_ref)
    lane = lax.broadcasted_iota(jnp.int32, (1, 128), 1)
    for j in range(cols):
        count_ref[j] = 0

    def place(b, carry):
        owner = owners_ref[b]
        column = owner % cols
        at = count_ref[column]
        count_ref[column] = at + 1
        out_ref[column, pl.ds(pl.multiple_of(at * rows, rows), rows), :] = cores_ref[b]
        cluster = (owner // cols) * cl_dev + slot_ref[b]
        entry = (
            jnp.where(lane == at, cluster, 0)
            + jnp.where(lane == slots + at, rows_ref[b], 0)
            + jnp.where(lane == 2 * slots, 1, 0)
        )
        meta_ref[pl.ds(column, 1), :] += entry.astype(jnp.float32)
        return carry

    lax.fori_loop(0, blocks, place, 0)
    for j in range(cols):
        out_ref[j, slots * rows :, :] = jnp.broadcast_to(
            meta_ref[j : j + 1, :], (16, 128)
        ).astype(jnp.bfloat16)


def dispatch(block_rows, owners, block_slot, cores, cols, slots, cl_dev):
    blocks, rows, _ = cores.shape
    return pl.pallas_call(
        functools.partial(dispatch_kernel, cols, slots, cl_dev),
        in_specs=[whole(SMEM), whole(SMEM), whole(SMEM), whole()],
        out_specs=whole(),
        out_shape=jax.ShapeDtypeStruct((cols, slots * rows + 16, 128), jnp.bfloat16),
        scratch_shapes=[SMEM((cols,), jnp.int32), VMEM((cols, 128), jnp.float32)],
        compiler_params=pltpu.CompilerParams(vmem_limit_bytes=16 * MIB),
        cost_estimate=pl.CostEstimate(flops=4 * MIB, bytes_accessed=3 * MIB, transcendentals=0),
        name="dispatch",
    )(block_rows, owners, block_slot, cores)


UNROLL = 8


def far_kernel(
    slots, rows, x_first, comp_ref, sent_ref, far_ref, next_ref, last_ref, next_sum_ref, last_sum_ref, own_ref,
    acc_ref, meta_ref, smem_ref, list_ref, sem,
):
    sources = sent_ref.shape[0]
    group_rows = acc_ref.shape[0]
    part = group_rows // 4
    me = lax.axis_index("ccol")
    here_x, here_z = me // 4, me % 4

    acc_ref[...] = jnp.zeros_like(acc_ref)
    meta = sent_ref[:, slots * rows : slots * rows + 16, :].astype(jnp.float32)
    meta_ref[...] = jnp.max(meta, axis=1).astype(jnp.int32)
    copy = pltpu.make_async_copy(meta_ref, smem_ref, sem)
    copy.start()
    copy.wait()

    def source(i, total):
        def entry(p, total):
            row = smem_ref[i, slots + p]
            to_x = (row // part - here_x + 4) % 4
            to_z = (row // (part // 4) % 4 - here_z + 4) % 4
            first, second = (to_x, to_z) if x_first else (to_z, to_x)
            at = first * part + second * (part // 4) + row % (part // 4)
            list_ref[total] = ((i * slots + p) << 16) + (smem_ref[i, p] << 8) + at
            return total + 1

        return lax.fori_loop(0, smem_ref[i, 2 * slots], entry, total)

    total = lax.fori_loop(0, sources, source, 0)
    for i in range(UNROLL):
        list_ref[total + i] = 0

    def group(g, carry):
        terms = []
        for i in range(UNROLL):
            at = g * UNROLL + i
            entry = list_ref[at]
            place = entry >> 16
            core = sent_ref[place // slots, pl.ds(pl.multiple_of((place % slots) * rows, rows), rows), :]
            core = jnp.where(at < total, core, jnp.zeros_like(core))
            half = core.shape[1] // 2
            core = jnp.concatenate([core[:, :half], core[:, half:]], axis=0)
            comp = comp_ref[(entry >> 8) & 255]
            terms.append((entry & 255, jnp.dot(core, comp, preferred_element_type=jnp.float32)))
        for row, term in terms:
            acc_ref[row] += term
        return carry

    lax.fori_loop(0, (total + UNROLL - 1) // UNROLL, group, 0)
    half = part // 2
    own_ref[...] = acc_ref[:part]
    next_sum_ref[...] = acc_ref[part : part + half]
    next_ref[...] = acc_ref[part + half : 2 * part].astype(jnp.bfloat16)
    far_ref[...] = acc_ref[2 * part : 3 * part].astype(jnp.bfloat16)
    last_ref[...] = acc_ref[3 * part : 3 * part + half].astype(jnp.bfloat16)
    last_sum_ref[...] = acc_ref[3 * part + half :]


def far_field(comp, sent, slots, rows, group_rows, x_first):
    clusters, rank, cols = comp.shape
    sources = sent.shape[0]
    width = cols // 2
    chunk = 0 if x_first else 1
    part = group_rows // 4
    kinds = [
        (part, jnp.bfloat16),
        (part // 2, jnp.bfloat16),
        (part // 2, jnp.bfloat16),
        (part // 2, jnp.float32),
        (part // 2, jnp.float32),
        (part, jnp.float32),
    ]
    return pl.pallas_call(
        functools.partial(far_kernel, slots, rows, x_first),
        grid=(1,),
        in_specs=[
            pl.BlockSpec((clusters, rank, width), lambda m: (0, 0, chunk)),
            pl.BlockSpec(sent.shape, lambda m: (0, 0, 0)),
        ],
        out_specs=[pl.BlockSpec((n, rank, width), lambda m: (0, 0, 0)) for n, _ in kinds],
        out_shape=[jax.ShapeDtypeStruct((n, rank, width), kind) for n, kind in kinds],
        scratch_shapes=[
            VMEM((group_rows, rank, width), jnp.float32),
            VMEM((sources, 128), jnp.int32),
            SMEM((sources, 128), jnp.int32),
            SMEM((sources * slots + UNROLL,), jnp.int32),
            pltpu.SemaphoreType.DMA,
        ],
        compiler_params=pltpu.CompilerParams(vmem_limit_bytes=40 * MIB),
        cost_estimate=pl.CostEstimate(
            flops=2 * 128 * rank * rank * width * 8, bytes_accessed=12 * MIB, transcendentals=0
        ),
        name="far_x" if x_first else "far_z",
    )(comp, sent)


def ring(axis_is_x, step):
    def to(i):
        x, z = i // 4, i % 4
        return ((x + step) % 4) * 4 + z if axis_is_x else x * 4 + (z + step) % 4

    return [(i, to(i)) for i in range(16)]


def f32(value):
    return value.astype(jnp.float32)


def reduce_parts(parts, x_first):
    far, following, last, following_sum, last_sum, own = parts
    half = far.shape[0] // 2
    to_next = functools.partial(lax.ppermute, axis_name="ccol", perm=ring(x_first, 1))
    to_last = functools.partial(lax.ppermute, axis_name="ccol", perm=ring(x_first, -1))
    far_up = to_next(far[:half])
    far_down = to_last(far[half:])
    own_b = f32(to_next(following))
    own_a = f32(to_last(last))
    up = f32(to_next((following_sum + f32(far_up)).astype(jnp.bfloat16)))
    down = f32(to_last((last_sum + f32(far_down)).astype(jnp.bfloat16)))
    first = own[:half] + own_a + up
    second = own[half:] + own_b + down
    quarter = half // 2
    here, following, far, last = first[:quarter], first[quarter:], second[:quarter], second[quarter:]

    half = quarter // 2
    to_next = functools.partial(lax.ppermute, axis_name="ccol", perm=ring(not x_first, 1))
    to_last = functools.partial(lax.ppermute, axis_name="ccol", perm=ring(not x_first, -1))
    far = far.astype(jnp.bfloat16)
    far_up = f32(to_next(far[:half]))
    far_down = f32(to_last(far[half:]))
    following = jnp.concatenate([following[:half] + far_up, following[half:]])
    last = jnp.concatenate([last[:half], last[half:] + far_down])
    up = f32(to_next(following.astype(jnp.bfloat16)))
    down = f32(to_last(last.astype(jnp.bfloat16)))
    return (here + up + down).astype(jnp.bfloat16)


def near_kernel(near_ref, before_ref, modes_ref, after_ref, basis_ref, out_ref, turned_ref, ext_ref):
    r = pl.program_id(0)
    halo, panels = before_ref.shape[0], modes_ref.shape[0]
    rank = basis_ref.shape[0]

    @pl.when(r == 0)
    def _():
        ext_ref[:halo] = before_ref[...]
        ext_ref[halo : halo + panels] = modes_ref[...]
        ext_ref[halo + panels :] = after_ref[...]

    window = ext_ref[pl.ds(pl.multiple_of(r * CS, CS), NEAR * CS), :]
    out_ref[...] = jnp.dot(near_ref[...], window, preferred_element_type=jnp.float32)
    have = lax.broadcasted_iota(jnp.int32, (rank, rank), 0)
    want = lax.broadcasted_iota(jnp.int32, (rank, rank), 1)
    order = jnp.where(want < rank // 2, 2 * want, 2 * want - rank + 1)
    select = jnp.where(order == have, 1.0, 0.0).astype(jnp.bfloat16)
    turned_ref[...] = lax.dot_general(
        basis_ref[...], select, (((0,), (0,)), ((), ())), preferred_element_type=jnp.float32
    ).astype(jnp.bfloat16)


def near_field(near_blocks, before, modes, after, row_basis):
    panels, band = near_blocks.shape
    cols = modes.shape[1]
    halo = before.shape[0]
    rank = row_basis.shape[0]
    return pl.pallas_call(
        near_kernel,
        grid=(panels // CS,),
        in_specs=[pl.BlockSpec((CS, band), lambda r: (r, 0))]
        + [whole()] * 3
        + [pl.BlockSpec((rank, CS), lambda r: (0, r))],
        out_specs=[
            pl.BlockSpec((CS, cols), lambda r: (r, 0)),
            pl.BlockSpec((CS, rank), lambda r: (r, 0)),
        ],
        out_shape=[
            jax.ShapeDtypeStruct((panels, cols), jnp.float32),
            jax.ShapeDtypeStruct((panels, rank), jnp.bfloat16),
        ],
        scratch_shapes=[VMEM((panels + 2 * halo, cols), jnp.bfloat16)],
        compiler_params=pltpu.CompilerParams(vmem_limit_bytes=32 * MIB),
        cost_estimate=pl.CostEstimate(
            flops=2 * panels * band * cols, bytes_accessed=18 * MIB, transcendentals=0
        ),
        name="near_field",
    )(near_blocks, before, modes, after, row_basis)


EXPAND = 2


def expand_kernel(near_ref, basis_ref, left_ref, right_ref, out_ref):
    width = left_ref.shape[2]
    for i in range(EXPAND):
        rows = pl.ds(i * CS, CS)
        for half, far_ref in enumerate((left_ref, right_ref)):
            cols = pl.ds(half * width, width)
            far = jnp.dot(basis_ref[rows, :], far_ref[i], preferred_element_type=jnp.float32)
            out_ref[rows, cols] = (near_ref[rows, cols] + far).astype(jnp.bfloat16)


def expand(near, basis, left, right):
    panels, cols = near.shape
    rank = basis.shape[1]
    width = cols // 2
    return pl.pallas_call(
        expand_kernel,
        grid=(panels // CS // EXPAND,),
        in_specs=[
            pl.BlockSpec((EXPAND * CS, cols), lambda r: (r, 0)),
            pl.BlockSpec((EXPAND * CS, rank), lambda r: (r, 0)),
            pl.BlockSpec((EXPAND, rank, width), lambda r: (r, 0, 0)),
            pl.BlockSpec((EXPAND, rank, width), lambda r: (r, 0, 0)),
        ],
        out_specs=pl.BlockSpec((EXPAND * CS, cols), lambda r: (r, 0)),
        out_shape=jax.ShapeDtypeStruct((panels, cols), jnp.bfloat16),
        compiler_params=pltpu.CompilerParams(vmem_limit_bytes=24 * MIB),
        cost_estimate=pl.CostEstimate(
            flops=2 * panels * rank * cols, bytes_accessed=7 * MIB, transcendentals=0
        ),
        name="expand",
    )(near, basis, left, right)


def per_device(modes, col_basis, row_basis, near_blocks, block_rows, block_owner, block_slot, cores):
    row_devices, col_devices = lax.axis_size("crow"), lax.axis_size("ccol")
    devices = row_devices * col_devices
    cluster_count = modes.shape[0] // CS
    rank = col_basis.shape[0]
    blocks = cores.shape[0]
    slots = CAP * row_devices

    compressed = compress(col_basis, modes)
    gathered = lax.all_gather(compressed, "crow", axis=0, tiled=True)

    edges, _ = lax.optimization_barrier((modes, compressed))
    up = [(i, i + 1) for i in range(devices - 1)]
    down = [(j, i) for i, j in up]
    before = lax.ppermute(edges[-NH * CS :], ("crow", "ccol"), up)
    after = lax.ppermute(edges[: NH * CS], ("crow", "ccol"), down)

    lines = rank * rank // 128
    sent = dispatch(
        block_rows, block_owner[:, 0], block_slot, cores.reshape(blocks, lines, 128),
        col_devices, slots, cluster_count,
    )
    sent = lax.all_to_all(sent, "ccol", split_axis=0, concat_axis=0, tiled=True)
    gathered, sent, before, after = lax.optimization_barrier((gathered, sent, before, after))
    group_rows = col_devices * cluster_count
    left = far_field(gathered, sent, slots, lines, group_rows, True)
    right = far_field(gathered, sent, slots, lines, group_rows, False)
    near, basis = near_field(near_blocks, before, modes, after, row_basis)
    return expand(near, basis, reduce_parts(left, True), reduce_parts(right, False))


def solution(mesh):
    both = ("crow", "ccol")
    in_specs = (
        P(both, None),
        P(None, both),
        P(None, both),
        P(both, None),
        P(both),
        P(both, None),
        P(both),
        P(both, None),
    )
    return jax.shard_map(
        per_device, mesh=mesh, in_specs=in_specs, out_specs=P(both, None), check_vma=False
    )
```

time: 227 us -> 181 us (0.80)
  starting transfers between devices: 5.98 us -> 49.1 us
  waiting for transfers between devices: 109 us -> 66.8 us
  blocking collectives: 37.1 us -> 0 us
  Pallas kernels: 48.8 us -> 42 us
  local copies, waits for them, and re-layouts: 9.86 us -> 3.86 us
    reduce_scatter x1 -> x0, waiting for transfers between devices: 65.6 us -> none  [per_device(): lax.psum_scatter(partial, 'ccol', scatter_dimension=0, tiled=True)]
    all_to_all x1 -> x0, blocking collectives: 37.1 us -> none  [per_device(): sent = lax.all_to_all(sent, 'ccol', split_axis=0, concat_axis=0, tiled=True)]
    ppermute x2 -> x22, starting transfers between devices: 5.9 us -> 40.9 us  [the longest x2 10 us: reduce_parts(): far_down = to_last(far[half:])]
    ppermute x2 -> x22, waiting for transfers between devices: 43.7 us -> 66.8 us  [the longest x1 40.4 us: per_device(): before = lax.ppermute(edges[-NH * CS:], ('crow', 'ccol'), up)]
    pallas_call x3 -> x4, Pallas kernels: 39.1 us -> 30.6 us  [the longest x2 25.4 us: far_field(): pl.pallas_call(functools.partial(far_kernel, slots, rows, x_first), grid=...]
    all_to_all x0 -> x1, starting transfers between devices: none -> 8.14 us  [per_device(): sent = lax.all_to_all(sent, 'ccol', split_axis=0, concat_axis=0, tiled=True)]
    unnamed x17 -> x25, local copies, waits for them, and re-layouts: 9.73 us -> 3.44 us
    another operation x0 -> x6, other arithmetic: none -> 2.59 us
  transfers between devices with their start and end apart: 4 -> 24, of which waited for: 3 -> 8; matrix products, arithmetic and copies ran while one was open for 0% -> 2% of each run, Pallas kernels for 4% -> 13%
where the time goes in v2:
time: 181 us; the launch traced here: 179 us
  waiting for transfers between devices  66.8 us (37%)
  starting transfers between devices  49.1 us (27%)
  Pallas kernels  42 us (23%)
  between operations  13.8 us (8%)
  local copies, waits for them, and re-layouts  3.86 us (2%)
  other arithmetic  3.43 us (2%)
    ppermute x1, waiting for transfers between devices, per_device(): before = lax.ppermute(edges[-NH * CS:], ('crow', 'ccol'), up)  40.4 us
    pallas_call x2, Pallas kernels, far_field(): pl.pallas_call(functools.partial(far_kernel, slots, rows, x_first), grid=...  25.4 us
    ppermute x2, starting transfers between devices, reduce_parts(): far_down = to_last(far[half:])  10 us
    ppermute x2, waiting for transfers between devices, reduce_parts(): far_up = to_next(far[:half])  9.28 us
    all_to_all x1, starting transfers between devices, per_device(): sent = lax.all_to_all(sent, 'ccol', split_axis=0, concat_axis=0, tiled=True)  8.14 us
    ppermute x2, waiting for transfers between devices, reduce_parts(): up = f32(to_next((following_sum + f32(far_up)).astype(jnp.bfloat16)))  8.07 us
    pallas_call x1, Pallas kernels, near_field(): pl.pallas_call(near_kernel, grid=(panels // CS,), in_specs=[pl.BlockSpec(...  6.79 us
    ppermute x2, starting transfers between devices, reduce_parts(): down = f32(to_last(last.astype(jnp.bfloat16)))  6.57 us
  transfers between devices with their start and end apart: 24, of which 8 were waited for; matrix products, arithmetic and copies ran while one was open for 2% of the time, Pallas kernels for 13%

profile of v2, /device:TPU:0, one launch (start us, length us, event | category | flops | bytes accessed | tf_op | source)
XLA Modules:
  0.0 179.0 jit_solution(5116047018911489160)
XLA Ops:
  6.6 2.7 %compress.1 = bf16[8,64,512]{2,1,0:T(8,128)(2,1)} custom-call(bf16[64,2048]{1,0:T(8,128)(2,1)} %basis_ref.2, bf16[2048,512]{1,0:T(8,128)(2,1)} %modes_ref.3), custom_call_target="tpu_custom_call" | custom-call | flops 134217728 | bytes 3145728 | tf_op jit(solution)/shard_map/compress/pallas_call | solution.py:39
  9.6 4.7 %dispatch.1 = bf16[16,528,128]{2,1,0:T(8,128)(2,1)} custom-call(s32[128]{0:T(128)S(1)} %copy-done.1, s32[128]{0:T(128)S(1)} %bitcast.4, s32[128]{0:T(128)S(1)} %copy-done.3, bf16[128,32,128]{2,1,0:T(8,128)(2,1)S(1)} %bitcast.3), custom_call_target="tpu_custom_call" | custom-call | flops 4194304 | bytes 3145728 | tf_op jit(solution)/shard_map/dispatch/pallas_call | solution.py:89
  14.3 8.1 %all-to-all-start = ((bf16[16,528,128]{2,1,0:T(8,128)(2,1)}), bf16[16,528,128]{2,1,0:T(8,128)(2,1)}, u32[]{:S(2)}, u32[]{:S(2)}) async-start(bf16[16,528,128]{2,1,0:T(8,128)(2,1)} %dispatch.1), calls=%async_computation | async-start | bytes 4325376 | tf_op jit(solution)/shard_map/all_to_all | solution.py:350
  22.6 3.8 %collective-permute-start = (bf16[1024,512]{1,0:T(8,128)(2,1)S(1)}, bf16[1024,512]{1,0:T(8,128)(2,1)S(1)}, u32[]{:S(2)}, u32[]{:S(2)}) collective-permute-start(bf16[1024,512]{1,0:T(8,128)(2,1)S(1)} %get-tuple-element.50), channel_id=1, source_target_pairs={{0,1},{1,2},{2,3},{3,4},{4,5},{5,6},{6,7},{7,8},{8,9},{9,10},{10,1... | collective-permute-start | bytes 3145736 | tf_op jit(solution)/shard_map/ppermute | solution.py:342
  27.7 40.4 %collective-permute-done.before_ref = bf16[1024,512]{1,0:T(8,128)(2,1)S(1)} collective-permute-done((bf16[1024,512]{1,0:T(8,128)(2,1)S(1)}, bf16[1024,512]{1,0:T(8,128)(2,1)S(1)}, u32[]{:S(2)}, u32[]{:S(2)}) %collective-permute-start) | collective-permute-done | bytes 1048608 | tf_op jit(solution)/shard_map/ppermute | solution.py:342
  68.1 2.2 %collective-permute-done.1.after_ref = bf16[1024,512]{1,0:T(8,128)(2,1)S(1)} collective-permute-done((bf16[1024,512]{1,0:T(8,128)(2,1)S(1)}, bf16[1024,512]{1,0:T(8,128)(2,1)S(1)}, u32[]{:S(2)}, u32[]{:S(2)}) %collective-permute-start.1) | collective-permute-done | bytes 1048608 | tf_op jit(solution)/shard_map/ppermute | solution.py:343
  71.3 2.2 %copy-done.4 = bf16[64,64,512]{2,1,0:T(8,128)(2,1)S(1)} copy-done((bf16[64,64,512]{2,1,0:T(8,128)(2,1)S(1)}, bf16[64,64,512]{2,1,0:T(8,128)(2,1)}, u32[]{:S(2)}) %copy-start.4) | copy-done | bytes 4194328
  73.5 12.7 %far_z.1 = (bf16[32,64,256]{2,1,0:T(8,128)(2,1)S(1)}, bf16[16,64,256]{2,1,0:T(8,128)(2,1)S(1)}, bf16[16,64,256]{2,1,0:T(8,128)(2,1)S(1)}, f32[16,64,256]{2,1,0:T...) custom-call(bf16[64,64,512]{2,1,0:T(8,128)(2,1)S(1)} %copy-done.4, ...), custom_call_target="tpu_custom_call" | custom-call | flops 2147483648 | bytes 12582912 | tf_op jit(solution)/shard_map/far_z/pallas_call | solution.py:177
  86.7 3.8 %collective-permute-start.16 = (bf16[16,64,256]{2,1,0:T(8,128)(2,1)S(1)}, bf16[16,64,256]{2,1,0:T(8,128)(2,1)S(1)}, u32[]{:S(2)}, u32[]{:S(2)}) collective-permute-start(bf16[16,64,256]{2,1,0:T(8,128)(2,1)S(1)} %get-tuple-element.51), channel_id=1, source_target_pairs={{0,3},{1,0},{2,1},{3,2},{4,7},{5,4},{6,5},{7,6},{8,11},{9,8},{10,9... | collective-permute-start | bytes 1572872 | tf_op jit(solution)/shard_map/ppermute | solution.py:219
  90.4 1.9 %collective-permute-start.12 = (bf16[16,64,256]{2,1,0:T(8,128)(2,1)S(1)}, bf16[16,64,256]{2,1,0:T(8,128)(2,1)}, u32[]{:S(2)}, u32[]{:S(2)}) collective-permute-start(bf16[16,64,256]{2,1,0:T(8,128)(2,1)S(1)} %get-tuple-element.38), channel_id=1, source_target_pairs={{0,3},{1,0},{2,1},{3,2},{4,7},{5,4},{6,5},{7,6},{8,11},{9,8},{10,9... | collective-permute-start | bytes 1572872 | tf_op jit(solution)/shard_map/ppermute | solution.py:221
  92.4 12.7 %far_x.1 = (bf16[32,64,256]{2,1,0:T(8,128)(2,1)S(1)}, bf16[16,64,256]{2,1,0:T(8,128)(2,1)S(1)}, bf16[16,64,256]{2,1,0:T(8,128)(2,1)S(1)}, f32[16,64,256]{2,1,0:T...) custom-call(bf16[64,64,512]{2,1,0:T(8,128)(2,1)S(1)} %copy-done.4, ...), custom_call_target="tpu_custom_call" | custom-call | flops 2147483648 | bytes 12582912 | tf_op jit(solution)/shard_map/far_x/pallas_call | solution.py:177
  105.3 2.1 %collective-permute-start.3 = (bf16[16,64,256]{2,1,0:T(8,128)(2,1)S(1)}, bf16[16,64,256]{2,1,0:T(8,128)(2,1)S(1)}, u32[]{:S(2)}, u32[]{:S(2)}) collective-permute-start(bf16[16,64,256]{2,1,0:T(8,128)(2,1)S(1)} %get-tuple-element.54), channel_id=1, source_target_pairs={{0,4},{1,5},{2,6},{3,7},{4,8},{5,9},{6,10},{7,11},{8,12},{9,13},{1... | collective-permute-start | bytes 1572872 | tf_op jit(solution)/shard_map/ppermute | solution.py:218
  107.4 6.3 %collective-permute-start.6 = (bf16[16,64,256]{2,1,0:T(8,128)(2,1)S(1)}, bf16[16,64,256]{2,1,0:T(8,128)(2,1)S(1)}, u32[]{:S(2)}, u32[]{:S(2)}) collective-permute-start(bf16[16,64,256]{2,1,0:T(8,128)(2,1)S(1)} %get-tuple-element.53), channel_id=1, source_target_pairs={{0,12},{1,13},{2,14},{3,15},{4,0},{5,1},{6,2},{7,3},{8,4},{9,5},{1... | collective-permute-start | bytes 1572872 | tf_op jit(solution)/shard_map/ppermute | solution.py:219
  114.0 9.3 %collective-permute-done.3 = bf16[16,64,256]{2,1,0:T(8,128)(2,1)S(1)} collective-permute-done((bf16[16,64,256]{2,1,0:T(8,128)(2,1)S(1)}, bf16[16,64,256]{2,1,0:T(8,128)(2,1)S(1)}, u32[]{:S(2)}, u32[]{:S(2)}) %collective-permute-start.3) | collective-permute-done | bytes 524320 | tf_op jit(solution)/shard_map/ppermute | solution.py:218
  123.4 2.9 %collective-permute-start.2 = (bf16[16,64,256]{2,1,0:T(8,128)(2,1)S(1)}, bf16[16,64,256]{2,1,0:T(8,128)(2,1)S(1)}, u32[]{:S(2)}, u32[]{:S(2)}) collective-permute-start(bf16[16,64,256]{2,1,0:T(8,128)(2,1)S(1)} %get-tuple-element.32), channel_id=1, source_target_pairs={{0,12},{1,13},{2,14},{3,15},{4,0},{5,1},{6,2},{7,3},{8,4},{9,5},{1... | collective-permute-start | bytes 1572872 | tf_op jit(solution)/shard_map/ppermute | solution.py:221
  127.1 2.7 %collective-permute-start.7 = (bf16[16,64,256]{2,1,0:T(8,128)(2,1)S(1)}, bf16[16,64,256]{2,1,0:T(8,128)(2,1)S(1)}, u32[]{:S(2)}, u32[]{:S(2)}) collective-permute-start(bf16[16,64,256]{2,1,0:T(8,128)(2,1)S(1)} %add_convert_fusion.2), channel_id=1, source_target_pairs={{0,12},{1,13},{2,14},{3,15},{4,0},{5,1},{6,2},{7,3},{8,4},{9,5},{1... | collective-permute-start | bytes 1572872 | tf_op jit(solution)/shard_map/ppermute | solution.py:223
  129.9 4.3 %collective-permute-done.17 = bf16[16,64,256]{2,1,0:T(8,128)(2,1)S(1)} collective-permute-done((bf16[16,64,256]{2,1,0:T(8,128)(2,1)S(1)}, bf16[16,64,256]{2,1,0:T(8,128)(2,1)S(1)}, u32[]{:S(2)}, u32[]{:S(2)}) %collective-permute-start.17) | collective-permute-done | bytes 524320 | tf_op jit(solution)/shard_map/ppermute | solution.py:223
  138.7 3.7 %collective-permute-start.20 = (bf16[4,64,256]{2,1,0:T(8,128)(2,1)S(1)}, bf16[4,64,256]{2,1,0:T(8,128)(2,1)S(1)}, u32[]{:S(2)}, u32[]{:S(2)}) collective-permute-start(bf16[4,64,256]{2,1,0:T(8,128)(2,1)S(1)} %get-tuple-element.56), channel_id=1, source_target_pairs={{0,12},{1,13},{2,14},{3,15},{4,0},{5,1},{6,2},{7,3},{8,4},{9,5},{1... | collective-permute-start | bytes 393224 | tf_op jit(solution)/shard_map/ppermute | solution.py:234
  142.6 8.1 %collective-permute-done.4 = bf16[16,64,256]{2,1,0:T(8,128)(2,1)S(1)} collective-permute-done((bf16[16,64,256]{2,1,0:T(8,128)(2,1)S(1)}, bf16[16,64,256]{2,1,0:T(8,128)(2,1)S(1)}, u32[]{:S(2)}, u32[]{:S(2)}) %collective-permute-start.4) | collective-permute-done | bytes 524320 | tf_op jit(solution)/shard_map/ppermute | solution.py:222
  152.2 2.6 %collective-permute-start.10 = (bf16[4,64,256]{2,1,0:T(8,128)(2,1)S(1)}, bf16[4,64,256]{2,1,0:T(8,128)(2,1)S(1)}, u32[]{:S(2)}, u32[]{:S(2)}) collective-permute-start(bf16[4,64,256]{2,1,0:T(8,128)(2,1)S(1)} %get-tuple-element.59), channel_id=1, source_target_pairs={{0,3},{1,0},{2,1},{3,2},{4,7},{5,4},{6,5},{7,6},{8,11},{9,8},{10,9... | collective-permute-start | bytes 393224 | tf_op jit(solution)/shard_map/ppermute | solution.py:234
  155.1 3.3 %collective-permute-start.21 = (bf16[8,64,256]{2,1,0:T(8,128)(2,1)S(1)}, bf16[8,64,256]{2,1,0:T(8,128)(2,1)S(1)}, u32[]{:S(2)}, u32[]{:S(2)}) collective-permute-start(bf16[8,64,256]{2,1,0:T(8,128)(2,1)S(1)} %pad_maximum_fusion.3), channel_id=1, source_target_pairs={{0,12},{1,13},{2,14},{3,15},{4,0},{5,1},{6,2},{7,3},{8,4},{9,5},{1... | collective-permute-start | bytes 786440 | tf_op jit(solution)/shard_map/ppermute | solution.py:238
  159.3 3.3 %collective-permute-start.11 = (bf16[8,64,256]{2,1,0:T(8,128)(2,1)S(1)}, bf16[8,64,256]{2,1,0:T(8,128)(2,1)S(1)}, u32[]{:S(2)}, u32[]{:S(2)}) collective-permute-start(bf16[8,64,256]{2,1,0:T(8,128)(2,1)S(1)} %pad_maximum_fusion.1), channel_id=1, source_target_pairs={{0,3},{1,0},{2,1},{3,2},{4,7},{5,4},{6,5},{7,6},{8,11},{9,8},{10,9... | collective-permute-start | bytes 786440 | tf_op jit(solution)/shard_map/ppermute | solution.py:238
  162.7 6.8 %near_field.1 = (f32[2048,512]{1,0:T(8,128)S(1)}, bf16[2048,64]{1,0:T(8,128)(2,1)S(1)}) custom-call(bf16[2048,2304]{1,0:T(8,128)(2,1)S(1)} %bitcast.6, bf16[1024,512]{1,0:T(8,128)(2,1)S(1)} %collective-permute-done.before_ref, bf16[2048,512]{1,0:T(8,128)(2,1)S(1)} %copy-done, bf16[1024,512]{1,0:T(8,128)(2,1)S(1)} %copy-done.6, bf16[64,2048]{1,0:T(8,128)(2,1)S(1)} %copy-done.7), custom_call_target="tpu_custom_call" | custom-call | flops 4831838208 | bytes 18874368 | tf_op jit(solution)/shard_map/near_field/pallas_call | solution.py:269
  169.7 2.4 %expand.1 = bf16[2048,512]{1,0:T(8,128)(2,1)} custom-call(f32[2048,512]{1,0:T(8,128)S(1)} %get-tuple-element.27.near_ref, bf16[2048,64]{1,0:T(8,128)(2,1)S(1)} %get-tuple-element.28.basis_ref, bf16[8,64,256]{2,1,0:T(8,128)(2,1)S(1)} %fusion.3.left_ref, bf16[8,64,256]{2,1,0:T(8,128)(2,1)S(1)} %fusion.1.right_ref), custom_call_target="tpu_custom_call" | custom-call | flops 134217728 | bytes 7340032 | tf_op jit(solution)/shard_map/expand/pallas_call | solution.py:309
  (80 shorter events, 12.3 us)
Async XLA Ops:
  6.5 64.7 %all-gather.2.cloned.1.call-start = ((), (), s32[]{:S(2)}) async-start(), calls=%async_computation.1 | async-start | bytes 4718592 | tf_op jit(solution)/shard_map/all_gather | solution.py:337
  14.3 57.0 %all-to-all-start = ((bf16[16,528,128]{2,1,0:T(8,128)(2,1)}), bf16[16,528,128]{2,1,0:T(8,128)(2,1)}, u32[]{:S(2)}, u32[]{:S(2)}) async-start(bf16[16,528,128]{2,1,0:T(8,128)(2,1)} %dispatch.1), calls=%async_computation | async-start | bytes 4325376 | tf_op jit(solution)/shard_map/all_to_all | solution.py:350
  22.6 45.5 %collective-permute-start = (bf16[1024,512]{1,0:T(8,128)(2,1)S(1)}, bf16[1024,512]{1,0:T(8,128)(2,1)S(1)}, u32[]{:S(2)}, u32[]{:S(2)}) collective-permute-start(bf16[1024,512]{1,0:T(8,128)(2,1)S(1)} %get-tuple-element.50), channel_id=1, source_target_pairs={{0,1},{1,2},{2,3},{3,4},{4,5},{5,6},{6,7},{7,8},{8,9},{9,10},{10,1... | collective-permute-start | bytes 3145736 | tf_op jit(solution)/shard_map/ppermute | solution.py:342
  26.4 43.8 %collective-permute-start.1 = (bf16[1024,512]{1,0:T(8,128)(2,1)S(1)}, bf16[1024,512]{1,0:T(8,128)(2,1)S(1)}, u32[]{:S(2)}, u32[]{:S(2)}) collective-permute-start(bf16[1024,512]{1,0:T(8,128)(2,1)S(1)} %get-tuple-element.49), channel_id=1, source_target_pairs={{1,0},{2,1},{3,2},{4,3},{5,4},{6,5},{7,6},{8,7},{9,8},{10,9},{11,1... | collective-permute-start | bytes 3145736 | tf_op jit(solution)/shard_map/ppermute | solution.py:343
  86.3 21.1 %collective-permute-start.13 = (bf16[16,64,256]{2,1,0:T(8,128)(2,1)S(1)}, bf16[16,64,256]{2,1,0:T(8,128)(2,1)S(1)}, u32[]{:S(2)}, u32[]{:S(2)}) collective-permute-start(bf16[16,64,256]{2,1,0:T(8,128)(2,1)S(1)} %get-tuple-element.52), channel_id=1, source_target_pairs={{0,1},{1,2},{2,3},{3,0},{4,5},{5,6},{6,7},{7,4},{8,9},{9,10},{10,1... | collective-permute-start | bytes 1572872 | tf_op jit(solution)/shard_map/ppermute | solution.py:218
  86.7 27.1 %collective-permute-start.16 = (bf16[16,64,256]{2,1,0:T(8,128)(2,1)S(1)}, bf16[16,64,256]{2,1,0:T(8,128)(2,1)S(1)}, u32[]{:S(2)}, u32[]{:S(2)}) collective-permute-start(bf16[16,64,256]{2,1,0:T(8,128)(2,1)S(1)} %get-tuple-element.51), channel_id=1, source_target_pairs={{0,3},{1,0},{2,1},{3,2},{4,7},{5,4},{6,5},{7,6},{8,11},{9,8},{10,9... | collective-permute-start | bytes 1572872 | tf_op jit(solution)/shard_map/ppermute | solution.py:219
  90.4 36.0 %collective-permute-start.12 = (bf16[16,64,256]{2,1,0:T(8,128)(2,1)S(1)}, bf16[16,64,256]{2,1,0:T(8,128)(2,1)}, u32[]{:S(2)}, u32[]{:S(2)}) collective-permute-start(bf16[16,64,256]{2,1,0:T(8,128)(2,1)S(1)} %get-tuple-element.38), channel_id=1, source_target_pairs={{0,3},{1,0},{2,1},{3,2},{4,7},{5,4},{6,5},{7,6},{8,11},{9,8},{10,9... | collective-permute-start | bytes 1572872 | tf_op jit(solution)/shard_map/ppermute | solution.py:221
  92.4 34.2 %collective-permute-start.15 = (bf16[16,64,256]{2,1,0:T(8,128)(2,1)S(1)}, bf16[16,64,256]{2,1,0:T(8,128)(2,1)}, u32[]{:S(2)}, u32[]{:S(2)}) collective-permute-start(bf16[16,64,256]{2,1,0:T(8,128)(2,1)S(1)} %get-tuple-element.41), channel_id=1, source_target_pairs={{0,1},{1,2},{2,3},{3,0},{4,5},{5,6},{6,7},{7,4},{8,9},{9,10},{10,1... | collective-permute-start | bytes 1572872 | tf_op jit(solution)/shard_map/ppermute | solution.py:220
  105.3 18.0 %collective-permute-start.3 = (bf16[16,64,256]{2,1,0:T(8,128)(2,1)S(1)}, bf16[16,64,256]{2,1,0:T(8,128)(2,1)S(1)}, u32[]{:S(2)}, u32[]{:S(2)}) collective-permute-start(bf16[16,64,256]{2,1,0:T(8,128)(2,1)S(1)} %get-tuple-element.54), channel_id=1, source_target_pairs={{0,4},{1,5},{2,6},{3,7},{4,8},{5,9},{6,10},{7,11},{8,12},{9,13},{1... | collective-permute-start | bytes 1572872 | tf_op jit(solution)/shard_map/ppermute | solution.py:218
  107.4 16.1 %collective-permute-start.6 = (bf16[16,64,256]{2,1,0:T(8,128)(2,1)S(1)}, bf16[16,64,256]{2,1,0:T(8,128)(2,1)S(1)}, u32[]{:S(2)}, u32[]{:S(2)}) collective-permute-start(bf16[16,64,256]{2,1,0:T(8,128)(2,1)S(1)} %get-tuple-element.53), channel_id=1, source_target_pairs={{0,12},{1,13},{2,14},{3,15},{4,0},{5,1},{6,2},{7,3},{8,4},{9,5},{1... | collective-permute-start | bytes 1572872 | tf_op jit(solution)/shard_map/ppermute | solution.py:219
  113.8 13.4 %collective-permute-start.14 = (bf16[16,64,256]{2,1,0:T(8,128)(2,1)S(1)}, bf16[16,64,256]{2,1,0:T(8,128)(2,1)S(1)}, u32[]{:S(2)}, u32[]{:S(2)}) collective-permute-start(bf16[16,64,256]{2,1,0:T(8,128)(2,1)S(1)} %add_convert_fusion.1), channel_id=1, source_target_pairs={{0,1},{1,2},{2,3},{3,0},{4,5},{5,6},{6,7},{7,4},{8,9},{9,10},{10,1... | collective-permute-start | bytes 1572872 | tf_op jit(solution)/shard_map/ppermute | solution.py:222
  123.3 10.9 %collective-permute-start.17 = (bf16[16,64,256]{2,1,0:T(8,128)(2,1)S(1)}, bf16[16,64,256]{2,1,0:T(8,128)(2,1)S(1)}, u32[]{:S(2)}, u32[]{:S(2)}) collective-permute-start(bf16[16,64,256]{2,1,0:T(8,128)(2,1)S(1)} %add_convert_fusion), channel_id=1, source_target_pairs={{0,3},{1,0},{2,1},{3,2},{4,7},{5,4},{6,5},{7,6},{8,11},{9,8},{10,9... | collective-permute-start | bytes 1572872 | tf_op jit(solution)/shard_map/ppermute | solution.py:223
  123.4 15.3 %collective-permute-start.2 = (bf16[16,64,256]{2,1,0:T(8,128)(2,1)S(1)}, bf16[16,64,256]{2,1,0:T(8,128)(2,1)S(1)}, u32[]{:S(2)}, u32[]{:S(2)}) collective-permute-start(bf16[16,64,256]{2,1,0:T(8,128)(2,1)S(1)} %get-tuple-element.32), channel_id=1, source_target_pairs={{0,12},{1,13},{2,14},{3,15},{4,0},{5,1},{6,2},{7,3},{8,4},{9,5},{1... | collective-permute-start | bytes 1572872 | tf_op jit(solution)/shard_map/ppermute | solution.py:221
  126.5 16.1 %collective-permute-start.5 = (bf16[16,64,256]{2,1,0:T(8,128)(2,1)S(1)}, bf16[16,64,256]{2,1,0:T(8,128)(2,1)S(1)}, u32[]{:S(2)}, u32[]{:S(2)}) collective-permute-start(bf16[16,64,256]{2,1,0:T(8,128)(2,1)S(1)} %get-tuple-element.35), channel_id=1, source_target_pairs={{0,4},{1,5},{2,6},{3,7},{4,8},{5,9},{6,10},{7,11},{8,12},{9,13},{1... | collective-permute-start | bytes 1572872 | tf_op jit(solution)/shard_map/ppermute | solution.py:220
  126.6 24.1 %collective-permute-start.4 = (bf16[16,64,256]{2,1,0:T(8,128)(2,1)S(1)}, bf16[16,64,256]{2,1,0:T(8,128)(2,1)S(1)}, u32[]{:S(2)}, u32[]{:S(2)}) collective-permute-start(bf16[16,64,256]{2,1,0:T(8,128)(2,1)S(1)} %add_convert_fusion.3), channel_id=1, source_target_pairs={{0,4},{1,5},{2,6},{3,7},{4,8},{5,9},{6,10},{7,11},{8,12},{9,13},{1... | collective-permute-start | bytes 1572872 | tf_op jit(solution)/shard_map/ppermute | solution.py:222
  127.1 23.5 %collective-permute-start.7 = (bf16[16,64,256]{2,1,0:T(8,128)(2,1)S(1)}, bf16[16,64,256]{2,1,0:T(8,128)(2,1)S(1)}, u32[]{:S(2)}, u32[]{:S(2)}) collective-permute-start(bf16[16,64,256]{2,1,0:T(8,128)(2,1)S(1)} %add_convert_fusion.2), channel_id=1, source_target_pairs={{0,12},{1,13},{2,14},{3,15},{4,0},{5,1},{6,2},{7,3},{8,4},{9,5},{1... | collective-permute-start | bytes 1572872 | tf_op jit(solution)/shard_map/ppermute | solution.py:223
  136.1 18.8 %collective-permute-start.18 = (bf16[4,64,256]{2,1,0:T(8,128)(2,1)S(1)}, bf16[4,64,256]{2,1,0:T(8,128)(2,1)S(1)}, u32[]{:S(2)}, u32[]{:S(2)}) collective-permute-start(bf16[4,64,256]{2,1,0:T(8,128)(2,1)S(1)} %get-tuple-element.55), channel_id=1, source_target_pairs={{0,4},{1,5},{2,6},{3,7},{4,8},{5,9},{6,10},{7,11},{8,12},{9,13},{1... | collective-permute-start | bytes 393224 | tf_op jit(solution)/shard_map/ppermute | solution.py:233
  138.7 16.3 %collective-permute-start.20 = (bf16[4,64,256]{2,1,0:T(8,128)(2,1)S(1)}, bf16[4,64,256]{2,1,0:T(8,128)(2,1)S(1)}, u32[]{:S(2)}, u32[]{:S(2)}) collective-permute-start(bf16[4,64,256]{2,1,0:T(8,128)(2,1)S(1)} %get-tuple-element.56), channel_id=1, source_target_pairs={{0,12},{1,13},{2,14},{3,15},{4,0},{5,1},{6,2},{7,3},{8,4},{9,5},{1... | collective-permute-start | bytes 393224 | tf_op jit(solution)/shard_map/ppermute | solution.py:234
  151.3 7.8 %collective-permute-start.8 = (bf16[4,64,256]{2,1,0:T(8,128)(2,1)S(1)}, bf16[4,64,256]{2,1,0:T(8,128)(2,1)S(1)}, u32[]{:S(2)}, u32[]{:S(2)}) collective-permute-start(bf16[4,64,256]{2,1,0:T(8,128)(2,1)S(1)} %get-tuple-element.58), channel_id=1, source_target_pairs={{0,1},{1,2},{2,3},{3,0},{4,5},{5,6},{6,7},{7,4},{8,9},{9,10},{10,1... | collective-permute-start | bytes 393224 | tf_op jit(solution)/shard_map/ppermute | solution.py:233
  152.2 7.0 %collective-permute-start.10 = (bf16[4,64,256]{2,1,0:T(8,128)(2,1)S(1)}, bf16[4,64,256]{2,1,0:T(8,128)(2,1)S(1)}, u32[]{:S(2)}, u32[]{:S(2)}) collective-permute-start(bf16[4,64,256]{2,1,0:T(8,128)(2,1)S(1)} %get-tuple-element.59), channel_id=1, source_target_pairs={{0,3},{1,0},{2,1},{3,2},{4,7},{5,4},{6,5},{7,6},{8,11},{9,8},{10,9... | collective-permute-start | bytes 393224 | tf_op jit(solution)/shard_map/ppermute | solution.py:234
  155.0 14.5 %collective-permute-start.19 = (bf16[8,64,256]{2,1,0:T(8,128)(2,1)S(1)}, bf16[8,64,256]{2,1,0:T(8,128)(2,1)S(1)}, u32[]{:S(2)}, u32[]{:S(2)}) collective-permute-start(bf16[8,64,256]{2,1,0:T(8,128)(2,1)S(1)} %pad_maximum_fusion.2), channel_id=1, source_target_pairs={{0,4},{1,5},{2,6},{3,7},{4,8},{5,9},{6,10},{7,11},{8,12},{9,13},{1... | collective-permute-start | bytes 786440 | tf_op jit(solution)/shard_map/ppermute | solution.py:237
  155.1 14.4 %collective-permute-start.21 = (bf16[8,64,256]{2,1,0:T(8,128)(2,1)S(1)}, bf16[8,64,256]{2,1,0:T(8,128)(2,1)S(1)}, u32[]{:S(2)}, u32[]{:S(2)}) collective-permute-start(bf16[8,64,256]{2,1,0:T(8,128)(2,1)S(1)} %pad_maximum_fusion.3), channel_id=1, source_target_pairs={{0,12},{1,13},{2,14},{3,15},{4,0},{5,1},{6,2},{7,3},{8,4},{9,5},{1... | collective-permute-start | bytes 786440 | tf_op jit(solution)/shard_map/ppermute | solution.py:238
  159.2 10.4 %collective-permute-start.9 = (bf16[8,64,256]{2,1,0:T(8,128)(2,1)S(1)}, bf16[8,64,256]{2,1,0:T(8,128)(2,1)S(1)}, u32[]{:S(2)}, u32[]{:S(2)}) collective-permute-start(bf16[8,64,256]{2,1,0:T(8,128)(2,1)S(1)} %pad_maximum_fusion), channel_id=1, source_target_pairs={{0,1},{1,2},{2,3},{3,0},{4,5},{5,6},{6,7},{7,4},{8,9},{9,10},{10,1... | collective-permute-start | bytes 786440 | tf_op jit(solution)/shard_map/ppermute | solution.py:237
  159.3 10.3 %collective-permute-start.11 = (bf16[8,64,256]{2,1,0:T(8,128)(2,1)S(1)}, bf16[8,64,256]{2,1,0:T(8,128)(2,1)S(1)}, u32[]{:S(2)}, u32[]{:S(2)}) collective-permute-start(bf16[8,64,256]{2,1,0:T(8,128)(2,1)S(1)} %pad_maximum_fusion.1), channel_id=1, source_target_pairs={{0,3},{1,0},{2,1},{3,2},{4,7},{5,4},{6,5},{7,6},{8,11},{9,8},{10,9... | collective-permute-start | bytes 786440 | tf_op jit(solution)/shard_map/ppermute | solution.py:238
  (12 other events, 113.1 us)
Sparse Core Ops, SparseCore 0:
  9.5 34.5 all-gather.1

commit v3 on v2

--- a/solution.py
+++ b/solution.py
@@ -210,19 +210,25 @@
     return value.astype(jnp.float32)
 
 
-def reduce_parts(parts, x_first):
+def first_stage(parts, x_first):
     far, following, last, following_sum, last_sum, own = parts
     half = far.shape[0] // 2
     to_next = functools.partial(lax.ppermute, axis_name="ccol", perm=ring(x_first, 1))
     to_last = functools.partial(lax.ppermute, axis_name="ccol", perm=ring(x_first, -1))
     far_up = to_next(far[:half])
     far_down = to_last(far[half:])
-    own_b = f32(to_next(following))
-    own_a = f32(to_last(last))
-    up = f32(to_next((following_sum + f32(far_up)).astype(jnp.bfloat16)))
-    down = f32(to_last((last_sum + f32(far_down)).astype(jnp.bfloat16)))
-    first = own[:half] + own_a + up
-    second = own[half:] + own_b + down
+    own_b = to_next(following)
+    own_a = to_last(last)
+    up = to_next((following_sum + f32(far_up)).astype(jnp.bfloat16))
+    down = to_last((last_sum + f32(far_down)).astype(jnp.bfloat16))
+    return own, own_a, own_b, up, down
+
+
+def second_stage(arrived, x_first):
+    own, own_a, own_b, up, down = arrived
+    half = own_a.shape[0]
+    first = own[:half] + f32(own_a) + f32(up)
+    second = own[half:] + f32(own_b) + f32(down)
     quarter = half // 2
     here, following, far, last = first[:quarter], first[quarter:], second[:quarter], second[quarter:]
 
@@ -336,24 +342,29 @@
     compressed = compress(col_basis, modes)
     gathered = lax.all_gather(compressed, "crow", axis=0, tiled=True)
 
-    edges, _ = lax.optimization_barrier((modes, compressed))
-    up = [(i, i + 1) for i in range(devices - 1)]
-    down = [(j, i) for i, j in up]
-    before = lax.ppermute(edges[-NH * CS :], ("crow", "ccol"), up)
-    after = lax.ppermute(edges[: NH * CS], ("crow", "ccol"), down)
-
     lines = rank * rank // 128
     sent = dispatch(
         block_rows, block_owner[:, 0], block_slot, cores.reshape(blocks, lines, 128),
         col_devices, slots, cluster_count,
     )
     sent = lax.all_to_all(sent, "ccol", split_axis=0, concat_axis=0, tiled=True)
-    gathered, sent, before, after = lax.optimization_barrier((gathered, sent, before, after))
+
+    edges, sent = lax.optimization_barrier((modes, sent))
+    up = [(i, i + 1) for i in range(devices - 1)]
+    down = [(j, i) for i, j in up]
+    before = lax.ppermute(edges[-NH * CS :], ("crow", "ccol"), up)
+    after = lax.ppermute(edges[: NH * CS], ("crow", "ccol"), down)
+
     group_rows = col_devices * cluster_count
-    left = far_field(gathered, sent, slots, lines, group_rows, True)
-    right = far_field(gathered, sent, slots, lines, group_rows, False)
+    left = list(far_field(gathered, sent, slots, lines, group_rows, True))
+    gathered, sent, left[0] = lax.optimization_barrier((gathered, sent, left[0]))
+    right = list(far_field(gathered, sent, slots, lines, group_rows, False))
+    right[0], before, after = lax.optimization_barrier((right[0], before, after))
     near, basis = near_field(near_blocks, before, modes, after, row_basis)
-    return expand(near, basis, reduce_parts(left, True), reduce_parts(right, False))
+    left = first_stage(left, True)
+    right = first_stage(right, False)
+    left, near, basis = lax.optimization_barrier((left, near, basis))
+    return expand(near, basis, second_stage(left, True), second_stage(right, False))
 
 
 def solution(mesh):

time: 181 us -> 171 us (0.945)
  blocking collectives: 0 us -> 37.3 us
  waiting for transfers between devices: 66.8 us -> 32.8 us
  starting transfers between devices: 49.1 us -> 32.6 us
  local copies, waits for them, and re-layouts: 3.86 us -> 11.1 us
  Pallas kernels: 42 us -> 38.1 us
    ppermute x1, waiting for transfers between devices: 40.4 us -> 0.01 us  [per_device(): before = lax.ppermute(edges[-NH * CS:], ('crow', 'ccol'), up)]
    all_to_all x0 -> x1, blocking collectives: none -> 37.3 us  [per_device(): sent = lax.all_to_all(sent, 'ccol', split_axis=0, concat_axis=0, tiled=True)]
    ppermute x20, waiting for transfers between devices: 24.2 us -> 32.7 us  [the longest x2 10 us: first_stage(): down = to_last((last_sum + f32(far_down)).astype(jnp.bfloat16))]
    all_to_all x1 -> x0, starting transfers between devices: 8.14 us -> none  [per_device(): sent = lax.all_to_all(sent, 'ccol', split_axis=0, concat_axis=0, tiled=True)]
    ppermute x20, starting transfers between devices: 35.8 us -> 28.8 us  [the longest x2 7.61 us: first_stage(): own_a = to_last(last)]
    unnamed x25 -> x19, local copies, waits for them, and re-layouts: 3.44 us -> 8.38 us
    pallas_call x2, Pallas kernels: 25.4 us -> 21.8 us  [far_field(): pl.pallas_call(functools.partial(far_kernel, slots, rows, x_first), grid=...]
    ppermute x1, waiting for transfers between devices: 2.16 us -> 0.01 us  [per_device(): after = lax.ppermute(edges[:NH * CS], ('crow', 'ccol'), down)]
  transfers between devices with their start and end apart: 24 -> 23, of which waited for: 8 -> 7; matrix products, arithmetic and copies ran while one was open for 2% -> 4% of each run, Pallas kernels for 13% -> 19%
where the time goes in v3:
time: 171 us; the launch traced here: 170 us
  Pallas kernels  38.1 us (22%)
  blocking collectives  37.3 us (22%)
  waiting for transfers between devices  32.8 us (19%)
  starting transfers between devices  32.6 us (19%)
  between operations  13.8 us (8%)
  local copies, waits for them, and re-layouts  11.1 us (6%)
  other arithmetic  4.29 us (3%)
    all_to_all x1, blocking collectives, per_device(): sent = lax.all_to_all(sent, 'ccol', split_axis=0, concat_axis=0, tiled=True)  37.3 us
    pallas_call x2, Pallas kernels, far_field(): pl.pallas_call(functools.partial(far_kernel, slots, rows, x_first), grid=...  21.8 us
    ppermute x2, waiting for transfers between devices, first_stage(): down = to_last((last_sum + f32(far_down)).astype(jnp.bfloat16))  10 us
    unnamed x19, local copies, waits for them, and re-layouts  8.38 us
    pallas_call x1, Pallas kernels, near_field(): pl.pallas_call(near_kernel, grid=(panels // CS,), in_specs=[pl.BlockSpec(...  7.99 us
    ppermute x2, waiting for transfers between devices, first_stage(): far_up = to_next(far[:half])  7.76 us
    ppermute x2, starting transfers between devices, first_stage(): own_a = to_last(last)  7.61 us
    ppermute x2, waiting for transfers between devices, second_stage(): up = f32(to_next(following.astype(jnp.bfloat16)))  7.28 us
  transfers between devices with their start and end apart: 23, of which 7 were waited for; matrix products, arithmetic and copies ran while one was open for 4% of the time, Pallas kernels for 19%

profile of v3, /device:TPU:0, one launch (start us, length us, event | category | flops | bytes accessed | tf_op | source)
XLA Modules:
  0.0 170.1 jit_solution(4648339510837735480)
XLA Ops:
  6.6 2.7 %compress.1 = bf16[8,64,512]{2,1,0:T(8,128)(2,1)} custom-call(bf16[64,2048]{1,0:T(8,128)(2,1)} %basis_ref.2, bf16[2048,512]{1,0:T(8,128)(2,1)} %modes_ref.3), custom_call_target="tpu_custom_call" | custom-call | flops 134217728 | bytes 3145728 | tf_op jit(solution)/shard_map/compress/pallas_call | solution.py:39
  9.6 3.2 %dispatch.1 = bf16[16,528,128]{2,1,0:T(8,128)(2,1)S(1)} custom-call(s32[128]{0:T(128)S(1)} %copy-done.2, s32[128]{0:T(128)S(1)} %bitcast.4, s32[128]{0:T(128)S(1)} %copy-done.4, bf16[128,32,128]{2,1,0:T(8,128)(2,1)S(1)} %bitcast.3), custom_call_target="tpu_custom_call" | custom-call | flops 4194304 | bytes 3145728 | tf_op jit(solution)/shard_map/dispatch/pallas_call | solution.py:89
  12.8 37.3 %all_to_all.5.sent_ref = bf16[16,528,128]{2,1,0:T(8,128)(2,1)} all-to-all(bf16[16,528,128]{2,1,0:T(8,128)(2,1)S(1)} %dispatch.1), channel_id=1, replica_groups=mesh['crow'=8,'ccol'=16] {'ccol'}, dimensions={0} | all-to-all | bytes 4325376 | tf_op jit(solution)/shard_map/all_to_all | solution.py:350
  51.6 2.5 %collective-permute-start.6 = (bf16[1024,512]{1,0:T(8,128)(2,1)}, bf16[1024,512]{1,0:T(8,128)(2,1)S(1)}, u32[]{:S(2)}, u32[]{:S(2)}) collective-permute-start(bf16[1024,512]{1,0:T(8,128)(2,1)} %get-tuple-element.70), channel_id=1, source_target_pairs={{0,1},{1,2},{2,3},{3,4},{4,5},{5,6},{6,7},{7,8},{8,9},{9,10},{10,1... | collective-permute-start | bytes 3145736 | tf_op jit(solution)/shard_map/ppermute | solution.py:355
  57.1 2.2 %copy-done.6 = bf16[64,64,512]{2,1,0:T(8,128)(2,1)S(1)} copy-done((bf16[64,64,512]{2,1,0:T(8,128)(2,1)S(1)}, bf16[64,64,512]{2,1,0:T(8,128)(2,1)}, u32[]{:S(2)}) %copy-start.6) | copy-done | bytes 4194328
  59.3 10.9 %far_x.1 = (bf16[32,64,256]{2,1,0:T(8,128)(2,1)S(1)}, bf16[16,64,256]{2,1,0:T(8,128)(2,1)S(1)}, bf16[16,64,256]{2,1,0:T(8,128)(2,1)S(1)}, f32[16,64,256]{2,1,0:T...) custom-call(bf16[64,64,512]{2,1,0:T(8,128)(2,1)S(1)} %copy-done.6, bf16[16,528,128]{2,1,0:T(8,128)(2,1)S(1)} %copy-done.1), custom_call_target="tpu_custom_call" | custom-call | flops 2147483648 | bytes 12582912 | tf_op jit(solution)/shard_map/far_x/pallas_call | solution.py:177
  70.2 4.3 %collective-permute-start = (bf16[16,64,256]{2,1,0:T(8,128)(2,1)S(1)}, bf16[16,64,256]{2,1,0:T(8,128)(2,1)}, u32[]{:S(2)}, u32[]{:S(2)}) collective-permute-start(bf16[16,64,256]{2,1,0:T(8,128)(2,1)S(1)} %get-tuple-element.36), channel_id=1, source_target_pairs={{0,12},{1,13},{2,14},{3,15},{4,0},{5,1},{6,2},{7,3},{8,4},{9,5},{1... | collective-permute-start | bytes 1572872 | tf_op jit(solution)/shard_map/ppermute | solution.py:221
  75.6 2.3 %collective-permute-start.2 = (bf16[16,64,256]{2,1,0:T(8,128)(2,1)}, bf16[16,64,256]{2,1,0:T(8,128)(2,1)}, u32[]{:S(2)}, u32[]{:S(2)}) collective-permute-start(bf16[16,64,256]{2,1,0:T(8,128)(2,1)} %get-tuple-element.74), channel_id=1, source_target_pairs={{0,4},{1,5},{2,6},{3,7},{4,8},{5,9},{6,10},{7,11},{8,12},{9,13},{1... | collective-permute-start | bytes 1572872 | tf_op jit(solution)/shard_map/ppermute | solution.py:218
  77.8 10.9 %far_z.1 = (bf16[32,64,256]{2,1,0:T(8,128)(2,1)S(1)}, bf16[16,64,256]{2,1,0:T(8,128)(2,1)S(1)}, bf16[16,64,256]{2,1,0:T(8,128)(2,1)S(1)}, f32[16,64,256]{2,1,0:T...) custom-call(bf16[64,64,512]{2,1,0:T(8,128)(2,1)S(1)} %copy-done.6, bf16[16,528,128]{2,1,0:T(8,128)(2,1)S(1)} %copy-done.1), custom_call_target="tpu_custom_call" | custom-call | flops 2147483648 | bytes 12582912 | tf_op jit(solution)/shard_map/far_z/pallas_call | solution.py:177
  89.7 3.7 %copy-done.5 = bf16[2048,2304]{1,0:T(8,128)(2,1)S(1)} copy-done((bf16[2048,2304]{1,0:T(8,128)(2,1)S(1)}, bf16[2048,2304]{1,0:T(8,128)(2,1)}, u32[]{:S(2)}) %copy-start.5) | copy-done | bytes 9437208
  93.4 8.0 %near_field.1 = (f32[2048,512]{1,0:T(8,128)S(1)}, bf16[2048,64]{1,0:T(8,128)(2,1)S(1)}) custom-call(bf16[2048,2304]{1,0:T(8,128)(2,1)S(1)} %copy-done.5, bf16[1024,512]{1,0:T(8,128)(2,1)S(1)} %collective-permute-done.6.before_ref, bf16[2048,512]{1,0:T(8,128)(2,1)S(1)} %copy-done, bf16[1024,512]{1,0:T(8,128)(2,1)} %collective-permute-done.7.after_ref, ...), custom_call_target="tpu_custom_call" | custom-call | flops 4831838208 | bytes 18874368 | tf_op jit(solution)/shard_map/near_field/pallas_call | solution.py:275
  104.0 2.1 %collective-permute-start.3 = (bf16[16,64,256]{2,1,0:T(8,128)(2,1)S(1)}, bf16[16,64,256]{2,1,0:T(8,128)(2,1)S(1)}, u32[]{:S(2)}, u32[]{:S(2)}) collective-permute-start(bf16[16,64,256]{2,1,0:T(8,128)(2,1)S(1)} %add_convert_fusion.3), channel_id=1, source_target_pairs={{0,4},{1,5},{2,6},{3,7},{4,8},{5,9},{6,10},{7,11},{8,12},{9,13},{1... | collective-permute-start | bytes 1572872 | tf_op jit(solution)/shard_map/ppermute | solution.py:222
  106.2 2.1 %collective-permute-start.5 = (bf16[16,64,256]{2,1,0:T(8,128)(2,1)S(1)}, bf16[16,64,256]{2,1,0:T(8,128)(2,1)S(1)}, u32[]{:S(2)}, u32[]{:S(2)}) collective-permute-start(bf16[16,64,256]{2,1,0:T(8,128)(2,1)S(1)} %add_convert_fusion.2), channel_id=1, source_target_pairs={{0,12},{1,13},{2,14},{3,15},{4,0},{5,1},{6,2},{7,3},{8,4},{9,5},{1... | collective-permute-start | bytes 1572872 | tf_op jit(solution)/shard_map/ppermute | solution.py:223
  108.5 7.8 %collective-permute-done.13 = bf16[16,64,256]{2,1,0:T(8,128)(2,1)S(1)} collective-permute-done((bf16[16,64,256]{2,1,0:T(8,128)(2,1)S(1)}, bf16[16,64,256]{2,1,0:T(8,128)(2,1)S(1)}, u32[]{:S(2)}, u32[]{:S(2)}) %collective-permute-start.13) | collective-permute-done | bytes 524320 | tf_op jit(solution)/shard_map/ppermute | solution.py:218
  116.4 3.3 %collective-permute-start.12 = (bf16[16,64,256]{2,1,0:T(8,128)(2,1)S(1)}, bf16[16,64,256]{2,1,0:T(8,128)(2,1)S(1)}, u32[]{:S(2)}, u32[]{:S(2)}) collective-permute-start(bf16[16,64,256]{2,1,0:T(8,128)(2,1)S(1)} %get-tuple-element.58), channel_id=1, source_target_pairs={{0,3},{1,0},{2,1},{3,2},{4,7},{5,4},{6,5},{7,6},{8,11},{9,8},{10,9... | collective-permute-start | bytes 1572872 | tf_op jit(solution)/shard_map/ppermute | solution.py:221
  123.6 1.8 %collective-permute-start.10 = (bf16[4,64,256]{2,1,0:T(8,128)(2,1)S(1)}, bf16[4,64,256]{2,1,0:T(8,128)(2,1)S(1)}, u32[]{:S(2)}, u32[]{:S(2)}) collective-permute-start(bf16[4,64,256]{2,1,0:T(8,128)(2,1)S(1)} %get-tuple-element.79), channel_id=1, source_target_pairs={{0,3},{1,0},{2,1},{3,2},{4,7},{5,4},{6,5},{7,6},{8,11},{9,8},{10,9... | collective-permute-start | bytes 393224 | tf_op jit(solution)/shard_map/ppermute | solution.py:240
  125.4 6.9 %collective-permute-done.15 = bf16[16,64,256]{2,1,0:T(8,128)(2,1)S(1)} collective-permute-done((bf16[16,64,256]{2,1,0:T(8,128)(2,1)S(1)}, bf16[16,64,256]{2,1,0:T(8,128)(2,1)S(1)}, u32[]{:S(2)}, u32[]{:S(2)}) %collective-permute-start.15) | collective-permute-done | bytes 524320 | tf_op jit(solution)/shard_map/ppermute | solution.py:220
  132.4 10.0 %collective-permute-done.17 = bf16[16,64,256]{2,1,0:T(8,128)(2,1)S(1)} collective-permute-done((bf16[16,64,256]{2,1,0:T(8,128)(2,1)S(1)}, bf16[16,64,256]{2,1,0:T(8,128)(2,1)S(1)}, u32[]{:S(2)}, u32[]{:S(2)}) %collective-permute-start.17) | collective-permute-done | bytes 524320 | tf_op jit(solution)/shard_map/ppermute | solution.py:223
  143.4 2.5 %collective-permute-start.20 = (bf16[4,64,256]{2,1,0:T(8,128)(2,1)S(1)}, bf16[4,64,256]{2,1,0:T(8,128)(2,1)S(1)}, u32[]{:S(2)}, u32[]{:S(2)}) collective-permute-start(bf16[4,64,256]{2,1,0:T(8,128)(2,1)S(1)} %get-tuple-element.76), channel_id=1, source_target_pairs={{0,12},{1,13},{2,14},{3,15},{4,0},{5,1},{6,2},{7,3},{8,4},{9,5},{1... | collective-permute-start | bytes 393224 | tf_op jit(solution)/shard_map/ppermute | solution.py:240
  146.1 3.3 %collective-permute-start.11 = (bf16[8,64,256]{2,1,0:T(8,128)(2,1)S(1)}, bf16[8,64,256]{2,1,0:T(8,128)(2,1)S(1)}, u32[]{:S(2)}, u32[]{:S(2)}) collective-permute-start(bf16[8,64,256]{2,1,0:T(8,128)(2,1)S(1)} %pad_maximum_fusion.1), channel_id=1, source_target_pairs={{0,3},{1,0},{2,1},{3,2},{4,7},{5,4},{6,5},{7,6},{8,11},{9,8},{10,9... | collective-permute-start | bytes 786440 | tf_op jit(solution)/shard_map/ppermute | solution.py:244
  149.6 3.3 %collective-permute-start.21 = (bf16[8,64,256]{2,1,0:T(8,128)(2,1)S(1)}, bf16[8,64,256]{2,1,0:T(8,128)(2,1)S(1)}, u32[]{:S(2)}, u32[]{:S(2)}) collective-permute-start(bf16[8,64,256]{2,1,0:T(8,128)(2,1)S(1)} %pad_maximum_fusion.3), channel_id=1, source_target_pairs={{0,12},{1,13},{2,14},{3,15},{4,0},{5,1},{6,2},{7,3},{8,4},{9,5},{1... | collective-permute-start | bytes 786440 | tf_op jit(solution)/shard_map/ppermute | solution.py:244
  153.3 3.8 %collective-permute-done.9 = bf16[8,64,256]{2,1,0:T(8,128)(2,1)S(1)} collective-permute-done((bf16[8,64,256]{2,1,0:T(8,128)(2,1)S(1)}, bf16[8,64,256]{2,1,0:T(8,128)(2,1)S(1)}, u32[]{:S(2)}, u32[]{:S(2)}) %collective-permute-start.9) | collective-permute-done | bytes 262176 | tf_op jit(solution)/shard_map/ppermute | solution.py:243
  157.2 3.5 %collective-permute-done.19 = bf16[8,64,256]{2,1,0:T(8,128)(2,1)S(1)} collective-permute-done((bf16[8,64,256]{2,1,0:T(8,128)(2,1)S(1)}, bf16[8,64,256]{2,1,0:T(8,128)(2,1)S(1)}, u32[]{:S(2)}, u32[]{:S(2)}) %collective-permute-start.19) | collective-permute-done | bytes 262176 | tf_op jit(solution)/shard_map/ppermute | solution.py:243
  160.8 2.4 %expand.1 = bf16[2048,512]{1,0:T(8,128)(2,1)} custom-call(f32[2048,512]{1,0:T(8,128)S(1)} %get-tuple-element.50.near_ref, bf16[2048,64]{1,0:T(8,128)(2,1)S(1)} %get-tuple-element.51.basis_ref, bf16[8,64,256]{2,1,0:T(8,128)(2,1)S(1)} %fusion.3.left_ref, bf16[8,64,256]{2,1,0:T(8,128)(2,1)S(1)} %fusion.1.right_ref), custom_call_target="tpu_custom_call" | custom-call | flops 134217728 | bytes 7340032 | tf_op jit(solution)/shard_map/expand/pallas_call | solution.py:315
  (72 shorter events, 15.5 us)
Async XLA Ops:
  6.5 48.9 %all-gather.2.cloned.1.call-start = ((), (), s32[]{:S(2)}) async-start(), calls=%async_computation.1 | async-start | bytes 4718592 | tf_op jit(solution)/shard_map/all_gather | solution.py:343
  12.8 37.4 %copy-start = (bf16[2048,512]{1,0:T(8,128)(2,1)S(1)}, bf16[2048,512]{1,0:T(8,128)(2,1)}, u32[]{:S(2)}) copy-start(bf16[2048,512]{1,0:T(8,128)(2,1)} %modes_ref.3) | copy-start | bytes 6291460
  51.6 37.1 %collective-permute-start.6 = (bf16[1024,512]{1,0:T(8,128)(2,1)}, bf16[1024,512]{1,0:T(8,128)(2,1)S(1)}, u32[]{:S(2)}, u32[]{:S(2)}) collective-permute-start(bf16[1024,512]{1,0:T(8,128)(2,1)} %get-tuple-element.70), channel_id=1, source_target_pairs={{0,1},{1,2},{2,3},{3,4},{4,5},{5,6},{6,7},{7,8},{8,9},{9,10},{10,1... | collective-permute-start | bytes 3145736 | tf_op jit(solution)/shard_map/ppermute | solution.py:355
  54.2 34.7 %collective-permute-start.7 = (bf16[1024,512]{1,0:T(8,128)(2,1)}, bf16[1024,512]{1,0:T(8,128)(2,1)}, u32[]{:S(2)}, u32[]{:S(2)}) collective-permute-start(bf16[1024,512]{1,0:T(8,128)(2,1)} %get-tuple-element.69), channel_id=1, source_target_pairs={{1,0},{2,1},{3,2},{4,3},{5,4},{6,5},{7,6},{8,7},{9,8},{10,9},{11,1... | collective-permute-start | bytes 3145736 | tf_op jit(solution)/shard_map/ppermute | solution.py:356
  70.2 46.2 %collective-permute-start = (bf16[16,64,256]{2,1,0:T(8,128)(2,1)S(1)}, bf16[16,64,256]{2,1,0:T(8,128)(2,1)}, u32[]{:S(2)}, u32[]{:S(2)}) collective-permute-start(bf16[16,64,256]{2,1,0:T(8,128)(2,1)S(1)} %get-tuple-element.36), channel_id=1, source_target_pairs={{0,12},{1,13},{2,14},{3,15},{4,0},{5,1},{6,2},{7,3},{8,4},{9,5},{1... | collective-permute-start | bytes 1572872 | tf_op jit(solution)/shard_map/ppermute | solution.py:221
  74.5 45.2 %collective-permute-start.1 = (bf16[16,64,256]{2,1,0:T(8,128)(2,1)S(1)}, bf16[16,64,256]{2,1,0:T(8,128)(2,1)}, u32[]{:S(2)}, u32[]{:S(2)}) collective-permute-start(bf16[16,64,256]{2,1,0:T(8,128)(2,1)S(1)} %get-tuple-element.37), channel_id=1, source_target_pairs={{0,4},{1,5},{2,6},{3,7},{4,8},{5,9},{6,10},{7,11},{8,12},{9,13},{1... | collective-permute-start | bytes 1572872 | tf_op jit(solution)/shard_map/ppermute | solution.py:220
  75.6 25.8 %collective-permute-start.2 = (bf16[16,64,256]{2,1,0:T(8,128)(2,1)}, bf16[16,64,256]{2,1,0:T(8,128)(2,1)}, u32[]{:S(2)}, u32[]{:S(2)}) collective-permute-start(bf16[16,64,256]{2,1,0:T(8,128)(2,1)} %get-tuple-element.74), channel_id=1, source_target_pairs={{0,4},{1,5},{2,6},{3,7},{4,8},{5,9},{6,10},{7,11},{8,12},{9,13},{1... | collective-permute-start | bytes 1572872 | tf_op jit(solution)/shard_map/ppermute | solution.py:218
  88.8 15.3 %collective-permute-start.4 = (bf16[16,64,256]{2,1,0:T(8,128)(2,1)}, bf16[16,64,256]{2,1,0:T(8,128)(2,1)S(1)}, u32[]{:S(2)}, u32[]{:S(2)}) collective-permute-start(bf16[16,64,256]{2,1,0:T(8,128)(2,1)} %get-tuple-element.73), channel_id=1, source_target_pairs={{0,12},{1,13},{2,14},{3,15},{4,0},{5,1},{6,2},{7,3},{8,4},{9,5},{1... | collective-permute-start | bytes 1572872 | tf_op jit(solution)/shard_map/ppermute | solution.py:219
  89.0 17.3 %collective-permute-start.16 = (bf16[16,64,256]{2,1,0:T(8,128)(2,1)S(1)}, bf16[16,64,256]{2,1,0:T(8,128)(2,1)S(1)}, u32[]{:S(2)}, u32[]{:S(2)}) collective-permute-start(bf16[16,64,256]{2,1,0:T(8,128)(2,1)S(1)} %get-tuple-element.71), channel_id=1, source_target_pairs={{0,3},{1,0},{2,1},{3,2},{4,7},{5,4},{6,5},{7,6},{8,11},{9,8},{10,9... | collective-permute-start | bytes 1572872 | tf_op jit(solution)/shard_map/ppermute | solution.py:219
  101.4 14.9 %collective-permute-start.13 = (bf16[16,64,256]{2,1,0:T(8,128)(2,1)S(1)}, bf16[16,64,256]{2,1,0:T(8,128)(2,1)S(1)}, u32[]{:S(2)}, u32[]{:S(2)}) collective-permute-start(bf16[16,64,256]{2,1,0:T(8,128)(2,1)S(1)} %get-tuple-element.72), channel_id=1, source_target_pairs={{0,1},{1,2},{2,3},{3,0},{4,5},{5,6},{6,7},{7,4},{8,9},{9,10},{10,1... | collective-permute-start | bytes 1572872 | tf_op jit(solution)/shard_map/ppermute | solution.py:218
  104.0 16.3 %collective-permute-start.3 = (bf16[16,64,256]{2,1,0:T(8,128)(2,1)S(1)}, bf16[16,64,256]{2,1,0:T(8,128)(2,1)S(1)}, u32[]{:S(2)}, u32[]{:S(2)}) collective-permute-start(bf16[16,64,256]{2,1,0:T(8,128)(2,1)S(1)} %add_convert_fusion.3), channel_id=1, source_target_pairs={{0,4},{1,5},{2,6},{3,7},{4,8},{5,9},{6,10},{7,11},{8,12},{9,13},{1... | collective-permute-start | bytes 1572872 | tf_op jit(solution)/shard_map/ppermute | solution.py:222
  106.2 15.5 %collective-permute-start.5 = (bf16[16,64,256]{2,1,0:T(8,128)(2,1)S(1)}, bf16[16,64,256]{2,1,0:T(8,128)(2,1)S(1)}, u32[]{:S(2)}, u32[]{:S(2)}) collective-permute-start(bf16[16,64,256]{2,1,0:T(8,128)(2,1)S(1)} %add_convert_fusion.2), channel_id=1, source_target_pairs={{0,12},{1,13},{2,14},{3,15},{4,0},{5,1},{6,2},{7,3},{8,4},{9,5},{1... | collective-permute-start | bytes 1572872 | tf_op jit(solution)/shard_map/ppermute | solution.py:223
  116.3 16.1 %collective-permute-start.15 = (bf16[16,64,256]{2,1,0:T(8,128)(2,1)S(1)}, bf16[16,64,256]{2,1,0:T(8,128)(2,1)S(1)}, u32[]{:S(2)}, u32[]{:S(2)}) collective-permute-start(bf16[16,64,256]{2,1,0:T(8,128)(2,1)S(1)} %get-tuple-element.61), channel_id=1, source_target_pairs={{0,1},{1,2},{2,3},{3,0},{4,5},{5,6},{6,7},{7,4},{8,9},{9,10},{10,1... | collective-permute-start | bytes 1572872 | tf_op jit(solution)/shard_map/ppermute | solution.py:220
  116.4 15.9 %collective-permute-start.12 = (bf16[16,64,256]{2,1,0:T(8,128)(2,1)S(1)}, bf16[16,64,256]{2,1,0:T(8,128)(2,1)S(1)}, u32[]{:S(2)}, u32[]{:S(2)}) collective-permute-start(bf16[16,64,256]{2,1,0:T(8,128)(2,1)S(1)} %get-tuple-element.58), channel_id=1, source_target_pairs={{0,3},{1,0},{2,1},{3,2},{4,7},{5,4},{6,5},{7,6},{8,11},{9,8},{10,9... | collective-permute-start | bytes 1572872 | tf_op jit(solution)/shard_map/ppermute | solution.py:221
  119.7 22.6 %collective-permute-start.17 = (bf16[16,64,256]{2,1,0:T(8,128)(2,1)S(1)}, bf16[16,64,256]{2,1,0:T(8,128)(2,1)S(1)}, u32[]{:S(2)}, u32[]{:S(2)}) collective-permute-start(bf16[16,64,256]{2,1,0:T(8,128)(2,1)S(1)} %add_convert_fusion), channel_id=1, source_target_pairs={{0,3},{1,0},{2,1},{3,2},{4,7},{5,4},{6,5},{7,6},{8,11},{9,8},{10,9... | collective-permute-start | bytes 1572872 | tf_op jit(solution)/shard_map/ppermute | solution.py:223
  120.3 22.6 %collective-permute-start.14 = (bf16[16,64,256]{2,1,0:T(8,128)(2,1)S(1)}, bf16[16,64,256]{2,1,0:T(8,128)(2,1)S(1)}, u32[]{:S(2)}, u32[]{:S(2)}) collective-permute-start(bf16[16,64,256]{2,1,0:T(8,128)(2,1)S(1)} %add_convert_fusion.1), channel_id=1, source_target_pairs={{0,1},{1,2},{2,3},{3,0},{4,5},{5,6},{6,7},{7,4},{8,9},{9,10},{10,1... | collective-permute-start | bytes 1572872 | tf_op jit(solution)/shard_map/ppermute | solution.py:222
  123.6 22.5 %collective-permute-start.10 = (bf16[4,64,256]{2,1,0:T(8,128)(2,1)S(1)}, bf16[4,64,256]{2,1,0:T(8,128)(2,1)S(1)}, u32[]{:S(2)}, u32[]{:S(2)}) collective-permute-start(bf16[4,64,256]{2,1,0:T(8,128)(2,1)S(1)} %get-tuple-element.79), channel_id=1, source_target_pairs={{0,3},{1,0},{2,1},{3,2},{4,7},{5,4},{6,5},{7,6},{8,11},{9,8},{10,9... | collective-permute-start | bytes 393224 | tf_op jit(solution)/shard_map/ppermute | solution.py:240
  132.3 17.0 %collective-permute-start.8 = (bf16[4,64,256]{2,1,0:T(8,128)(2,1)S(1)}, bf16[4,64,256]{2,1,0:T(8,128)(2,1)S(1)}, u32[]{:S(2)}, u32[]{:S(2)}) collective-permute-start(bf16[4,64,256]{2,1,0:T(8,128)(2,1)S(1)} %get-tuple-element.78), channel_id=1, source_target_pairs={{0,1},{1,2},{2,3},{3,0},{4,5},{5,6},{6,7},{7,4},{8,9},{9,10},{10,1... | collective-permute-start | bytes 393224 | tf_op jit(solution)/shard_map/ppermute | solution.py:239
  143.4 6.1 %collective-permute-start.20 = (bf16[4,64,256]{2,1,0:T(8,128)(2,1)S(1)}, bf16[4,64,256]{2,1,0:T(8,128)(2,1)S(1)}, u32[]{:S(2)}, u32[]{:S(2)}) collective-permute-start(bf16[4,64,256]{2,1,0:T(8,128)(2,1)S(1)} %get-tuple-element.76), channel_id=1, source_target_pairs={{0,12},{1,13},{2,14},{3,15},{4,0},{5,1},{6,2},{7,3},{8,4},{9,5},{1... | collective-permute-start | bytes 393224 | tf_op jit(solution)/shard_map/ppermute | solution.py:240
  146.0 7.0 %collective-permute-start.18 = (bf16[4,64,256]{2,1,0:T(8,128)(2,1)S(1)}, bf16[4,64,256]{2,1,0:T(8,128)(2,1)S(1)}, u32[]{:S(2)}, u32[]{:S(2)}) collective-permute-start(bf16[4,64,256]{2,1,0:T(8,128)(2,1)S(1)} %get-tuple-element.75), channel_id=1, source_target_pairs={{0,4},{1,5},{2,6},{3,7},{4,8},{5,9},{6,10},{7,11},{8,12},{9,13},{1... | collective-permute-start | bytes 393224 | tf_op jit(solution)/shard_map/ppermute | solution.py:239
  146.1 7.1 %collective-permute-start.11 = (bf16[8,64,256]{2,1,0:T(8,128)(2,1)S(1)}, bf16[8,64,256]{2,1,0:T(8,128)(2,1)S(1)}, u32[]{:S(2)}, u32[]{:S(2)}) collective-permute-start(bf16[8,64,256]{2,1,0:T(8,128)(2,1)S(1)} %pad_maximum_fusion.1), channel_id=1, source_target_pairs={{0,3},{1,0},{2,1},{3,2},{4,7},{5,4},{6,5},{7,6},{8,11},{9,8},{10,9... | collective-permute-start | bytes 786440 | tf_op jit(solution)/shard_map/ppermute | solution.py:244
  149.4 7.7 %collective-permute-start.9 = (bf16[8,64,256]{2,1,0:T(8,128)(2,1)S(1)}, bf16[8,64,256]{2,1,0:T(8,128)(2,1)S(1)}, u32[]{:S(2)}, u32[]{:S(2)}) collective-permute-start(bf16[8,64,256]{2,1,0:T(8,128)(2,1)S(1)} %pad_maximum_fusion), channel_id=1, source_target_pairs={{0,1},{1,2},{2,3},{3,0},{4,5},{5,6},{6,7},{7,4},{8,9},{9,10},{10,1... | collective-permute-start | bytes 786440 | tf_op jit(solution)/shard_map/ppermute | solution.py:243
  149.6 7.6 %collective-permute-start.21 = (bf16[8,64,256]{2,1,0:T(8,128)(2,1)S(1)}, bf16[8,64,256]{2,1,0:T(8,128)(2,1)S(1)}, u32[]{:S(2)}, u32[]{:S(2)}) collective-permute-start(bf16[8,64,256]{2,1,0:T(8,128)(2,1)S(1)} %pad_maximum_fusion.3), channel_id=1, source_target_pairs={{0,12},{1,13},{2,14},{3,15},{4,0},{5,1},{6,2},{7,3},{8,4},{9,5},{1... | collective-permute-start | bytes 786440 | tf_op jit(solution)/shard_map/ppermute | solution.py:244
  153.0 7.7 %collective-permute-start.19 = (bf16[8,64,256]{2,1,0:T(8,128)(2,1)S(1)}, bf16[8,64,256]{2,1,0:T(8,128)(2,1)S(1)}, u32[]{:S(2)}, u32[]{:S(2)}) collective-permute-start(bf16[8,64,256]{2,1,0:T(8,128)(2,1)S(1)} %pad_maximum_fusion.2), channel_id=1, source_target_pairs={{0,4},{1,5},{2,6},{3,7},{4,8},{5,9},{6,10},{7,11},{8,12},{9,13},{1... | collective-permute-start | bytes 786440 | tf_op jit(solution)/shard_map/ppermute | solution.py:243
  (8 other events, 20.5 us)
Sparse Core Ops, SparseCore 0:
  9.5 34.5 all-gather.1

commit v4 on v3

--- a/solution.py
+++ b/solution.py
@@ -23,7 +23,17 @@
 COMPRESS = 4
 
 
-def compress_kernel(basis_ref, modes_ref, out_ref):
+def compress_kernel(basis_ref, modes_ref, out_ref, low_ref, high_ref):
+    step = pl.program_id(0)
+
+    @pl.when(step == 0)
+    def _():
+        low_ref[...] = modes_ref[: NH * CS, :]
+
+    @pl.when(step == pl.num_programs(0) - 1)
+    def _():
+        high_ref[...] = modes_ref[(COMPRESS - NH) * CS :, :]
+
     for i in range(COMPRESS):
         out_ref[i] = jnp.dot(
             basis_ref[:, i * CS : (i + 1) * CS],
@@ -43,8 +53,17 @@
             pl.BlockSpec((rank, COMPRESS * CS), lambda r: (0, r)),
             pl.BlockSpec((COMPRESS * CS, cols), lambda r: (r, 0)),
         ],
-        out_specs=pl.BlockSpec((COMPRESS, rank, cols), lambda r: (r, 0, 0)),
-        out_shape=jax.ShapeDtypeStruct((count, rank, cols), jnp.bfloat16),
+        out_specs=[
+            pl.BlockSpec((COMPRESS, rank, cols), lambda r: (r, 0, 0)),
+            pl.BlockSpec((NH * CS, cols), lambda r: (0, 0)),
+            pl.BlockSpec((NH * CS, cols), lambda r: (0, 0)),
+        ],
+        out_shape=[
+            jax.ShapeDtypeStruct((count, rank, cols), jnp.bfloat16),
+            jax.ShapeDtypeStruct((NH * CS, cols), jnp.bfloat16),
+            jax.ShapeDtypeStruct((NH * CS, cols), jnp.bfloat16),
+        ],
+        compiler_params=pltpu.CompilerParams(vmem_limit_bytes=58 * MIB),
         cost_estimate=pl.CostEstimate(
             flops=2 * rank * panels * cols, bytes_accessed=3 * MIB, transcendentals=0
         ),
@@ -102,7 +121,7 @@
 
 
 def far_kernel(
-    slots, rows, x_first, comp_ref, sent_ref, far_ref, next_ref, last_ref, next_sum_ref, last_sum_ref, own_ref,
+    slots, rows, x_first, comp_ref, sent_ref, up_ref, down_ref, next_ref, last_ref, own_ref,
     acc_ref, meta_ref, smem_ref, list_ref, sem,
 ):
     sources = sent_ref.shape[0]
@@ -153,11 +172,12 @@
     lax.fori_loop(0, (total + UNROLL - 1) // UNROLL, group, 0)
     half = part // 2
     own_ref[...] = acc_ref[:part]
-    next_sum_ref[...] = acc_ref[part : part + half]
-    next_ref[...] = acc_ref[part + half : 2 * part].astype(jnp.bfloat16)
-    far_ref[...] = acc_ref[2 * part : 3 * part].astype(jnp.bfloat16)
-    last_ref[...] = acc_ref[3 * part : 3 * part + half].astype(jnp.bfloat16)
-    last_sum_ref[...] = acc_ref[3 * part + half :]
+    next_ref[...] = acc_ref[part : part + half]
+    up_ref[half:] = acc_ref[part + half : 2 * part].astype(jnp.bfloat16)
+    up_ref[:half] = acc_ref[2 * part : 2 * part + half].astype(jnp.bfloat16)
+    down_ref[half:] = acc_ref[2 * part + half : 3 * part].astype(jnp.bfloat16)
+    down_ref[:half] = acc_ref[3 * part : 3 * part + half].astype(jnp.bfloat16)
+    last_ref[...] = acc_ref[3 * part + half :]
 
 
 def far_field(comp, sent, slots, rows, group_rows, x_first):
@@ -168,8 +188,7 @@
     part = group_rows // 4
     kinds = [
         (part, jnp.bfloat16),
-        (part // 2, jnp.bfloat16),
-        (part // 2, jnp.bfloat16),
+        (part, jnp.bfloat16),
         (part // 2, jnp.float32),
         (part // 2, jnp.float32),
         (part, jnp.float32),
@@ -190,7 +209,7 @@
             SMEM((sources * slots + UNROLL,), jnp.int32),
             pltpu.SemaphoreType.DMA,
         ],
-        compiler_params=pltpu.CompilerParams(vmem_limit_bytes=40 * MIB),
+        compiler_params=pltpu.CompilerParams(vmem_limit_bytes=58 * MIB),
         cost_estimate=pl.CostEstimate(
             flops=2 * 128 * rank * rank * width * 8, bytes_accessed=12 * MIB, transcendentals=0
         ),
@@ -210,39 +229,87 @@
     return value.astype(jnp.float32)
 
 
-def first_stage(parts, x_first):
-    far, following, last, following_sum, last_sum, own = parts
-    half = far.shape[0] // 2
-    to_next = functools.partial(lax.ppermute, axis_name="ccol", perm=ring(x_first, 1))
-    to_last = functools.partial(lax.ppermute, axis_name="ccol", perm=ring(x_first, -1))
-    far_up = to_next(far[:half])
-    far_down = to_last(far[half:])
-    own_b = to_next(following)
-    own_a = to_last(last)
-    up = to_next((following_sum + f32(far_up)).astype(jnp.bfloat16))
-    down = to_last((last_sum + f32(far_down)).astype(jnp.bfloat16))
-    return own, own_a, own_b, up, down
-
-
-def second_stage(arrived, x_first):
-    own, own_a, own_b, up, down = arrived
-    half = own_a.shape[0]
-    first = own[:half] + f32(own_a) + f32(up)
-    second = own[half:] + f32(own_b) + f32(down)
-    quarter = half // 2
-    here, following, far, last = first[:quarter], first[quarter:], second[:quarter], second[quarter:]
-
-    half = quarter // 2
-    to_next = functools.partial(lax.ppermute, axis_name="ccol", perm=ring(not x_first, 1))
-    to_last = functools.partial(lax.ppermute, axis_name="ccol", perm=ring(not x_first, -1))
-    far = far.astype(jnp.bfloat16)
-    far_up = f32(to_next(far[:half]))
-    far_down = f32(to_last(far[half:]))
-    following = jnp.concatenate([following[:half] + far_up, following[half:]])
-    last = jnp.concatenate([last[:half], last[half:] + far_down])
-    up = f32(to_next(following.astype(jnp.bfloat16)))
-    down = f32(to_last(last.astype(jnp.bfloat16)))
-    return (here + up + down).astype(jnp.bfloat16)
+def both_ways(up, down, along_x):
+    return lax.ppermute(up, "ccol", ring(along_x, 1)), lax.ppermute(down, "ccol", ring(along_x, -1))
+
+
+SMALL = pl.CostEstimate(flops=0, bytes_accessed=0, transcendentals=0)
+
+
+def pass_kernel(following_ref, last_ref, up_ref, down_ref, up_out_ref, down_out_ref):
+    half = following_ref.shape[0]
+    up_out_ref[...] = (following_ref[...] + f32(up_ref[:half])).astype(jnp.bfloat16)
+    down_out_ref[...] = (last_ref[...] + f32(down_ref[half:])).astype(jnp.bfloat16)
+
+
+def passed_on(following, last, up, down):
+    shape = jax.ShapeDtypeStruct(following.shape, jnp.bfloat16)
+    return pl.pallas_call(
+        pass_kernel,
+        in_specs=[whole()] * 4,
+        out_specs=[whole()] * 2,
+        out_shape=[shape] * 2,
+        compiler_params=pltpu.CompilerParams(vmem_limit_bytes=24 * MIB),
+        cost_estimate=SMALL,
+        name="passed_on",
+    )(following, last, up, down)
+
+
+def ring_sum(place, own, up_ref, down_ref, up_rest_ref, down_rest_ref):
+    half = up_rest_ref.shape[0]
+    if place < half:
+        return own + f32(down_ref[place]) + f32(up_rest_ref[place])
+    return own + f32(up_ref[place]) + f32(down_rest_ref[place - half])
+
+
+def turn_kernel(own_ref, *refs):
+    arrived, (up_ref, down_ref, next_ref, last_ref, here_ref) = refs[:4], refs[4:]
+    part = here_ref.shape[0]
+    half = part // 2
+    for place in range(4 * part):
+        value = ring_sum(place, own_ref[place], *arrived)
+        kind, at = place // part, place % part
+        if kind == 0:
+            here_ref[at] = value
+        elif kind == 1 and at < half:
+            next_ref[at] = value
+        elif kind == 1:
+            up_ref[at] = value.astype(jnp.bfloat16)
+        elif kind == 2 and at < half:
+            up_ref[at] = value.astype(jnp.bfloat16)
+        elif kind == 2:
+            down_ref[at] = value.astype(jnp.bfloat16)
+        elif at < half:
+            down_ref[at] = value.astype(jnp.bfloat16)
+        else:
+            last_ref[at - half] = value
+
+
+def turn(own, up, down, up_rest, down_rest):
+    rows, rank, width = own.shape
+    part = rows // 4
+    kinds = [
+        (part, jnp.bfloat16),
+        (part, jnp.bfloat16),
+        (part // 2, jnp.float32),
+        (part // 2, jnp.float32),
+        (part, jnp.float32),
+    ]
+    return pl.pallas_call(
+        turn_kernel,
+        in_specs=[whole()] * 5,
+        out_specs=[whole()] * 5,
+        out_shape=[jax.ShapeDtypeStruct((n, rank, width), kind) for n, kind in kinds],
+        compiler_params=pltpu.CompilerParams(vmem_limit_bytes=24 * MIB),
+        cost_estimate=SMALL,
+        name="turn",
+    )(own, up, down, up_rest, down_rest)
+
+
+def second_stage(parts, along_x):
+    up, down, following, last, own = parts
+    up, down = both_ways(up, down, along_x)
+    return own, up, down, *both_ways(*passed_on(following, last, up, down), along_x)
 
 
 def near_kernel(near_ref, before_ref, modes_ref, after_ref, basis_ref, out_ref, turned_ref, ext_ref):
@@ -287,9 +354,9 @@
             jax.ShapeDtypeStruct((panels, rank), jnp.bfloat16),
         ],
         scratch_shapes=[VMEM((panels + 2 * halo, cols), jnp.bfloat16)],
-        compiler_params=pltpu.CompilerParams(vmem_limit_bytes=32 * MIB),
+        compiler_params=pltpu.CompilerParams(vmem_limit_bytes=58 * MIB),
         cost_estimate=pl.CostEstimate(
-            flops=2 * panels * band * cols, bytes_accessed=18 * MIB, transcendentals=0
+            flops=16 * panels * band * cols, bytes_accessed=18 * MIB, transcendentals=0
         ),
         name="near_field",
     )(near_blocks, before, modes, after, row_basis)
@@ -298,29 +365,35 @@
 EXPAND = 2
 
 
-def expand_kernel(near_ref, basis_ref, left_ref, right_ref, out_ref):
-    width = left_ref.shape[2]
-    for i in range(EXPAND):
-        rows = pl.ds(i * CS, CS)
-        for half, far_ref in enumerate((left_ref, right_ref)):
-            cols = pl.ds(half * width, width)
-            far = jnp.dot(basis_ref[rows, :], far_ref[i], preferred_element_type=jnp.float32)
-            out_ref[rows, cols] = (near_ref[rows, cols] + far).astype(jnp.bfloat16)
+def expand_kernel(near_ref, basis_ref, *refs):
+    halves, out_ref = (refs[:5], refs[5:10]), refs[10]
+    clusters, _, width = halves[0][0].shape
+    step = pl.program_id(0)
+    for group in range(clusters // EXPAND):
+
+        @pl.when(step == group)
+        def _():
+            for i in range(EXPAND):
+                rows = pl.ds(i * CS, CS)
+                for side, half in enumerate(halves):
+                    place = group * EXPAND + i
+                    far = ring_sum(place, half[0][place], *half[1:]).astype(jnp.bfloat16)
+                    cols = pl.ds(side * width, width)
+                    value = jnp.dot(basis_ref[rows, :], far, preferred_element_type=jnp.float32)
+                    out_ref[rows, cols] = (near_ref[rows, cols] + value).astype(jnp.bfloat16)
 
 
 def expand(near, basis, left, right):
     panels, cols = near.shape
     rank = basis.shape[1]
-    width = cols // 2
     return pl.pallas_call(
         expand_kernel,
         grid=(panels // CS // EXPAND,),
         in_specs=[
             pl.BlockSpec((EXPAND * CS, cols), lambda r: (r, 0)),
             pl.BlockSpec((EXPAND * CS, rank), lambda r: (r, 0)),
-            pl.BlockSpec((EXPAND, rank, width), lambda r: (r, 0, 0)),
-            pl.BlockSpec((EXPAND, rank, width), lambda r: (r, 0, 0)),
-        ],
+        ]
+        + [pl.BlockSpec(v.shape, lambda r: (0, 0, 0)) for v in (*left, *right)],
         out_specs=pl.BlockSpec((EXPAND * CS, cols), lambda r: (r, 0)),
         out_shape=jax.ShapeDtypeStruct((panels, cols), jnp.bfloat16),
         compiler_params=pltpu.CompilerParams(vmem_limit_bytes=24 * MIB),
@@ -328,7 +401,7 @@
             flops=2 * panels * rank * cols, bytes_accessed=7 * MIB, transcendentals=0
         ),
         name="expand",
-    )(near, basis, left, right)
+    )(near, basis, *left, *right)
 
 
 def per_device(modes, col_basis, row_basis, near_blocks, block_rows, block_owner, block_slot, cores):
@@ -339,7 +412,7 @@
     blocks = cores.shape[0]
     slots = CAP * row_devices
 
-    compressed = compress(col_basis, modes)
+    compressed, low, high = compress(col_basis, modes)
     gathered = lax.all_gather(compressed, "crow", axis=0, tiled=True)
 
     lines = rank * rank // 128
@@ -349,22 +422,31 @@
     )
     sent = lax.all_to_all(sent, "ccol", split_axis=0, concat_axis=0, tiled=True)
 
-    edges, sent = lax.optimization_barrier((modes, sent))
+    low, high, sent = lax.optimization_barrier((low, high, sent))
     up = [(i, i + 1) for i in range(devices - 1)]
     down = [(j, i) for i, j in up]
-    before = lax.ppermute(edges[-NH * CS :], ("crow", "ccol"), up)
-    after = lax.ppermute(edges[: NH * CS], ("crow", "ccol"), down)
+    before = lax.ppermute(high, ("crow", "ccol"), up)
+    after = lax.ppermute(low, ("crow", "ccol"), down)
 
     group_rows = col_devices * cluster_count
     left = list(far_field(gathered, sent, slots, lines, group_rows, True))
     gathered, sent, left[0] = lax.optimization_barrier((gathered, sent, left[0]))
     right = list(far_field(gathered, sent, slots, lines, group_rows, False))
     right[0], before, after = lax.optimization_barrier((right[0], before, after))
+
+    left_up, left_down = both_ways(left[0], left[1], True)
+    right_up, right_down = both_ways(right[0], right[1], False)
+    left_up, left_down, before, after = lax.optimization_barrier((left_up, left_down, before, after))
+    left_rest = both_ways(*passed_on(left[2], left[3], left_up, left_down), True)
     near, basis = near_field(near_blocks, before, modes, after, row_basis)
-    left = first_stage(left, True)
-    right = first_stage(right, False)
-    left, near, basis = lax.optimization_barrier((left, near, basis))
-    return expand(near, basis, second_stage(left, True), second_stage(right, False))
+    right_up, right_down, near, basis = lax.optimization_barrier((right_up, right_down, near, basis))
+    right_rest = passed_on(right[2], right[3], right_up, right_down)
+    left_rest, _ = lax.optimization_barrier((left_rest, right_rest))
+    right_rest = both_ways(*right_rest, False)
+    left = second_stage(turn(left[4], left_up, left_down, *left_rest), False)
+    left, right_rest = lax.optimization_barrier((left, right_rest))
+    right = second_stage(turn(right[4], right_up, right_down, *right_rest), True)
+    return expand(near, basis, left, right)
 
 
 def solution(mesh):

time: 171 us -> 173 us (1.012)
  Pallas kernels: 38.1 us -> 52 us
  local copies, waits for them, and re-layouts: 11.1 us -> 2.87 us
  starting transfers between devices: 32.6 us -> 40 us
  waiting for transfers between devices: 32.8 us -> 25.7 us
  other arithmetic: 4.29 us -> 0 us
    ppermute x22 -> x18, starting transfers between devices: 32.6 us -> 40 us  [the longest x8 28.7 us: both_ways(): lax.ppermute(down, 'ccol', ring(along_x, -1))]
    ppermute x22 -> x18, waiting for transfers between devices: 32.8 us -> 25.7 us  [the longest x8 21.2 us: both_ways(): lax.ppermute(up, 'ccol', ring(along_x, 1))]
    pallas_call x2, Pallas kernels: 21.8 us -> 27.5 us  [far_field(): pl.pallas_call(functools.partial(far_kernel, slots, rows, x_first), grid=...]
    unnamed x19 -> x25, local copies, waits for them, and re-layouts: 8.38 us -> 2.87 us
    pallas_call x1, Pallas kernels: 7.99 us -> 12.4 us  [near_field(): pl.pallas_call(near_kernel, grid=(panels // CS,), in_specs=[pl.BlockSpec(...]
    pallas_call x0 -> x6, Pallas kernels: none -> 3.18 us  [the longest x2 1.77 us: turn(): pl.pallas_call(turn_kernel, in_specs=[whole()] * 5, out_specs=[whole()] *...]
    slice x7 -> x0, local copies, waits for them, and re-layouts: 2.71 us -> none  [the longest x1 1.44 us: per_device(): after = lax.ppermute(edges[:NH * CS], ('crow', 'ccol'), down)]
    another operation x6 -> x0, other arithmetic: 2.39 us -> none
  transfers between devices with their start and end apart: 23 -> 19, of which waited for: 7 -> 6; matrix products, arithmetic and copies ran while one was open for 4% -> 0% of each run, Pallas kernels for 19% -> 27%
where the time goes in v4:
time: 173 us; the launch traced here: 171 us
  Pallas kernels  52 us (30%)
  starting transfers between devices  40 us (23%)
  blocking collectives  37.2 us (22%)
  waiting for transfers between devices  25.7 us (15%)
  between operations  13.6 us (8%)
  local copies, waits for them, and re-layouts  2.87 us (2%)
    all_to_all x1, blocking collectives, per_device(): sent = lax.all_to_all(sent, 'ccol', split_axis=0, concat_axis=0, tiled=True)  37.2 us
    ppermute x8, starting transfers between devices, both_ways(): lax.ppermute(down, 'ccol', ring(along_x, -1))  28.7 us
    pallas_call x2, Pallas kernels, far_field(): pl.pallas_call(functools.partial(far_kernel, slots, rows, x_first), grid=...  27.5 us
    ppermute x8, waiting for transfers between devices, both_ways(): lax.ppermute(up, 'ccol', ring(along_x, 1))  21.2 us
    pallas_call x1, Pallas kernels, near_field(): pl.pallas_call(near_kernel, grid=(panels // CS,), in_specs=[pl.BlockSpec(...  12.4 us
    ppermute x8, starting transfers between devices, both_ways(): lax.ppermute(up, 'ccol', ring(along_x, 1))  6.57 us
    ppermute x8, waiting for transfers between devices, both_ways(): lax.ppermute(down, 'ccol', ring(along_x, -1))  4.46 us
  transfers between devices with their start and end apart: 19, of which 6 were waited for; matrix products, arithmetic and copies ran while one was open for 0% of the time, Pallas kernels for 27%

profile of v4, /device:TPU:0, one launch (start us, length us, event | category | flops | bytes accessed | tf_op | source)
XLA Modules:
  0.0 171.5 jit_solution(10669970759327782567)
XLA Ops:
  6.6 3.3 %compress.1 = (bf16[8,64,512]{2,1,0:T(8,128)(2,1)}, bf16[1024,512]{1,0:T(8,128)(2,1)}, bf16[1024,512]{1,0:T(8,128)(2,1)}) custom-call(bf16[64,2048]{1,0:T(8,128)(2,1)} %basis_ref.2, bf16[2048,512]{1,0:T(8,128)(2,1)} %modes_ref.3), custom_call_target="tpu_custom_call" | custom-call | flops 134217728 | bytes 3145728 | tf_op jit(solution)/shard_map/compress/pallas_call | solution.py:49
  10.2 3.2 %dispatch.1 = bf16[16,528,128]{2,1,0:T(8,128)(2,1)S(1)} custom-call(s32[128]{0:T(128)S(1)} %copy-done.8, s32[128]{0:T(128)S(1)} %bitcast.4, s32[128]{0:T(128)S(1)} %copy-done.10, bf16[128,32,128]{2,1,0:T(8,128)(2,1)S(1)} %bitcast.3), custom_call_target="tpu_custom_call" | custom-call | flops 4194304 | bytes 3145728 | tf_op jit(solution)/shard_map/dispatch/pallas_call | solution.py:108
  13.4 37.2 %all_to_all.5.sent_ref = bf16[16,528,128]{2,1,0:T(8,128)(2,1)} all-to-all(bf16[16,528,128]{2,1,0:T(8,128)(2,1)S(1)} %dispatch.1), channel_id=1, replica_groups=mesh['crow'=8,'ccol'=16] {'ccol'}, dimensions={0} | all-to-all | bytes 4325376 | tf_op jit(solution)/shard_map/all_to_all | solution.py:423
  50.6 3.4 %collective-permute-start = (bf16[1024,512]{1,0:T(8,128)(2,1)}, bf16[1024,512]{1,0:T(8,128)(2,1)}, u32[]{:S(2)}, u32[]{:S(2)}) collective-permute-start(bf16[1024,512]{1,0:T(8,128)(2,1)} %get-tuple-element.72), channel_id=1, source_target_pairs={{0,1},{1,2},{2,3},{3,4},{4,5},{5,6},{6,7},{7,8},{8,9},{9,10},{10,1... | collective-permute-start | bytes 3145736 | tf_op jit(solution)/shard_map/ppermute | solution.py:428
  55.3 13.8 %far_x.1 = (bf16[32,64,256]{2,1,0:T(8,128)(2,1)}, bf16[32,64,256]{2,1,0:T(8,128)(2,1)}, f32[16,64,256]{2,1,0:T(8,128)}, f32[16,64,256]{2,1,0:T(8,128)}, f32[32,64,256]{2,1,0:T(8,128)}) custom-call(bf16[64,64,512]{2,1,0:T(8,128)(2,1)} %all-gather.2.cloned.1.call-done.comp_ref, bf16[16,528,128]{2,1,0:T(8,128)(2,1)} %all_to_all.5.sent_ref), custom_call_target="tpu_custom_call" | custom-call | flops 2147483648 | bytes 12582912 | tf_op jit(solution)/shard_map/far_x/pallas_call | solution.py:196
  69.1 4.4 %collective-permute-start.4 = (bf16[32,64,256]{2,1,0:T(8,128)(2,1)}, bf16[32,64,256]{2,1,0:T(8,128)(2,1)S(1)}, u32[]{:S(2)}, u32[]{:S(2)}) collective-permute-start(bf16[32,64,256]{2,1,0:T(8,128)(2,1)} %get-tuple-element.76), channel_id=1, source_target_pairs={{0,4},{1,5},{2,6},{3,7},{4,8},{5,9},{6,10},{7,11},{8,12},{9,13},{1... | collective-permute-start | bytes 3145736 | tf_op jit(solution)/shard_map/ppermute | solution.py:233
  73.5 1.9 %collective-permute-start.5 = (bf16[32,64,256]{2,1,0:T(8,128)(2,1)}, bf16[32,64,256]{2,1,0:T(8,128)(2,1)S(1)}, u32[]{:S(2)}, u32[]{:S(2)}) collective-permute-start(bf16[32,64,256]{2,1,0:T(8,128)(2,1)} %get-tuple-element.77), channel_id=1, source_target_pairs={{0,12},{1,13},{2,14},{3,15},{4,0},{5,1},{6,2},{7,3},{8,4},{9,5},{1... | collective-permute-start | bytes 3145736 | tf_op jit(solution)/shard_map/ppermute | solution.py:233
  75.4 13.7 %far_z.1 = (bf16[32,64,256]{2,1,0:T(8,128)(2,1)}, bf16[32,64,256]{2,1,0:T(8,128)(2,1)}, f32[16,64,256]{2,1,0:T(8,128)}, f32[16,64,256]{2,1,0:T(8,128)}, f32[32,64,256]{2,1,0:T(8,128)}) custom-call(bf16[64,64,512]{2,1,0:T(8,128)(2,1)} %all-gather.2.cloned.1.call-done.comp_ref, bf16[16,528,128]{2,1,0:T(8,128)(2,1)} %all_to_all.5.sent_ref), custom_call_target="tpu_custom_call" | custom-call | flops 2147483648 | bytes 12582912 | tf_op jit(solution)/shard_map/far_z/pallas_call | solution.py:196
  89.9 8.4 %collective-permute-start.3 = (bf16[32,64,256]{2,1,0:T(8,128)(2,1)}, bf16[32,64,256]{2,1,0:T(8,128)(2,1)S(1)}, u32[]{:S(2)}, u32[]{:S(2)}) collective-permute-start(bf16[32,64,256]{2,1,0:T(8,128)(2,1)} %get-tuple-element.75), channel_id=1, source_target_pairs={{0,3},{1,0},{2,1},{3,2},{4,7},{5,4},{6,5},{7,6},{8,11},{9,8},{10,9... | collective-permute-start | bytes 3145736 | tf_op jit(solution)/shard_map/ppermute | solution.py:233
  98.4 4.4 %collective-permute-done.5.down_ref.refs_1_ = bf16[32,64,256]{2,1,0:T(8,128)(2,1)S(1)} collective-permute-done((bf16[32,64,256]{2,1,0:T(8,128)(2,1)}, bf16[32,64,256]{2,1,0:T(8,128)(2,1)S(1)}, u32[]{:S(2)}, u32[]{:S(2)}) %collective-permute-start.5) | collective-permute-done | bytes 1048608 | tf_op jit(solution)/shard_map/ppermute | solution.py:233
  106.1 2.4 %collective-permute-start.7 = (bf16[16,64,256]{2,1,0:T(8,128)(2,1)}, bf16[16,64,256]{2,1,0:T(8,128)(2,1)}, u32[]{:S(2)}, u32[]{:S(2)}) collective-permute-start(bf16[16,64,256]{2,1,0:T(8,128)(2,1)} %get-tuple-element.92), channel_id=1, source_target_pairs={{0,12},{1,13},{2,14},{3,15},{4,0},{5,1},{6,2},{7,3},{8,4},{9,5},{1... | collective-permute-start | bytes 1572872 | tf_op jit(solution)/shard_map/ppermute | solution.py:233
  108.5 12.4 %near_field.1 = (f32[2048,512]{1,0:T(8,128)}, bf16[2048,64]{1,0:T(8,128)(2,1)}) custom-call(bf16[2048,2304]{1,0:T(8,128)(2,1)} %near_ref.1, bf16[1024,512]{1,0:T(8,128)(2,1)} %collective-permute-done.before_ref, bf16[2048,512]{1,0:T(8,128)(2,1)} %modes_ref.3, bf16[1024,512]{1,0:T(8,128)(2,1)} %collective-permute-done.1.after_ref, bf16[64,2048]{1,0:T(8,128)(2,1)} %basis_ref.3), custom_call_target="tpu_custom_call" | custom-call | flops 38654705664 | bytes 18874368 | tf_op jit(solution)/shard_map/near_field/pallas_call | solution.py:342
  120.9 1.4 copy-done.4
  122.5 3.2 %collective-permute-start.13 = (bf16[16,64,256]{2,1,0:T(8,128)(2,1)S(1)}, bf16[16,64,256]{2,1,0:T(8,128)(2,1)S(1)}, u32[]{:S(2)}, u32[]{:S(2)}) collective-permute-start(bf16[16,64,256]{2,1,0:T(8,128)(2,1)S(1)} %get-tuple-element.98), channel_id=1, source_target_pairs={{0,3},{1,0},{2,1},{3,2},{4,7},{5,4},{6,5},{7,6},{8,11},{9,8},{10,9... | collective-permute-start | bytes 1572872 | tf_op jit(solution)/shard_map/ppermute | solution.py:233
  125.8 1.5 turn.2
  127.3 3.2 %collective-permute-start.9 = (bf16[8,64,256]{2,1,0:T(8,128)(2,1)S(1)}, bf16[8,64,256]{2,1,0:T(8,128)(2,1)S(1)}, u32[]{:S(2)}, u32[]{:S(2)}) collective-permute-start(bf16[8,64,256]{2,1,0:T(8,128)(2,1)S(1)} %get-tuple-element.103), channel_id=1, source_target_pairs={{0,3},{1,0},{2,1},{3,2},{4,7},{5,4},{6,5},{7,6},{8,11},{9,8},{10,9... | collective-permute-start | bytes 786440 | tf_op jit(solution)/shard_map/ppermute | solution.py:233
  130.6 9.5 %collective-permute-done.8.up_ref.refs_1_ = bf16[8,64,256]{2,1,0:T(8,128)(2,1)S(1)} collective-permute-done((bf16[8,64,256]{2,1,0:T(8,128)(2,1)S(1)}, bf16[8,64,256]{2,1,0:T(8,128)(2,1)S(1)}, u32[]{:S(2)}, u32[]{:S(2)}) %collective-permute-start.8) | collective-permute-done | bytes 262176 | tf_op jit(solution)/shard_map/ppermute | solution.py:233
  140.4 3.1 %collective-permute-start.11 = (bf16[4,64,256]{2,1,0:T(8,128)(2,1)S(1)}, bf16[4,64,256]{2,1,0:T(8,128)(2,1)S(1)}, u32[]{:S(2)}, u32[]{:S(2)}) collective-permute-start(bf16[4,64,256]{2,1,0:T(8,128)(2,1)S(1)} %get-tuple-element.107), channel_id=1, source_target_pairs={{0,3},{1,0},{2,1},{3,2},{4,7},{5,4},{6,5},{7,6},{8,11},{9,8},{10,9... | collective-permute-start | bytes 393224 | tf_op jit(solution)/shard_map/ppermute | solution.py:233
  143.5 2.9 %collective-permute-done.10.refs_3_ = bf16[4,64,256]{2,1,0:T(8,128)(2,1)S(1)} collective-permute-done((bf16[4,64,256]{2,1,0:T(8,128)(2,1)S(1)}, bf16[4,64,256]{2,1,0:T(8,128)(2,1)S(1)}, u32[]{:S(2)}, u32[]{:S(2)}) %collective-permute-start.10) | collective-permute-done | bytes 131104 | tf_op jit(solution)/shard_map/ppermute | solution.py:233
  146.8 3.2 %collective-permute-start.15 = (bf16[8,64,256]{2,1,0:T(8,128)(2,1)S(1)}, bf16[8,64,256]{2,1,0:T(8,128)(2,1)S(1)}, u32[]{:S(2)}, u32[]{:S(2)}) collective-permute-start(bf16[8,64,256]{2,1,0:T(8,128)(2,1)S(1)} %get-tuple-element.118), channel_id=1, source_target_pairs={{0,12},{1,13},{2,14},{3,15},{4,0},{5,1},{6,2},{7,3},{8,4},{9,5},{1... | collective-permute-start | bytes 786440 | tf_op jit(solution)/shard_map/ppermute | solution.py:233
  150.0 5.8 %collective-permute-done.14.up_ref.refs_6_ = bf16[8,64,256]{2,1,0:T(8,128)(2,1)S(1)} collective-permute-done((bf16[8,64,256]{2,1,0:T(8,128)(2,1)S(1)}, bf16[8,64,256]{2,1,0:T(8,128)(2,1)S(1)}, u32[]{:S(2)}, u32[]{:S(2)}) %collective-permute-start.14) | collective-permute-done | bytes 262176 | tf_op jit(solution)/shard_map/ppermute | solution.py:233
  155.9 3.3 %collective-permute-start.17 = (bf16[4,64,256]{2,1,0:T(8,128)(2,1)S(1)}, bf16[4,64,256]{2,1,0:T(8,128)(2,1)S(1)}, u32[]{:S(2)}, u32[]{:S(2)}) collective-permute-start(bf16[4,64,256]{2,1,0:T(8,128)(2,1)S(1)} %get-tuple-element.122), channel_id=1, source_target_pairs={{0,12},{1,13},{2,14},{3,15},{4,0},{5,1},{6,2},{7,3},{8,4},{9,5},{1... | collective-permute-start | bytes 393224 | tf_op jit(solution)/shard_map/ppermute | solution.py:233
  159.2 2.9 %collective-permute-done.16.refs_8_ = bf16[4,64,256]{2,1,0:T(8,128)(2,1)S(1)} collective-permute-done((bf16[4,64,256]{2,1,0:T(8,128)(2,1)S(1)}, bf16[4,64,256]{2,1,0:T(8,128)(2,1)S(1)}, u32[]{:S(2)}, u32[]{:S(2)}) %collective-permute-start.16) | collective-permute-done | bytes 131104 | tf_op jit(solution)/shard_map/ppermute | solution.py:233
  162.1 2.5 %expand.1 = bf16[2048,512]{1,0:T(8,128)(2,1)} custom-call(f32[2048,512]{1,0:T(8,128)S(1)} %copy-done, bf16[2048,64]{1,0:T(8,128)(2,1)S(1)} %copy-done.7, f32[8,64,256]{2,1,0:T(8,128)S(1)} %get-tuple-element.108.refs_0_, bf16[8,64,256]{2,1,0:T(8,128)(2,1)S(1)} %collective-permute-done.8.up_ref.refs_1_, ...), custom_call_target="tpu_custom_call" | custom-call | flops 134217728 | bytes 7340032 | tf_op jit(solution)/shard_map/expand/pallas_call | solution.py:389
  (53 shorter events, 6.9 us)
Async XLA Ops:
  6.5 48.8 %all-gather.2.cloned.1.call-start = ((), (), s32[]{:S(2)}) async-start(), calls=%async_computation.1 | async-start | bytes 4718592 | tf_op jit(solution)/shard_map/all_gather | solution.py:416
  50.6 38.5 %collective-permute-start = (bf16[1024,512]{1,0:T(8,128)(2,1)}, bf16[1024,512]{1,0:T(8,128)(2,1)}, u32[]{:S(2)}, u32[]{:S(2)}) collective-permute-start(bf16[1024,512]{1,0:T(8,128)(2,1)} %get-tuple-element.72), channel_id=1, source_target_pairs={{0,1},{1,2},{2,3},{3,4},{4,5},{5,6},{6,7},{7,8},{8,9},{9,10},{10,1... | collective-permute-start | bytes 3145736 | tf_op jit(solution)/shard_map/ppermute | solution.py:428
  54.0 35.1 %collective-permute-start.1 = (bf16[1024,512]{1,0:T(8,128)(2,1)}, bf16[1024,512]{1,0:T(8,128)(2,1)}, u32[]{:S(2)}, u32[]{:S(2)}) collective-permute-start(bf16[1024,512]{1,0:T(8,128)(2,1)} %get-tuple-element.73), channel_id=1, source_target_pairs={{1,0},{2,1},{3,2},{4,3},{5,4},{6,5},{7,6},{8,7},{9,8},{10,9},{11,1... | collective-permute-start | bytes 3145736 | tf_op jit(solution)/shard_map/ppermute | solution.py:429
  69.1 29.3 %collective-permute-start.4 = (bf16[32,64,256]{2,1,0:T(8,128)(2,1)}, bf16[32,64,256]{2,1,0:T(8,128)(2,1)S(1)}, u32[]{:S(2)}, u32[]{:S(2)}) collective-permute-start(bf16[32,64,256]{2,1,0:T(8,128)(2,1)} %get-tuple-element.76), channel_id=1, source_target_pairs={{0,4},{1,5},{2,6},{3,7},{4,8},{5,9},{6,10},{7,11},{8,12},{9,13},{1... | collective-permute-start | bytes 3145736 | tf_op jit(solution)/shard_map/ppermute | solution.py:233
  73.5 29.4 %copy-start.5 = (f32[16,64,256]{2,1,0:T(8,128)S(1)}, f32[16,64,256]{2,1,0:T(8,128)}, u32[]{:S(2)}) copy-start(f32[16,64,256]{2,1,0:T(8,128)} %get-tuple-element.89.following_ref) | copy-start | bytes 3145732
  73.5 29.4 %collective-permute-start.5 = (bf16[32,64,256]{2,1,0:T(8,128)(2,1)}, bf16[32,64,256]{2,1,0:T(8,128)(2,1)S(1)}, u32[]{:S(2)}, u32[]{:S(2)}) collective-permute-start(bf16[32,64,256]{2,1,0:T(8,128)(2,1)} %get-tuple-element.77), channel_id=1, source_target_pairs={{0,12},{1,13},{2,14},{3,15},{4,0},{5,1},{6,2},{7,3},{8,4},{9,5},{1... | collective-permute-start | bytes 3145736 | tf_op jit(solution)/shard_map/ppermute | solution.py:233
  89.1 31.8 %collective-permute-start.2 = (bf16[32,64,256]{2,1,0:T(8,128)(2,1)}, bf16[32,64,256]{2,1,0:T(8,128)(2,1)S(1)}, u32[]{:S(2)}, u32[]{:S(2)}) collective-permute-start(bf16[32,64,256]{2,1,0:T(8,128)(2,1)} %get-tuple-element.74), channel_id=1, source_target_pairs={{0,1},{1,2},{2,3},{3,0},{4,5},{5,6},{6,7},{7,4},{8,9},{9,10},{10,1... | collective-permute-start | bytes 3145736 | tf_op jit(solution)/shard_map/ppermute | solution.py:233
  89.9 31.0 %collective-permute-start.3 = (bf16[32,64,256]{2,1,0:T(8,128)(2,1)}, bf16[32,64,256]{2,1,0:T(8,128)(2,1)S(1)}, u32[]{:S(2)}, u32[]{:S(2)}) collective-permute-start(bf16[32,64,256]{2,1,0:T(8,128)(2,1)} %get-tuple-element.75), channel_id=1, source_target_pairs={{0,3},{1,0},{2,1},{3,2},{4,7},{5,4},{6,5},{7,6},{8,11},{9,8},{10,9... | collective-permute-start | bytes 3145736 | tf_op jit(solution)/shard_map/ppermute | solution.py:233
  105.3 20.5 %collective-permute-start.6 = (bf16[16,64,256]{2,1,0:T(8,128)(2,1)}, bf16[16,64,256]{2,1,0:T(8,128)(2,1)S(1)}, u32[]{:S(2)}, u32[]{:S(2)}) collective-permute-start(bf16[16,64,256]{2,1,0:T(8,128)(2,1)} %get-tuple-element.91), channel_id=1, source_target_pairs={{0,4},{1,5},{2,6},{3,7},{4,8},{5,9},{6,10},{7,11},{8,12},{9,13},{1... | collective-permute-start | bytes 1572872 | tf_op jit(solution)/shard_map/ppermute | solution.py:233
  106.1 14.8 %copy-start.3 = (f32[16,64,256]{2,1,0:T(8,128)S(1)}, f32[16,64,256]{2,1,0:T(8,128)}, u32[]{:S(2)}) copy-start(f32[16,64,256]{2,1,0:T(8,128)} %get-tuple-element.93.following_ref) | copy-start | bytes 3145732
  106.1 19.6 %collective-permute-start.7 = (bf16[16,64,256]{2,1,0:T(8,128)(2,1)}, bf16[16,64,256]{2,1,0:T(8,128)(2,1)}, u32[]{:S(2)}, u32[]{:S(2)}) collective-permute-start(bf16[16,64,256]{2,1,0:T(8,128)(2,1)} %get-tuple-element.92), channel_id=1, source_target_pairs={{0,12},{1,13},{2,14},{3,15},{4,0},{5,1},{6,2},{7,3},{8,4},{9,5},{1... | collective-permute-start | bytes 1572872 | tf_op jit(solution)/shard_map/ppermute | solution.py:233
  122.4 21.0 %collective-permute-start.12 = (bf16[16,64,256]{2,1,0:T(8,128)(2,1)S(1)}, bf16[16,64,256]{2,1,0:T(8,128)(2,1)S(1)}, u32[]{:S(2)}, u32[]{:S(2)}) collective-permute-start(bf16[16,64,256]{2,1,0:T(8,128)(2,1)S(1)} %get-tuple-element.97), channel_id=1, source_target_pairs={{0,1},{1,2},{2,3},{3,0},{4,5},{5,6},{6,7},{7,4},{8,9},{9,10},{10,1... | collective-permute-start | bytes 1572872 | tf_op jit(solution)/shard_map/ppermute | solution.py:233
  122.5 20.9 %collective-permute-start.13 = (bf16[16,64,256]{2,1,0:T(8,128)(2,1)S(1)}, bf16[16,64,256]{2,1,0:T(8,128)(2,1)S(1)}, u32[]{:S(2)}, u32[]{:S(2)}) collective-permute-start(bf16[16,64,256]{2,1,0:T(8,128)(2,1)S(1)} %get-tuple-element.98), channel_id=1, source_target_pairs={{0,3},{1,0},{2,1},{3,2},{4,7},{5,4},{6,5},{7,6},{8,11},{9,8},{10,9... | collective-permute-start | bytes 1572872 | tf_op jit(solution)/shard_map/ppermute | solution.py:233
  125.8 20.6 %copy-start.1 = (f32[32,64,256]{2,1,0:T(8,128)S(1)}, f32[32,64,256]{2,1,0:T(8,128)}, u32[]{:S(2)}) copy-start(f32[32,64,256]{2,1,0:T(8,128)} %get-tuple-element.113.own_ref) | copy-start | bytes 6291460
  127.3 12.8 %collective-permute-start.8 = (bf16[8,64,256]{2,1,0:T(8,128)(2,1)S(1)}, bf16[8,64,256]{2,1,0:T(8,128)(2,1)S(1)}, u32[]{:S(2)}, u32[]{:S(2)}) collective-permute-start(bf16[8,64,256]{2,1,0:T(8,128)(2,1)S(1)} %get-tuple-element.102), channel_id=1, source_target_pairs={{0,1},{1,2},{2,3},{3,0},{4,5},{5,6},{6,7},{7,4},{8,9},{9,10},{10,1... | collective-permute-start | bytes 786440 | tf_op jit(solution)/shard_map/ppermute | solution.py:233
  127.3 12.8 %collective-permute-start.9 = (bf16[8,64,256]{2,1,0:T(8,128)(2,1)S(1)}, bf16[8,64,256]{2,1,0:T(8,128)(2,1)S(1)}, u32[]{:S(2)}, u32[]{:S(2)}) collective-permute-start(bf16[8,64,256]{2,1,0:T(8,128)(2,1)S(1)} %get-tuple-element.103), channel_id=1, source_target_pairs={{0,3},{1,0},{2,1},{3,2},{4,7},{5,4},{6,5},{7,6},{8,11},{9,8},{10,9... | collective-permute-start | bytes 786440 | tf_op jit(solution)/shard_map/ppermute | solution.py:233
  140.1 6.2 %collective-permute-start.10 = (bf16[4,64,256]{2,1,0:T(8,128)(2,1)S(1)}, bf16[4,64,256]{2,1,0:T(8,128)(2,1)S(1)}, u32[]{:S(2)}, u32[]{:S(2)}) collective-permute-start(bf16[4,64,256]{2,1,0:T(8,128)(2,1)S(1)} %get-tuple-element.106), channel_id=1, source_target_pairs={{0,1},{1,2},{2,3},{3,0},{4,5},{5,6},{6,7},{7,4},{8,9},{9,10},{10,1... | collective-permute-start | bytes 393224 | tf_op jit(solution)/shard_map/ppermute | solution.py:233
  140.4 6.0 %collective-permute-start.11 = (bf16[4,64,256]{2,1,0:T(8,128)(2,1)S(1)}, bf16[4,64,256]{2,1,0:T(8,128)(2,1)S(1)}, u32[]{:S(2)}, u32[]{:S(2)}) collective-permute-start(bf16[4,64,256]{2,1,0:T(8,128)(2,1)S(1)} %get-tuple-element.107), channel_id=1, source_target_pairs={{0,3},{1,0},{2,1},{3,2},{4,7},{5,4},{6,5},{7,6},{8,11},{9,8},{10,9... | collective-permute-start | bytes 393224 | tf_op jit(solution)/shard_map/ppermute | solution.py:233
  146.4 15.7 %copy-start = (f32[2048,512]{1,0:T(8,128)S(1)}, f32[2048,512]{1,0:T(8,128)}, u32[]{:S(2)}) copy-start(f32[2048,512]{1,0:T(8,128)} %get-tuple-element.84.near_ref) | copy-start | bytes 12582916
  146.4 15.7 %copy-start.7 = (bf16[2048,64]{1,0:T(8,128)(2,1)S(1)}, bf16[2048,64]{1,0:T(8,128)(2,1)}, u32[]{:S(2)}) copy-start(bf16[2048,64]{1,0:T(8,128)(2,1)} %get-tuple-element.85.basis_ref) | copy-start | bytes 786436
  146.7 9.1 %collective-permute-start.14 = (bf16[8,64,256]{2,1,0:T(8,128)(2,1)S(1)}, bf16[8,64,256]{2,1,0:T(8,128)(2,1)S(1)}, u32[]{:S(2)}, u32[]{:S(2)}) collective-permute-start(bf16[8,64,256]{2,1,0:T(8,128)(2,1)S(1)} %get-tuple-element.117), channel_id=1, source_target_pairs={{0,4},{1,5},{2,6},{3,7},{4,8},{5,9},{6,10},{7,11},{8,12},{9,13},{1... | collective-permute-start | bytes 786440 | tf_op jit(solution)/shard_map/ppermute | solution.py:233
  146.8 9.0 %collective-permute-start.15 = (bf16[8,64,256]{2,1,0:T(8,128)(2,1)S(1)}, bf16[8,64,256]{2,1,0:T(8,128)(2,1)S(1)}, u32[]{:S(2)}, u32[]{:S(2)}) collective-permute-start(bf16[8,64,256]{2,1,0:T(8,128)(2,1)S(1)} %get-tuple-element.118), channel_id=1, source_target_pairs={{0,12},{1,13},{2,14},{3,15},{4,0},{5,1},{6,2},{7,3},{8,4},{9,5},{1... | collective-permute-start | bytes 786440 | tf_op jit(solution)/shard_map/ppermute | solution.py:233
  155.8 6.2 %collective-permute-start.16 = (bf16[4,64,256]{2,1,0:T(8,128)(2,1)S(1)}, bf16[4,64,256]{2,1,0:T(8,128)(2,1)S(1)}, u32[]{:S(2)}, u32[]{:S(2)}) collective-permute-start(bf16[4,64,256]{2,1,0:T(8,128)(2,1)S(1)} %get-tuple-element.121), channel_id=1, source_target_pairs={{0,4},{1,5},{2,6},{3,7},{4,8},{5,9},{6,10},{7,11},{8,12},{9,13},{1... | collective-permute-start | bytes 393224 | tf_op jit(solution)/shard_map/ppermute | solution.py:233
  155.9 6.2 %collective-permute-start.17 = (bf16[4,64,256]{2,1,0:T(8,128)(2,1)S(1)}, bf16[4,64,256]{2,1,0:T(8,128)(2,1)S(1)}, u32[]{:S(2)}, u32[]{:S(2)}) collective-permute-start(bf16[4,64,256]{2,1,0:T(8,128)(2,1)S(1)} %get-tuple-element.122), channel_id=1, source_target_pairs={{0,12},{1,13},{2,14},{3,15},{4,0},{5,1},{6,2},{7,3},{8,4},{9,5},{1... | collective-permute-start | bytes 393224 | tf_op jit(solution)/shard_map/ppermute | solution.py:233
  (7 other events, 21.6 us)
Sparse Core Ops, SparseCore 0:
  10.0 34.5 all-gather.1

commit v5 on v4

--- a/solution.py
+++ b/solution.py
@@ -209,7 +209,7 @@
             SMEM((sources * slots + UNROLL,), jnp.int32),
             pltpu.SemaphoreType.DMA,
         ],
-        compiler_params=pltpu.CompilerParams(vmem_limit_bytes=58 * MIB),
+        compiler_params=pltpu.CompilerParams(vmem_limit_bytes=40 * MIB),
         cost_estimate=pl.CostEstimate(
             flops=2 * 128 * rank * rank * width * 8, bytes_accessed=12 * MIB, transcendentals=0
         ),
@@ -306,12 +306,6 @@
     )(own, up, down, up_rest, down_rest)
 
 
-def second_stage(parts, along_x):
-    up, down, following, last, own = parts
-    up, down = both_ways(up, down, along_x)
-    return own, up, down, *both_ways(*passed_on(following, last, up, down), along_x)
-
-
 def near_kernel(near_ref, before_ref, modes_ref, after_ref, basis_ref, out_ref, turned_ref, ext_ref):
     r = pl.program_id(0)
     halo, panels = before_ref.shape[0], modes_ref.shape[0]
@@ -354,7 +348,7 @@
             jax.ShapeDtypeStruct((panels, rank), jnp.bfloat16),
         ],
         scratch_shapes=[VMEM((panels + 2 * halo, cols), jnp.bfloat16)],
-        compiler_params=pltpu.CompilerParams(vmem_limit_bytes=58 * MIB),
+        compiler_params=pltpu.CompilerParams(vmem_limit_bytes=32 * MIB),
         cost_estimate=pl.CostEstimate(
             flops=16 * panels * band * cols, bytes_accessed=18 * MIB, transcendentals=0
         ),
@@ -443,9 +437,15 @@
     right_rest = passed_on(right[2], right[3], right_up, right_down)
     left_rest, _ = lax.optimization_barrier((left_rest, right_rest))
     right_rest = both_ways(*right_rest, False)
-    left = second_stage(turn(left[4], left_up, left_down, *left_rest), False)
-    left, right_rest = lax.optimization_barrier((left, right_rest))
-    right = second_stage(turn(right[4], right_up, right_down, *right_rest), True)
+    left = turn(left[4], left_up, left_down, *left_rest)
+    left_up, left_down = both_ways(left[0], left[1], False)
+    right = turn(right[4], right_up, right_down, *right_rest)
+    right_up, right_down = both_ways(right[0], right[1], True)
+    (left_up, left_down), _ = lax.optimization_barrier(((left_up, left_down), right))
+    left_rest = both_ways(*passed_on(left[2], left[3], left_up, left_down), False)
+    right_rest = both_ways(*passed_on(right[2], right[3], right_up, right_down), True)
+    left = (left[4], left_up, left_down, *left_rest)
+    right = (right[4], right_up, right_down, *right_rest)
     return expand(near, basis, left, right)
 
 

time: 173 us -> 159 us (0.919)
  Pallas kernels: 52 us -> 41.9 us
  starting transfers between devices: 40 us -> 32.9 us
  local copies, waits for them, and re-layouts: 2.87 us -> 6.13 us
    ppermute x8, starting transfers between devices: 28.7 us -> 21.4 us  [both_ways(): lax.ppermute(down, 'ccol', ring(along_x, -1))]
    pallas_call x1, Pallas kernels: 12.4 us -> 8 us  [near_field(): pl.pallas_call(near_kernel, grid=(panels // CS,), in_specs=[pl.BlockSpec(...]
    pallas_call x2, Pallas kernels: 27.5 us -> 23.9 us  [far_field(): pl.pallas_call(functools.partial(far_kernel, slots, rows, x_first), grid=...]
    unnamed x25 -> x17, local copies, waits for them, and re-layouts: 2.87 us -> 6.13 us
    ppermute x8, waiting for transfers between devices: 21.2 us -> 19.2 us  [both_ways(): lax.ppermute(up, 'ccol', ring(along_x, 1))]
  transfers between devices with their start and end apart: 19 -> 19, of which waited for: 6 -> 5; matrix products, arithmetic and copies ran while one was open for 0% -> 0% of each run, Pallas kernels for 27% -> 23%
where the time goes in v5:
time: 159 us; the launch traced here: 156 us
  Pallas kernels  41.9 us (26%)
  blocking collectives  37.1 us (23%)
  starting transfers between devices  32.9 us (21%)
  waiting for transfers between devices  24.8 us (16%)
  between operations  13.6 us (9%)
  local copies, waits for them, and re-layouts  6.13 us (4%)
    all_to_all x1, blocking collectives, per_device(): sent = lax.all_to_all(sent, 'ccol', split_axis=0, concat_axis=0, tiled=True)  37.1 us
    pallas_call x2, Pallas kernels, far_field(): pl.pallas_call(functools.partial(far_kernel, slots, rows, x_first), grid=...  23.9 us
    ppermute x8, starting transfers between devices, both_ways(): lax.ppermute(down, 'ccol', ring(along_x, -1))  21.4 us
    ppermute x8, waiting for transfers between devices, both_ways(): lax.ppermute(up, 'ccol', ring(along_x, 1))  19.2 us
    pallas_call x1, Pallas kernels, near_field(): pl.pallas_call(near_kernel, grid=(panels // CS,), in_specs=[pl.BlockSpec(...  8 us
    ppermute x8, starting transfers between devices, both_ways(): lax.ppermute(up, 'ccol', ring(along_x, 1))  7.71 us
    unnamed x17, local copies, waits for them, and re-layouts  6.13 us
    ppermute x8, waiting for transfers between devices, both_ways(): lax.ppermute(down, 'ccol', ring(along_x, -1))  5.62 us
  transfers between devices with their start and end apart: 19, of which 5 were waited for; matrix products, arithmetic and copies ran while one was open for 0% of the time, Pallas kernels for 23%

profile of v5, /device:TPU:0, one launch (start us, length us, event | category | flops | bytes accessed | tf_op | source)
XLA Modules:
  0.0 156.5 jit_solution(7368207453275759117)
XLA Ops:
  6.6 3.3 %compress.1 = (bf16[8,64,512]{2,1,0:T(8,128)(2,1)}, bf16[1024,512]{1,0:T(8,128)(2,1)}, bf16[1024,512]{1,0:T(8,128)(2,1)}) custom-call(bf16[64,2048]{1,0:T(8,128)(2,1)} %basis_ref.2, bf16[2048,512]{1,0:T(8,128)(2,1)} %modes_ref.3), custom_call_target="tpu_custom_call" | custom-call | flops 134217728 | bytes 3145728 | tf_op jit(solution)/shard_map/compress/pallas_call | solution.py:49
  10.2 3.2 %dispatch.1 = bf16[16,528,128]{2,1,0:T(8,128)(2,1)S(1)} custom-call(s32[128]{0:T(128)S(1)} %copy-done.1, s32[128]{0:T(128)S(1)} %bitcast.4, s32[128]{0:T(128)S(1)} %copy-done.3, bf16[128,32,128]{2,1,0:T(8,128)(2,1)S(1)} %bitcast.3), custom_call_target="tpu_custom_call" | custom-call | flops 4194304 | bytes 3145728 | tf_op jit(solution)/shard_map/dispatch/pallas_call | solution.py:108
  13.4 37.1 %all_to_all.5.sent_ref = bf16[16,528,128]{2,1,0:T(8,128)(2,1)S(1)} all-to-all(bf16[16,528,128]{2,1,0:T(8,128)(2,1)S(1)} %dispatch.1), channel_id=1, replica_groups=mesh['crow'=8,'ccol'=16] {'ccol'}, dimensions={0} | all-to-all | bytes 4325376 | tf_op jit(solution)/shard_map/all_to_all | solution.py:417
  50.5 2.5 %collective-permute-start = (bf16[1024,512]{1,0:T(8,128)(2,1)}, bf16[1024,512]{1,0:T(8,128)(2,1)S(1)}, u32[]{:S(2)}, u32[]{:S(2)}) collective-permute-start(bf16[1024,512]{1,0:T(8,128)(2,1)} %get-tuple-element.67), channel_id=1, source_target_pairs={{0,1},{1,2},{2,3},{3,4},{4,5},{5,6},{6,7},{7,8},{8,9},{9,10},{10,1... | collective-permute-start | bytes 3145736 | tf_op jit(solution)/shard_map/ppermute | solution.py:422
  53.0 1.3 collective-permute-start.1
  54.3 2.2 %copy-done.5 = bf16[64,64,512]{2,1,0:T(8,128)(2,1)S(1)} copy-done((bf16[64,64,512]{2,1,0:T(8,128)(2,1)S(1)}, bf16[64,64,512]{2,1,0:T(8,128)(2,1)}, u32[]{:S(2)}) %copy-start.5) | copy-done | bytes 4194328
  56.5 11.7 %far_x.1 = (bf16[32,64,256]{2,1,0:T(8,128)(2,1)}, bf16[32,64,256]{2,1,0:T(8,128)(2,1)S(1)}, f32[16,64,256]{2,1,0:T(8,128)S(1)}, f32[16,64,256]{2,1,0:T(8,128)S(1)}, f32[32,64,256]{2,1,0:T(8,128)S(1)}) custom-call(bf16[64,64,512]{2,1,0:T(8,128)(2,1)S(1)} %copy-done.5, bf16[16,528,128]{2,1,0:T(8,128)(2,1)S(1)} %all_to_all.5.sent_ref), custom_call_target="tpu_custom_call" | custom-call | flops 2147483648 | bytes 12582912 | tf_op jit(solution)/shard_map/far_x/pallas_call | solution.py:196
  68.2 5.9 %collective-permute-start.4 = (bf16[32,64,256]{2,1,0:T(8,128)(2,1)}, bf16[32,64,256]{2,1,0:T(8,128)(2,1)S(1)}, u32[]{:S(2)}, u32[]{:S(2)}) collective-permute-start(bf16[32,64,256]{2,1,0:T(8,128)(2,1)} %get-tuple-element.71), channel_id=1, source_target_pairs={{0,4},{1,5},{2,6},{3,7},{4,8},{5,9},{6,10},{7,11},{8,12},{9,13},{1... | collective-permute-start | bytes 3145736 | tf_op jit(solution)/shard_map/ppermute | solution.py:233
  74.1 12.2 %far_z.1 = (bf16[32,64,256]{2,1,0:T(8,128)(2,1)}, bf16[32,64,256]{2,1,0:T(8,128)(2,1)}, f32[16,64,256]{2,1,0:T(8,128)S(1)}, f32[16,64,256]{2,1,0:T(8,128)S(1)}, f32[32,64,256]{2,1,0:T(8,128)S(1)}) custom-call(bf16[64,64,512]{2,1,0:T(8,128)(2,1)S(1)} %copy-done.5, bf16[16,528,128]{2,1,0:T(8,128)(2,1)S(1)} %all_to_all.5.sent_ref), custom_call_target="tpu_custom_call" | custom-call | flops 2147483648 | bytes 12582912 | tf_op jit(solution)/shard_map/far_z/pallas_call | solution.py:196
  86.4 3.2 %collective-permute-start.3 = (bf16[32,64,256]{2,1,0:T(8,128)(2,1)}, bf16[32,64,256]{2,1,0:T(8,128)(2,1)S(1)}, u32[]{:S(2)}, u32[]{:S(2)}) collective-permute-start(bf16[32,64,256]{2,1,0:T(8,128)(2,1)} %get-tuple-element.70), channel_id=1, source_target_pairs={{0,3},{1,0},{2,1},{3,2},{4,7},{5,4},{6,5},{7,6},{8,11},{9,8},{10,9... | collective-permute-start | bytes 3145736 | tf_op jit(solution)/shard_map/ppermute | solution.py:233
  89.7 7.5 %collective-permute-done.4.up_ref.refs_0_ = bf16[32,64,256]{2,1,0:T(8,128)(2,1)S(1)} collective-permute-done((bf16[32,64,256]{2,1,0:T(8,128)(2,1)}, bf16[32,64,256]{2,1,0:T(8,128)(2,1)S(1)}, u32[]{:S(2)}, u32[]{:S(2)}) %collective-permute-start.4) | collective-permute-done | bytes 1048608 | tf_op jit(solution)/shard_map/ppermute | solution.py:233
  97.2 5.6 %collective-permute-done.5.down_ref.refs_1_ = bf16[32,64,256]{2,1,0:T(8,128)(2,1)S(1)} collective-permute-done((bf16[32,64,256]{2,1,0:T(8,128)(2,1)S(1)}, bf16[32,64,256]{2,1,0:T(8,128)(2,1)S(1)}, u32[]{:S(2)}, u32[]{:S(2)}) %collective-permute-start.5) | collective-permute-done | bytes 1048608 | tf_op jit(solution)/shard_map/ppermute | solution.py:233
  103.9 2.4 %collective-permute-start.7 = (bf16[16,64,256]{2,1,0:T(8,128)(2,1)S(1)}, bf16[16,64,256]{2,1,0:T(8,128)(2,1)S(1)}, u32[]{:S(2)}, u32[]{:S(2)}) collective-permute-start(bf16[16,64,256]{2,1,0:T(8,128)(2,1)S(1)} %get-tuple-element.87), channel_id=1, source_target_pairs={{0,12},{1,13},{2,14},{3,15},{4,0},{5,1},{6,2},{7,3},{8,4},{9,5},{1... | collective-permute-start | bytes 1572872 | tf_op jit(solution)/shard_map/ppermute | solution.py:233
  106.3 3.7 %copy-done.4 = bf16[2048,2304]{1,0:T(8,128)(2,1)S(1)} copy-done((bf16[2048,2304]{1,0:T(8,128)(2,1)S(1)}, bf16[2048,2304]{1,0:T(8,128)(2,1)}, u32[]{:S(2)}) %copy-start.4) | copy-done | bytes 9437208
  110.0 8.0 %near_field.1 = (f32[2048,512]{1,0:T(8,128)S(1)}, bf16[2048,64]{1,0:T(8,128)(2,1)S(1)}) custom-call(bf16[2048,2304]{1,0:T(8,128)(2,1)S(1)} %copy-done.4, bf16[1024,512]{1,0:T(8,128)(2,1)S(1)} %collective-permute-done.before_ref, bf16[2048,512]{1,0:T(8,128)(2,1)S(1)} %copy-done, bf16[1024,512]{1,0:T(8,128)(2,1)} %collective-permute-done.1.after_ref, ...), custom_call_target="tpu_custom_call" | custom-call | flops 38654705664 | bytes 18874368 | tf_op jit(solution)/shard_map/near_field/pallas_call | solution.py:336
  118.3 3.2 %collective-permute-start.11 = (bf16[16,64,256]{2,1,0:T(8,128)(2,1)S(1)}, bf16[16,64,256]{2,1,0:T(8,128)(2,1)S(1)}, u32[]{:S(2)}, u32[]{:S(2)}) collective-permute-start(bf16[16,64,256]{2,1,0:T(8,128)(2,1)S(1)} %get-tuple-element.93), channel_id=1, source_target_pairs={{0,3},{1,0},{2,1},{3,2},{4,7},{5,4},{6,5},{7,6},{8,11},{9,8},{10,9... | collective-permute-start | bytes 1572872 | tf_op jit(solution)/shard_map/ppermute | solution.py:233
  121.9 3.2 %collective-permute-start.9 = (bf16[8,64,256]{2,1,0:T(8,128)(2,1)S(1)}, bf16[8,64,256]{2,1,0:T(8,128)(2,1)S(1)}, u32[]{:S(2)}, u32[]{:S(2)}) collective-permute-start(bf16[8,64,256]{2,1,0:T(8,128)(2,1)S(1)} %get-tuple-element.98), channel_id=1, source_target_pairs={{0,3},{1,0},{2,1},{3,2},{4,7},{5,4},{6,5},{7,6},{8,11},{9,8},{10,9... | collective-permute-start | bytes 786440 | tf_op jit(solution)/shard_map/ppermute | solution.py:233
  125.1 7.8 %collective-permute-done.10.refs_2_ = bf16[16,64,256]{2,1,0:T(8,128)(2,1)S(1)} collective-permute-done((bf16[16,64,256]{2,1,0:T(8,128)(2,1)S(1)}, bf16[16,64,256]{2,1,0:T(8,128)(2,1)S(1)}, u32[]{:S(2)}, u32[]{:S(2)}) %collective-permute-start.10) | collective-permute-done | bytes 524320 | tf_op jit(solution)/shard_map/ppermute | solution.py:233
  133.3 3.2 %collective-permute-start.15 = (bf16[8,64,256]{2,1,0:T(8,128)(2,1)S(1)}, bf16[8,64,256]{2,1,0:T(8,128)(2,1)S(1)}, u32[]{:S(2)}, u32[]{:S(2)}) collective-permute-start(bf16[8,64,256]{2,1,0:T(8,128)(2,1)S(1)} %get-tuple-element.101), channel_id=1, source_target_pairs={{0,12},{1,13},{2,14},{3,15},{4,0},{5,1},{6,2},{7,3},{8,4},{9,5},{1... | collective-permute-start | bytes 786440 | tf_op jit(solution)/shard_map/ppermute | solution.py:233
  136.6 3.2 %collective-permute-start.13 = (bf16[4,64,256]{2,1,0:T(8,128)(2,1)S(1)}, bf16[4,64,256]{2,1,0:T(8,128)(2,1)S(1)}, u32[]{:S(2)}, u32[]{:S(2)}) collective-permute-start(bf16[4,64,256]{2,1,0:T(8,128)(2,1)S(1)} %get-tuple-element.110), channel_id=1, source_target_pairs={{0,3},{1,0},{2,1},{3,2},{4,7},{5,4},{6,5},{7,6},{8,11},{9,8},{10,9... | collective-permute-start | bytes 393224 | tf_op jit(solution)/shard_map/ppermute | solution.py:233
  139.9 1.0 collective-permute-done.14.up_ref.refs_6_
  141.4 2.9 %collective-permute-start.17 = (bf16[4,64,256]{2,1,0:T(8,128)(2,1)S(1)}, bf16[4,64,256]{2,1,0:T(8,128)(2,1)S(1)}, u32[]{:S(2)}, u32[]{:S(2)}) collective-permute-start(bf16[4,64,256]{2,1,0:T(8,128)(2,1)S(1)} %get-tuple-element.112), channel_id=1, source_target_pairs={{0,12},{1,13},{2,14},{3,15},{4,0},{5,1},{6,2},{7,3},{8,4},{9,5},{1... | collective-permute-start | bytes 393224 | tf_op jit(solution)/shard_map/ppermute | solution.py:233
  144.3 2.9 %collective-permute-done.16.refs_8_ = bf16[4,64,256]{2,1,0:T(8,128)(2,1)S(1)} collective-permute-done((bf16[4,64,256]{2,1,0:T(8,128)(2,1)S(1)}, bf16[4,64,256]{2,1,0:T(8,128)(2,1)S(1)}, u32[]{:S(2)}, u32[]{:S(2)}) %collective-permute-start.16) | collective-permute-done | bytes 131104 | tf_op jit(solution)/shard_map/ppermute | solution.py:233
  147.1 2.5 %expand.1 = bf16[2048,512]{1,0:T(8,128)(2,1)} custom-call(f32[2048,512]{1,0:T(8,128)S(1)} %get-tuple-element.79.near_ref, bf16[2048,64]{1,0:T(8,128)(2,1)S(1)} %get-tuple-element.80.basis_ref, f32[8,64,256]{2,1,0:T(8,128)S(1)} %get-tuple-element.96.refs_0_, bf16[8,64,256]{2,1,0:T(8,128)(2,1)S(1)} %collective-permute-done.8.up_ref.refs_1_, ...), custom_call_target="tpu_custom_call" | custom-call | flops 134217728 | bytes 7340032 | tf_op jit(solution)/shard_map/expand/pallas_call | solution.py:383
  (45 shorter events, 3.2 us)
Async XLA Ops:
  6.5 3.6 %copy-start.2 = (s32[128,1]{0,1:T(1,128)S(1)}, s32[128,1]{0,1:T(1,128)}, u32[]{:S(2)}) copy-start(s32[128,1]{0,1:T(1,128)} %param.13) | copy-start | bytes 1540
  6.5 3.6 %copy-start.1 = (s32[128]{0:T(128)S(1)}, s32[128]{0:T(128)}, u32[]{:S(2)}) copy-start(s32[128]{0:T(128)} %rows_ref.1) | copy-start | bytes 1540
  6.5 47.8 %all-gather.2.cloned.1.call-start = ((), (), s32[]{:S(2)}) async-start(), calls=%async_computation.1 | async-start | bytes 4718592 | tf_op jit(solution)/shard_map/all_gather | solution.py:410
  50.5 35.9 %collective-permute-start = (bf16[1024,512]{1,0:T(8,128)(2,1)}, bf16[1024,512]{1,0:T(8,128)(2,1)S(1)}, u32[]{:S(2)}, u32[]{:S(2)}) collective-permute-start(bf16[1024,512]{1,0:T(8,128)(2,1)} %get-tuple-element.67), channel_id=1, source_target_pairs={{0,1},{1,2},{2,3},{3,4},{4,5},{5,6},{6,7},{7,8},{8,9},{9,10},{10,1... | collective-permute-start | bytes 3145736 | tf_op jit(solution)/shard_map/ppermute | solution.py:422
  53.0 33.4 %collective-permute-start.1 = (bf16[1024,512]{1,0:T(8,128)(2,1)}, bf16[1024,512]{1,0:T(8,128)(2,1)}, u32[]{:S(2)}, u32[]{:S(2)}) collective-permute-start(bf16[1024,512]{1,0:T(8,128)(2,1)} %get-tuple-element.68), channel_id=1, source_target_pairs={{1,0},{2,1},{3,2},{4,3},{5,4},{6,5},{7,6},{8,7},{9,8},{10,9},{11,1... | collective-permute-start | bytes 3145736 | tf_op jit(solution)/shard_map/ppermute | solution.py:423
  68.2 29.0 %collective-permute-start.4 = (bf16[32,64,256]{2,1,0:T(8,128)(2,1)}, bf16[32,64,256]{2,1,0:T(8,128)(2,1)S(1)}, u32[]{:S(2)}, u32[]{:S(2)}) collective-permute-start(bf16[32,64,256]{2,1,0:T(8,128)(2,1)} %get-tuple-element.71), channel_id=1, source_target_pairs={{0,4},{1,5},{2,6},{3,7},{4,8},{5,9},{6,10},{7,11},{8,12},{9,13},{1... | collective-permute-start | bytes 3145736 | tf_op jit(solution)/shard_map/ppermute | solution.py:233
  74.1 28.7 %collective-permute-start.5 = (bf16[32,64,256]{2,1,0:T(8,128)(2,1)S(1)}, bf16[32,64,256]{2,1,0:T(8,128)(2,1)S(1)}, u32[]{:S(2)}, u32[]{:S(2)}) collective-permute-start(bf16[32,64,256]{2,1,0:T(8,128)(2,1)S(1)} %get-tuple-element.72), channel_id=1, source_target_pairs={{0,12},{1,13},{2,14},{3,15},{4,0},{5,1},{6,2},{7,3},{8,4},{9,5},{1... | collective-permute-start | bytes 3145736 | tf_op jit(solution)/shard_map/ppermute | solution.py:233
  86.3 20.0 %copy-start = (bf16[2048,512]{1,0:T(8,128)(2,1)S(1)}, bf16[2048,512]{1,0:T(8,128)(2,1)}, u32[]{:S(2)}) copy-start(bf16[2048,512]{1,0:T(8,128)(2,1)} %modes_ref.3) | copy-start | bytes 6291460
  86.3 20.0 %copy-start.6 = (bf16[64,2048]{1,0:T(8,128)(2,1)S(1)}, bf16[64,2048]{1,0:T(8,128)(2,1)}, u32[]{:S(2)}) copy-start(bf16[64,2048]{1,0:T(8,128)(2,1)} %basis_ref.3) | copy-start | bytes 786436
  86.4 31.6 %collective-permute-start.2 = (bf16[32,64,256]{2,1,0:T(8,128)(2,1)}, bf16[32,64,256]{2,1,0:T(8,128)(2,1)S(1)}, u32[]{:S(2)}, u32[]{:S(2)}) collective-permute-start(bf16[32,64,256]{2,1,0:T(8,128)(2,1)} %get-tuple-element.69), channel_id=1, source_target_pairs={{0,1},{1,2},{2,3},{3,0},{4,5},{5,6},{6,7},{7,4},{8,9},{9,10},{10,1... | collective-permute-start | bytes 3145736 | tf_op jit(solution)/shard_map/ppermute | solution.py:233
  86.4 31.5 %collective-permute-start.3 = (bf16[32,64,256]{2,1,0:T(8,128)(2,1)}, bf16[32,64,256]{2,1,0:T(8,128)(2,1)S(1)}, u32[]{:S(2)}, u32[]{:S(2)}) collective-permute-start(bf16[32,64,256]{2,1,0:T(8,128)(2,1)} %get-tuple-element.70), channel_id=1, source_target_pairs={{0,3},{1,0},{2,1},{3,2},{4,7},{5,4},{6,5},{7,6},{8,11},{9,8},{10,9... | collective-permute-start | bytes 3145736 | tf_op jit(solution)/shard_map/ppermute | solution.py:233
  103.0 18.5 %collective-permute-start.6 = (bf16[16,64,256]{2,1,0:T(8,128)(2,1)S(1)}, bf16[16,64,256]{2,1,0:T(8,128)(2,1)S(1)}, u32[]{:S(2)}, u32[]{:S(2)}) collective-permute-start(bf16[16,64,256]{2,1,0:T(8,128)(2,1)S(1)} %get-tuple-element.86), channel_id=1, source_target_pairs={{0,4},{1,5},{2,6},{3,7},{4,8},{5,9},{6,10},{7,11},{8,12},{9,13},{1... | collective-permute-start | bytes 1572872 | tf_op jit(solution)/shard_map/ppermute | solution.py:233
  103.9 17.6 %collective-permute-start.7 = (bf16[16,64,256]{2,1,0:T(8,128)(2,1)S(1)}, bf16[16,64,256]{2,1,0:T(8,128)(2,1)S(1)}, u32[]{:S(2)}, u32[]{:S(2)}) collective-permute-start(bf16[16,64,256]{2,1,0:T(8,128)(2,1)S(1)} %get-tuple-element.87), channel_id=1, source_target_pairs={{0,12},{1,13},{2,14},{3,15},{4,0},{5,1},{6,2},{7,3},{8,4},{9,5},{1... | collective-permute-start | bytes 1572872 | tf_op jit(solution)/shard_map/ppermute | solution.py:233
  106.3 3.7 %copy-start.4 = (bf16[2048,2304]{1,0:T(8,128)(2,1)S(1)}, bf16[2048,2304]{1,0:T(8,128)(2,1)}, u32[]{:S(2)}) copy-start(bf16[2048,2304]{1,0:T(8,128)(2,1)} %near_ref.1) | copy-start | bytes 28311556
  118.2 14.7 %collective-permute-start.10 = (bf16[16,64,256]{2,1,0:T(8,128)(2,1)S(1)}, bf16[16,64,256]{2,1,0:T(8,128)(2,1)S(1)}, u32[]{:S(2)}, u32[]{:S(2)}) collective-permute-start(bf16[16,64,256]{2,1,0:T(8,128)(2,1)S(1)} %get-tuple-element.92), channel_id=1, source_target_pairs={{0,1},{1,2},{2,3},{3,0},{4,5},{5,6},{6,7},{7,4},{8,9},{9,10},{10,1... | collective-permute-start | bytes 1572872 | tf_op jit(solution)/shard_map/ppermute | solution.py:233
  118.3 14.6 %collective-permute-start.11 = (bf16[16,64,256]{2,1,0:T(8,128)(2,1)S(1)}, bf16[16,64,256]{2,1,0:T(8,128)(2,1)S(1)}, u32[]{:S(2)}, u32[]{:S(2)}) collective-permute-start(bf16[16,64,256]{2,1,0:T(8,128)(2,1)S(1)} %get-tuple-element.93), channel_id=1, source_target_pairs={{0,3},{1,0},{2,1},{3,2},{4,7},{5,4},{6,5},{7,6},{8,11},{9,8},{10,9... | collective-permute-start | bytes 1572872 | tf_op jit(solution)/shard_map/ppermute | solution.py:233
  121.8 14.7 %collective-permute-start.8 = (bf16[8,64,256]{2,1,0:T(8,128)(2,1)S(1)}, bf16[8,64,256]{2,1,0:T(8,128)(2,1)S(1)}, u32[]{:S(2)}, u32[]{:S(2)}) collective-permute-start(bf16[8,64,256]{2,1,0:T(8,128)(2,1)S(1)} %get-tuple-element.97), channel_id=1, source_target_pairs={{0,1},{1,2},{2,3},{3,0},{4,5},{5,6},{6,7},{7,4},{8,9},{9,10},{10,1... | collective-permute-start | bytes 786440 | tf_op jit(solution)/shard_map/ppermute | solution.py:233
  121.9 14.6 %collective-permute-start.9 = (bf16[8,64,256]{2,1,0:T(8,128)(2,1)S(1)}, bf16[8,64,256]{2,1,0:T(8,128)(2,1)S(1)}, u32[]{:S(2)}, u32[]{:S(2)}) collective-permute-start(bf16[8,64,256]{2,1,0:T(8,128)(2,1)S(1)} %get-tuple-element.98), channel_id=1, source_target_pairs={{0,3},{1,0},{2,1},{3,2},{4,7},{5,4},{6,5},{7,6},{8,11},{9,8},{10,9... | collective-permute-start | bytes 786440 | tf_op jit(solution)/shard_map/ppermute | solution.py:233
  133.2 7.7 %collective-permute-start.14 = (bf16[8,64,256]{2,1,0:T(8,128)(2,1)S(1)}, bf16[8,64,256]{2,1,0:T(8,128)(2,1)S(1)}, u32[]{:S(2)}, u32[]{:S(2)}) collective-permute-start(bf16[8,64,256]{2,1,0:T(8,128)(2,1)S(1)} %get-tuple-element.100), channel_id=1, source_target_pairs={{0,4},{1,5},{2,6},{3,7},{4,8},{5,9},{6,10},{7,11},{8,12},{9,13},{1... | collective-permute-start | bytes 786440 | tf_op jit(solution)/shard_map/ppermute | solution.py:233
  133.3 7.6 %collective-permute-start.15 = (bf16[8,64,256]{2,1,0:T(8,128)(2,1)S(1)}, bf16[8,64,256]{2,1,0:T(8,128)(2,1)S(1)}, u32[]{:S(2)}, u32[]{:S(2)}) collective-permute-start(bf16[8,64,256]{2,1,0:T(8,128)(2,1)S(1)} %get-tuple-element.101), channel_id=1, source_target_pairs={{0,12},{1,13},{2,14},{3,15},{4,0},{5,1},{6,2},{7,3},{8,4},{9,5},{1... | collective-permute-start | bytes 786440 | tf_op jit(solution)/shard_map/ppermute | solution.py:233
  136.5 7.7 %collective-permute-start.12 = (bf16[4,64,256]{2,1,0:T(8,128)(2,1)S(1)}, bf16[4,64,256]{2,1,0:T(8,128)(2,1)S(1)}, u32[]{:S(2)}, u32[]{:S(2)}) collective-permute-start(bf16[4,64,256]{2,1,0:T(8,128)(2,1)S(1)} %get-tuple-element.109), channel_id=1, source_target_pairs={{0,1},{1,2},{2,3},{3,0},{4,5},{5,6},{6,7},{7,4},{8,9},{9,10},{10,1... | collective-permute-start | bytes 393224 | tf_op jit(solution)/shard_map/ppermute | solution.py:233
  136.6 7.6 %collective-permute-start.13 = (bf16[4,64,256]{2,1,0:T(8,128)(2,1)S(1)}, bf16[4,64,256]{2,1,0:T(8,128)(2,1)S(1)}, u32[]{:S(2)}, u32[]{:S(2)}) collective-permute-start(bf16[4,64,256]{2,1,0:T(8,128)(2,1)S(1)} %get-tuple-element.110), channel_id=1, source_target_pairs={{0,3},{1,0},{2,1},{3,2},{4,7},{5,4},{6,5},{7,6},{8,11},{9,8},{10,9... | collective-permute-start | bytes 393224 | tf_op jit(solution)/shard_map/ppermute | solution.py:233
  140.9 6.2 %collective-permute-start.16 = (bf16[4,64,256]{2,1,0:T(8,128)(2,1)S(1)}, bf16[4,64,256]{2,1,0:T(8,128)(2,1)S(1)}, u32[]{:S(2)}, u32[]{:S(2)}) collective-permute-start(bf16[4,64,256]{2,1,0:T(8,128)(2,1)S(1)} %get-tuple-element.111), channel_id=1, source_target_pairs={{0,4},{1,5},{2,6},{3,7},{4,8},{5,9},{6,10},{7,11},{8,12},{9,13},{1... | collective-permute-start | bytes 393224 | tf_op jit(solution)/shard_map/ppermute | solution.py:233
  141.4 5.8 %collective-permute-start.17 = (bf16[4,64,256]{2,1,0:T(8,128)(2,1)S(1)}, bf16[4,64,256]{2,1,0:T(8,128)(2,1)S(1)}, u32[]{:S(2)}, u32[]{:S(2)}) collective-permute-start(bf16[4,64,256]{2,1,0:T(8,128)(2,1)S(1)} %get-tuple-element.112), channel_id=1, source_target_pairs={{0,12},{1,13},{2,14},{3,15},{4,0},{5,1},{6,2},{7,3},{8,4},{9,5},{1... | collective-permute-start | bytes 393224 | tf_op jit(solution)/shard_map/ppermute | solution.py:233
  (3 other events, 9.1 us)
Sparse Core Ops, SparseCore 0:
  10.0 34.5 all-gather.1

commit v6 on v5

--- a/solution.py
+++ b/solution.py
@@ -117,74 +117,74 @@
     )(block_rows, owners, block_slot, cores)
 
 
-UNROLL = 8
-
-
-def far_kernel(
-    slots, rows, x_first, comp_ref, sent_ref, up_ref, down_ref, next_ref, last_ref, own_ref,
-    acc_ref, meta_ref, smem_ref, list_ref, sem,
-):
+UNROLL = 32
+
+
+def far_kernel(slots, rows, comp_ref, sent_ref, *refs):
+    outs, (left_ref, right_ref, meta_ref, smem_ref, list_ref, sem) = (refs[:5], refs[5:10]), refs[10:]
     sources = sent_ref.shape[0]
-    group_rows = acc_ref.shape[0]
+    group_rows, _, width = left_ref.shape
     part = group_rows // 4
+    row_part = part // 4
     me = lax.axis_index("ccol")
     here_x, here_z = me // 4, me % 4
 
-    acc_ref[...] = jnp.zeros_like(acc_ref)
     meta = sent_ref[:, slots * rows : slots * rows + 16, :].astype(jnp.float32)
-    meta_ref[...] = jnp.max(meta, axis=1).astype(jnp.int32)
+    meta = jnp.max(meta, axis=1).astype(jnp.int32)
+    lane = lax.broadcasted_iota(jnp.int32, meta.shape, 1)
+    row = pltpu.roll(meta, 128 - slots, axis=1) & (group_rows - 1)
+    to_x = (row // part - here_x) & 3
+    to_z = (row // row_part - here_z) & 3
+    rest = row & (row_part - 1)
+    left = to_x * part + to_z * row_part + rest
+    right = to_z * part + to_x * row_part + rest
+    place = lax.broadcasted_iota(jnp.int32, meta.shape, 0) * slots + lane
+    words = (place << 22) + (meta << 14) + (left << 7) + right
+    meta_ref[...] = jnp.where(lane < slots, words, meta)
     copy = pltpu.make_async_copy(meta_ref, smem_ref, sem)
     copy.start()
+    left_ref[...] = jnp.zeros_like(left_ref)
+    right_ref[...] = jnp.zeros_like(right_ref)
     copy.wait()
 
-    def source(i, total):
-        def entry(p, total):
-            row = smem_ref[i, slots + p]
-            to_x = (row // part - here_x + 4) % 4
-            to_z = (row // (part // 4) % 4 - here_z + 4) % 4
-            first, second = (to_x, to_z) if x_first else (to_z, to_x)
-            at = first * part + second * (part // 4) + row % (part // 4)
-            list_ref[total] = ((i * slots + p) << 16) + (smem_ref[i, p] << 8) + at
-            return total + 1
-
-        return lax.fori_loop(0, smem_ref[i, 2 * slots], entry, total)
-
-    total = lax.fori_loop(0, sources, source, 0)
+    total = 0
+    for i in range(sources):
+        for p in range(slots):
+            list_ref[total + p] = smem_ref[i, p]
+        total = total + smem_ref[i, 2 * slots]
     for i in range(UNROLL):
         list_ref[total + i] = 0
 
     def group(g, carry):
-        terms = []
         for i in range(UNROLL):
             at = g * UNROLL + i
             entry = list_ref[at]
-            place = entry >> 16
+            place = entry >> 22
             core = sent_ref[place // slots, pl.ds(pl.multiple_of((place % slots) * rows, rows), rows), :]
             core = jnp.where(at < total, core, jnp.zeros_like(core))
             half = core.shape[1] // 2
             core = jnp.concatenate([core[:, :half], core[:, half:]], axis=0)
-            comp = comp_ref[(entry >> 8) & 255]
-            terms.append((entry & 255, jnp.dot(core, comp, preferred_element_type=jnp.float32)))
-        for row, term in terms:
-            acc_ref[row] += term
+            comp = comp_ref[(entry >> 14) & 255]
+            left_ref[(entry >> 7) & 127] += jnp.dot(core, comp[:, :width], preferred_element_type=jnp.float32)
+            right_ref[entry & 127] += jnp.dot(core, comp[:, width:], preferred_element_type=jnp.float32)
         return carry
 
     lax.fori_loop(0, (total + UNROLL - 1) // UNROLL, group, 0)
     half = part // 2
-    own_ref[...] = acc_ref[:part]
-    next_ref[...] = acc_ref[part : part + half]
-    up_ref[half:] = acc_ref[part + half : 2 * part].astype(jnp.bfloat16)
-    up_ref[:half] = acc_ref[2 * part : 2 * part + half].astype(jnp.bfloat16)
-    down_ref[half:] = acc_ref[2 * part + half : 3 * part].astype(jnp.bfloat16)
-    down_ref[:half] = acc_ref[3 * part : 3 * part + half].astype(jnp.bfloat16)
-    last_ref[...] = acc_ref[3 * part + half :]
-
-
-def far_field(comp, sent, slots, rows, group_rows, x_first):
-    clusters, rank, cols = comp.shape
+    for acc_ref, (up_ref, down_ref, next_ref, last_ref, own_ref) in zip((left_ref, right_ref), outs):
+        own_ref[...] = acc_ref[:part]
+        next_ref[...] = acc_ref[part : part + half]
+        up_ref[half:] = acc_ref[part + half : 2 * part].astype(jnp.bfloat16)
+        up_ref[:half] = acc_ref[2 * part : 2 * part + half].astype(jnp.bfloat16)
+        down_ref[half:] = acc_ref[2 * part + half : 3 * part].astype(jnp.bfloat16)
+        down_ref[:half] = acc_ref[3 * part : 3 * part + half].astype(jnp.bfloat16)
+        last_ref[...] = acc_ref[3 * part + half :]
+
+
+def far_field(comp, sent, slots, rows, group_rows):
+    _, rank, cols = comp.shape
     sources = sent.shape[0]
     width = cols // 2
-    chunk = 0 if x_first else 1
     part = group_rows // 4
     kinds = [
         (part, jnp.bfloat16),
@@ -192,29 +192,27 @@
         (part // 2, jnp.float32),
         (part // 2, jnp.float32),
         (part, jnp.float32),
-    ]
-    return pl.pallas_call(
-        functools.partial(far_kernel, slots, rows, x_first),
-        grid=(1,),
-        in_specs=[
-            pl.BlockSpec((clusters, rank, width), lambda m: (0, 0, chunk)),
-            pl.BlockSpec(sent.shape, lambda m: (0, 0, 0)),
-        ],
-        out_specs=[pl.BlockSpec((n, rank, width), lambda m: (0, 0, 0)) for n, _ in kinds],
+    ] * 2
+    parts = pl.pallas_call(
+        functools.partial(far_kernel, slots, rows),
+        in_specs=[whole()] * 2,
+        out_specs=[whole()] * len(kinds),
         out_shape=[jax.ShapeDtypeStruct((n, rank, width), kind) for n, kind in kinds],
         scratch_shapes=[
             VMEM((group_rows, rank, width), jnp.float32),
+            VMEM((group_rows, rank, width), jnp.float32),
             VMEM((sources, 128), jnp.int32),
             SMEM((sources, 128), jnp.int32),
-            SMEM((sources * slots + UNROLL,), jnp.int32),
+            SMEM((sources * slots + UNROLL + slots,), jnp.int32),
             pltpu.SemaphoreType.DMA,
         ],
         compiler_params=pltpu.CompilerParams(vmem_limit_bytes=40 * MIB),
         cost_estimate=pl.CostEstimate(
-            flops=2 * 128 * rank * rank * width * 8, bytes_accessed=12 * MIB, transcendentals=0
+            flops=2 * 128 * rank * rank * cols * 8, bytes_accessed=24 * MIB, transcendentals=0
         ),
-        name="far_x" if x_first else "far_z",
+        name="far_field",
     )(comp, sent)
+    return parts[:5], parts[5:]
 
 
 def ring(axis_is_x, step):
@@ -422,30 +420,22 @@
     before = lax.ppermute(high, ("crow", "ccol"), up)
     after = lax.ppermute(low, ("crow", "ccol"), down)
 
-    group_rows = col_devices * cluster_count
-    left = list(far_field(gathered, sent, slots, lines, group_rows, True))
-    gathered, sent, left[0] = lax.optimization_barrier((gathered, sent, left[0]))
-    right = list(far_field(gathered, sent, slots, lines, group_rows, False))
-    right[0], before, after = lax.optimization_barrier((right[0], before, after))
-
-    left_up, left_down = both_ways(left[0], left[1], True)
-    right_up, right_down = both_ways(right[0], right[1], False)
-    left_up, left_down, before, after = lax.optimization_barrier((left_up, left_down, before, after))
-    left_rest = both_ways(*passed_on(left[2], left[3], left_up, left_down), True)
-    near, basis = near_field(near_blocks, before, modes, after, row_basis)
-    right_up, right_down, near, basis = lax.optimization_barrier((right_up, right_down, near, basis))
-    right_rest = passed_on(right[2], right[3], right_up, right_down)
-    left_rest, _ = lax.optimization_barrier((left_rest, right_rest))
-    right_rest = both_ways(*right_rest, False)
-    left = turn(left[4], left_up, left_down, *left_rest)
-    left_up, left_down = both_ways(left[0], left[1], False)
-    right = turn(right[4], right_up, right_down, *right_rest)
-    right_up, right_down = both_ways(right[0], right[1], True)
-    (left_up, left_down), _ = lax.optimization_barrier(((left_up, left_down), right))
-    left_rest = both_ways(*passed_on(left[2], left[3], left_up, left_down), False)
-    right_rest = both_ways(*passed_on(right[2], right[3], right_up, right_down), True)
-    left = (left[4], left_up, left_down, *left_rest)
-    right = (right[4], right_up, right_down, *right_rest)
+    left, right = far_field(gathered, sent, slots, lines, col_devices * cluster_count)
+    for along_x in (True, False):
+        left_up, left_down = both_ways(left[0], left[1], along_x)
+        right_up, right_down = both_ways(right[0], right[1], not along_x)
+        if along_x:
+            (before, after), _ = lax.optimization_barrier(((before, after), left[0]))
+            near, basis = near_field(near_blocks, before, modes, after, row_basis)
+            (left_up, left_down), _ = lax.optimization_barrier(((left_up, left_down), near))
+        left_rest = passed_on(left[2], left[3], left_up, left_down)
+        right_rest = passed_on(right[2], right[3], right_up, right_down)
+        left_rest = both_ways(*left_rest, along_x)
+        right_rest = both_ways(*right_rest, not along_x)
+        left = (left[4], left_up, left_down, *left_rest)
+        right = (right[4], right_up, right_down, *right_rest)
+        if along_x:
+            left, right = turn(*left), turn(*right)
     return expand(near, basis, left, right)
 
 

time: 159 us -> 155 us (0.975)
  Pallas kernels: 41.9 us -> 28.4 us
  waiting for transfers between devices: 24.8 us -> 32.2 us
  starting transfers between devices: 32.9 us -> 36.5 us
    pallas_call x2 -> x1, Pallas kernels: 23.9 us -> 10.1 us  [far_field(): pl.pallas_call(functools.partial(far_kernel, slots, rows), in_specs=[whol...]
    ppermute x8, starting transfers between devices: 21.4 us -> 25.5 us  [both_ways(): lax.ppermute(down, 'ccol', ring(along_x, -1))]
    ppermute x1, waiting for transfers between devices: 0.01 us -> 4.12 us  [per_device(): after = lax.ppermute(low, ('crow', 'ccol'), down)]
    ppermute x8, waiting for transfers between devices: 5.62 us -> 2.26 us  [both_ways(): lax.ppermute(down, 'ccol', ring(along_x, -1))]
    ppermute x8, waiting for transfers between devices: 19.2 us -> 22.5 us  [both_ways(): lax.ppermute(up, 'ccol', ring(along_x, 1))]
    ppermute x1, waiting for transfers between devices: 0.01 us -> 3.24 us  [per_device(): before = lax.ppermute(high, ('crow', 'ccol'), up)]
    ppermute x8, starting transfers between devices: 7.71 us -> 6 us  [both_ways(): lax.ppermute(up, 'ccol', ring(along_x, 1))]
    unnamed x17 -> x19, local copies, waits for them, and re-layouts: 6.13 us -> 4.9 us
  transfers between devices with their start and end apart: 19 -> 19, of which waited for: 5 -> 10; matrix products, arithmetic and copies ran while one was open for 0% -> 0% of each run, Pallas kernels for 23% -> 15%
where the time goes in v6:
time: 155 us; the launch traced here: 153 us
  blocking collectives  37.2 us (24%)
  starting transfers between devices  36.5 us (24%)
  waiting for transfers between devices  32.2 us (21%)
  Pallas kernels  28.4 us (18%)
  between operations  13.6 us (9%)
  local copies, waits for them, and re-layouts  4.9 us (3%)
    all_to_all x1, blocking collectives, per_device(): sent = lax.all_to_all(sent, 'ccol', split_axis=0, concat_axis=0, tiled=True)  37.2 us
    ppermute x8, starting transfers between devices, both_ways(): lax.ppermute(down, 'ccol', ring(along_x, -1))  25.5 us
    ppermute x8, waiting for transfers between devices, both_ways(): lax.ppermute(up, 'ccol', ring(along_x, 1))  22.5 us
    pallas_call x1, Pallas kernels, far_field(): pl.pallas_call(functools.partial(far_kernel, slots, rows), in_specs=[whol...  10.1 us
    pallas_call x1, Pallas kernels, near_field(): pl.pallas_call(near_kernel, grid=(panels // CS,), in_specs=[pl.BlockSpec(...  8.33 us
    ppermute x8, starting transfers between devices, both_ways(): lax.ppermute(up, 'ccol', ring(along_x, 1))  6 us
    unnamed x19, local copies, waits for them, and re-layouts  4.9 us
    ppermute x1, waiting for transfers between devices, per_device(): after = lax.ppermute(low, ('crow', 'ccol'), down)  4.12 us
  transfers between devices with their start and end apart: 19, of which 10 were waited for; matrix products, arithmetic and copies ran while one was open for 0% of the time, Pallas kernels for 15%

profile of v6, /device:TPU:0, one launch (start us, length us, event | category | flops | bytes accessed | tf_op | source)
XLA Modules:
  0.0 152.8 jit_solution(1032394572314338346)
XLA Ops:
  6.6 3.3 %compress.1 = (bf16[8,64,512]{2,1,0:T(8,128)(2,1)}, bf16[1024,512]{1,0:T(8,128)(2,1)}, bf16[1024,512]{1,0:T(8,128)(2,1)}) custom-call(bf16[64,2048]{1,0:T(8,128)(2,1)} %basis_ref.2, bf16[2048,512]{1,0:T(8,128)(2,1)} %modes_ref.3), custom_call_target="tpu_custom_call" | custom-call | flops 134217728 | bytes 3145728 | tf_op jit(solution)/shard_map/compress/pallas_call | solution.py:49
  10.2 3.2 %dispatch.1 = bf16[16,528,128]{2,1,0:T(8,128)(2,1)S(1)} custom-call(s32[128]{0:T(128)S(1)} %copy-done.3, s32[128]{0:T(128)S(1)} %bitcast.4, s32[128]{0:T(128)S(1)} %copy-done.5, bf16[128,32,128]{2,1,0:T(8,128)(2,1)S(1)} %bitcast.3), custom_call_target="tpu_custom_call" | custom-call | flops 4194304 | bytes 3145728 | tf_op jit(solution)/shard_map/dispatch/pallas_call | solution.py:108
  13.4 37.2 %all_to_all.5.sent_ref = bf16[16,528,128]{2,1,0:T(8,128)(2,1)} all-to-all(bf16[16,528,128]{2,1,0:T(8,128)(2,1)S(1)} %dispatch.1), channel_id=1, replica_groups=mesh['crow'=8,'ccol'=16] {'ccol'}, dimensions={0} | all-to-all | bytes 4325376 | tf_op jit(solution)/shard_map/all_to_all | solution.py:415
  50.6 3.7 %collective-permute-start = (bf16[1024,512]{1,0:T(8,128)(2,1)}, bf16[1024,512]{1,0:T(8,128)(2,1)}, u32[]{:S(2)}, u32[]{:S(2)}) collective-permute-start(bf16[1024,512]{1,0:T(8,128)(2,1)} %get-tuple-element.47), channel_id=1, source_target_pairs={{0,1},{1,2},{2,3},{3,4},{4,5},{5,6},{6,7},{7,8},{8,9},{9,10},{10,1... | collective-permute-start | bytes 3145736 | tf_op jit(solution)/shard_map/ppermute | solution.py:420
  55.6 10.1 %far_field.1 = (bf16[32,64,256]{2,1,0:T(8,128)(2,1)}, bf16[32,64,256]{2,1,0:T(8,128)(2,1)}, f32[16,64,256]{2,1,0:T(8,128)S(1)}, f32[16,64,256]{2,1,0:T(8,128)S(1...) custom-call(bf16[64,64,512]{2,1,0:T(8,128)(2,1)} %all-gather.2.clone, ...), custom_call_target="tpu_custom_call" | custom-call | flops 4294967296 | bytes 25165824 | tf_op jit(solution)/shard_map/far_field/pallas_call | solution.py:196
  66.7 4.4 %collective-permute-start.2 = (bf16[32,64,256]{2,1,0:T(8,128)(2,1)}, bf16[32,64,256]{2,1,0:T(8,128)(2,1)S(1)}, u32[]{:S(2)}, u32[]{:S(2)}) collective-permute-start(bf16[32,64,256]{2,1,0:T(8,128)(2,1)} %get-tuple-element.51), channel_id=1, source_target_pairs={{0,4},{1,5},{2,6},{3,7},{4,8},{5,9},{6,10},{7,11},{8,12},{9,13},{1... | collective-permute-start | bytes 3145736 | tf_op jit(solution)/shard_map/ppermute | solution.py:231
  71.1 3.2 %collective-permute-done.before_ref = bf16[1024,512]{1,0:T(8,128)(2,1)} collective-permute-done((bf16[1024,512]{1,0:T(8,128)(2,1)}, bf16[1024,512]{1,0:T(8,128)(2,1)}, u32[]{:S(2)}, u32[]{:S(2)}) %collective-permute-start) | collective-permute-done | bytes 1048608 | tf_op jit(solution)/shard_map/ppermute | solution.py:420
  74.3 4.1 %collective-permute-done.1.after_ref = bf16[1024,512]{1,0:T(8,128)(2,1)} collective-permute-done((bf16[1024,512]{1,0:T(8,128)(2,1)}, bf16[1024,512]{1,0:T(8,128)(2,1)}, u32[]{:S(2)}, u32[]{:S(2)}) %collective-permute-start.1) | collective-permute-done | bytes 1048608 | tf_op jit(solution)/shard_map/ppermute | solution.py:421
  78.5 3.8 %collective-permute-start.3 = (bf16[32,64,256]{2,1,0:T(8,128)(2,1)}, bf16[32,64,256]{2,1,0:T(8,128)(2,1)S(1)}, u32[]{:S(2)}, u32[]{:S(2)}) collective-permute-start(bf16[32,64,256]{2,1,0:T(8,128)(2,1)} %get-tuple-element.57), channel_id=1, source_target_pairs={{0,12},{1,13},{2,14},{3,15},{4,0},{5,1},{6,2},{7,3},{8,4},{9,5},{1... | collective-permute-start | bytes 3145736 | tf_op jit(solution)/shard_map/ppermute | solution.py:231
  82.3 3.2 %collective-permute-start.11 = (bf16[32,64,256]{2,1,0:T(8,128)(2,1)}, bf16[32,64,256]{2,1,0:T(8,128)(2,1)S(1)}, u32[]{:S(2)}, u32[]{:S(2)}) collective-permute-start(bf16[32,64,256]{2,1,0:T(8,128)(2,1)} %get-tuple-element.73), channel_id=1, source_target_pairs={{0,3},{1,0},{2,1},{3,2},{4,7},{5,4},{6,5},{7,6},{8,11},{9,8},{10,9... | collective-permute-start | bytes 3145736 | tf_op jit(solution)/shard_map/ppermute | solution.py:231
  85.5 3.7 %copy-done.6 = bf16[2048,2304]{1,0:T(8,128)(2,1)S(1)} copy-done((bf16[2048,2304]{1,0:T(8,128)(2,1)S(1)}, bf16[2048,2304]{1,0:T(8,128)(2,1)}, u32[]{:S(2)}) %copy-start.6) | copy-done | bytes 9437208
  89.2 8.3 %near_field.1 = (f32[2048,512]{1,0:T(8,128)S(1)}, bf16[2048,64]{1,0:T(8,128)(2,1)S(1)}) custom-call(bf16[2048,2304]{1,0:T(8,128)(2,1)S(1)} %copy-done.6, bf16[1024,512]{1,0:T(8,128)(2,1)} %collective-permute-done.before_ref, bf16[2048,512]{1,0:T(8,128)(2,1)S(1)} %copy-done, bf16[1024,512]{1,0:T(8,128)(2,1)} %collective-permute-done.1.after_ref, ...), custom_call_target="tpu_custom_call" | custom-call | flops 38654705664 | bytes 18874368 | tf_op jit(solution)/shard_map/near_field/pallas_call | solution.py:334
  97.5 7.9 %collective-permute-done.10.up_ref.refs_0_ = bf16[32,64,256]{2,1,0:T(8,128)(2,1)S(1)} collective-permute-done((bf16[32,64,256]{2,1,0:T(8,128)(2,1)}, bf16[32,64,256]{2,1,0:T(8,128)(2,1)S(1)}, u32[]{:S(2)}, u32[]{:S(2)}) %collective-permute-start.10) | collective-permute-done | bytes 1048608 | tf_op jit(solution)/shard_map/ppermute | solution.py:231
  105.4 2.2 %collective-permute-done.11.down_ref.refs_1_ = bf16[32,64,256]{2,1,0:T(8,128)(2,1)S(1)} collective-permute-done((bf16[32,64,256]{2,1,0:T(8,128)(2,1)}, bf16[32,64,256]{2,1,0:T(8,128)(2,1)S(1)}, u32[]{:S(2)}, u32[]{:S(2)}) %collective-permute-start.11) | collective-permute-done | bytes 1048608 | tf_op jit(solution)/shard_map/ppermute | solution.py:231
  107.9 3.2 %collective-permute-start.13 = (bf16[16,64,256]{2,1,0:T(8,128)(2,1)S(1)}, bf16[16,64,256]{2,1,0:T(8,128)(2,1)S(1)}, u32[]{:S(2)}, u32[]{:S(2)}) collective-permute-start(bf16[16,64,256]{2,1,0:T(8,128)(2,1)S(1)} %get-tuple-element.77), channel_id=1, source_target_pairs={{0,3},{1,0},{2,1},{3,2},{4,7},{5,4},{6,5},{7,6},{8,11},{9,8},{10,9... | collective-permute-start | bytes 1572872 | tf_op jit(solution)/shard_map/ppermute | solution.py:231
  111.4 3.2 %collective-permute-start.5 = (bf16[16,64,256]{2,1,0:T(8,128)(2,1)S(1)}, bf16[16,64,256]{2,1,0:T(8,128)(2,1)S(1)}, u32[]{:S(2)}, u32[]{:S(2)}) collective-permute-start(bf16[16,64,256]{2,1,0:T(8,128)(2,1)S(1)} %get-tuple-element.63), channel_id=1, source_target_pairs={{0,12},{1,13},{2,14},{3,15},{4,0},{5,1},{6,2},{7,3},{8,4},{9,5},{1... | collective-permute-start | bytes 1572872 | tf_op jit(solution)/shard_map/ppermute | solution.py:231
  114.6 8.0 %collective-permute-done.12.refs_2_ = bf16[16,64,256]{2,1,0:T(8,128)(2,1)S(1)} collective-permute-done((bf16[16,64,256]{2,1,0:T(8,128)(2,1)S(1)}, bf16[16,64,256]{2,1,0:T(8,128)(2,1)S(1)}, u32[]{:S(2)}, u32[]{:S(2)}) %collective-permute-start.12) | collective-permute-done | bytes 524320 | tf_op jit(solution)/shard_map/ppermute | solution.py:231
  123.0 3.2 %collective-permute-start.15 = (bf16[8,64,256]{2,1,0:T(8,128)(2,1)S(1)}, bf16[8,64,256]{2,1,0:T(8,128)(2,1)S(1)}, u32[]{:S(2)}, u32[]{:S(2)}) collective-permute-start(bf16[8,64,256]{2,1,0:T(8,128)(2,1)S(1)} %get-tuple-element.80), channel_id=1, source_target_pairs={{0,12},{1,13},{2,14},{3,15},{4,0},{5,1},{6,2},{7,3},{8,4},{9,5},{1... | collective-permute-start | bytes 786440 | tf_op jit(solution)/shard_map/ppermute | solution.py:231
  127.2 3.1 %collective-permute-start.7 = (bf16[8,64,256]{2,1,0:T(8,128)(2,1)S(1)}, bf16[8,64,256]{2,1,0:T(8,128)(2,1)S(1)}, u32[]{:S(2)}, u32[]{:S(2)}) collective-permute-start(bf16[8,64,256]{2,1,0:T(8,128)(2,1)S(1)} %get-tuple-element.66), channel_id=1, source_target_pairs={{0,3},{1,0},{2,1},{3,2},{4,7},{5,4},{6,5},{7,6},{8,11},{9,8},{10,9... | collective-permute-start | bytes 786440 | tf_op jit(solution)/shard_map/ppermute | solution.py:231
  130.3 2.8 %collective-permute-done.14.up_ref.refs_6_ = bf16[8,64,256]{2,1,0:T(8,128)(2,1)S(1)} collective-permute-done((bf16[8,64,256]{2,1,0:T(8,128)(2,1)S(1)}, bf16[8,64,256]{2,1,0:T(8,128)(2,1)S(1)}, u32[]{:S(2)}, u32[]{:S(2)}) %collective-permute-start.14) | collective-permute-done | bytes 262176 | tf_op jit(solution)/shard_map/ppermute | solution.py:231
  133.2 3.5 %collective-permute-start.17 = (bf16[4,64,256]{2,1,0:T(8,128)(2,1)S(1)}, bf16[4,64,256]{2,1,0:T(8,128)(2,1)S(1)}, u32[]{:S(2)}, u32[]{:S(2)}) collective-permute-start(bf16[4,64,256]{2,1,0:T(8,128)(2,1)S(1)} %get-tuple-element.84), channel_id=1, source_target_pairs={{0,12},{1,13},{2,14},{3,15},{4,0},{5,1},{6,2},{7,3},{8,4},{9,5},{1... | collective-permute-start | bytes 393224 | tf_op jit(solution)/shard_map/ppermute | solution.py:231
  138.1 2.3 %collective-permute-start.9 = (bf16[4,64,256]{2,1,0:T(8,128)(2,1)S(1)}, bf16[4,64,256]{2,1,0:T(8,128)(2,1)S(1)}, u32[]{:S(2)}, u32[]{:S(2)}) collective-permute-start(bf16[4,64,256]{2,1,0:T(8,128)(2,1)S(1)} %get-tuple-element.70), channel_id=1, source_target_pairs={{0,3},{1,0},{2,1},{3,2},{4,7},{5,4},{6,5},{7,6},{8,11},{9,8},{10,9... | collective-permute-start | bytes 393224 | tf_op jit(solution)/shard_map/ppermute | solution.py:231
  140.5 3.0 %collective-permute-done.8.refs_3_ = bf16[4,64,256]{2,1,0:T(8,128)(2,1)S(1)} collective-permute-done((bf16[4,64,256]{2,1,0:T(8,128)(2,1)S(1)}, bf16[4,64,256]{2,1,0:T(8,128)(2,1)S(1)}, u32[]{:S(2)}, u32[]{:S(2)}) %collective-permute-start.8) | collective-permute-done | bytes 131104 | tf_op jit(solution)/shard_map/ppermute | solution.py:231
  143.5 2.5 %expand.1 = bf16[2048,512]{1,0:T(8,128)(2,1)} custom-call(f32[2048,512]{1,0:T(8,128)S(1)} %get-tuple-element.54.near_ref, bf16[2048,64]{1,0:T(8,128)(2,1)S(1)} %get-tuple-element.55.basis_ref, f32[8,64,256]{2,1,0:T(8,128)S(1)} %get-tuple-element.64.refs_0_, bf16[8,64,256]{2,1,0:T(8,128)(2,1)S(1)} %collective-permute-done.6.up_ref.refs_1_, ...), custom_call_target="tpu_custom_call" | custom-call | flops 134217728 | bytes 7340032 | tf_op jit(solution)/shard_map/expand/pallas_call | solution.py:381
  (46 shorter events, 6.1 us)
Async XLA Ops:
  6.5 3.6 %copy-start.3 = (s32[128]{0:T(128)S(1)}, s32[128]{0:T(128)}, u32[]{:S(2)}) copy-start(s32[128]{0:T(128)} %rows_ref.1) | copy-start | bytes 1540
  6.5 49.0 %all-gather.2.cloned.1.call-start = ((), (), s32[]{:S(2)}) async-start(), calls=%async_computation.1 | async-start | bytes 4718592 | tf_op jit(solution)/shard_map/all_gather | solution.py:408
  50.6 34.9 %copy-start = (bf16[2048,512]{1,0:T(8,128)(2,1)S(1)}, bf16[2048,512]{1,0:T(8,128)(2,1)}, u32[]{:S(2)}) copy-start(bf16[2048,512]{1,0:T(8,128)(2,1)} %modes_ref.3) | copy-start | bytes 6291460
  50.6 34.9 %copy-start.7 = (bf16[64,2048]{1,0:T(8,128)(2,1)S(1)}, bf16[64,2048]{1,0:T(8,128)(2,1)}, u32[]{:S(2)}) copy-start(bf16[64,2048]{1,0:T(8,128)(2,1)} %basis_ref.3) | copy-start | bytes 786436
  50.6 23.8 %collective-permute-start = (bf16[1024,512]{1,0:T(8,128)(2,1)}, bf16[1024,512]{1,0:T(8,128)(2,1)}, u32[]{:S(2)}, u32[]{:S(2)}) collective-permute-start(bf16[1024,512]{1,0:T(8,128)(2,1)} %get-tuple-element.47), channel_id=1, source_target_pairs={{0,1},{1,2},{2,3},{3,4},{4,5},{5,6},{6,7},{7,8},{8,9},{9,10},{10,1... | collective-permute-start | bytes 3145736 | tf_op jit(solution)/shard_map/ppermute | solution.py:420
  54.3 24.2 %collective-permute-start.1 = (bf16[1024,512]{1,0:T(8,128)(2,1)}, bf16[1024,512]{1,0:T(8,128)(2,1)}, u32[]{:S(2)}, u32[]{:S(2)}) collective-permute-start(bf16[1024,512]{1,0:T(8,128)(2,1)} %get-tuple-element.48), channel_id=1, source_target_pairs={{1,0},{2,1},{3,2},{4,3},{5,4},{6,5},{7,6},{8,7},{9,8},{10,9},{11,1... | collective-permute-start | bytes 3145736 | tf_op jit(solution)/shard_map/ppermute | solution.py:421
  66.7 44.4 %collective-permute-start.2 = (bf16[32,64,256]{2,1,0:T(8,128)(2,1)}, bf16[32,64,256]{2,1,0:T(8,128)(2,1)S(1)}, u32[]{:S(2)}, u32[]{:S(2)}) collective-permute-start(bf16[32,64,256]{2,1,0:T(8,128)(2,1)} %get-tuple-element.51), channel_id=1, source_target_pairs={{0,4},{1,5},{2,6},{3,7},{4,8},{5,9},{6,10},{7,11},{8,12},{9,13},{1... | collective-permute-start | bytes 3145736 | tf_op jit(solution)/shard_map/ppermute | solution.py:231
  78.5 32.6 %collective-permute-start.3 = (bf16[32,64,256]{2,1,0:T(8,128)(2,1)}, bf16[32,64,256]{2,1,0:T(8,128)(2,1)S(1)}, u32[]{:S(2)}, u32[]{:S(2)}) collective-permute-start(bf16[32,64,256]{2,1,0:T(8,128)(2,1)} %get-tuple-element.57), channel_id=1, source_target_pairs={{0,12},{1,13},{2,14},{3,15},{4,0},{5,1},{6,2},{7,3},{8,4},{9,5},{1... | collective-permute-start | bytes 3145736 | tf_op jit(solution)/shard_map/ppermute | solution.py:231
  82.3 23.1 %collective-permute-start.10 = (bf16[32,64,256]{2,1,0:T(8,128)(2,1)}, bf16[32,64,256]{2,1,0:T(8,128)(2,1)S(1)}, u32[]{:S(2)}, u32[]{:S(2)}) collective-permute-start(bf16[32,64,256]{2,1,0:T(8,128)(2,1)} %get-tuple-element.72), channel_id=1, source_target_pairs={{0,1},{1,2},{2,3},{3,0},{4,5},{5,6},{6,7},{7,4},{8,9},{9,10},{10,1... | collective-permute-start | bytes 3145736 | tf_op jit(solution)/shard_map/ppermute | solution.py:231
  82.3 25.4 %copy-start.2 = (f32[16,64,256]{2,1,0:T(8,128)S(1)}, f32[16,64,256]{2,1,0:T(8,128)}, u32[]{:S(2)}) copy-start(f32[16,64,256]{2,1,0:T(8,128)} %copy-done.1) | copy-start | bytes 3145732
  82.3 25.4 %collective-permute-start.11 = (bf16[32,64,256]{2,1,0:T(8,128)(2,1)}, bf16[32,64,256]{2,1,0:T(8,128)(2,1)S(1)}, u32[]{:S(2)}, u32[]{:S(2)}) collective-permute-start(bf16[32,64,256]{2,1,0:T(8,128)(2,1)} %get-tuple-element.73), channel_id=1, source_target_pairs={{0,3},{1,0},{2,1},{3,2},{4,7},{5,4},{6,5},{7,6},{8,11},{9,8},{10,9... | collective-permute-start | bytes 3145736 | tf_op jit(solution)/shard_map/ppermute | solution.py:231
  85.5 3.7 %copy-start.6 = (bf16[2048,2304]{1,0:T(8,128)(2,1)S(1)}, bf16[2048,2304]{1,0:T(8,128)(2,1)}, u32[]{:S(2)}) copy-start(bf16[2048,2304]{1,0:T(8,128)(2,1)} %near_ref.1) | copy-start | bytes 28311556
  107.8 14.8 %collective-permute-start.12 = (bf16[16,64,256]{2,1,0:T(8,128)(2,1)S(1)}, bf16[16,64,256]{2,1,0:T(8,128)(2,1)S(1)}, u32[]{:S(2)}, u32[]{:S(2)}) collective-permute-start(bf16[16,64,256]{2,1,0:T(8,128)(2,1)S(1)} %get-tuple-element.76), channel_id=1, source_target_pairs={{0,1},{1,2},{2,3},{3,0},{4,5},{5,6},{6,7},{7,4},{8,9},{9,10},{10,1... | collective-permute-start | bytes 1572872 | tf_op jit(solution)/shard_map/ppermute | solution.py:231
  107.9 14.7 %collective-permute-start.13 = (bf16[16,64,256]{2,1,0:T(8,128)(2,1)S(1)}, bf16[16,64,256]{2,1,0:T(8,128)(2,1)S(1)}, u32[]{:S(2)}, u32[]{:S(2)}) collective-permute-start(bf16[16,64,256]{2,1,0:T(8,128)(2,1)S(1)} %get-tuple-element.77), channel_id=1, source_target_pairs={{0,3},{1,0},{2,1},{3,2},{4,7},{5,4},{6,5},{7,6},{8,11},{9,8},{10,9... | collective-permute-start | bytes 1572872 | tf_op jit(solution)/shard_map/ppermute | solution.py:231
  111.3 15.4 %collective-permute-start.4 = (bf16[16,64,256]{2,1,0:T(8,128)(2,1)S(1)}, bf16[16,64,256]{2,1,0:T(8,128)(2,1)S(1)}, u32[]{:S(2)}, u32[]{:S(2)}) collective-permute-start(bf16[16,64,256]{2,1,0:T(8,128)(2,1)S(1)} %get-tuple-element.62), channel_id=1, source_target_pairs={{0,4},{1,5},{2,6},{3,7},{4,8},{5,9},{6,10},{7,11},{8,12},{9,13},{1... | collective-permute-start | bytes 1572872 | tf_op jit(solution)/shard_map/ppermute | solution.py:231
  111.4 15.3 %collective-permute-start.5 = (bf16[16,64,256]{2,1,0:T(8,128)(2,1)S(1)}, bf16[16,64,256]{2,1,0:T(8,128)(2,1)S(1)}, u32[]{:S(2)}, u32[]{:S(2)}) collective-permute-start(bf16[16,64,256]{2,1,0:T(8,128)(2,1)S(1)} %get-tuple-element.63), channel_id=1, source_target_pairs={{0,12},{1,13},{2,14},{3,15},{4,0},{5,1},{6,2},{7,3},{8,4},{9,5},{1... | collective-permute-start | bytes 1572872 | tf_op jit(solution)/shard_map/ppermute | solution.py:231
  122.9 10.1 %collective-permute-start.14 = (bf16[8,64,256]{2,1,0:T(8,128)(2,1)S(1)}, bf16[8,64,256]{2,1,0:T(8,128)(2,1)S(1)}, u32[]{:S(2)}, u32[]{:S(2)}) collective-permute-start(bf16[8,64,256]{2,1,0:T(8,128)(2,1)S(1)} %get-tuple-element.79), channel_id=1, source_target_pairs={{0,4},{1,5},{2,6},{3,7},{4,8},{5,9},{6,10},{7,11},{8,12},{9,13},{1... | collective-permute-start | bytes 786440 | tf_op jit(solution)/shard_map/ppermute | solution.py:231
  123.0 10.0 %collective-permute-start.15 = (bf16[8,64,256]{2,1,0:T(8,128)(2,1)S(1)}, bf16[8,64,256]{2,1,0:T(8,128)(2,1)S(1)}, u32[]{:S(2)}, u32[]{:S(2)}) collective-permute-start(bf16[8,64,256]{2,1,0:T(8,128)(2,1)S(1)} %get-tuple-element.80), channel_id=1, source_target_pairs={{0,12},{1,13},{2,14},{3,15},{4,0},{5,1},{6,2},{7,3},{8,4},{9,5},{1... | collective-permute-start | bytes 786440 | tf_op jit(solution)/shard_map/ppermute | solution.py:231
  126.9 10.0 %collective-permute-start.6 = (bf16[8,64,256]{2,1,0:T(8,128)(2,1)S(1)}, bf16[8,64,256]{2,1,0:T(8,128)(2,1)S(1)}, u32[]{:S(2)}, u32[]{:S(2)}) collective-permute-start(bf16[8,64,256]{2,1,0:T(8,128)(2,1)S(1)} %get-tuple-element.65), channel_id=1, source_target_pairs={{0,1},{1,2},{2,3},{3,0},{4,5},{5,6},{6,7},{7,4},{8,9},{9,10},{10,1... | collective-permute-start | bytes 786440 | tf_op jit(solution)/shard_map/ppermute | solution.py:231
  127.2 9.8 %collective-permute-start.7 = (bf16[8,64,256]{2,1,0:T(8,128)(2,1)S(1)}, bf16[8,64,256]{2,1,0:T(8,128)(2,1)S(1)}, u32[]{:S(2)}, u32[]{:S(2)}) collective-permute-start(bf16[8,64,256]{2,1,0:T(8,128)(2,1)S(1)} %get-tuple-element.66), channel_id=1, source_target_pairs={{0,3},{1,0},{2,1},{3,2},{4,7},{5,4},{6,5},{7,6},{8,11},{9,8},{10,9... | collective-permute-start | bytes 786440 | tf_op jit(solution)/shard_map/ppermute | solution.py:231
  133.1 7.4 %collective-permute-start.16 = (bf16[4,64,256]{2,1,0:T(8,128)(2,1)S(1)}, bf16[4,64,256]{2,1,0:T(8,128)(2,1)S(1)}, u32[]{:S(2)}, u32[]{:S(2)}) collective-permute-start(bf16[4,64,256]{2,1,0:T(8,128)(2,1)S(1)} %get-tuple-element.83), channel_id=1, source_target_pairs={{0,4},{1,5},{2,6},{3,7},{4,8},{5,9},{6,10},{7,11},{8,12},{9,13},{1... | collective-permute-start | bytes 393224 | tf_op jit(solution)/shard_map/ppermute | solution.py:231
  133.2 7.3 %collective-permute-start.17 = (bf16[4,64,256]{2,1,0:T(8,128)(2,1)S(1)}, bf16[4,64,256]{2,1,0:T(8,128)(2,1)S(1)}, u32[]{:S(2)}, u32[]{:S(2)}) collective-permute-start(bf16[4,64,256]{2,1,0:T(8,128)(2,1)S(1)} %get-tuple-element.84), channel_id=1, source_target_pairs={{0,12},{1,13},{2,14},{3,15},{4,0},{5,1},{6,2},{7,3},{8,4},{9,5},{1... | collective-permute-start | bytes 393224 | tf_op jit(solution)/shard_map/ppermute | solution.py:231
  137.0 6.4 %collective-permute-start.8 = (bf16[4,64,256]{2,1,0:T(8,128)(2,1)S(1)}, bf16[4,64,256]{2,1,0:T(8,128)(2,1)S(1)}, u32[]{:S(2)}, u32[]{:S(2)}) collective-permute-start(bf16[4,64,256]{2,1,0:T(8,128)(2,1)S(1)} %get-tuple-element.69), channel_id=1, source_target_pairs={{0,1},{1,2},{2,3},{3,0},{4,5},{5,6},{6,7},{7,4},{8,9},{9,10},{10,1... | collective-permute-start | bytes 393224 | tf_op jit(solution)/shard_map/ppermute | solution.py:231
  138.1 5.4 %collective-permute-start.9 = (bf16[4,64,256]{2,1,0:T(8,128)(2,1)S(1)}, bf16[4,64,256]{2,1,0:T(8,128)(2,1)S(1)}, u32[]{:S(2)}, u32[]{:S(2)}) collective-permute-start(bf16[4,64,256]{2,1,0:T(8,128)(2,1)S(1)} %get-tuple-element.70), channel_id=1, source_target_pairs={{0,3},{1,0},{2,1},{3,2},{4,7},{5,4},{6,5},{7,6},{8,11},{9,8},{10,9... | collective-permute-start | bytes 393224 | tf_op jit(solution)/shard_map/ppermute | solution.py:231
  (4 other events, 11.5 us)
Sparse Core Ops, SparseCore 0:
  10.0 34.5 all-gather.1

commit v7 on v6

--- a/solution.py
+++ b/solution.py
@@ -83,11 +83,11 @@
 
     def place(b, carry):
         owner = owners_ref[b]
-        column = owner % cols
+        column = owner & (cols - 1)
         at = count_ref[column]
         count_ref[column] = at + 1
         out_ref[column, pl.ds(pl.multiple_of(at * rows, rows), rows), :] = cores_ref[b]
-        cluster = (owner // cols) * cl_dev + slot_ref[b]
+        cluster = (owner >> (cols.bit_length() - 1)) * cl_dev + slot_ref[b]
         entry = (
             jnp.where(lane == at, cluster, 0)
             + jnp.where(lane == slots + at, rows_ref[b], 0)
@@ -96,7 +96,7 @@
         meta_ref[pl.ds(column, 1), :] += entry.astype(jnp.float32)
         return carry
 
-    lax.fori_loop(0, blocks, place, 0)
+    lax.fori_loop(0, blocks, place, 0, unroll=8)
     for j in range(cols):
         out_ref[j, slots * rows :, :] = jnp.broadcast_to(
             meta_ref[j : j + 1, :], (16, 128)
@@ -118,12 +118,13 @@
 
 
 UNROLL = 32
+X_ROWS = 5
 
 
 def far_kernel(slots, rows, comp_ref, sent_ref, *refs):
-    outs, (left_ref, right_ref, meta_ref, smem_ref, list_ref, sem) = (refs[:5], refs[5:10]), refs[10:]
+    outs, (acc_ref, meta_ref, smem_ref, list_ref, sem) = (refs[:5], refs[5:10]), refs[10:]
     sources = sent_ref.shape[0]
-    group_rows, _, width = left_ref.shape
+    group_rows = acc_ref.shape[0]
     part = group_rows // 4
     row_part = part // 4
     me = lax.axis_index("ccol")
@@ -136,15 +137,16 @@
     to_x = (row // part - here_x) & 3
     to_z = (row // row_part - here_z) & 3
     rest = row & (row_part - 1)
-    left = to_x * part + to_z * row_part + rest
-    right = to_z * part + to_x * row_part + rest
+    z_rows = row_part - X_ROWS
+    x_place = (to_x * 4 + to_z) * X_ROWS + rest
+    z_place = 16 * X_ROWS + (to_z * 4 + to_x) * z_rows + rest - X_ROWS
+    filed = jnp.where(rest < X_ROWS, x_place, z_place)
     place = lax.broadcasted_iota(jnp.int32, meta.shape, 0) * slots + lane
-    words = (place << 22) + (meta << 14) + (left << 7) + right
+    words = (place << 14) + (meta << 7) + filed
     meta_ref[...] = jnp.where(lane < slots, words, meta)
     copy = pltpu.make_async_copy(meta_ref, smem_ref, sem)
     copy.start()
-    left_ref[...] = jnp.zeros_like(left_ref)
-    right_ref[...] = jnp.zeros_like(right_ref)
+    acc_ref[...] = jnp.zeros_like(acc_ref)
     copy.wait()
 
     total = 0
@@ -159,48 +161,52 @@
         for i in range(UNROLL):
             at = g * UNROLL + i
             entry = list_ref[at]
-            place = entry >> 22
+            place = entry >> 14
             core = sent_ref[place // slots, pl.ds(pl.multiple_of((place % slots) * rows, rows), rows), :]
             core = jnp.where(at < total, core, jnp.zeros_like(core))
             half = core.shape[1] // 2
             core = jnp.concatenate([core[:, :half], core[:, half:]], axis=0)
-            comp = comp_ref[(entry >> 14) & 255]
-            left_ref[(entry >> 7) & 127] += jnp.dot(core, comp[:, :width], preferred_element_type=jnp.float32)
-            right_ref[entry & 127] += jnp.dot(core, comp[:, width:], preferred_element_type=jnp.float32)
+            comp = comp_ref[(entry >> 7) & 127]
+            acc_ref[entry & 127] += jnp.dot(core, comp, preferred_element_type=jnp.float32)
         return carry
 
     lax.fori_loop(0, (total + UNROLL - 1) // UNROLL, group, 0)
-    half = part // 2
-    for acc_ref, (up_ref, down_ref, next_ref, last_ref, own_ref) in zip((left_ref, right_ref), outs):
-        own_ref[...] = acc_ref[:part]
-        next_ref[...] = acc_ref[part : part + half]
-        up_ref[half:] = acc_ref[part + half : 2 * part].astype(jnp.bfloat16)
-        up_ref[:half] = acc_ref[2 * part : 2 * part + half].astype(jnp.bfloat16)
-        down_ref[half:] = acc_ref[2 * part + half : 3 * part].astype(jnp.bfloat16)
-        down_ref[:half] = acc_ref[3 * part : 3 * part + half].astype(jnp.bfloat16)
-        last_ref[...] = acc_ref[3 * part + half :]
+    begin = 0
+    for up_ref, down_ref, next_ref, last_ref, own_ref in outs:
+        part = own_ref.shape[0]
+        half = part // 2
+        own, following, far, last, begin = (begin + i * part for i in range(5))
+        own_ref[...] = acc_ref[own : own + part]
+        next_ref[...] = acc_ref[following : following + half]
+        up_ref[half:] = acc_ref[following + half : following + part].astype(jnp.bfloat16)
+        up_ref[:half] = acc_ref[far : far + half].astype(jnp.bfloat16)
+        down_ref[half:] = acc_ref[far + half : far + part].astype(jnp.bfloat16)
+        down_ref[:half] = acc_ref[last : last + half].astype(jnp.bfloat16)
+        last_ref[...] = acc_ref[last + half : last + part]
 
 
 def far_field(comp, sent, slots, rows, group_rows):
     _, rank, cols = comp.shape
     sources = sent.shape[0]
-    width = cols // 2
-    part = group_rows // 4
+    x_part = X_ROWS * 4
     kinds = [
-        (part, jnp.bfloat16),
-        (part, jnp.bfloat16),
-        (part // 2, jnp.float32),
-        (part // 2, jnp.float32),
-        (part, jnp.float32),
-    ] * 2
+        (n, kind)
+        for part in (x_part, group_rows // 4 - x_part)
+        for n, kind in (
+            (part, jnp.bfloat16),
+            (part, jnp.bfloat16),
+            (part // 2, jnp.float32),
+            (part // 2, jnp.float32),
+            (part, jnp.float32),
+        )
+    ]
     parts = pl.pallas_call(
         functools.partial(far_kernel, slots, rows),
         in_specs=[whole()] * 2,
         out_specs=[whole()] * len(kinds),
-        out_shape=[jax.ShapeDtypeStruct((n, rank, width), kind) for n, kind in kinds],
+        out_shape=[jax.ShapeDtypeStruct((n, rank, cols), kind) for n, kind in kinds],
         scratch_shapes=[
-            VMEM((group_rows, rank, width), jnp.float32),
-            VMEM((group_rows, rank, width), jnp.float32),
+            VMEM((group_rows, rank, cols), jnp.float32),
             VMEM((sources, 128), jnp.int32),
             SMEM((sources, 128), jnp.int32),
             SMEM((sources * slots + UNROLL + slots,), jnp.int32),
@@ -253,51 +259,42 @@
     )(following, last, up, down)
 
 
-def ring_sum(place, own, up_ref, down_ref, up_rest_ref, down_rest_ref):
+def turn_kernel(own_ref, up_in_ref, down_in_ref, up_rest_ref, down_rest_ref, up_ref, down_ref, next_ref, last_ref, here_ref):
+    part, _, width = next_ref.shape
     half = up_rest_ref.shape[0]
-    if place < half:
-        return own + f32(down_ref[place]) + f32(up_rest_ref[place])
-    return own + f32(up_ref[place]) + f32(down_rest_ref[place - half])
-
-
-def turn_kernel(own_ref, *refs):
-    arrived, (up_ref, down_ref, next_ref, last_ref, here_ref) = refs[:4], refs[4:]
-    part = here_ref.shape[0]
-    half = part // 2
-    for place in range(4 * part):
-        value = ring_sum(place, own_ref[place], *arrived)
-        kind, at = place // part, place % part
-        if kind == 0:
-            here_ref[at] = value
-        elif kind == 1 and at < half:
-            next_ref[at] = value
-        elif kind == 1:
-            up_ref[at] = value.astype(jnp.bfloat16)
-        elif kind == 2 and at < half:
-            up_ref[at] = value.astype(jnp.bfloat16)
-        elif kind == 2:
-            down_ref[at] = value.astype(jnp.bfloat16)
-        elif at < half:
-            down_ref[at] = value.astype(jnp.bfloat16)
-        else:
-            last_ref[at - half] = value
+
+    def total(kind):
+        at = kind * part
+        rows = pl.ds(at, part)
+        if at < half:
+            return own_ref[rows] + f32(down_in_ref[rows]) + f32(up_rest_ref[rows])
+        return own_ref[rows] + f32(up_in_ref[rows]) + f32(down_rest_ref[pl.ds(at - half, part)])
+
+    here_ref[...] = total(0)
+    following, far, last = total(1), total(2), total(3)
+    next_ref[...] = following[:, :, :width]
+    up_ref[part:] = following[:, :, width:].astype(jnp.bfloat16)
+    up_ref[:part] = far[:, :, :width].astype(jnp.bfloat16)
+    down_ref[part:] = far[:, :, width:].astype(jnp.bfloat16)
+    down_ref[:part] = last[:, :, :width].astype(jnp.bfloat16)
+    last_ref[...] = last[:, :, width:]
 
 
 def turn(own, up, down, up_rest, down_rest):
-    rows, rank, width = own.shape
-    part = rows // 4
+    rows, rank, cols = own.shape
+    part, width = rows // 4, cols // 2
     kinds = [
-        (part, jnp.bfloat16),
-        (part, jnp.bfloat16),
-        (part // 2, jnp.float32),
-        (part // 2, jnp.float32),
-        (part, jnp.float32),
+        (2 * part, width, jnp.bfloat16),
+        (2 * part, width, jnp.bfloat16),
+        (part, width, jnp.float32),
+        (part, width, jnp.float32),
+        (part, cols, jnp.float32),
     ]
     return pl.pallas_call(
         turn_kernel,
         in_specs=[whole()] * 5,
         out_specs=[whole()] * 5,
-        out_shape=[jax.ShapeDtypeStruct((n, rank, width), kind) for n, kind in kinds],
+        out_shape=[jax.ShapeDtypeStruct((n, rank, w), kind) for n, w, kind in kinds],
         compiler_params=pltpu.CompilerParams(vmem_limit_bytes=24 * MIB),
         cost_estimate=SMALL,
         name="turn",
@@ -348,7 +345,7 @@
         scratch_shapes=[VMEM((panels + 2 * halo, cols), jnp.bfloat16)],
         compiler_params=pltpu.CompilerParams(vmem_limit_bytes=32 * MIB),
         cost_estimate=pl.CostEstimate(
-            flops=16 * panels * band * cols, bytes_accessed=18 * MIB, transcendentals=0
+            flops=2 * panels * band * cols, bytes_accessed=2 * MIB, transcendentals=0
         ),
         name="near_field",
     )(near_blocks, before, modes, after, row_basis)
@@ -358,20 +355,23 @@
 
 
 def expand_kernel(near_ref, basis_ref, *refs):
-    halves, out_ref = (refs[:5], refs[5:10]), refs[10]
-    clusters, _, width = halves[0][0].shape
+    sides, out_ref = (refs[:5], refs[5:10]), refs[10]
+    places = [(side, at) for side in sides for at in range(side[0].shape[0])]
+    width = sides[0][3].shape[2]
     step = pl.program_id(0)
-    for group in range(clusters // EXPAND):
+    for group in range(len(places) // EXPAND):
 
         @pl.when(step == group)
         def _():
             for i in range(EXPAND):
                 rows = pl.ds(i * CS, CS)
-                for side, half in enumerate(halves):
-                    place = group * EXPAND + i
-                    far = ring_sum(place, half[0][place], *half[1:]).astype(jnp.bfloat16)
-                    cols = pl.ds(side * width, width)
-                    value = jnp.dot(basis_ref[rows, :], far, preferred_element_type=jnp.float32)
+                (own_ref, up_ref, down_ref, up_rest_ref, down_rest_ref), at = places[group * EXPAND + i]
+                part = own_ref.shape[0]
+                own = own_ref[at]
+                first = own[:, :width] + f32(down_ref[at]) + f32(up_rest_ref[at])
+                second = own[:, width:] + f32(up_ref[part + at]) + f32(down_rest_ref[at])
+                for far, cols in ((first, pl.ds(0, width)), (second, pl.ds(width, width))):
+                    value = jnp.dot(basis_ref[rows, :], far.astype(jnp.bfloat16), preferred_element_type=jnp.float32)
                     out_ref[rows, cols] = (near_ref[rows, cols] + value).astype(jnp.bfloat16)
 
 

time: 155 us -> 153 us (0.987)
    ppermute x8, waiting for transfers between devices: 22.5 us -> 13.5 us  [both_ways(): lax.ppermute(up, 'ccol', ring(along_x, 1))]
    ppermute x8, waiting for transfers between devices: 2.26 us -> 10.4 us  [both_ways(): lax.ppermute(down, 'ccol', ring(along_x, -1))]
    ppermute x8, starting transfers between devices: 6 us -> 3.99 us  [both_ways(): lax.ppermute(up, 'ccol', ring(along_x, 1))]
    ppermute x8, starting transfers between devices: 25.5 us -> 27.3 us  [both_ways(): lax.ppermute(down, 'ccol', ring(along_x, -1))]
    unnamed x19 -> x17, local copies, waits for them, and re-layouts: 4.9 us -> 3.95 us
  transfers between devices with their start and end apart: 19 -> 19, of which waited for: 10 -> 6; matrix products, arithmetic and copies ran while one was open for 0% -> 0% of each run, Pallas kernels for 15% -> 14%
where the time goes in v7:
time: 153 us; the launch traced here: 151 us
  blocking collectives  37.1 us (24%)
  starting transfers between devices  36.2 us (24%)
  waiting for transfers between devices  32.6 us (21%)
  Pallas kernels  27.4 us (18%)
  between operations  13.6 us (9%)
  local copies, waits for them, and re-layouts  3.95 us (3%)
    all_to_all x1, blocking collectives, per_device(): sent = lax.all_to_all(sent, 'ccol', split_axis=0, concat_axis=0, tiled=True)  37.1 us
    ppermute x8, starting transfers between devices, both_ways(): lax.ppermute(down, 'ccol', ring(along_x, -1))  27.3 us
    ppermute x8, waiting for transfers between devices, both_ways(): lax.ppermute(up, 'ccol', ring(along_x, 1))  13.5 us
    pallas_call x1, Pallas kernels, far_field(): pl.pallas_call(functools.partial(far_kernel, slots, rows), in_specs=[whol...  10.6 us
    ppermute x8, waiting for transfers between devices, both_ways(): lax.ppermute(down, 'ccol', ring(along_x, -1))  10.4 us
    pallas_call x1, Pallas kernels, near_field(): pl.pallas_call(near_kernel, grid=(panels // CS,), in_specs=[pl.BlockSpec(...  8.33 us
    ppermute x1, waiting for transfers between devices, per_device(): before = lax.ppermute(high, ('crow', 'ccol'), up)  4.65 us
    ppermute x1, waiting for transfers between devices, per_device(): after = lax.ppermute(low, ('crow', 'ccol'), down)  4.12 us
  transfers between devices with their start and end apart: 19, of which 6 were waited for; matrix products, arithmetic and copies ran while one was open for 0% of the time, Pallas kernels for 14%

profile of v7, /device:TPU:0, one launch (start us, length us, event | category | flops | bytes accessed | tf_op | source)
XLA Modules:
  0.0 150.8 jit_solution(8798153777580968365)
XLA Ops:
  6.6 3.3 %compress.1 = (bf16[8,64,512]{2,1,0:T(8,128)(2,1)}, bf16[1024,512]{1,0:T(8,128)(2,1)}, bf16[1024,512]{1,0:T(8,128)(2,1)}) custom-call(bf16[64,2048]{1,0:T(8,128)(2,1)} %basis_ref.2, bf16[2048,512]{1,0:T(8,128)(2,1)} %modes_ref.3), custom_call_target="tpu_custom_call" | custom-call | flops 134217728 | bytes 3145728 | tf_op jit(solution)/shard_map/compress/pallas_call | solution.py:49
  10.1 1.7 %dispatch.1 = bf16[16,528,128]{2,1,0:T(8,128)(2,1)S(1)} custom-call(s32[128]{0:T(128)S(1)} %copy-done.2, s32[128]{0:T(128)S(1)} %bitcast.4, s32[128]{0:T(128)S(1)} %copy-done.4, bf16[128,32,128]{2,1,0:T(8,128)(2,1)S(1)} %bitcast.3), custom_call_target="tpu_custom_call" | custom-call | flops 4194304 | bytes 3145728 | tf_op jit(solution)/shard_map/dispatch/pallas_call | solution.py:108
  11.8 37.1 %all_to_all.5.sent_ref = bf16[16,528,128]{2,1,0:T(8,128)(2,1)S(1)} all-to-all(bf16[16,528,128]{2,1,0:T(8,128)(2,1)S(1)} %dispatch.1), channel_id=1, replica_groups=mesh['crow'=8,'ccol'=16] {'ccol'}, dimensions={0} | all-to-all | bytes 4325376 | tf_op jit(solution)/shard_map/all_to_all | solution.py:415
  48.9 3.6 %collective-permute-start = (bf16[1024,512]{1,0:T(8,128)(2,1)}, bf16[1024,512]{1,0:T(8,128)(2,1)}, u32[]{:S(2)}, u32[]{:S(2)}) collective-permute-start(bf16[1024,512]{1,0:T(8,128)(2,1)} %get-tuple-element.47), channel_id=1, source_target_pairs={{0,1},{1,2},{2,3},{3,4},{4,5},{5,6},{6,7},{7,8},{8,9},{9,10},{10,1... | collective-permute-start | bytes 3145736 | tf_op jit(solution)/shard_map/ppermute | solution.py:420
  52.5 1.3 collective-permute-start.1
  53.8 10.6 %far_field.1 = (bf16[20,64,512]{2,1,0:T(8,128)(2,1)S(1)}, bf16[20,64,512]{2,1,0:T(8,128)(2,1)}, f32[10,64,512]{2,1,0:T(8,128)S(1)}, f32[10,64,512]{2,1,0:T(8,128...) custom-call(bf16[64,64,512]{2,1,0:T(8,128)(2,1)} %all-gather.2.clone, ...), custom_call_target="tpu_custom_call" | custom-call | flops 4294967296 | bytes 25165824 | tf_op jit(solution)/shard_map/far_field/pallas_call | solution.py:203
  64.4 3.7 %collective-permute-start.3 = (bf16[20,64,512]{2,1,0:T(8,128)(2,1)}, bf16[20,64,512]{2,1,0:T(8,128)(2,1)S(1)}, u32[]{:S(2)}, u32[]{:S(2)}) collective-permute-start(bf16[20,64,512]{2,1,0:T(8,128)(2,1)} %get-tuple-element.57), channel_id=1, source_target_pairs={{0,12},{1,13},{2,14},{3,15},{4,0},{5,1},{6,2},{7,3},{8,4},{9,5},{1... | collective-permute-start | bytes 3932168 | tf_op jit(solution)/shard_map/ppermute | solution.py:237
  68.0 4.6 %collective-permute-done.before_ref = bf16[1024,512]{1,0:T(8,128)(2,1)} collective-permute-done((bf16[1024,512]{1,0:T(8,128)(2,1)}, bf16[1024,512]{1,0:T(8,128)(2,1)}, u32[]{:S(2)}, u32[]{:S(2)}) %collective-permute-start) | collective-permute-done | bytes 1048608 | tf_op jit(solution)/shard_map/ppermute | solution.py:420
  72.7 4.1 %collective-permute-done.1.after_ref = bf16[1024,512]{1,0:T(8,128)(2,1)} collective-permute-done((bf16[1024,512]{1,0:T(8,128)(2,1)}, bf16[1024,512]{1,0:T(8,128)(2,1)}, u32[]{:S(2)}, u32[]{:S(2)}) %collective-permute-start.1) | collective-permute-done | bytes 1048608 | tf_op jit(solution)/shard_map/ppermute | solution.py:421
  77.9 6.8 %collective-permute-start.11 = (bf16[12,64,512]{2,1,0:T(8,128)(2,1)S(1)}, bf16[12,64,512]{2,1,0:T(8,128)(2,1)S(1)}, u32[]{:S(2)}, u32[]{:S(2)}) collective-permute-start(bf16[12,64,512]{2,1,0:T(8,128)(2,1)S(1)} %get-tuple-element.73), channel_id=1, source_target_pairs={{0,3},{1,0},{2,1},{3,2},{4,7},{5,4},{6,5},{7,6},{8,11},{9,8},{10,9... | collective-permute-start | bytes 2359304 | tf_op jit(solution)/shard_map/ppermute | solution.py:237
  84.6 3.7 %copy-done.5 = bf16[2048,2304]{1,0:T(8,128)(2,1)S(1)} copy-done((bf16[2048,2304]{1,0:T(8,128)(2,1)S(1)}, bf16[2048,2304]{1,0:T(8,128)(2,1)}, u32[]{:S(2)}) %copy-start.5) | copy-done | bytes 9437208
  88.3 8.3 %near_field.1 = (f32[2048,512]{1,0:T(8,128)S(1)}, bf16[2048,64]{1,0:T(8,128)(2,1)S(1)}) custom-call(bf16[2048,2304]{1,0:T(8,128)(2,1)S(1)} %copy-done.5, bf16[1024,512]{1,0:T(8,128)(2,1)} %collective-permute-done.before_ref, bf16[2048,512]{1,0:T(8,128)(2,1)S(1)} %copy-done.1, bf16[1024,512]{1,0:T(8,128)(2,1)} %collective-permute-done.1.after_ref, ...), custom_call_target="tpu_custom_call" | custom-call | flops 4831838208 | bytes 2097152 | tf_op jit(solution)/shard_map/near_field/pallas_call | solution.py:331
  96.6 10.4 %collective-permute-done.3.down_ref.down_in_ref = bf16[20,64,512]{2,1,0:T(8,128)(2,1)S(1)} collective-permute-done((bf16[20,64,512]{2,1,0:T(8,128)(2,1)}, bf16[20,64,512]{2,1,0:T(8,128)(2,1)S(1)}, u32[]{:S(2)}, u32[]{:S(2)}) %collective-permute-start.3) | collective-permute-done | bytes 1310752 | tf_op jit(solution)/shard_map/ppermute | solution.py:237
  108.2 2.4 %collective-permute-start.5 = (bf16[10,64,512]{2,1,0:T(8,128)(2,1)S(1)}, bf16[10,64,512]{2,1,0:T(8,128)(2,1)S(1)}, u32[]{:S(2)}, u32[]{:S(2)}) collective-permute-start(bf16[10,64,512]{2,1,0:T(8,128)(2,1)S(1)} %get-tuple-element.63), channel_id=1, source_target_pairs={{0,12},{1,13},{2,14},{3,15},{4,0},{5,1},{6,2},{7,3},{8,4},{9,5},{1... | collective-permute-start | bytes 1966088 | tf_op jit(solution)/shard_map/ppermute | solution.py:237
  110.8 3.2 %collective-permute-start.13 = (bf16[6,64,512]{2,1,0:T(8,128)(2,1)S(1)}, bf16[6,64,512]{2,1,0:T(8,128)(2,1)S(1)}, u32[]{:S(2)}, u32[]{:S(2)}) collective-permute-start(bf16[6,64,512]{2,1,0:T(8,128)(2,1)S(1)} %get-tuple-element.77), channel_id=1, source_target_pairs={{0,3},{1,0},{2,1},{3,2},{4,7},{5,4},{6,5},{7,6},{8,11},{9,8},{10,9... | collective-permute-start | bytes 1179656 | tf_op jit(solution)/shard_map/ppermute | solution.py:237
  114.0 8.3 %collective-permute-done.4.up_rest_ref = bf16[10,64,512]{2,1,0:T(8,128)(2,1)S(1)} collective-permute-done((bf16[10,64,512]{2,1,0:T(8,128)(2,1)S(1)}, bf16[10,64,512]{2,1,0:T(8,128)(2,1)S(1)}, u32[]{:S(2)}, u32[]{:S(2)}) %collective-permute-start.4) | collective-permute-done | bytes 655392 | tf_op jit(solution)/shard_map/ppermute | solution.py:237
  122.8 3.2 %collective-permute-start.7 = (bf16[10,64,256]{2,1,0:T(8,128)(2,1)S(1)}, bf16[10,64,256]{2,1,0:T(8,128)(2,1)S(1)}, u32[]{:S(2)}, u32[]{:S(2)}) collective-permute-start(bf16[10,64,256]{2,1,0:T(8,128)(2,1)S(1)} %get-tuple-element.66), channel_id=1, source_target_pairs={{0,3},{1,0},{2,1},{3,2},{4,7},{5,4},{6,5},{7,6},{8,11},{9,8},{10,9... | collective-permute-start | bytes 983048 | tf_op jit(solution)/shard_map/ppermute | solution.py:237
  126.8 2.7 %collective-permute-start.15 = (bf16[6,64,256]{2,1,0:T(8,128)(2,1)S(1)}, bf16[6,64,256]{2,1,0:T(8,128)(2,1)S(1)}, u32[]{:S(2)}, u32[]{:S(2)}) collective-permute-start(bf16[6,64,256]{2,1,0:T(8,128)(2,1)S(1)} %get-tuple-element.80), channel_id=1, source_target_pairs={{0,12},{1,13},{2,14},{3,15},{4,0},{5,1},{6,2},{7,3},{8,4},{9,5},{1... | collective-permute-start | bytes 589832 | tf_op jit(solution)/shard_map/ppermute | solution.py:237
  129.5 2.5 %collective-permute-done.6.up_ref.refs_1_ = bf16[10,64,256]{2,1,0:T(8,128)(2,1)S(1)} collective-permute-done((bf16[10,64,256]{2,1,0:T(8,128)(2,1)S(1)}, bf16[10,64,256]{2,1,0:T(8,128)(2,1)S(1)}, u32[]{:S(2)}, u32[]{:S(2)}) %collective-permute-start.6) | collective-permute-done | bytes 327712 | tf_op jit(solution)/shard_map/ppermute | solution.py:237
  132.1 1.2 collective-permute-start.8
  133.3 2.1 %collective-permute-start.9 = (bf16[5,64,256]{2,1,0:T(8,128)(2,1)S(1)}, bf16[5,64,256]{2,1,0:T(8,128)(2,1)S(1)}, u32[]{:S(2)}, u32[]{:S(2)}) collective-permute-start(bf16[5,64,256]{2,1,0:T(8,128)(2,1)S(1)} %get-tuple-element.70), channel_id=1, source_target_pairs={{0,3},{1,0},{2,1},{3,2},{4,7},{5,4},{6,5},{7,6},{8,11},{9,8},{10,9... | collective-permute-start | bytes 491528 | tf_op jit(solution)/shard_map/ppermute | solution.py:237
  135.6 3.2 %collective-permute-start.17 = (bf16[3,64,256]{2,1,0:T(8,128)(2,1)S(1)}, bf16[3,64,256]{2,1,0:T(8,128)(2,1)S(1)}, u32[]{:S(2)}, u32[]{:S(2)}) collective-permute-start(bf16[3,64,256]{2,1,0:T(8,128)(2,1)S(1)} %get-tuple-element.84), channel_id=1, source_target_pairs={{0,12},{1,13},{2,14},{3,15},{4,0},{5,1},{6,2},{7,3},{8,4},{9,5},{1... | collective-permute-start | bytes 294920 | tf_op jit(solution)/shard_map/ppermute | solution.py:237
  138.8 2.6 %collective-permute-done.16.refs_8_ = bf16[3,64,256]{2,1,0:T(8,128)(2,1)S(1)} collective-permute-done((bf16[3,64,256]{2,1,0:T(8,128)(2,1)S(1)}, bf16[3,64,256]{2,1,0:T(8,128)(2,1)S(1)}, u32[]{:S(2)}, u32[]{:S(2)}) %collective-permute-start.16) | collective-permute-done | bytes 98336 | tf_op jit(solution)/shard_map/ppermute | solution.py:237
  141.4 2.5 %expand.1 = bf16[2048,512]{1,0:T(8,128)(2,1)} custom-call(f32[2048,512]{1,0:T(8,128)S(1)} %get-tuple-element.54.near_ref, bf16[2048,64]{1,0:T(8,128)(2,1)S(1)} %get-tuple-element.55.basis_ref, f32[5,64,512]{2,1,0:T(8,128)S(1)} %get-tuple-element.64.refs_0_, bf16[10,64,256]{2,1,0:T(8,128)(2,1)S(1)} %collective-permute-done.6.up_ref.refs_1_, ...), custom_call_target="tpu_custom_call" | custom-call | flops 134217728 | bytes 7340032 | tf_op jit(solution)/shard_map/expand/pallas_call | solution.py:381
  (44 shorter events, 4.2 us)
Async XLA Ops:
  6.5 3.6 %copy-start.2 = (s32[128]{0:T(128)S(1)}, s32[128]{0:T(128)}, u32[]{:S(2)}) copy-start(s32[128]{0:T(128)} %rows_ref.1) | copy-start | bytes 1540
  6.5 47.2 %all-gather.2.cloned.1.call-start = ((), (), s32[]{:S(2)}) async-start(), calls=%async_computation.1 | async-start | bytes 4718592 | tf_op jit(solution)/shard_map/all_gather | solution.py:408
  48.9 35.7 %copy-start.6 = (bf16[64,2048]{1,0:T(8,128)(2,1)S(1)}, bf16[64,2048]{1,0:T(8,128)(2,1)}, u32[]{:S(2)}) copy-start(bf16[64,2048]{1,0:T(8,128)(2,1)} %basis_ref.3) | copy-start | bytes 786436
  48.9 23.8 %collective-permute-start = (bf16[1024,512]{1,0:T(8,128)(2,1)}, bf16[1024,512]{1,0:T(8,128)(2,1)}, u32[]{:S(2)}, u32[]{:S(2)}) collective-permute-start(bf16[1024,512]{1,0:T(8,128)(2,1)} %get-tuple-element.47), channel_id=1, source_target_pairs={{0,1},{1,2},{2,3},{3,4},{4,5},{5,6},{6,7},{7,8},{8,9},{9,10},{10,1... | collective-permute-start | bytes 3145736 | tf_op jit(solution)/shard_map/ppermute | solution.py:420
  52.5 24.3 %collective-permute-start.1 = (bf16[1024,512]{1,0:T(8,128)(2,1)}, bf16[1024,512]{1,0:T(8,128)(2,1)}, u32[]{:S(2)}, u32[]{:S(2)}) collective-permute-start(bf16[1024,512]{1,0:T(8,128)(2,1)} %get-tuple-element.48), channel_id=1, source_target_pairs={{1,0},{2,1},{3,2},{4,3},{5,4},{6,5},{7,6},{8,7},{9,8},{10,9},{11,1... | collective-permute-start | bytes 3145736 | tf_op jit(solution)/shard_map/ppermute | solution.py:421
  53.8 30.8 %copy-start.1 = (bf16[2048,512]{1,0:T(8,128)(2,1)S(1)}, bf16[2048,512]{1,0:T(8,128)(2,1)}, u32[]{:S(2)}) copy-start(bf16[2048,512]{1,0:T(8,128)(2,1)} %modes_ref.3) | copy-start | bytes 6291460
  64.4 42.6 %collective-permute-start.3 = (bf16[20,64,512]{2,1,0:T(8,128)(2,1)}, bf16[20,64,512]{2,1,0:T(8,128)(2,1)S(1)}, u32[]{:S(2)}, u32[]{:S(2)}) collective-permute-start(bf16[20,64,512]{2,1,0:T(8,128)(2,1)} %get-tuple-element.57), channel_id=1, source_target_pairs={{0,12},{1,13},{2,14},{3,15},{4,0},{5,1},{6,2},{7,3},{8,4},{9,5},{1... | collective-permute-start | bytes 3932168 | tf_op jit(solution)/shard_map/ppermute | solution.py:237
  68.0 39.0 %collective-permute-start.2 = (bf16[20,64,512]{2,1,0:T(8,128)(2,1)S(1)}, bf16[20,64,512]{2,1,0:T(8,128)(2,1)S(1)}, u32[]{:S(2)}, u32[]{:S(2)}) collective-permute-start(bf16[20,64,512]{2,1,0:T(8,128)(2,1)S(1)} %get-tuple-element.51), channel_id=1, source_target_pairs={{0,4},{1,5},{2,6},{3,7},{4,8},{5,9},{6,10},{7,11},{8,12},{9,13},{1... | collective-permute-start | bytes 3932168 | tf_op jit(solution)/shard_map/ppermute | solution.py:237
  76.8 33.7 %collective-permute-start.10 = (bf16[12,64,512]{2,1,0:T(8,128)(2,1)}, bf16[12,64,512]{2,1,0:T(8,128)(2,1)S(1)}, u32[]{:S(2)}, u32[]{:S(2)}) collective-permute-start(bf16[12,64,512]{2,1,0:T(8,128)(2,1)} %get-tuple-element.72), channel_id=1, source_target_pairs={{0,1},{1,2},{2,3},{3,0},{4,5},{5,6},{6,7},{7,4},{8,9},{9,10},{10,1... | collective-permute-start | bytes 2359304 | tf_op jit(solution)/shard_map/ppermute | solution.py:237
  77.9 32.7 %collective-permute-start.11 = (bf16[12,64,512]{2,1,0:T(8,128)(2,1)S(1)}, bf16[12,64,512]{2,1,0:T(8,128)(2,1)S(1)}, u32[]{:S(2)}, u32[]{:S(2)}) collective-permute-start(bf16[12,64,512]{2,1,0:T(8,128)(2,1)S(1)} %get-tuple-element.73), channel_id=1, source_target_pairs={{0,3},{1,0},{2,1},{3,2},{4,7},{5,4},{6,5},{7,6},{8,11},{9,8},{10,9... | collective-permute-start | bytes 2359304 | tf_op jit(solution)/shard_map/ppermute | solution.py:237
  84.6 3.7 %copy-start.5 = (bf16[2048,2304]{1,0:T(8,128)(2,1)S(1)}, bf16[2048,2304]{1,0:T(8,128)(2,1)}, u32[]{:S(2)}) copy-start(bf16[2048,2304]{1,0:T(8,128)(2,1)} %near_ref.1) | copy-start | bytes 28311556
  107.2 15.1 %copy-start = (f32[20,64,512]{2,1,0:T(8,128)S(1)}, f32[20,64,512]{2,1,0:T(8,128)}, u32[]{:S(2)}) copy-start(f32[20,64,512]{2,1,0:T(8,128)} %get-tuple-element.56.own_ref) | copy-start | bytes 7864324
  107.2 15.1 %collective-permute-start.4 = (bf16[10,64,512]{2,1,0:T(8,128)(2,1)S(1)}, bf16[10,64,512]{2,1,0:T(8,128)(2,1)S(1)}, u32[]{:S(2)}, u32[]{:S(2)}) collective-permute-start(bf16[10,64,512]{2,1,0:T(8,128)(2,1)S(1)} %get-tuple-element.62), channel_id=1, source_target_pairs={{0,4},{1,5},{2,6},{3,7},{4,8},{5,9},{6,10},{7,11},{8,12},{9,13},{1... | collective-permute-start | bytes 1966088 | tf_op jit(solution)/shard_map/ppermute | solution.py:237
  108.2 14.2 %collective-permute-start.5 = (bf16[10,64,512]{2,1,0:T(8,128)(2,1)S(1)}, bf16[10,64,512]{2,1,0:T(8,128)(2,1)S(1)}, u32[]{:S(2)}, u32[]{:S(2)}) collective-permute-start(bf16[10,64,512]{2,1,0:T(8,128)(2,1)S(1)} %get-tuple-element.63), channel_id=1, source_target_pairs={{0,12},{1,13},{2,14},{3,15},{4,0},{5,1},{6,2},{7,3},{8,4},{9,5},{1... | collective-permute-start | bytes 1966088 | tf_op jit(solution)/shard_map/ppermute | solution.py:237
  110.7 15.3 %collective-permute-start.12 = (bf16[6,64,512]{2,1,0:T(8,128)(2,1)S(1)}, bf16[6,64,512]{2,1,0:T(8,128)(2,1)S(1)}, u32[]{:S(2)}, u32[]{:S(2)}) collective-permute-start(bf16[6,64,512]{2,1,0:T(8,128)(2,1)S(1)} %get-tuple-element.76), channel_id=1, source_target_pairs={{0,1},{1,2},{2,3},{3,0},{4,5},{5,6},{6,7},{7,4},{8,9},{9,10},{10,1... | collective-permute-start | bytes 1179656 | tf_op jit(solution)/shard_map/ppermute | solution.py:237
  110.8 15.3 %collective-permute-start.13 = (bf16[6,64,512]{2,1,0:T(8,128)(2,1)S(1)}, bf16[6,64,512]{2,1,0:T(8,128)(2,1)S(1)}, u32[]{:S(2)}, u32[]{:S(2)}) collective-permute-start(bf16[6,64,512]{2,1,0:T(8,128)(2,1)S(1)} %get-tuple-element.77), channel_id=1, source_target_pairs={{0,3},{1,0},{2,1},{3,2},{4,7},{5,4},{6,5},{7,6},{8,11},{9,8},{10,9... | collective-permute-start | bytes 1179656 | tf_op jit(solution)/shard_map/ppermute | solution.py:237
  122.7 9.3 %collective-permute-start.6 = (bf16[10,64,256]{2,1,0:T(8,128)(2,1)S(1)}, bf16[10,64,256]{2,1,0:T(8,128)(2,1)S(1)}, u32[]{:S(2)}, u32[]{:S(2)}) collective-permute-start(bf16[10,64,256]{2,1,0:T(8,128)(2,1)S(1)} %get-tuple-element.65), channel_id=1, source_target_pairs={{0,1},{1,2},{2,3},{3,0},{4,5},{5,6},{6,7},{7,4},{8,9},{9,10},{10,1... | collective-permute-start | bytes 983048 | tf_op jit(solution)/shard_map/ppermute | solution.py:237
  122.8 9.3 %collective-permute-start.7 = (bf16[10,64,256]{2,1,0:T(8,128)(2,1)S(1)}, bf16[10,64,256]{2,1,0:T(8,128)(2,1)S(1)}, u32[]{:S(2)}, u32[]{:S(2)}) collective-permute-start(bf16[10,64,256]{2,1,0:T(8,128)(2,1)S(1)} %get-tuple-element.66), channel_id=1, source_target_pairs={{0,3},{1,0},{2,1},{3,2},{4,7},{5,4},{6,5},{7,6},{8,11},{9,8},{10,9... | collective-permute-start | bytes 983048 | tf_op jit(solution)/shard_map/ppermute | solution.py:237
  126.2 9.2 %collective-permute-start.14 = (bf16[6,64,256]{2,1,0:T(8,128)(2,1)S(1)}, bf16[6,64,256]{2,1,0:T(8,128)(2,1)S(1)}, u32[]{:S(2)}, u32[]{:S(2)}) collective-permute-start(bf16[6,64,256]{2,1,0:T(8,128)(2,1)S(1)} %get-tuple-element.79), channel_id=1, source_target_pairs={{0,4},{1,5},{2,6},{3,7},{4,8},{5,9},{6,10},{7,11},{8,12},{9,13},{1... | collective-permute-start | bytes 589832 | tf_op jit(solution)/shard_map/ppermute | solution.py:237
  126.8 8.6 %collective-permute-start.15 = (bf16[6,64,256]{2,1,0:T(8,128)(2,1)S(1)}, bf16[6,64,256]{2,1,0:T(8,128)(2,1)S(1)}, u32[]{:S(2)}, u32[]{:S(2)}) collective-permute-start(bf16[6,64,256]{2,1,0:T(8,128)(2,1)S(1)} %get-tuple-element.80), channel_id=1, source_target_pairs={{0,12},{1,13},{2,14},{3,15},{4,0},{5,1},{6,2},{7,3},{8,4},{9,5},{1... | collective-permute-start | bytes 589832 | tf_op jit(solution)/shard_map/ppermute | solution.py:237
  132.1 9.3 %collective-permute-start.8 = (bf16[5,64,256]{2,1,0:T(8,128)(2,1)S(1)}, bf16[5,64,256]{2,1,0:T(8,128)(2,1)S(1)}, u32[]{:S(2)}, u32[]{:S(2)}) collective-permute-start(bf16[5,64,256]{2,1,0:T(8,128)(2,1)S(1)} %get-tuple-element.69), channel_id=1, source_target_pairs={{0,1},{1,2},{2,3},{3,0},{4,5},{5,6},{6,7},{7,4},{8,9},{9,10},{10,1... | collective-permute-start | bytes 491528 | tf_op jit(solution)/shard_map/ppermute | solution.py:237
  133.3 8.1 %collective-permute-start.9 = (bf16[5,64,256]{2,1,0:T(8,128)(2,1)S(1)}, bf16[5,64,256]{2,1,0:T(8,128)(2,1)S(1)}, u32[]{:S(2)}, u32[]{:S(2)}) collective-permute-start(bf16[5,64,256]{2,1,0:T(8,128)(2,1)S(1)} %get-tuple-element.70), channel_id=1, source_target_pairs={{0,3},{1,0},{2,1},{3,2},{4,7},{5,4},{6,5},{7,6},{8,11},{9,8},{10,9... | collective-permute-start | bytes 491528 | tf_op jit(solution)/shard_map/ppermute | solution.py:237
  135.5 5.9 %collective-permute-start.16 = (bf16[3,64,256]{2,1,0:T(8,128)(2,1)S(1)}, bf16[3,64,256]{2,1,0:T(8,128)(2,1)S(1)}, u32[]{:S(2)}, u32[]{:S(2)}) collective-permute-start(bf16[3,64,256]{2,1,0:T(8,128)(2,1)S(1)} %get-tuple-element.83), channel_id=1, source_target_pairs={{0,4},{1,5},{2,6},{3,7},{4,8},{5,9},{6,10},{7,11},{8,12},{9,13},{1... | collective-permute-start | bytes 294920 | tf_op jit(solution)/shard_map/ppermute | solution.py:237
  135.6 5.8 %collective-permute-start.17 = (bf16[3,64,256]{2,1,0:T(8,128)(2,1)S(1)}, bf16[3,64,256]{2,1,0:T(8,128)(2,1)S(1)}, u32[]{:S(2)}, u32[]{:S(2)}) collective-permute-start(bf16[3,64,256]{2,1,0:T(8,128)(2,1)S(1)} %get-tuple-element.84), channel_id=1, source_target_pairs={{0,12},{1,13},{2,14},{3,15},{4,0},{5,1},{6,2},{7,3},{8,4},{9,5},{1... | collective-permute-start | bytes 294920 | tf_op jit(solution)/shard_map/ppermute | solution.py:237
  (3 other events, 10.5 us)
Sparse Core Ops, SparseCore 0:
  10.0 34.5 all-gather.1

commit v8 on v7

--- a/solution.py
+++ b/solution.py
@@ -118,7 +118,7 @@
 
 
 UNROLL = 32
-X_ROWS = 5
+X_ROWS = 4
 
 
 def far_kernel(slots, rows, comp_ref, sent_ref, *refs):
@@ -345,7 +345,7 @@
         scratch_shapes=[VMEM((panels + 2 * halo, cols), jnp.bfloat16)],
         compiler_params=pltpu.CompilerParams(vmem_limit_bytes=32 * MIB),
         cost_estimate=pl.CostEstimate(
-            flops=2 * panels * band * cols, bytes_accessed=2 * MIB, transcendentals=0
+            flops=16 * panels * band * cols, bytes_accessed=16 * MIB, transcendentals=0
         ),
         name="near_field",
     )(near_blocks, before, modes, after, row_basis)
@@ -414,20 +414,17 @@
     )
     sent = lax.all_to_all(sent, "ccol", split_axis=0, concat_axis=0, tiled=True)
 
-    low, high, sent = lax.optimization_barrier((low, high, sent))
     up = [(i, i + 1) for i in range(devices - 1)]
     down = [(j, i) for i, j in up]
     before = lax.ppermute(high, ("crow", "ccol"), up)
     after = lax.ppermute(low, ("crow", "ccol"), down)
+    near, basis = near_field(near_blocks, before, modes, after, row_basis)
+    gathered, _ = lax.optimization_barrier((gathered, near))
 
     left, right = far_field(gathered, sent, slots, lines, col_devices * cluster_count)
     for along_x in (True, False):
         left_up, left_down = both_ways(left[0], left[1], along_x)
         right_up, right_down = both_ways(right[0], right[1], not along_x)
-        if along_x:
-            (before, after), _ = lax.optimization_barrier(((before, after), left[0]))
-            near, basis = near_field(near_blocks, before, modes, after, row_basis)
-            (left_up, left_down), _ = lax.optimization_barrier(((left_up, left_down), near))
         left_rest = passed_on(left[2], left[3], left_up, left_down)
         right_rest = passed_on(right[2], right[3], right_up, right_down)
         left_rest = both_ways(*left_rest, along_x)

time: 153 us -> 154 us (level)
  blocking collectives: 37.1 us -> 0 us
  waiting for transfers between devices: 32.6 us -> 52.5 us
  starting transfers between devices: 36.2 us -> 50.4 us
  local copies, waits for them, and re-layouts: 3.95 us -> 8.21 us
    all_to_all x1 -> x0, blocking collectives: 37.1 us -> none  [per_device(): sent = lax.all_to_all(sent, 'ccol', split_axis=0, concat_axis=0, tiled=True)]
    ppermute x8, starting transfers between devices: 3.99 us -> 17.7 us  [both_ways(): lax.ppermute(up, 'ccol', ring(along_x, 1))]
    ppermute x8, waiting for transfers between devices: 13.5 us -> 26.8 us  [both_ways(): lax.ppermute(up, 'ccol', ring(along_x, 1))]
    ppermute x1, waiting for transfers between devices: 4.65 us -> 15.9 us  [per_device(): before = lax.ppermute(high, ('crow', 'ccol'), up)]
    ppermute x8, waiting for transfers between devices: 10.4 us -> 0.02 us  [both_ways(): lax.ppermute(down, 'ccol', ring(along_x, -1))]
    all_to_all x0 -> x1, starting transfers between devices: none -> 8.85 us  [per_device(): sent = lax.all_to_all(sent, 'ccol', split_axis=0, concat_axis=0, tiled=True)]
    ppermute x8, starting transfers between devices: 27.3 us -> 18.6 us  [both_ways(): lax.ppermute(down, 'ccol', ring(along_x, -1))]
    unnamed x17 -> x23, local copies, waits for them, and re-layouts: 3.95 us -> 8.21 us
  transfers between devices with their start and end apart: 19 -> 20, of which waited for: 6 -> 9; matrix products, arithmetic and copies ran while one was open for 0% -> 0% of each run, Pallas kernels for 14% -> 8%
where the time goes in v8:
time: 154 us; the launch traced here: 152 us
  waiting for transfers between devices  52.5 us (34%)
  starting transfers between devices  50.4 us (33%)
  Pallas kernels  27.6 us (18%)
  between operations  13.5 us (9%)
  local copies, waits for them, and re-layouts  8.21 us (5%)
    ppermute x8, waiting for transfers between devices, both_ways(): lax.ppermute(up, 'ccol', ring(along_x, 1))  26.8 us
    ppermute x8, starting transfers between devices, both_ways(): lax.ppermute(down, 'ccol', ring(along_x, -1))  18.6 us
    ppermute x8, starting transfers between devices, both_ways(): lax.ppermute(up, 'ccol', ring(along_x, 1))  17.7 us
    ppermute x1, waiting for transfers between devices, per_device(): before = lax.ppermute(high, ('crow', 'ccol'), up)  15.9 us
    pallas_call x1, Pallas kernels, far_field(): pl.pallas_call(functools.partial(far_kernel, slots, rows), in_specs=[whol...  9.72 us
    all_to_all x1, starting transfers between devices, per_device(): sent = lax.all_to_all(sent, 'ccol', split_axis=0, concat_axis=0, tiled=True)  8.85 us
    unnamed x23, local copies, waits for them, and re-layouts  8.21 us
    pallas_call x1, Pallas kernels, near_field(): pl.pallas_call(near_kernel, grid=(panels // CS,), in_specs=[pl.BlockSpec(...  7.99 us
  transfers between devices with their start and end apart: 20, of which 9 were waited for; matrix products, arithmetic and copies ran while one was open for 0% of the time, Pallas kernels for 8%

profile of v8, /device:TPU:0, one launch (start us, length us, event | category | flops | bytes accessed | tf_op | source)
XLA Modules:
  0.0 152.3 jit_solution(409665343032303797)
XLA Ops:
  6.6 3.3 %compress.1 = (bf16[8,64,512]{2,1,0:T(8,128)(2,1)}, bf16[1024,512]{1,0:T(8,128)(2,1)}, bf16[1024,512]{1,0:T(8,128)(2,1)}) custom-call(bf16[64,2048]{1,0:T(8,128)(2,1)} %basis_ref.2, bf16[2048,512]{1,0:T(8,128)(2,1)} %modes_ref.3), custom_call_target="tpu_custom_call" | custom-call | flops 134217728 | bytes 3145728 | tf_op jit(solution)/shard_map/compress/pallas_call | solution.py:49
  9.9 4.0 %collective-permute-start = (bf16[1024,512]{1,0:T(8,128)(2,1)}, bf16[1024,512]{1,0:T(8,128)(2,1)S(1)}, u32[]{:S(2)}, u32[]{:S(2)}) collective-permute-start(bf16[1024,512]{1,0:T(8,128)(2,1)} %get-tuple-element.39), channel_id=1, source_target_pairs={{0,1},{1,2},{2,3},{3,4},{4,5},{5,6},{6,7},{7,8},{8,9},{9,10},{10,1... | collective-permute-start | bytes 3145736 | tf_op jit(solution)/shard_map/ppermute | solution.py:419
  15.4 3.1 %dispatch.1 = bf16[16,528,128]{2,1,0:T(8,128)(2,1)} custom-call(s32[128]{0:T(128)S(1)} %copy-done.3, s32[128]{0:T(128)S(1)} %bitcast.4, s32[128]{0:T(128)S(1)} %copy-done.5, bf16[128,32,128]{2,1,0:T(8,128)(2,1)S(1)} %bitcast.3), custom_call_target="tpu_custom_call" | custom-call | flops 4194304 | bytes 3145728 | tf_op jit(solution)/shard_map/dispatch/pallas_call | solution.py:108
  18.5 8.8 %all-to-all-start = ((bf16[16,528,128]{2,1,0:T(8,128)(2,1)}), bf16[16,528,128]{2,1,0:T(8,128)(2,1)}, u32[]{:S(2)}, u32[]{:S(2)}) async-start(bf16[16,528,128]{2,1,0:T(8,128)(2,1)} %dispatch.1), calls=%async_computation | async-start | bytes 4325376 | tf_op jit(solution)/shard_map/all_to_all | solution.py:415
  27.4 15.9 %collective-permute-done.before_ref = bf16[1024,512]{1,0:T(8,128)(2,1)S(1)} collective-permute-done((bf16[1024,512]{1,0:T(8,128)(2,1)}, bf16[1024,512]{1,0:T(8,128)(2,1)S(1)}, u32[]{:S(2)}, u32[]{:S(2)}) %collective-permute-start) | collective-permute-done | bytes 1048608 | tf_op jit(solution)/shard_map/ppermute | solution.py:419
  44.3 7.6 %collective-permute-done.1.after_ref = bf16[1024,512]{1,0:T(8,128)(2,1)} collective-permute-done((bf16[1024,512]{1,0:T(8,128)(2,1)}, bf16[1024,512]{1,0:T(8,128)(2,1)}, u32[]{:S(2)}, u32[]{:S(2)}) %collective-permute-start.1) | collective-permute-done | bytes 1048608 | tf_op jit(solution)/shard_map/ppermute | solution.py:420
  52.0 3.7 %copy-done.6 = bf16[2048,2304]{1,0:T(8,128)(2,1)S(1)} copy-done((bf16[2048,2304]{1,0:T(8,128)(2,1)S(1)}, bf16[2048,2304]{1,0:T(8,128)(2,1)}, u32[]{:S(2)}) %copy-start.6) | copy-done | bytes 9437208
  56.9 8.0 %near_field.1 = (f32[2048,512]{1,0:T(8,128)S(1)}, bf16[2048,64]{1,0:T(8,128)(2,1)S(1)}) custom-call(bf16[2048,2304]{1,0:T(8,128)(2,1)S(1)} %copy-done.6, bf16[1024,512]{1,0:T(8,128)(2,1)S(1)} %copy-done.8, bf16[2048,512]{1,0:T(8,128)(2,1)S(1)} %copy-done.2, bf16[1024,512]{1,0:T(8,128)(2,1)} %collective-permute-done.1.after_ref, bf16[64,2048]{1,0:T(8,128)(2,1)S(1)} %copy-done.9), custom_call_target="tpu_custom_call" | custom-call | flops 38654705664 | bytes 16777216 | tf_op jit(solution)/shard_map/near_field/pallas_call | solution.py:331
  64.9 2.0 %copy-done = f32[2048,512]{1,0:T(8,128)} copy-done((f32[2048,512]{1,0:T(8,128)}, f32[2048,512]{1,0:T(8,128)S(1)}, u32[]{:S(2)}) %copy-start) | copy-done | bytes 4194328
  66.9 2.1 %all-to-all-done.sent_ref = bf16[16,528,128]{2,1,0:T(8,128)(2,1)} async-done(((bf16[16,528,128]{2,1,0:T(8,128)(2,1)}), bf16[16,528,128]{2,1,0:T(8,128)(2,1)}, u32[]{:S(2)}, u32[]{:S(2)}) %all-to-all-start) | async-done | bytes 2162720 | tf_op jit(solution)/shard_map/all_to_all | solution.py:415
  69.0 9.7 %far_field.1 = (bf16[16,64,512]{2,1,0:T(8,128)(2,1)S(1)}, bf16[16,64,512]{2,1,0:T(8,128)(2,1)S(1)}, f32[8,64,512]{2,1,0:T(8,128)S(1)}, f32[8,64,512]{2,1,0:T(8,1...) custom-call(bf16[64,64,512]{2,1,0:T(8,128)(2,1)} %all-gather.2.clone, ...), custom_call_target="tpu_custom_call" | custom-call | flops 4294967296 | bytes 25165824 | tf_op jit(solution)/shard_map/far_field/pallas_call | solution.py:203
  78.7 6.2 %collective-permute-start.2 = (bf16[16,64,512]{2,1,0:T(8,128)(2,1)S(1)}, bf16[16,64,512]{2,1,0:T(8,128)(2,1)S(1)}, u32[]{:S(2)}, u32[]{:S(2)}) collective-permute-start(bf16[16,64,512]{2,1,0:T(8,128)(2,1)S(1)} %get-tuple-element.46), channel_id=1, source_target_pairs={{0,4},{1,5},{2,6},{3,7},{4,8},{5,9},{6,10},{7,11},{8,12},{9,13},{1... | collective-permute-start | bytes 3145736 | tf_op jit(solution)/shard_map/ppermute | solution.py:237
  86.6 4.9 %collective-permute-start.10 = (bf16[16,64,512]{2,1,0:T(8,128)(2,1)S(1)}, bf16[16,64,512]{2,1,0:T(8,128)(2,1)S(1)}, u32[]{:S(2)}, u32[]{:S(2)}) collective-permute-start(bf16[16,64,512]{2,1,0:T(8,128)(2,1)S(1)} %get-tuple-element.60), channel_id=1, source_target_pairs={{0,1},{1,2},{2,3},{3,0},{4,5},{5,6},{6,7},{7,4},{8,9},{9,10},{10,1... | collective-permute-start | bytes 3145736 | tf_op jit(solution)/shard_map/ppermute | solution.py:237
  91.5 17.4 %collective-permute-done.2.up_ref.up_in_ref = bf16[16,64,512]{2,1,0:T(8,128)(2,1)S(1)} collective-permute-done((bf16[16,64,512]{2,1,0:T(8,128)(2,1)S(1)}, bf16[16,64,512]{2,1,0:T(8,128)(2,1)S(1)}, u32[]{:S(2)}, u32[]{:S(2)}) %collective-permute-start.2) | collective-permute-done | bytes 1048608 | tf_op jit(solution)/shard_map/ppermute | solution.py:237
  110.2 2.1 %collective-permute-start.5 = (bf16[8,64,512]{2,1,0:T(8,128)(2,1)S(1)}, bf16[8,64,512]{2,1,0:T(8,128)(2,1)S(1)}, u32[]{:S(2)}, u32[]{:S(2)}) collective-permute-start(bf16[8,64,512]{2,1,0:T(8,128)(2,1)S(1)} %get-tuple-element.51), channel_id=1, source_target_pairs={{0,12},{1,13},{2,14},{3,15},{4,0},{5,1},{6,2},{7,3},{8,4},{9,5},{1... | collective-permute-start | bytes 1572872 | tf_op jit(solution)/shard_map/ppermute | solution.py:237
  112.5 2.3 %collective-permute-start.12 = (bf16[8,64,512]{2,1,0:T(8,128)(2,1)S(1)}, bf16[8,64,512]{2,1,0:T(8,128)(2,1)S(1)}, u32[]{:S(2)}, u32[]{:S(2)}) collective-permute-start(bf16[8,64,512]{2,1,0:T(8,128)(2,1)S(1)} %get-tuple-element.64), channel_id=1, source_target_pairs={{0,1},{1,2},{2,3},{3,0},{4,5},{5,6},{6,7},{7,4},{8,9},{9,10},{10,1... | collective-permute-start | bytes 1572872 | tf_op jit(solution)/shard_map/ppermute | solution.py:237
  114.8 2.8 %collective-permute-start.13 = (bf16[8,64,512]{2,1,0:T(8,128)(2,1)S(1)}, bf16[8,64,512]{2,1,0:T(8,128)(2,1)S(1)}, u32[]{:S(2)}, u32[]{:S(2)}) collective-permute-start(bf16[8,64,512]{2,1,0:T(8,128)(2,1)S(1)} %get-tuple-element.65), channel_id=1, source_target_pairs={{0,3},{1,0},{2,1},{3,2},{4,7},{5,4},{6,5},{7,6},{8,11},{9,8},{10,9... | collective-permute-start | bytes 1572872 | tf_op jit(solution)/shard_map/ppermute | solution.py:237
  117.6 4.9 %collective-permute-done.4.up_rest_ref = bf16[8,64,512]{2,1,0:T(8,128)(2,1)S(1)} collective-permute-done((bf16[8,64,512]{2,1,0:T(8,128)(2,1)S(1)}, bf16[8,64,512]{2,1,0:T(8,128)(2,1)S(1)}, u32[]{:S(2)}, u32[]{:S(2)}) %collective-permute-start.4) | collective-permute-done | bytes 524320 | tf_op jit(solution)/shard_map/ppermute | solution.py:237
  123.2 4.7 %collective-permute-start.7 = (bf16[8,64,256]{2,1,0:T(8,128)(2,1)S(1)}, bf16[8,64,256]{2,1,0:T(8,128)(2,1)S(1)}, u32[]{:S(2)}, u32[]{:S(2)}) collective-permute-start(bf16[8,64,256]{2,1,0:T(8,128)(2,1)S(1)} %get-tuple-element.54), channel_id=1, source_target_pairs={{0,3},{1,0},{2,1},{3,2},{4,7},{5,4},{6,5},{7,6},{8,11},{9,8},{10,9... | collective-permute-start | bytes 786440 | tf_op jit(solution)/shard_map/ppermute | solution.py:237
  130.0 2.3 %collective-permute-start.15 = (bf16[8,64,256]{2,1,0:T(8,128)(2,1)S(1)}, bf16[8,64,256]{2,1,0:T(8,128)(2,1)S(1)}, u32[]{:S(2)}, u32[]{:S(2)}) collective-permute-start(bf16[8,64,256]{2,1,0:T(8,128)(2,1)S(1)} %get-tuple-element.68), channel_id=1, source_target_pairs={{0,12},{1,13},{2,14},{3,15},{4,0},{5,1},{6,2},{7,3},{8,4},{9,5},{1... | collective-permute-start | bytes 786440 | tf_op jit(solution)/shard_map/ppermute | solution.py:237
  134.3 2.1 %collective-permute-start.9 = (bf16[4,64,256]{2,1,0:T(8,128)(2,1)S(1)}, bf16[4,64,256]{2,1,0:T(8,128)(2,1)S(1)}, u32[]{:S(2)}, u32[]{:S(2)}) collective-permute-start(bf16[4,64,256]{2,1,0:T(8,128)(2,1)S(1)} %get-tuple-element.58), channel_id=1, source_target_pairs={{0,3},{1,0},{2,1},{3,2},{4,7},{5,4},{6,5},{7,6},{8,11},{9,8},{10,9... | collective-permute-start | bytes 393224 | tf_op jit(solution)/shard_map/ppermute | solution.py:237
  137.1 2.9 %collective-permute-start.17 = (bf16[4,64,256]{2,1,0:T(8,128)(2,1)S(1)}, bf16[4,64,256]{2,1,0:T(8,128)(2,1)S(1)}, u32[]{:S(2)}, u32[]{:S(2)}) collective-permute-start(bf16[4,64,256]{2,1,0:T(8,128)(2,1)S(1)} %get-tuple-element.72), channel_id=1, source_target_pairs={{0,12},{1,13},{2,14},{3,15},{4,0},{5,1},{6,2},{7,3},{8,4},{9,5},{1... | collective-permute-start | bytes 393224 | tf_op jit(solution)/shard_map/ppermute | solution.py:237
  140.0 2.9 %collective-permute-done.16.refs_8_ = bf16[4,64,256]{2,1,0:T(8,128)(2,1)S(1)} collective-permute-done((bf16[4,64,256]{2,1,0:T(8,128)(2,1)S(1)}, bf16[4,64,256]{2,1,0:T(8,128)(2,1)S(1)}, u32[]{:S(2)}, u32[]{:S(2)}) %collective-permute-start.16) | collective-permute-done | bytes 131104 | tf_op jit(solution)/shard_map/ppermute | solution.py:237
  142.9 2.5 %expand.1 = bf16[2048,512]{1,0:T(8,128)(2,1)} custom-call(f32[2048,512]{1,0:T(8,128)S(1)} %copy-done.1, bf16[2048,64]{1,0:T(8,128)(2,1)S(1)} %get-tuple-element.42.basis_ref, f32[4,64,512]{2,1,0:T(8,128)S(1)} %get-tuple-element.52.refs_0_, bf16[8,64,256]{2,1,0:T(8,128)(2,1)S(1)} %collective-permute-done.6.up_ref.refs_1_, ...), custom_call_target="tpu_custom_call" | custom-call | flops 134217728 | bytes 7340032 | tf_op jit(solution)/shard_map/expand/pallas_call | solution.py:381
  (51 shorter events, 12.7 us)
Async XLA Ops:
  6.5 8.9 %copy-start.3 = (s32[128]{0:T(128)S(1)}, s32[128]{0:T(128)}, u32[]{:S(2)}) copy-start(s32[128]{0:T(128)} %rows_ref.1) | copy-start | bytes 1540
  6.5 60.4 %all-gather.2.cloned.1.call-start = ((), (), s32[]{:S(2)}) async-start(), calls=%async_computation.1 | async-start | bytes 4718592 | tf_op jit(solution)/shard_map/all_gather | solution.py:408
  9.9 33.4 %collective-permute-start = (bf16[1024,512]{1,0:T(8,128)(2,1)}, bf16[1024,512]{1,0:T(8,128)(2,1)S(1)}, u32[]{:S(2)}, u32[]{:S(2)}) collective-permute-start(bf16[1024,512]{1,0:T(8,128)(2,1)} %get-tuple-element.39), channel_id=1, source_target_pairs={{0,1},{1,2},{2,3},{3,4},{4,5},{5,6},{6,7},{7,8},{8,9},{9,10},{10,1... | collective-permute-start | bytes 3145736 | tf_op jit(solution)/shard_map/ppermute | solution.py:419
  13.8 38.1 %collective-permute-start.1 = (bf16[1024,512]{1,0:T(8,128)(2,1)}, bf16[1024,512]{1,0:T(8,128)(2,1)}, u32[]{:S(2)}, u32[]{:S(2)}) collective-permute-start(bf16[1024,512]{1,0:T(8,128)(2,1)} %get-tuple-element.40), channel_id=1, source_target_pairs={{1,0},{2,1},{3,2},{4,3},{5,4},{6,5},{7,6},{8,7},{9,8},{10,9},{11,1... | collective-permute-start | bytes 3145736 | tf_op jit(solution)/shard_map/ppermute | solution.py:420
  18.5 33.4 %copy-start.2 = (bf16[2048,512]{1,0:T(8,128)(2,1)S(1)}, bf16[2048,512]{1,0:T(8,128)(2,1)}, u32[]{:S(2)}) copy-start(bf16[2048,512]{1,0:T(8,128)(2,1)} %modes_ref.3) | copy-start | bytes 6291460
  18.5 33.4 %copy-start.9 = (bf16[64,2048]{1,0:T(8,128)(2,1)S(1)}, bf16[64,2048]{1,0:T(8,128)(2,1)}, u32[]{:S(2)}) copy-start(bf16[64,2048]{1,0:T(8,128)(2,1)} %basis_ref.3) | copy-start | bytes 786436
  18.5 50.4 %all-to-all-start = ((bf16[16,528,128]{2,1,0:T(8,128)(2,1)}), bf16[16,528,128]{2,1,0:T(8,128)(2,1)}, u32[]{:S(2)}, u32[]{:S(2)}) async-start(bf16[16,528,128]{2,1,0:T(8,128)(2,1)} %dispatch.1), calls=%async_computation | async-start | bytes 4325376 | tf_op jit(solution)/shard_map/all_to_all | solution.py:415
  78.7 30.1 %collective-permute-start.2 = (bf16[16,64,512]{2,1,0:T(8,128)(2,1)S(1)}, bf16[16,64,512]{2,1,0:T(8,128)(2,1)S(1)}, u32[]{:S(2)}, u32[]{:S(2)}) collective-permute-start(bf16[16,64,512]{2,1,0:T(8,128)(2,1)S(1)} %get-tuple-element.46), channel_id=1, source_target_pairs={{0,4},{1,5},{2,6},{3,7},{4,8},{5,9},{6,10},{7,11},{8,12},{9,13},{1... | collective-permute-start | bytes 3145736 | tf_op jit(solution)/shard_map/ppermute | solution.py:237
  84.9 23.9 %collective-permute-start.3 = (bf16[16,64,512]{2,1,0:T(8,128)(2,1)S(1)}, bf16[16,64,512]{2,1,0:T(8,128)(2,1)S(1)}, u32[]{:S(2)}, u32[]{:S(2)}) collective-permute-start(bf16[16,64,512]{2,1,0:T(8,128)(2,1)S(1)} %get-tuple-element.47), channel_id=1, source_target_pairs={{0,12},{1,13},{2,14},{3,15},{4,0},{5,1},{6,2},{7,3},{8,4},{9,5},{1... | collective-permute-start | bytes 3145736 | tf_op jit(solution)/shard_map/ppermute | solution.py:237
  86.6 25.7 %collective-permute-start.10 = (bf16[16,64,512]{2,1,0:T(8,128)(2,1)S(1)}, bf16[16,64,512]{2,1,0:T(8,128)(2,1)S(1)}, u32[]{:S(2)}, u32[]{:S(2)}) collective-permute-start(bf16[16,64,512]{2,1,0:T(8,128)(2,1)S(1)} %get-tuple-element.60), channel_id=1, source_target_pairs={{0,1},{1,2},{2,3},{3,0},{4,5},{5,6},{6,7},{7,4},{8,9},{9,10},{10,1... | collective-permute-start | bytes 3145736 | tf_op jit(solution)/shard_map/ppermute | solution.py:237
  91.5 20.9 %collective-permute-start.11 = (bf16[16,64,512]{2,1,0:T(8,128)(2,1)S(1)}, bf16[16,64,512]{2,1,0:T(8,128)(2,1)S(1)}, u32[]{:S(2)}, u32[]{:S(2)}) collective-permute-start(bf16[16,64,512]{2,1,0:T(8,128)(2,1)S(1)} %get-tuple-element.61), channel_id=1, source_target_pairs={{0,3},{1,0},{2,1},{3,2},{4,7},{5,4},{6,5},{7,6},{8,11},{9,8},{10,9... | collective-permute-start | bytes 3145736 | tf_op jit(solution)/shard_map/ppermute | solution.py:237
  109.0 13.4 %collective-permute-start.4 = (bf16[8,64,512]{2,1,0:T(8,128)(2,1)S(1)}, bf16[8,64,512]{2,1,0:T(8,128)(2,1)S(1)}, u32[]{:S(2)}, u32[]{:S(2)}) collective-permute-start(bf16[8,64,512]{2,1,0:T(8,128)(2,1)S(1)} %get-tuple-element.50), channel_id=1, source_target_pairs={{0,4},{1,5},{2,6},{3,7},{4,8},{5,9},{6,10},{7,11},{8,12},{9,13},{1... | collective-permute-start | bytes 1572872 | tf_op jit(solution)/shard_map/ppermute | solution.py:237
  110.2 12.2 %collective-permute-start.5 = (bf16[8,64,512]{2,1,0:T(8,128)(2,1)S(1)}, bf16[8,64,512]{2,1,0:T(8,128)(2,1)S(1)}, u32[]{:S(2)}, u32[]{:S(2)}) collective-permute-start(bf16[8,64,512]{2,1,0:T(8,128)(2,1)S(1)} %get-tuple-element.51), channel_id=1, source_target_pairs={{0,12},{1,13},{2,14},{3,15},{4,0},{5,1},{6,2},{7,3},{8,4},{9,5},{1... | collective-permute-start | bytes 1572872 | tf_op jit(solution)/shard_map/ppermute | solution.py:237
  112.5 16.1 %collective-permute-start.12 = (bf16[8,64,512]{2,1,0:T(8,128)(2,1)S(1)}, bf16[8,64,512]{2,1,0:T(8,128)(2,1)S(1)}, u32[]{:S(2)}, u32[]{:S(2)}) collective-permute-start(bf16[8,64,512]{2,1,0:T(8,128)(2,1)S(1)} %get-tuple-element.64), channel_id=1, source_target_pairs={{0,1},{1,2},{2,3},{3,0},{4,5},{5,6},{6,7},{7,4},{8,9},{9,10},{10,1... | collective-permute-start | bytes 1572872 | tf_op jit(solution)/shard_map/ppermute | solution.py:237
  114.8 13.9 %collective-permute-start.13 = (bf16[8,64,512]{2,1,0:T(8,128)(2,1)S(1)}, bf16[8,64,512]{2,1,0:T(8,128)(2,1)S(1)}, u32[]{:S(2)}, u32[]{:S(2)}) collective-permute-start(bf16[8,64,512]{2,1,0:T(8,128)(2,1)S(1)} %get-tuple-element.65), channel_id=1, source_target_pairs={{0,3},{1,0},{2,1},{3,2},{4,7},{5,4},{6,5},{7,6},{8,11},{9,8},{10,9... | collective-permute-start | bytes 1572872 | tf_op jit(solution)/shard_map/ppermute | solution.py:237
  122.7 10.3 %collective-permute-start.6 = (bf16[8,64,256]{2,1,0:T(8,128)(2,1)S(1)}, bf16[8,64,256]{2,1,0:T(8,128)(2,1)S(1)}, u32[]{:S(2)}, u32[]{:S(2)}) collective-permute-start(bf16[8,64,256]{2,1,0:T(8,128)(2,1)S(1)} %get-tuple-element.53), channel_id=1, source_target_pairs={{0,1},{1,2},{2,3},{3,0},{4,5},{5,6},{6,7},{7,4},{8,9},{9,10},{10,1... | collective-permute-start | bytes 786440 | tf_op jit(solution)/shard_map/ppermute | solution.py:237
  123.2 9.9 %collective-permute-start.7 = (bf16[8,64,256]{2,1,0:T(8,128)(2,1)S(1)}, bf16[8,64,256]{2,1,0:T(8,128)(2,1)S(1)}, u32[]{:S(2)}, u32[]{:S(2)}) collective-permute-start(bf16[8,64,256]{2,1,0:T(8,128)(2,1)S(1)} %get-tuple-element.54), channel_id=1, source_target_pairs={{0,3},{1,0},{2,1},{3,2},{4,7},{5,4},{6,5},{7,6},{8,11},{9,8},{10,9... | collective-permute-start | bytes 786440 | tf_op jit(solution)/shard_map/ppermute | solution.py:237
  128.6 14.3 %copy-start.1 = (f32[2048,512]{1,0:T(8,128)S(1)}, f32[2048,512]{1,0:T(8,128)}, u32[]{:S(2)}) copy-start(f32[2048,512]{1,0:T(8,128)} %copy-done) | copy-start | bytes 12582916
  128.9 7.7 %collective-permute-start.14 = (bf16[8,64,256]{2,1,0:T(8,128)(2,1)S(1)}, bf16[8,64,256]{2,1,0:T(8,128)(2,1)S(1)}, u32[]{:S(2)}, u32[]{:S(2)}) collective-permute-start(bf16[8,64,256]{2,1,0:T(8,128)(2,1)S(1)} %get-tuple-element.67), channel_id=1, source_target_pairs={{0,4},{1,5},{2,6},{3,7},{4,8},{5,9},{6,10},{7,11},{8,12},{9,13},{1... | collective-permute-start | bytes 786440 | tf_op jit(solution)/shard_map/ppermute | solution.py:237
  130.0 6.6 %collective-permute-start.15 = (bf16[8,64,256]{2,1,0:T(8,128)(2,1)S(1)}, bf16[8,64,256]{2,1,0:T(8,128)(2,1)S(1)}, u32[]{:S(2)}, u32[]{:S(2)}) collective-permute-start(bf16[8,64,256]{2,1,0:T(8,128)(2,1)S(1)} %get-tuple-element.68), channel_id=1, source_target_pairs={{0,12},{1,13},{2,14},{3,15},{4,0},{5,1},{6,2},{7,3},{8,4},{9,5},{1... | collective-permute-start | bytes 786440 | tf_op jit(solution)/shard_map/ppermute | solution.py:237
  133.1 6.9 %collective-permute-start.8 = (bf16[4,64,256]{2,1,0:T(8,128)(2,1)S(1)}, bf16[4,64,256]{2,1,0:T(8,128)(2,1)S(1)}, u32[]{:S(2)}, u32[]{:S(2)}) collective-permute-start(bf16[4,64,256]{2,1,0:T(8,128)(2,1)S(1)} %get-tuple-element.57), channel_id=1, source_target_pairs={{0,1},{1,2},{2,3},{3,0},{4,5},{5,6},{6,7},{7,4},{8,9},{9,10},{10,1... | collective-permute-start | bytes 393224 | tf_op jit(solution)/shard_map/ppermute | solution.py:237
  134.3 5.7 %collective-permute-start.9 = (bf16[4,64,256]{2,1,0:T(8,128)(2,1)S(1)}, bf16[4,64,256]{2,1,0:T(8,128)(2,1)S(1)}, u32[]{:S(2)}, u32[]{:S(2)}) collective-permute-start(bf16[4,64,256]{2,1,0:T(8,128)(2,1)S(1)} %get-tuple-element.58), channel_id=1, source_target_pairs={{0,3},{1,0},{2,1},{3,2},{4,7},{5,4},{6,5},{7,6},{8,11},{9,8},{10,9... | collective-permute-start | bytes 393224 | tf_op jit(solution)/shard_map/ppermute | solution.py:237
  136.6 6.2 %collective-permute-start.16 = (bf16[4,64,256]{2,1,0:T(8,128)(2,1)S(1)}, bf16[4,64,256]{2,1,0:T(8,128)(2,1)S(1)}, u32[]{:S(2)}, u32[]{:S(2)}) collective-permute-start(bf16[4,64,256]{2,1,0:T(8,128)(2,1)S(1)} %get-tuple-element.71), channel_id=1, source_target_pairs={{0,4},{1,5},{2,6},{3,7},{4,8},{5,9},{6,10},{7,11},{8,12},{9,13},{1... | collective-permute-start | bytes 393224 | tf_op jit(solution)/shard_map/ppermute | solution.py:237
  137.1 5.8 %collective-permute-start.17 = (bf16[4,64,256]{2,1,0:T(8,128)(2,1)S(1)}, bf16[4,64,256]{2,1,0:T(8,128)(2,1)S(1)}, u32[]{:S(2)}, u32[]{:S(2)}) collective-permute-start(bf16[4,64,256]{2,1,0:T(8,128)(2,1)S(1)} %get-tuple-element.72), channel_id=1, source_target_pairs={{0,12},{1,13},{2,14},{3,15},{4,0},{5,1},{6,2},{7,3},{8,4},{9,5},{1... | collective-permute-start | bytes 393224 | tf_op jit(solution)/shard_map/ppermute | solution.py:237
  (7 other events, 34.3 us)
Sparse Core Ops, SparseCore 0:
  10.0 34.5 all-gather.1

commit v9 on v7

--- a/solution.py
+++ b/solution.py
@@ -118,10 +118,10 @@
 
 
 UNROLL = 32
-X_ROWS = 5
-
-
-def far_kernel(slots, rows, comp_ref, sent_ref, *refs):
+X_ROWS = 4
+
+
+def far_kernel(slots, rows, here_ref, comp_ref, sent_ref, *refs):
     outs, (acc_ref, meta_ref, smem_ref, list_ref, sem) = (refs[:5], refs[5:10]), refs[10:]
     sources = sent_ref.shape[0]
     group_rows = acc_ref.shape[0]
@@ -185,7 +185,7 @@
         last_ref[...] = acc_ref[last + half : last + part]
 
 
-def far_field(comp, sent, slots, rows, group_rows):
+def far_field(here, comp, sent, slots, rows, group_rows):
     _, rank, cols = comp.shape
     sources = sent.shape[0]
     x_part = X_ROWS * 4
@@ -202,7 +202,7 @@
     ]
     parts = pl.pallas_call(
         functools.partial(far_kernel, slots, rows),
-        in_specs=[whole()] * 2,
+        in_specs=[whole(pl.ANY)] + [whole()] * 2,
         out_specs=[whole()] * len(kinds),
         out_shape=[jax.ShapeDtypeStruct((n, rank, cols), kind) for n, kind in kinds],
         scratch_shapes=[
@@ -217,7 +217,7 @@
             flops=2 * 128 * rank * rank * cols * 8, bytes_accessed=24 * MIB, transcendentals=0
         ),
         name="far_field",
-    )(comp, sent)
+    )(here, comp, sent)
     return parts[:5], parts[5:]
 
 
@@ -349,6 +349,21 @@
         ),
         name="near_field",
     )(near_blocks, before, modes, after, row_basis)
+
+
+def arrival_kernel(before_ref, after_ref, out_ref):
+    out_ref[...] = jnp.zeros_like(out_ref)
+
+
+def arrival(before, after):
+    return pl.pallas_call(
+        arrival_kernel,
+        in_specs=[whole(pl.ANY)] * 2,
+        out_specs=whole(),
+        out_shape=jax.ShapeDtypeStruct((8, 128), jnp.float32),
+        cost_estimate=pl.CostEstimate(flops=40 << 30, bytes_accessed=16 * MIB, transcendentals=0),
+        name="arrival",
+    )(before, after)
 
 
 EXPAND = 2
@@ -414,13 +429,12 @@
     )
     sent = lax.all_to_all(sent, "ccol", split_axis=0, concat_axis=0, tiled=True)
 
-    low, high, sent = lax.optimization_barrier((low, high, sent))
     up = [(i, i + 1) for i in range(devices - 1)]
     down = [(j, i) for i, j in up]
     before = lax.ppermute(high, ("crow", "ccol"), up)
     after = lax.ppermute(low, ("crow", "ccol"), down)
-
-    left, right = far_field(gathered, sent, slots, lines, col_devices * cluster_count)
+    here = arrival(before, after)
+    left, right = far_field(here, gathered, sent, slots, lines, col_devices * cluster_count)
     for along_x in (True, False):
         left_up, left_down = both_ways(left[0], left[1], along_x)
         right_up, right_down = both_ways(right[0], right[1], not along_x)

time: 153 us -> 157 us (1.026); the launches traced: 151 us -> 156 us
  blocking collectives: 37.1 us -> 0 us
  waiting for transfers between devices: 32.6 us -> 57.6 us
  starting transfers between devices: 36.2 us -> 50 us
  local copies, waits for them, and re-layouts: 3.95 us -> 7.81 us
    all_to_all x1 -> x0, blocking collectives: 37.1 us -> none  [per_device(): sent = lax.all_to_all(sent, 'ccol', split_axis=0, concat_axis=0, tiled=True)]
    all_to_all x0 -> x1, waiting for transfers between devices: none -> 15.5 us  [per_device(): sent = lax.all_to_all(sent, 'ccol', split_axis=0, concat_axis=0, tiled=True)]
    ppermute x8, starting transfers between devices: 3.99 us -> 15.8 us  [both_ways(): lax.ppermute(up, 'ccol', ring(along_x, 1))]
    ppermute x1, waiting for transfers between devices: 4.65 us -> 16.4 us  [per_device(): before = lax.ppermute(high, ('crow', 'ccol'), up)]
    all_to_all x0 -> x1, starting transfers between devices: none -> 8.58 us  [per_device(): sent = lax.all_to_all(sent, 'ccol', split_axis=0, concat_axis=0, tiled=True)]
    ppermute x8, starting transfers between devices: 27.3 us -> 20.3 us  [both_ways(): lax.ppermute(down, 'ccol', ring(along_x, -1))]
    ppermute x8, waiting for transfers between devices: 10.4 us -> 5.7 us  [both_ways(): lax.ppermute(down, 'ccol', ring(along_x, -1))]
    ppermute x1, waiting for transfers between devices: 4.12 us -> 8.31 us  [per_device(): after = lax.ppermute(low, ('crow', 'ccol'), down)]
  transfers between devices with their start and end apart: 19 -> 20, of which waited for: 6 -> 13; matrix products, arithmetic and copies ran while one was open for 0% -> 0% of each run, Pallas kernels for 14% -> 7%
where the time goes in v9:
time: 157 us; the launch traced here: 156 us
  waiting for transfers between devices  57.6 us (37%)
  starting transfers between devices  50 us (32%)
  Pallas kernels  27.4 us (17%)
  between operations  13.6 us (9%)
  local copies, waits for them, and re-layouts  7.81 us (5%)
    ppermute x8, starting transfers between devices, both_ways(): lax.ppermute(down, 'ccol', ring(along_x, -1))  20.3 us
    ppermute x1, waiting for transfers between devices, per_device(): before = lax.ppermute(high, ('crow', 'ccol'), up)  16.4 us
    ppermute x8, starting transfers between devices, both_ways(): lax.ppermute(up, 'ccol', ring(along_x, 1))  15.8 us
    all_to_all x1, waiting for transfers between devices, per_device(): sent = lax.all_to_all(sent, 'ccol', split_axis=0, concat_axis=0, tiled=True)  15.5 us
    ppermute x8, waiting for transfers between devices, both_ways(): lax.ppermute(up, 'ccol', ring(along_x, 1))  11.7 us
    pallas_call x1, Pallas kernels, far_field(): pl.pallas_call(functools.partial(far_kernel, slots, rows), in_specs=[whol...  10.2 us
    all_to_all x1, starting transfers between devices, per_device(): sent = lax.all_to_all(sent, 'ccol', split_axis=0, concat_axis=0, tiled=True)  8.58 us
    ppermute x1, waiting for transfers between devices, per_device(): after = lax.ppermute(low, ('crow', 'ccol'), down)  8.31 us
  transfers between devices with their start and end apart: 20, of which 13 were waited for; matrix products, arithmetic and copies ran while one was open for 0% of the time, Pallas kernels for 7%

profile of v9, /device:TPU:0, one launch (start us, length us, event | category | flops | bytes accessed | tf_op | source)
XLA Modules:
  0.0 156.4 jit_solution(14688566919823069694)
XLA Ops:
  6.6 3.3 %compress.1 = (bf16[8,64,512]{2,1,0:T(8,128)(2,1)}, bf16[1024,512]{1,0:T(8,128)(2,1)}, bf16[1024,512]{1,0:T(8,128)(2,1)}) custom-call(bf16[64,2048]{1,0:T(8,128)(2,1)} %basis_ref.2, bf16[2048,512]{1,0:T(8,128)(2,1)} %modes_ref.3), custom_call_target="tpu_custom_call" | custom-call | flops 134217728 | bytes 3145728 | tf_op jit(solution)/shard_map/compress/pallas_call | solution.py:49
  9.9 4.0 %collective-permute-start = (bf16[1024,512]{1,0:T(8,128)(2,1)}, bf16[1024,512]{1,0:T(8,128)(2,1)S(1)}, u32[]{:S(2)}, u32[]{:S(2)}) collective-permute-start(bf16[1024,512]{1,0:T(8,128)(2,1)} %get-tuple-element.42), channel_id=1, source_target_pairs={{0,1},{1,2},{2,3},{3,4},{4,5},{5,6},{6,7},{7,8},{8,9},{9,10},{10,1... | collective-permute-start | bytes 3145736 | tf_op jit(solution)/shard_map/ppermute | solution.py:434
  15.4 3.1 %dispatch.1 = bf16[16,528,128]{2,1,0:T(8,128)(2,1)} custom-call(s32[128]{0:T(128)S(1)} %copy-done.3, s32[128]{0:T(128)S(1)} %bitcast.4, s32[128]{0:T(128)S(1)} %copy-done.5, bf16[128,32,128]{2,1,0:T(8,128)(2,1)S(1)} %bitcast.3), custom_call_target="tpu_custom_call" | custom-call | flops 4194304 | bytes 3145728 | tf_op jit(solution)/shard_map/dispatch/pallas_call | solution.py:108
  18.5 8.6 %all-to-all-start = ((bf16[16,528,128]{2,1,0:T(8,128)(2,1)}), bf16[16,528,128]{2,1,0:T(8,128)(2,1)}, u32[]{:S(2)}, u32[]{:S(2)}) async-start(bf16[16,528,128]{2,1,0:T(8,128)(2,1)} %dispatch.1), calls=%async_computation | async-start | bytes 4325376 | tf_op jit(solution)/shard_map/all_to_all | solution.py:430
  27.1 16.4 %collective-permute-done.before_ref = bf16[1024,512]{1,0:T(8,128)(2,1)S(1)} collective-permute-done((bf16[1024,512]{1,0:T(8,128)(2,1)}, bf16[1024,512]{1,0:T(8,128)(2,1)S(1)}, u32[]{:S(2)}, u32[]{:S(2)}) %collective-permute-start) | collective-permute-done | bytes 1048608 | tf_op jit(solution)/shard_map/ppermute | solution.py:434
  43.5 8.3 %collective-permute-done.1.after_ref = bf16[1024,512]{1,0:T(8,128)(2,1)S(1)} collective-permute-done((bf16[1024,512]{1,0:T(8,128)(2,1)}, bf16[1024,512]{1,0:T(8,128)(2,1)S(1)}, u32[]{:S(2)}, u32[]{:S(2)}) %collective-permute-start.1) | collective-permute-done | bytes 1048608 | tf_op jit(solution)/shard_map/ppermute | solution.py:435
  53.4 15.5 %all-to-all-done.sent_ref = bf16[16,528,128]{2,1,0:T(8,128)(2,1)} async-done(((bf16[16,528,128]{2,1,0:T(8,128)(2,1)}), bf16[16,528,128]{2,1,0:T(8,128)(2,1)}, u32[]{:S(2)}, u32[]{:S(2)}) %all-to-all-start) | async-done | bytes 2162720 | tf_op jit(solution)/shard_map/all_to_all | solution.py:430
  69.5 10.2 %far_field.1 = (bf16[16,64,512]{2,1,0:T(8,128)(2,1)}, bf16[16,64,512]{2,1,0:T(8,128)(2,1)}, f32[8,64,512]{2,1,0:T(8,128)S(1)}, f32[8,64,512]{2,1,0:T(8,128)S(1)}...) custom-call(f32[8,128]{1,0:T(8,128)S(1)} %copy-done.12, ...), custom_call_target="tpu_custom_call" | custom-call | flops 4294967296 | bytes 25165824 | tf_op jit(solution)/shard_map/far_field/pallas_call | solution.py:203
  80.7 2.3 %collective-permute-start.10 = (bf16[16,64,512]{2,1,0:T(8,128)(2,1)}, bf16[16,64,512]{2,1,0:T(8,128)(2,1)S(1)}, u32[]{:S(2)}, u32[]{:S(2)}) collective-permute-start(bf16[16,64,512]{2,1,0:T(8,128)(2,1)} %get-tuple-element.66), channel_id=1, source_target_pairs={{0,1},{1,2},{2,3},{3,0},{4,5},{5,6},{6,7},{7,4},{8,9},{9,10},{10,1... | collective-permute-start | bytes 3145736 | tf_op jit(solution)/shard_map/ppermute | solution.py:237
  83.0 2.1 %collective-permute-start.11 = (bf16[16,64,512]{2,1,0:T(8,128)(2,1)}, bf16[16,64,512]{2,1,0:T(8,128)(2,1)S(1)}, u32[]{:S(2)}, u32[]{:S(2)}) collective-permute-start(bf16[16,64,512]{2,1,0:T(8,128)(2,1)} %get-tuple-element.67), channel_id=1, source_target_pairs={{0,3},{1,0},{2,1},{3,2},{4,7},{5,4},{6,5},{7,6},{8,11},{9,8},{10,9... | collective-permute-start | bytes 3145736 | tf_op jit(solution)/shard_map/ppermute | solution.py:237
  85.1 7.6 %collective-permute-start.3 = (bf16[16,64,512]{2,1,0:T(8,128)(2,1)}, bf16[16,64,512]{2,1,0:T(8,128)(2,1)S(1)}, u32[]{:S(2)}, u32[]{:S(2)}) collective-permute-start(bf16[16,64,512]{2,1,0:T(8,128)(2,1)} %get-tuple-element.51), channel_id=1, source_target_pairs={{0,12},{1,13},{2,14},{3,15},{4,0},{5,1},{6,2},{7,3},{8,4},{9,5},{1... | collective-permute-start | bytes 3145736 | tf_op jit(solution)/shard_map/ppermute | solution.py:237
  94.0 3.7 %copy-done.6 = bf16[2048,2304]{1,0:T(8,128)(2,1)S(1)} copy-done((bf16[2048,2304]{1,0:T(8,128)(2,1)S(1)}, bf16[2048,2304]{1,0:T(8,128)(2,1)}, u32[]{:S(2)}) %copy-start.6) | copy-done | bytes 9437208
  98.9 6.8 %near_field.1 = (f32[2048,512]{1,0:T(8,128)S(1)}, bf16[2048,64]{1,0:T(8,128)(2,1)S(1)}) custom-call(bf16[2048,2304]{1,0:T(8,128)(2,1)S(1)} %copy-done.6, bf16[1024,512]{1,0:T(8,128)(2,1)S(1)} %copy-done.8, bf16[2048,512]{1,0:T(8,128)(2,1)S(1)} %copy-done, bf16[1024,512]{1,0:T(8,128)(2,1)S(1)} %copy-done.10, bf16[64,2048]{1,0:T(8,128)(2,1)S(1)} %copy-done.11), custom_call_target="tpu_custom_call" | custom-call | flops 4831838208 | bytes 2097152 | tf_op jit(solution)/shard_map/near_field/pallas_call | solution.py:331
  105.7 2.0 %collective-permute-done.10.up_ref.up_in_ref = bf16[16,64,512]{2,1,0:T(8,128)(2,1)S(1)} collective-permute-done((bf16[16,64,512]{2,1,0:T(8,128)(2,1)}, bf16[16,64,512]{2,1,0:T(8,128)(2,1)S(1)}, u32[]{:S(2)}, u32[]{:S(2)}) %collective-permute-start.10) | collective-permute-done | bytes 1048608 | tf_op jit(solution)/shard_map/ppermute | solution.py:237
  112.9 3.3 %collective-permute-done.3.down_ref.down_in_ref = bf16[16,64,512]{2,1,0:T(8,128)(2,1)S(1)} collective-permute-done((bf16[16,64,512]{2,1,0:T(8,128)(2,1)}, bf16[16,64,512]{2,1,0:T(8,128)(2,1)S(1)}, u32[]{:S(2)}, u32[]{:S(2)}) %collective-permute-start.3) | collective-permute-done | bytes 1048608 | tf_op jit(solution)/shard_map/ppermute | solution.py:237
  117.4 2.7 %collective-permute-start.4 = (bf16[8,64,512]{2,1,0:T(8,128)(2,1)S(1)}, bf16[8,64,512]{2,1,0:T(8,128)(2,1)S(1)}, u32[]{:S(2)}, u32[]{:S(2)}) collective-permute-start(bf16[8,64,512]{2,1,0:T(8,128)(2,1)S(1)} %get-tuple-element.56), channel_id=1, source_target_pairs={{0,4},{1,5},{2,6},{3,7},{4,8},{5,9},{6,10},{7,11},{8,12},{9,13},{1... | collective-permute-start | bytes 1572872 | tf_op jit(solution)/shard_map/ppermute | solution.py:237
  120.7 2.9 %collective-permute-done.12.up_rest_ref = bf16[8,64,512]{2,1,0:T(8,128)(2,1)S(1)} collective-permute-done((bf16[8,64,512]{2,1,0:T(8,128)(2,1)S(1)}, bf16[8,64,512]{2,1,0:T(8,128)(2,1)S(1)}, u32[]{:S(2)}, u32[]{:S(2)}) %collective-permute-start.12) | collective-permute-done | bytes 524320 | tf_op jit(solution)/shard_map/ppermute | solution.py:237
  124.0 6.2 %collective-permute-start.14 = (bf16[8,64,256]{2,1,0:T(8,128)(2,1)S(1)}, bf16[8,64,256]{2,1,0:T(8,128)(2,1)S(1)}, u32[]{:S(2)}, u32[]{:S(2)}) collective-permute-start(bf16[8,64,256]{2,1,0:T(8,128)(2,1)S(1)} %get-tuple-element.73), channel_id=1, source_target_pairs={{0,4},{1,5},{2,6},{3,7},{4,8},{5,9},{6,10},{7,11},{8,12},{9,13},{1... | collective-permute-start | bytes 786440 | tf_op jit(solution)/shard_map/ppermute | solution.py:237
  130.2 2.3 %collective-permute-done.4.up_rest_ref = bf16[8,64,512]{2,1,0:T(8,128)(2,1)S(1)} collective-permute-done((bf16[8,64,512]{2,1,0:T(8,128)(2,1)S(1)}, bf16[8,64,512]{2,1,0:T(8,128)(2,1)S(1)}, u32[]{:S(2)}, u32[]{:S(2)}) %collective-permute-start.4) | collective-permute-done | bytes 524320 | tf_op jit(solution)/shard_map/ppermute | solution.py:237
  133.1 3.2 %collective-permute-start.7 = (bf16[8,64,256]{2,1,0:T(8,128)(2,1)S(1)}, bf16[8,64,256]{2,1,0:T(8,128)(2,1)S(1)}, u32[]{:S(2)}, u32[]{:S(2)}) collective-permute-start(bf16[8,64,256]{2,1,0:T(8,128)(2,1)S(1)} %get-tuple-element.60), channel_id=1, source_target_pairs={{0,3},{1,0},{2,1},{3,2},{4,7},{5,4},{6,5},{7,6},{8,11},{9,8},{10,9... | collective-permute-start | bytes 786440 | tf_op jit(solution)/shard_map/ppermute | solution.py:237
  137.4 2.9 %collective-permute-start.17 = (bf16[4,64,256]{2,1,0:T(8,128)(2,1)S(1)}, bf16[4,64,256]{2,1,0:T(8,128)(2,1)S(1)}, u32[]{:S(2)}, u32[]{:S(2)}) collective-permute-start(bf16[4,64,256]{2,1,0:T(8,128)(2,1)S(1)} %get-tuple-element.78), channel_id=1, source_target_pairs={{0,12},{1,13},{2,14},{3,15},{4,0},{5,1},{6,2},{7,3},{8,4},{9,5},{1... | collective-permute-start | bytes 393224 | tf_op jit(solution)/shard_map/ppermute | solution.py:237
  141.7 2.5 %collective-permute-start.9 = (bf16[4,64,256]{2,1,0:T(8,128)(2,1)S(1)}, bf16[4,64,256]{2,1,0:T(8,128)(2,1)S(1)}, u32[]{:S(2)}, u32[]{:S(2)}) collective-permute-start(bf16[4,64,256]{2,1,0:T(8,128)(2,1)S(1)} %get-tuple-element.64), channel_id=1, source_target_pairs={{0,3},{1,0},{2,1},{3,2},{4,7},{5,4},{6,5},{7,6},{8,11},{9,8},{10,9... | collective-permute-start | bytes 393224 | tf_op jit(solution)/shard_map/ppermute | solution.py:237
  144.1 2.9 %collective-permute-done.8.refs_3_ = bf16[4,64,256]{2,1,0:T(8,128)(2,1)S(1)} collective-permute-done((bf16[4,64,256]{2,1,0:T(8,128)(2,1)S(1)}, bf16[4,64,256]{2,1,0:T(8,128)(2,1)S(1)}, u32[]{:S(2)}, u32[]{:S(2)}) %collective-permute-start.8) | collective-permute-done | bytes 131104 | tf_op jit(solution)/shard_map/ppermute | solution.py:237
  147.0 2.5 %expand.1 = bf16[2048,512]{1,0:T(8,128)(2,1)} custom-call(f32[2048,512]{1,0:T(8,128)S(1)} %get-tuple-element.48.near_ref, bf16[2048,64]{1,0:T(8,128)(2,1)S(1)} %get-tuple-element.49.basis_ref, f32[4,64,512]{2,1,0:T(8,128)S(1)} %get-tuple-element.58.refs_0_, bf16[8,64,256]{2,1,0:T(8,128)(2,1)S(1)} %collective-permute-done.6.up_ref.refs_1_, ...), custom_call_target="tpu_custom_call" | custom-call | flops 134217728 | bytes 7340032 | tf_op jit(solution)/shard_map/expand/pallas_call | solution.py:396
  (58 shorter events, 17.8 us)
Async XLA Ops:
  6.5 62.3 %all-gather.2.cloned.1.call-start = ((), (), s32[]{:S(2)}) async-start(), calls=%async_computation.1 | async-start | bytes 4718592 | tf_op jit(solution)/shard_map/all_gather | solution.py:423
  9.9 33.6 %collective-permute-start = (bf16[1024,512]{1,0:T(8,128)(2,1)}, bf16[1024,512]{1,0:T(8,128)(2,1)S(1)}, u32[]{:S(2)}, u32[]{:S(2)}) collective-permute-start(bf16[1024,512]{1,0:T(8,128)(2,1)} %get-tuple-element.42), channel_id=1, source_target_pairs={{0,1},{1,2},{2,3},{3,4},{4,5},{5,6},{6,7},{7,8},{8,9},{9,10},{10,1... | collective-permute-start | bytes 3145736 | tf_op jit(solution)/shard_map/ppermute | solution.py:434
  13.9 38.0 %collective-permute-start.1 = (bf16[1024,512]{1,0:T(8,128)(2,1)}, bf16[1024,512]{1,0:T(8,128)(2,1)S(1)}, u32[]{:S(2)}, u32[]{:S(2)}) collective-permute-start(bf16[1024,512]{1,0:T(8,128)(2,1)} %get-tuple-element.43), channel_id=1, source_target_pairs={{1,0},{2,1},{3,2},{4,3},{5,4},{6,5},{7,6},{8,7},{9,8},{10,9},{11,1... | collective-permute-start | bytes 3145736 | tf_op jit(solution)/shard_map/ppermute | solution.py:435
  18.5 50.4 %all-to-all-start = ((bf16[16,528,128]{2,1,0:T(8,128)(2,1)}), bf16[16,528,128]{2,1,0:T(8,128)(2,1)}, u32[]{:S(2)}, u32[]{:S(2)}) async-start(bf16[16,528,128]{2,1,0:T(8,128)(2,1)} %dispatch.1), calls=%async_computation | async-start | bytes 4325376 | tf_op jit(solution)/shard_map/all_to_all | solution.py:430
  53.4 40.6 %copy-start = (bf16[2048,512]{1,0:T(8,128)(2,1)S(1)}, bf16[2048,512]{1,0:T(8,128)(2,1)}, u32[]{:S(2)}) copy-start(bf16[2048,512]{1,0:T(8,128)(2,1)} %modes_ref.3) | copy-start | bytes 6291460
  53.4 40.6 %copy-start.11 = (bf16[64,2048]{1,0:T(8,128)(2,1)S(1)}, bf16[64,2048]{1,0:T(8,128)(2,1)}, u32[]{:S(2)}) copy-start(bf16[64,2048]{1,0:T(8,128)(2,1)} %basis_ref.3) | copy-start | bytes 786436
  69.5 24.5 %copy-start.10 = (bf16[1024,512]{1,0:T(8,128)(2,1)S(1)}, bf16[1024,512]{1,0:T(8,128)(2,1)}, u32[]{:S(2)}) copy-start(bf16[1024,512]{1,0:T(8,128)(2,1)} %copy-done.9) | copy-start | bytes 3145732
  80.7 27.0 %collective-permute-start.10 = (bf16[16,64,512]{2,1,0:T(8,128)(2,1)}, bf16[16,64,512]{2,1,0:T(8,128)(2,1)S(1)}, u32[]{:S(2)}, u32[]{:S(2)}) collective-permute-start(bf16[16,64,512]{2,1,0:T(8,128)(2,1)} %get-tuple-element.66), channel_id=1, source_target_pairs={{0,1},{1,2},{2,3},{3,0},{4,5},{5,6},{6,7},{7,4},{8,9},{9,10},{10,1... | collective-permute-start | bytes 3145736 | tf_op jit(solution)/shard_map/ppermute | solution.py:237
  83.0 26.4 %collective-permute-start.11 = (bf16[16,64,512]{2,1,0:T(8,128)(2,1)}, bf16[16,64,512]{2,1,0:T(8,128)(2,1)S(1)}, u32[]{:S(2)}, u32[]{:S(2)}) collective-permute-start(bf16[16,64,512]{2,1,0:T(8,128)(2,1)} %get-tuple-element.67), channel_id=1, source_target_pairs={{0,3},{1,0},{2,1},{3,2},{4,7},{5,4},{6,5},{7,6},{8,11},{9,8},{10,9... | collective-permute-start | bytes 3145736 | tf_op jit(solution)/shard_map/ppermute | solution.py:237
  85.1 31.1 %collective-permute-start.3 = (bf16[16,64,512]{2,1,0:T(8,128)(2,1)}, bf16[16,64,512]{2,1,0:T(8,128)(2,1)S(1)}, u32[]{:S(2)}, u32[]{:S(2)}) collective-permute-start(bf16[16,64,512]{2,1,0:T(8,128)(2,1)} %get-tuple-element.51), channel_id=1, source_target_pairs={{0,12},{1,13},{2,14},{3,15},{4,0},{5,1},{6,2},{7,3},{8,4},{9,5},{1... | collective-permute-start | bytes 3145736 | tf_op jit(solution)/shard_map/ppermute | solution.py:237
  92.6 16.7 %copy-start.2 = (f32[8,64,512]{2,1,0:T(8,128)S(1)}, f32[8,64,512]{2,1,0:T(8,128)}, u32[]{:S(2)}) copy-start(f32[8,64,512]{2,1,0:T(8,128)} %copy-done.1) | copy-start | bytes 3145732
  92.6 24.6 %collective-permute-start.2 = (bf16[16,64,512]{2,1,0:T(8,128)(2,1)}, bf16[16,64,512]{2,1,0:T(8,128)(2,1)S(1)}, u32[]{:S(2)}, u32[]{:S(2)}) collective-permute-start(bf16[16,64,512]{2,1,0:T(8,128)(2,1)} %get-tuple-element.45), channel_id=1, source_target_pairs={{0,4},{1,5},{2,6},{3,7},{4,8},{5,9},{6,10},{7,11},{8,12},{9,13},{1... | collective-permute-start | bytes 3145736 | tf_op jit(solution)/shard_map/ppermute | solution.py:237
  109.5 14.1 %collective-permute-start.12 = (bf16[8,64,512]{2,1,0:T(8,128)(2,1)S(1)}, bf16[8,64,512]{2,1,0:T(8,128)(2,1)S(1)}, u32[]{:S(2)}, u32[]{:S(2)}) collective-permute-start(bf16[8,64,512]{2,1,0:T(8,128)(2,1)S(1)} %get-tuple-element.70), channel_id=1, source_target_pairs={{0,1},{1,2},{2,3},{3,0},{4,5},{5,6},{6,7},{7,4},{8,9},{9,10},{10,1... | collective-permute-start | bytes 1572872 | tf_op jit(solution)/shard_map/ppermute | solution.py:237
  111.4 12.3 %collective-permute-start.13 = (bf16[8,64,512]{2,1,0:T(8,128)(2,1)S(1)}, bf16[8,64,512]{2,1,0:T(8,128)(2,1)S(1)}, u32[]{:S(2)}, u32[]{:S(2)}) collective-permute-start(bf16[8,64,512]{2,1,0:T(8,128)(2,1)S(1)} %get-tuple-element.71), channel_id=1, source_target_pairs={{0,3},{1,0},{2,1},{3,2},{4,7},{5,4},{6,5},{7,6},{8,11},{9,8},{10,9... | collective-permute-start | bytes 1572872 | tf_op jit(solution)/shard_map/ppermute | solution.py:237
  117.4 15.1 %collective-permute-start.4 = (bf16[8,64,512]{2,1,0:T(8,128)(2,1)S(1)}, bf16[8,64,512]{2,1,0:T(8,128)(2,1)S(1)}, u32[]{:S(2)}, u32[]{:S(2)}) collective-permute-start(bf16[8,64,512]{2,1,0:T(8,128)(2,1)S(1)} %get-tuple-element.56), channel_id=1, source_target_pairs={{0,4},{1,5},{2,6},{3,7},{4,8},{5,9},{6,10},{7,11},{8,12},{9,13},{1... | collective-permute-start | bytes 1572872 | tf_op jit(solution)/shard_map/ppermute | solution.py:237
  120.1 12.6 %collective-permute-start.5 = (bf16[8,64,512]{2,1,0:T(8,128)(2,1)S(1)}, bf16[8,64,512]{2,1,0:T(8,128)(2,1)S(1)}, u32[]{:S(2)}, u32[]{:S(2)}) collective-permute-start(bf16[8,64,512]{2,1,0:T(8,128)(2,1)S(1)} %get-tuple-element.57), channel_id=1, source_target_pairs={{0,12},{1,13},{2,14},{3,15},{4,0},{5,1},{6,2},{7,3},{8,4},{9,5},{1... | collective-permute-start | bytes 1572872 | tf_op jit(solution)/shard_map/ppermute | solution.py:237
  124.0 12.3 %collective-permute-start.14 = (bf16[8,64,256]{2,1,0:T(8,128)(2,1)S(1)}, bf16[8,64,256]{2,1,0:T(8,128)(2,1)S(1)}, u32[]{:S(2)}, u32[]{:S(2)}) collective-permute-start(bf16[8,64,256]{2,1,0:T(8,128)(2,1)S(1)} %get-tuple-element.73), channel_id=1, source_target_pairs={{0,4},{1,5},{2,6},{3,7},{4,8},{5,9},{6,10},{7,11},{8,12},{9,13},{1... | collective-permute-start | bytes 786440 | tf_op jit(solution)/shard_map/ppermute | solution.py:237
  130.2 6.7 %collective-permute-start.15 = (bf16[8,64,256]{2,1,0:T(8,128)(2,1)S(1)}, bf16[8,64,256]{2,1,0:T(8,128)(2,1)S(1)}, u32[]{:S(2)}, u32[]{:S(2)}) collective-permute-start(bf16[8,64,256]{2,1,0:T(8,128)(2,1)S(1)} %get-tuple-element.74), channel_id=1, source_target_pairs={{0,12},{1,13},{2,14},{3,15},{4,0},{5,1},{6,2},{7,3},{8,4},{9,5},{1... | collective-permute-start | bytes 786440 | tf_op jit(solution)/shard_map/ppermute | solution.py:237
  133.0 7.7 %collective-permute-start.6 = (bf16[8,64,256]{2,1,0:T(8,128)(2,1)S(1)}, bf16[8,64,256]{2,1,0:T(8,128)(2,1)S(1)}, u32[]{:S(2)}, u32[]{:S(2)}) collective-permute-start(bf16[8,64,256]{2,1,0:T(8,128)(2,1)S(1)} %get-tuple-element.59), channel_id=1, source_target_pairs={{0,1},{1,2},{2,3},{3,0},{4,5},{5,6},{6,7},{7,4},{8,9},{9,10},{10,1... | collective-permute-start | bytes 786440 | tf_op jit(solution)/shard_map/ppermute | solution.py:237
  133.1 7.6 %collective-permute-start.7 = (bf16[8,64,256]{2,1,0:T(8,128)(2,1)S(1)}, bf16[8,64,256]{2,1,0:T(8,128)(2,1)S(1)}, u32[]{:S(2)}, u32[]{:S(2)}) collective-permute-start(bf16[8,64,256]{2,1,0:T(8,128)(2,1)S(1)} %get-tuple-element.60), channel_id=1, source_target_pairs={{0,3},{1,0},{2,1},{3,2},{4,7},{5,4},{6,5},{7,6},{8,11},{9,8},{10,9... | collective-permute-start | bytes 786440 | tf_op jit(solution)/shard_map/ppermute | solution.py:237
  137.0 7.2 %collective-permute-start.16 = (bf16[4,64,256]{2,1,0:T(8,128)(2,1)S(1)}, bf16[4,64,256]{2,1,0:T(8,128)(2,1)S(1)}, u32[]{:S(2)}, u32[]{:S(2)}) collective-permute-start(bf16[4,64,256]{2,1,0:T(8,128)(2,1)S(1)} %get-tuple-element.77), channel_id=1, source_target_pairs={{0,4},{1,5},{2,6},{3,7},{4,8},{5,9},{6,10},{7,11},{8,12},{9,13},{1... | collective-permute-start | bytes 393224 | tf_op jit(solution)/shard_map/ppermute | solution.py:237
  137.4 6.7 %collective-permute-start.17 = (bf16[4,64,256]{2,1,0:T(8,128)(2,1)S(1)}, bf16[4,64,256]{2,1,0:T(8,128)(2,1)S(1)}, u32[]{:S(2)}, u32[]{:S(2)}) collective-permute-start(bf16[4,64,256]{2,1,0:T(8,128)(2,1)S(1)} %get-tuple-element.78), channel_id=1, source_target_pairs={{0,12},{1,13},{2,14},{3,15},{4,0},{5,1},{6,2},{7,3},{8,4},{9,5},{1... | collective-permute-start | bytes 393224 | tf_op jit(solution)/shard_map/ppermute | solution.py:237
  140.7 6.3 %collective-permute-start.8 = (bf16[4,64,256]{2,1,0:T(8,128)(2,1)S(1)}, bf16[4,64,256]{2,1,0:T(8,128)(2,1)S(1)}, u32[]{:S(2)}, u32[]{:S(2)}) collective-permute-start(bf16[4,64,256]{2,1,0:T(8,128)(2,1)S(1)} %get-tuple-element.63), channel_id=1, source_target_pairs={{0,1},{1,2},{2,3},{3,0},{4,5},{5,6},{6,7},{7,4},{8,9},{9,10},{10,1... | collective-permute-start | bytes 393224 | tf_op jit(solution)/shard_map/ppermute | solution.py:237
  141.7 5.3 %collective-permute-start.9 = (bf16[4,64,256]{2,1,0:T(8,128)(2,1)S(1)}, bf16[4,64,256]{2,1,0:T(8,128)(2,1)S(1)}, u32[]{:S(2)}, u32[]{:S(2)}) collective-permute-start(bf16[4,64,256]{2,1,0:T(8,128)(2,1)S(1)} %get-tuple-element.64), channel_id=1, source_target_pairs={{0,3},{1,0},{2,1},{3,2},{4,7},{5,4},{6,5},{7,6},{8,11},{9,8},{10,9... | collective-permute-start | bytes 393224 | tf_op jit(solution)/shard_map/ppermute | solution.py:237
  (10 other events, 51.2 us)
Sparse Core Ops, SparseCore 0:
  10.0 34.5 all-gather.1

commit v10 on v7

--- a/solution.py
+++ b/solution.py
@@ -118,7 +118,7 @@
 
 
 UNROLL = 32
-X_ROWS = 5
+X_ROWS = 4
 
 
 def far_kernel(slots, rows, comp_ref, sent_ref, *refs):
@@ -414,12 +414,10 @@
     )
     sent = lax.all_to_all(sent, "ccol", split_axis=0, concat_axis=0, tiled=True)
 
-    low, high, sent = lax.optimization_barrier((low, high, sent))
     up = [(i, i + 1) for i in range(devices - 1)]
     down = [(j, i) for i, j in up]
     before = lax.ppermute(high, ("crow", "ccol"), up)
     after = lax.ppermute(low, ("crow", "ccol"), down)
-
     left, right = far_field(gathered, sent, slots, lines, col_devices * cluster_count)
     for along_x in (True, False):
         left_up, left_down = both_ways(left[0], left[1], along_x)

time: 153 us -> 140 us (0.915)
  blocking collectives: 37.1 us -> 0 us
  waiting for transfers between devices: 32.6 us -> 49.5 us
  starting transfers between devices: 36.2 us -> 42.2 us
    all_to_all x1 -> x0, blocking collectives: 37.1 us -> none  [per_device(): sent = lax.all_to_all(sent, 'ccol', split_axis=0, concat_axis=0, tiled=True)]
    all_to_all x0 -> x1, waiting for transfers between devices: none -> 25.1 us  [per_device(): sent = lax.all_to_all(sent, 'ccol', split_axis=0, concat_axis=0, tiled=True)]
    ppermute x8, starting transfers between devices: 27.3 us -> 18.4 us  [both_ways(): lax.ppermute(down, 'ccol', ring(along_x, -1))]
    ppermute x8, waiting for transfers between devices: 10.4 us -> 1.63 us  [both_ways(): lax.ppermute(down, 'ccol', ring(along_x, -1))]
    ppermute x8, waiting for transfers between devices: 13.5 us -> 22 us  [both_ways(): lax.ppermute(up, 'ccol', ring(along_x, 1))]
    all_to_all x0 -> x1, starting transfers between devices: none -> 8 us  [per_device(): sent = lax.all_to_all(sent, 'ccol', split_axis=0, concat_axis=0, tiled=True)]
    ppermute x8, starting transfers between devices: 3.99 us -> 9.59 us  [both_ways(): lax.ppermute(up, 'ccol', ring(along_x, 1))]
    ppermute x1, waiting for transfers between devices: 4.12 us -> 0.01 us  [per_device(): after = lax.ppermute(low, ('crow', 'ccol'), down)]
  transfers between devices with their start and end apart: 19 -> 20, of which waited for: 6 -> 10; matrix products, arithmetic and copies ran while one was open for 0% -> 0% of each run, Pallas kernels for 14% -> 16%
where the time goes in v10:
time: 140 us; the launch traced here: 138 us
  waiting for transfers between devices  49.5 us (35%)
  starting transfers between devices  42.2 us (30%)
  Pallas kernels  28.3 us (20%)
  between operations  13.5 us (10%)
  local copies, waits for them, and re-layouts  4.91 us (4%)
    all_to_all x1, waiting for transfers between devices, per_device(): sent = lax.all_to_all(sent, 'ccol', split_axis=0, concat_axis=0, tiled=True)  25.1 us
    ppermute x8, waiting for transfers between devices, both_ways(): lax.ppermute(up, 'ccol', ring(along_x, 1))  22 us
    ppermute x8, starting transfers between devices, both_ways(): lax.ppermute(down, 'ccol', ring(along_x, -1))  18.4 us
    pallas_call x1, Pallas kernels, far_field(): pl.pallas_call(functools.partial(far_kernel, slots, rows), in_specs=[whol...  10.2 us
    ppermute x8, starting transfers between devices, both_ways(): lax.ppermute(up, 'ccol', ring(along_x, 1))  9.59 us
    pallas_call x1, Pallas kernels, near_field(): pl.pallas_call(near_kernel, grid=(panels // CS,), in_specs=[pl.BlockSpec(...  8.33 us
    all_to_all x1, starting transfers between devices, per_device(): sent = lax.all_to_all(sent, 'ccol', split_axis=0, concat_axis=0, tiled=True)  8 us
    unnamed x19, local copies, waits for them, and re-layouts  4.91 us
  transfers between devices with their start and end apart: 20, of which 10 were waited for; matrix products, arithmetic and copies ran while one was open for 0% of the time, Pallas kernels for 16%

profile of v10, /device:TPU:0, one launch (start us, length us, event | category | flops | bytes accessed | tf_op | source)
XLA Modules:
  0.0 138.5 jit_solution(16284440817763572397)
XLA Ops:
  6.6 3.3 %compress.1 = (bf16[8,64,512]{2,1,0:T(8,128)(2,1)}, bf16[1024,512]{1,0:T(8,128)(2,1)}, bf16[1024,512]{1,0:T(8,128)(2,1)}) custom-call(bf16[64,2048]{1,0:T(8,128)(2,1)} %basis_ref.2, bf16[2048,512]{1,0:T(8,128)(2,1)} %modes_ref.3), custom_call_target="tpu_custom_call" | custom-call | flops 134217728 | bytes 3145728 | tf_op jit(solution)/shard_map/compress/pallas_call | solution.py:49
  10.1 3.1 %dispatch.1 = bf16[16,528,128]{2,1,0:T(8,128)(2,1)} custom-call(s32[128]{0:T(128)S(1)} %copy-done.3, s32[128]{0:T(128)S(1)} %bitcast.4, s32[128]{0:T(128)S(1)} %copy-done.5, bf16[128,32,128]{2,1,0:T(8,128)(2,1)S(1)} %bitcast.3), custom_call_target="tpu_custom_call" | custom-call | flops 4194304 | bytes 3145728 | tf_op jit(solution)/shard_map/dispatch/pallas_call | solution.py:108
  13.2 8.0 %all-to-all-start = ((bf16[16,528,128]{2,1,0:T(8,128)(2,1)}), bf16[16,528,128]{2,1,0:T(8,128)(2,1)}, u32[]{:S(2)}, u32[]{:S(2)}) async-start(bf16[16,528,128]{2,1,0:T(8,128)(2,1)} %dispatch.1), calls=%async_computation | async-start | bytes 4325376 | tf_op jit(solution)/shard_map/all_to_all | solution.py:415
  21.2 4.8 %collective-permute-start = (bf16[1024,512]{1,0:T(8,128)(2,1)}, bf16[1024,512]{1,0:T(8,128)(2,1)}, u32[]{:S(2)}, u32[]{:S(2)}) collective-permute-start(bf16[1024,512]{1,0:T(8,128)(2,1)} %get-tuple-element.42), channel_id=1, source_target_pairs={{0,1},{1,2},{2,3},{3,4},{4,5},{5,6},{6,7},{7,8},{8,9},{9,10},{10,1... | collective-permute-start | bytes 3145736 | tf_op jit(solution)/shard_map/ppermute | solution.py:419
  26.0 1.4 %collective-permute-start.1 = (bf16[1024,512]{1,0:T(8,128)(2,1)}, bf16[1024,512]{1,0:T(8,128)(2,1)}, u32[]{:S(2)}, u32[]{:S(2)}) collective-permute-start(bf16[1024,512]{1,0:T(8,128)(2,1)} %get-tuple-element.43), channel_id=1, source_target_pairs={{1,0},{2,1},{3,2},{4,3},{5,4},{6,5},{7,6},{8,7},{9,8},{10,9},{11,1... | collective-permute-start | bytes 3145736 | tf_op jit(solution)/shard_map/ppermute | solution.py:420
  27.4 25.1 %all-to-all-done.sent_ref = bf16[16,528,128]{2,1,0:T(8,128)(2,1)} async-done(((bf16[16,528,128]{2,1,0:T(8,128)(2,1)}), bf16[16,528,128]{2,1,0:T(8,128)(2,1)}, u32[]{:S(2)}, u32[]{:S(2)}) %all-to-all-start) | async-done | bytes 2162720 | tf_op jit(solution)/shard_map/all_to_all | solution.py:415
  52.5 10.2 %far_field.1 = (bf16[16,64,512]{2,1,0:T(8,128)(2,1)}, bf16[16,64,512]{2,1,0:T(8,128)(2,1)}, f32[8,64,512]{2,1,0:T(8,128)S(1)}, f32[8,64,512]{2,1,0:T(8,128)S(1)}...) custom-call(bf16[64,64,512]{2,1,0:T(8,128)(2,1)} %all-gather.2.clone, ...), custom_call_target="tpu_custom_call" | custom-call | flops 4294967296 | bytes 25165824 | tf_op jit(solution)/shard_map/far_field/pallas_call | solution.py:203
  65.1 1.9 %collective-permute-start.11 = (bf16[16,64,512]{2,1,0:T(8,128)(2,1)}, bf16[16,64,512]{2,1,0:T(8,128)(2,1)S(1)}, u32[]{:S(2)}, u32[]{:S(2)}) collective-permute-start(bf16[16,64,512]{2,1,0:T(8,128)(2,1)} %get-tuple-element.67), channel_id=1, source_target_pairs={{0,3},{1,0},{2,1},{3,2},{4,7},{5,4},{6,5},{7,6},{8,11},{9,8},{10,9... | collective-permute-start | bytes 3145736 | tf_op jit(solution)/shard_map/ppermute | solution.py:237
  68.2 4.0 %collective-permute-start.2 = (bf16[16,64,512]{2,1,0:T(8,128)(2,1)}, bf16[16,64,512]{2,1,0:T(8,128)(2,1)S(1)}, u32[]{:S(2)}, u32[]{:S(2)}) collective-permute-start(bf16[16,64,512]{2,1,0:T(8,128)(2,1)} %get-tuple-element.45), channel_id=1, source_target_pairs={{0,4},{1,5},{2,6},{3,7},{4,8},{5,9},{6,10},{7,11},{8,12},{9,13},{1... | collective-permute-start | bytes 3145736 | tf_op jit(solution)/shard_map/ppermute | solution.py:237
  72.2 3.7 %copy-done.6 = bf16[2048,2304]{1,0:T(8,128)(2,1)S(1)} copy-done((bf16[2048,2304]{1,0:T(8,128)(2,1)S(1)}, bf16[2048,2304]{1,0:T(8,128)(2,1)}, u32[]{:S(2)}) %copy-start.6) | copy-done | bytes 9437208
  75.9 8.3 %near_field.1 = (f32[2048,512]{1,0:T(8,128)S(1)}, bf16[2048,64]{1,0:T(8,128)(2,1)S(1)}) custom-call(bf16[2048,2304]{1,0:T(8,128)(2,1)S(1)} %copy-done.6, bf16[1024,512]{1,0:T(8,128)(2,1)} %collective-permute-done.before_ref, bf16[2048,512]{1,0:T(8,128)(2,1)S(1)} %copy-done, bf16[1024,512]{1,0:T(8,128)(2,1)} %collective-permute-done.1.after_ref, ...), custom_call_target="tpu_custom_call" | custom-call | flops 4831838208 | bytes 2097152 | tf_op jit(solution)/shard_map/near_field/pallas_call | solution.py:331
  84.2 7.6 %collective-permute-done.10.up_ref.up_in_ref = bf16[16,64,512]{2,1,0:T(8,128)(2,1)S(1)} collective-permute-done((bf16[16,64,512]{2,1,0:T(8,128)(2,1)}, bf16[16,64,512]{2,1,0:T(8,128)(2,1)S(1)}, u32[]{:S(2)}, u32[]{:S(2)}) %collective-permute-start.10) | collective-permute-done | bytes 1048608 | tf_op jit(solution)/shard_map/ppermute | solution.py:237
  91.8 1.6 %collective-permute-done.11.down_ref.down_in_ref = bf16[16,64,512]{2,1,0:T(8,128)(2,1)S(1)} collective-permute-done((bf16[16,64,512]{2,1,0:T(8,128)(2,1)}, bf16[16,64,512]{2,1,0:T(8,128)(2,1)S(1)}, u32[]{:S(2)}, u32[]{:S(2)}) %collective-permute-start.11) | collective-permute-done | bytes 1048608 | tf_op jit(solution)/shard_map/ppermute | solution.py:237
  93.7 3.7 %collective-permute-start.13 = (bf16[8,64,512]{2,1,0:T(8,128)(2,1)S(1)}, bf16[8,64,512]{2,1,0:T(8,128)(2,1)S(1)}, u32[]{:S(2)}, u32[]{:S(2)}) collective-permute-start(bf16[8,64,512]{2,1,0:T(8,128)(2,1)S(1)} %get-tuple-element.71), channel_id=1, source_target_pairs={{0,3},{1,0},{2,1},{3,2},{4,7},{5,4},{6,5},{7,6},{8,11},{9,8},{10,9... | collective-permute-start | bytes 1572872 | tf_op jit(solution)/shard_map/ppermute | solution.py:237
  98.3 2.7 %collective-permute-start.5 = (bf16[8,64,512]{2,1,0:T(8,128)(2,1)S(1)}, bf16[8,64,512]{2,1,0:T(8,128)(2,1)S(1)}, u32[]{:S(2)}, u32[]{:S(2)}) collective-permute-start(bf16[8,64,512]{2,1,0:T(8,128)(2,1)S(1)} %get-tuple-element.57), channel_id=1, source_target_pairs={{0,12},{1,13},{2,14},{3,15},{4,0},{5,1},{6,2},{7,3},{8,4},{9,5},{1... | collective-permute-start | bytes 1572872 | tf_op jit(solution)/shard_map/ppermute | solution.py:237
  100.9 8.6 %collective-permute-done.12.up_rest_ref = bf16[8,64,512]{2,1,0:T(8,128)(2,1)S(1)} collective-permute-done((bf16[8,64,512]{2,1,0:T(8,128)(2,1)S(1)}, bf16[8,64,512]{2,1,0:T(8,128)(2,1)S(1)}, u32[]{:S(2)}, u32[]{:S(2)}) %collective-permute-start.12) | collective-permute-done | bytes 524320 | tf_op jit(solution)/shard_map/ppermute | solution.py:237
  110.3 2.8 %collective-permute-start.15 = (bf16[8,64,256]{2,1,0:T(8,128)(2,1)S(1)}, bf16[8,64,256]{2,1,0:T(8,128)(2,1)S(1)}, u32[]{:S(2)}, u32[]{:S(2)}) collective-permute-start(bf16[8,64,256]{2,1,0:T(8,128)(2,1)S(1)} %get-tuple-element.74), channel_id=1, source_target_pairs={{0,12},{1,13},{2,14},{3,15},{4,0},{5,1},{6,2},{7,3},{8,4},{9,5},{1... | collective-permute-start | bytes 786440 | tf_op jit(solution)/shard_map/ppermute | solution.py:237
  114.6 2.3 %collective-permute-start.7 = (bf16[8,64,256]{2,1,0:T(8,128)(2,1)S(1)}, bf16[8,64,256]{2,1,0:T(8,128)(2,1)S(1)}, u32[]{:S(2)}, u32[]{:S(2)}) collective-permute-start(bf16[8,64,256]{2,1,0:T(8,128)(2,1)S(1)} %get-tuple-element.60), channel_id=1, source_target_pairs={{0,3},{1,0},{2,1},{3,2},{4,7},{5,4},{6,5},{7,6},{8,11},{9,8},{10,9... | collective-permute-start | bytes 786440 | tf_op jit(solution)/shard_map/ppermute | solution.py:237
  116.9 2.0 %collective-permute-done.14.up_ref.refs_6_ = bf16[8,64,256]{2,1,0:T(8,128)(2,1)S(1)} collective-permute-done((bf16[8,64,256]{2,1,0:T(8,128)(2,1)S(1)}, bf16[8,64,256]{2,1,0:T(8,128)(2,1)S(1)}, u32[]{:S(2)}, u32[]{:S(2)}) %collective-permute-start.14) | collective-permute-done | bytes 262176 | tf_op jit(solution)/shard_map/ppermute | solution.py:237
  118.9 1.6 %collective-permute-start.16 = (bf16[4,64,256]{2,1,0:T(8,128)(2,1)S(1)}, bf16[4,64,256]{2,1,0:T(8,128)(2,1)S(1)}, u32[]{:S(2)}, u32[]{:S(2)}) collective-permute-start(bf16[4,64,256]{2,1,0:T(8,128)(2,1)S(1)} %get-tuple-element.77), channel_id=1, source_target_pairs={{0,4},{1,5},{2,6},{3,7},{4,8},{5,9},{6,10},{7,11},{8,12},{9,13},{1... | collective-permute-start | bytes 393224 | tf_op jit(solution)/shard_map/ppermute | solution.py:237
  120.6 1.7 %collective-permute-start.17 = (bf16[4,64,256]{2,1,0:T(8,128)(2,1)S(1)}, bf16[4,64,256]{2,1,0:T(8,128)(2,1)S(1)}, u32[]{:S(2)}, u32[]{:S(2)}) collective-permute-start(bf16[4,64,256]{2,1,0:T(8,128)(2,1)S(1)} %get-tuple-element.78), channel_id=1, source_target_pairs={{0,12},{1,13},{2,14},{3,15},{4,0},{5,1},{6,2},{7,3},{8,4},{9,5},{1... | collective-permute-start | bytes 393224 | tf_op jit(solution)/shard_map/ppermute | solution.py:237
  123.2 3.0 %collective-permute-start.9 = (bf16[4,64,256]{2,1,0:T(8,128)(2,1)S(1)}, bf16[4,64,256]{2,1,0:T(8,128)(2,1)S(1)}, u32[]{:S(2)}, u32[]{:S(2)}) collective-permute-start(bf16[4,64,256]{2,1,0:T(8,128)(2,1)S(1)} %get-tuple-element.64), channel_id=1, source_target_pairs={{0,3},{1,0},{2,1},{3,2},{4,7},{5,4},{6,5},{7,6},{8,11},{9,8},{10,9... | collective-permute-start | bytes 393224 | tf_op jit(solution)/shard_map/ppermute | solution.py:237
  126.2 2.9 %collective-permute-done.8.refs_3_ = bf16[4,64,256]{2,1,0:T(8,128)(2,1)S(1)} collective-permute-done((bf16[4,64,256]{2,1,0:T(8,128)(2,1)S(1)}, bf16[4,64,256]{2,1,0:T(8,128)(2,1)S(1)}, u32[]{:S(2)}, u32[]{:S(2)}) %collective-permute-start.8) | collective-permute-done | bytes 131104 | tf_op jit(solution)/shard_map/ppermute | solution.py:237
  129.1 2.5 %expand.1 = bf16[2048,512]{1,0:T(8,128)(2,1)} custom-call(f32[2048,512]{1,0:T(8,128)S(1)} %get-tuple-element.48.near_ref, bf16[2048,64]{1,0:T(8,128)(2,1)S(1)} %get-tuple-element.49.basis_ref, f32[4,64,512]{2,1,0:T(8,128)S(1)} %get-tuple-element.58.refs_0_, bf16[8,64,256]{2,1,0:T(8,128)(2,1)S(1)} %collective-permute-done.6.up_ref.refs_1_, ...), custom_call_target="tpu_custom_call" | custom-call | flops 134217728 | bytes 7340032 | tf_op jit(solution)/shard_map/expand/pallas_call | solution.py:381
  (47 shorter events, 8.4 us)
Async XLA Ops:
  6.5 46.0 %all-gather.2.cloned.1.call-start = ((), (), s32[]{:S(2)}) async-start(), calls=%async_computation.1 | async-start | bytes 4718592 | tf_op jit(solution)/shard_map/all_gather | solution.py:408
  13.2 39.3 %all-to-all-start = ((bf16[16,528,128]{2,1,0:T(8,128)(2,1)}), bf16[16,528,128]{2,1,0:T(8,128)(2,1)}, u32[]{:S(2)}, u32[]{:S(2)}) async-start(bf16[16,528,128]{2,1,0:T(8,128)(2,1)} %dispatch.1), calls=%async_computation | async-start | bytes 4325376 | tf_op jit(solution)/shard_map/all_to_all | solution.py:415
  21.2 47.0 %collective-permute-start = (bf16[1024,512]{1,0:T(8,128)(2,1)}, bf16[1024,512]{1,0:T(8,128)(2,1)}, u32[]{:S(2)}, u32[]{:S(2)}) collective-permute-start(bf16[1024,512]{1,0:T(8,128)(2,1)} %get-tuple-element.42), channel_id=1, source_target_pairs={{0,1},{1,2},{2,3},{3,4},{4,5},{5,6},{6,7},{7,8},{8,9},{9,10},{10,1... | collective-permute-start | bytes 3145736 | tf_op jit(solution)/shard_map/ppermute | solution.py:419
  26.0 46.2 %copy-start = (bf16[2048,512]{1,0:T(8,128)(2,1)S(1)}, bf16[2048,512]{1,0:T(8,128)(2,1)}, u32[]{:S(2)}) copy-start(bf16[2048,512]{1,0:T(8,128)(2,1)} %modes_ref.3) | copy-start | bytes 6291460
  26.0 46.2 %copy-start.7 = (bf16[64,2048]{1,0:T(8,128)(2,1)S(1)}, bf16[64,2048]{1,0:T(8,128)(2,1)}, u32[]{:S(2)}) copy-start(bf16[64,2048]{1,0:T(8,128)(2,1)} %basis_ref.3) | copy-start | bytes 786436
  26.0 46.2 %collective-permute-start.1 = (bf16[1024,512]{1,0:T(8,128)(2,1)}, bf16[1024,512]{1,0:T(8,128)(2,1)}, u32[]{:S(2)}, u32[]{:S(2)}) collective-permute-start(bf16[1024,512]{1,0:T(8,128)(2,1)} %get-tuple-element.43), channel_id=1, source_target_pairs={{1,0},{2,1},{3,2},{4,3},{5,4},{6,5},{7,6},{8,7},{9,8},{10,9},{11,1... | collective-permute-start | bytes 3145736 | tf_op jit(solution)/shard_map/ppermute | solution.py:420
  63.7 28.1 %collective-permute-start.10 = (bf16[16,64,512]{2,1,0:T(8,128)(2,1)}, bf16[16,64,512]{2,1,0:T(8,128)(2,1)S(1)}, u32[]{:S(2)}, u32[]{:S(2)}) collective-permute-start(bf16[16,64,512]{2,1,0:T(8,128)(2,1)} %get-tuple-element.66), channel_id=1, source_target_pairs={{0,1},{1,2},{2,3},{3,0},{4,5},{5,6},{6,7},{7,4},{8,9},{9,10},{10,1... | collective-permute-start | bytes 3145736 | tf_op jit(solution)/shard_map/ppermute | solution.py:237
  65.1 28.4 %collective-permute-start.11 = (bf16[16,64,512]{2,1,0:T(8,128)(2,1)}, bf16[16,64,512]{2,1,0:T(8,128)(2,1)S(1)}, u32[]{:S(2)}, u32[]{:S(2)}) collective-permute-start(bf16[16,64,512]{2,1,0:T(8,128)(2,1)} %get-tuple-element.67), channel_id=1, source_target_pairs={{0,3},{1,0},{2,1},{3,2},{4,7},{5,4},{6,5},{7,6},{8,11},{9,8},{10,9... | collective-permute-start | bytes 3145736 | tf_op jit(solution)/shard_map/ppermute | solution.py:237
  66.9 30.4 %collective-permute-start.3 = (bf16[16,64,512]{2,1,0:T(8,128)(2,1)}, bf16[16,64,512]{2,1,0:T(8,128)(2,1)S(1)}, u32[]{:S(2)}, u32[]{:S(2)}) collective-permute-start(bf16[16,64,512]{2,1,0:T(8,128)(2,1)} %get-tuple-element.51), channel_id=1, source_target_pairs={{0,12},{1,13},{2,14},{3,15},{4,0},{5,1},{6,2},{7,3},{8,4},{9,5},{1... | collective-permute-start | bytes 3145736 | tf_op jit(solution)/shard_map/ppermute | solution.py:237
  68.2 25.3 %copy-start.2 = (f32[8,64,512]{2,1,0:T(8,128)S(1)}, f32[8,64,512]{2,1,0:T(8,128)}, u32[]{:S(2)}) copy-start(f32[8,64,512]{2,1,0:T(8,128)} %copy-done.1) | copy-start | bytes 3145732
  68.2 29.3 %collective-permute-start.2 = (bf16[16,64,512]{2,1,0:T(8,128)(2,1)}, bf16[16,64,512]{2,1,0:T(8,128)(2,1)S(1)}, u32[]{:S(2)}, u32[]{:S(2)}) collective-permute-start(bf16[16,64,512]{2,1,0:T(8,128)(2,1)} %get-tuple-element.45), channel_id=1, source_target_pairs={{0,4},{1,5},{2,6},{3,7},{4,8},{5,9},{6,10},{7,11},{8,12},{9,13},{1... | collective-permute-start | bytes 3145736 | tf_op jit(solution)/shard_map/ppermute | solution.py:237
  72.2 3.7 %copy-start.6 = (bf16[2048,2304]{1,0:T(8,128)(2,1)S(1)}, bf16[2048,2304]{1,0:T(8,128)(2,1)}, u32[]{:S(2)}) copy-start(bf16[2048,2304]{1,0:T(8,128)(2,1)} %near_ref.1) | copy-start | bytes 28311556
  93.6 15.9 %collective-permute-start.12 = (bf16[8,64,512]{2,1,0:T(8,128)(2,1)S(1)}, bf16[8,64,512]{2,1,0:T(8,128)(2,1)S(1)}, u32[]{:S(2)}, u32[]{:S(2)}) collective-permute-start(bf16[8,64,512]{2,1,0:T(8,128)(2,1)S(1)} %get-tuple-element.70), channel_id=1, source_target_pairs={{0,1},{1,2},{2,3},{3,0},{4,5},{5,6},{6,7},{7,4},{8,9},{9,10},{10,1... | collective-permute-start | bytes 1572872 | tf_op jit(solution)/shard_map/ppermute | solution.py:237
  93.7 15.8 %collective-permute-start.13 = (bf16[8,64,512]{2,1,0:T(8,128)(2,1)S(1)}, bf16[8,64,512]{2,1,0:T(8,128)(2,1)S(1)}, u32[]{:S(2)}, u32[]{:S(2)}) collective-permute-start(bf16[8,64,512]{2,1,0:T(8,128)(2,1)S(1)} %get-tuple-element.71), channel_id=1, source_target_pairs={{0,3},{1,0},{2,1},{3,2},{4,7},{5,4},{6,5},{7,6},{8,11},{9,8},{10,9... | collective-permute-start | bytes 1572872 | tf_op jit(solution)/shard_map/ppermute | solution.py:237
  97.6 15.6 %collective-permute-start.4 = (bf16[8,64,512]{2,1,0:T(8,128)(2,1)S(1)}, bf16[8,64,512]{2,1,0:T(8,128)(2,1)S(1)}, u32[]{:S(2)}, u32[]{:S(2)}) collective-permute-start(bf16[8,64,512]{2,1,0:T(8,128)(2,1)S(1)} %get-tuple-element.56), channel_id=1, source_target_pairs={{0,4},{1,5},{2,6},{3,7},{4,8},{5,9},{6,10},{7,11},{8,12},{9,13},{1... | collective-permute-start | bytes 1572872 | tf_op jit(solution)/shard_map/ppermute | solution.py:237
  98.3 15.0 %collective-permute-start.5 = (bf16[8,64,512]{2,1,0:T(8,128)(2,1)S(1)}, bf16[8,64,512]{2,1,0:T(8,128)(2,1)S(1)}, u32[]{:S(2)}, u32[]{:S(2)}) collective-permute-start(bf16[8,64,512]{2,1,0:T(8,128)(2,1)S(1)} %get-tuple-element.57), channel_id=1, source_target_pairs={{0,12},{1,13},{2,14},{3,15},{4,0},{5,1},{6,2},{7,3},{8,4},{9,5},{1... | collective-permute-start | bytes 1572872 | tf_op jit(solution)/shard_map/ppermute | solution.py:237
  109.8 9.1 %collective-permute-start.14 = (bf16[8,64,256]{2,1,0:T(8,128)(2,1)S(1)}, bf16[8,64,256]{2,1,0:T(8,128)(2,1)S(1)}, u32[]{:S(2)}, u32[]{:S(2)}) collective-permute-start(bf16[8,64,256]{2,1,0:T(8,128)(2,1)S(1)} %get-tuple-element.73), channel_id=1, source_target_pairs={{0,4},{1,5},{2,6},{3,7},{4,8},{5,9},{6,10},{7,11},{8,12},{9,13},{1... | collective-permute-start | bytes 786440 | tf_op jit(solution)/shard_map/ppermute | solution.py:237
  110.3 8.5 %collective-permute-start.15 = (bf16[8,64,256]{2,1,0:T(8,128)(2,1)S(1)}, bf16[8,64,256]{2,1,0:T(8,128)(2,1)S(1)}, u32[]{:S(2)}, u32[]{:S(2)}) collective-permute-start(bf16[8,64,256]{2,1,0:T(8,128)(2,1)S(1)} %get-tuple-element.74), channel_id=1, source_target_pairs={{0,12},{1,13},{2,14},{3,15},{4,0},{5,1},{6,2},{7,3},{8,4},{9,5},{1... | collective-permute-start | bytes 786440 | tf_op jit(solution)/shard_map/ppermute | solution.py:237
  113.6 9.3 %collective-permute-start.6 = (bf16[8,64,256]{2,1,0:T(8,128)(2,1)S(1)}, bf16[8,64,256]{2,1,0:T(8,128)(2,1)S(1)}, u32[]{:S(2)}, u32[]{:S(2)}) collective-permute-start(bf16[8,64,256]{2,1,0:T(8,128)(2,1)S(1)} %get-tuple-element.59), channel_id=1, source_target_pairs={{0,1},{1,2},{2,3},{3,0},{4,5},{5,6},{6,7},{7,4},{8,9},{9,10},{10,1... | collective-permute-start | bytes 786440 | tf_op jit(solution)/shard_map/ppermute | solution.py:237
  114.6 8.2 %collective-permute-start.7 = (bf16[8,64,256]{2,1,0:T(8,128)(2,1)S(1)}, bf16[8,64,256]{2,1,0:T(8,128)(2,1)S(1)}, u32[]{:S(2)}, u32[]{:S(2)}) collective-permute-start(bf16[8,64,256]{2,1,0:T(8,128)(2,1)S(1)} %get-tuple-element.60), channel_id=1, source_target_pairs={{0,3},{1,0},{2,1},{3,2},{4,7},{5,4},{6,5},{7,6},{8,11},{9,8},{10,9... | collective-permute-start | bytes 786440 | tf_op jit(solution)/shard_map/ppermute | solution.py:237
  118.9 7.2 %collective-permute-start.16 = (bf16[4,64,256]{2,1,0:T(8,128)(2,1)S(1)}, bf16[4,64,256]{2,1,0:T(8,128)(2,1)S(1)}, u32[]{:S(2)}, u32[]{:S(2)}) collective-permute-start(bf16[4,64,256]{2,1,0:T(8,128)(2,1)S(1)} %get-tuple-element.77), channel_id=1, source_target_pairs={{0,4},{1,5},{2,6},{3,7},{4,8},{5,9},{6,10},{7,11},{8,12},{9,13},{1... | collective-permute-start | bytes 393224 | tf_op jit(solution)/shard_map/ppermute | solution.py:237
  120.6 5.6 %collective-permute-start.17 = (bf16[4,64,256]{2,1,0:T(8,128)(2,1)S(1)}, bf16[4,64,256]{2,1,0:T(8,128)(2,1)S(1)}, u32[]{:S(2)}, u32[]{:S(2)}) collective-permute-start(bf16[4,64,256]{2,1,0:T(8,128)(2,1)S(1)} %get-tuple-element.78), channel_id=1, source_target_pairs={{0,12},{1,13},{2,14},{3,15},{4,0},{5,1},{6,2},{7,3},{8,4},{9,5},{1... | collective-permute-start | bytes 393224 | tf_op jit(solution)/shard_map/ppermute | solution.py:237
  122.9 6.2 %collective-permute-start.8 = (bf16[4,64,256]{2,1,0:T(8,128)(2,1)S(1)}, bf16[4,64,256]{2,1,0:T(8,128)(2,1)S(1)}, u32[]{:S(2)}, u32[]{:S(2)}) collective-permute-start(bf16[4,64,256]{2,1,0:T(8,128)(2,1)S(1)} %get-tuple-element.63), channel_id=1, source_target_pairs={{0,1},{1,2},{2,3},{3,0},{4,5},{5,6},{6,7},{7,4},{8,9},{9,10},{10,1... | collective-permute-start | bytes 393224 | tf_op jit(solution)/shard_map/ppermute | solution.py:237
  123.2 5.9 %collective-permute-start.9 = (bf16[4,64,256]{2,1,0:T(8,128)(2,1)S(1)}, bf16[4,64,256]{2,1,0:T(8,128)(2,1)S(1)}, u32[]{:S(2)}, u32[]{:S(2)}) collective-permute-start(bf16[4,64,256]{2,1,0:T(8,128)(2,1)S(1)} %get-tuple-element.64), channel_id=1, source_target_pairs={{0,3},{1,0},{2,1},{3,2},{4,7},{5,4},{6,5},{7,6},{8,11},{9,8},{10,9... | collective-permute-start | bytes 393224 | tf_op jit(solution)/shard_map/ppermute | solution.py:237
  (5 other events, 15.1 us)
Sparse Core Ops, SparseCore 0:
  10.0 34.5 all-gather.1

commit v11 on v10

--- a/solution.py
+++ b/solution.py
@@ -343,7 +343,7 @@
             jax.ShapeDtypeStruct((panels, rank), jnp.bfloat16),
         ],
         scratch_shapes=[VMEM((panels + 2 * halo, cols), jnp.bfloat16)],
-        compiler_params=pltpu.CompilerParams(vmem_limit_bytes=32 * MIB),
+        compiler_params=pltpu.CompilerParams(vmem_limit_bytes=26 * MIB),
         cost_estimate=pl.CostEstimate(
             flops=2 * panels * band * cols, bytes_accessed=2 * MIB, transcendentals=0
         ),

time: 140 us -> 140 us (level)
  waiting for transfers between devices: 49.5 us -> 52.3 us
  Pallas kernels: 28.3 us -> 26.8 us
    ppermute x1, waiting for transfers between devices: 0.74 us -> 2.88 us  [per_device(): before = lax.ppermute(high, ('crow', 'ccol'), up)]
    unnamed x19 -> x15, local copies, waits for them, and re-layouts: 4.91 us -> 3.94 us
  transfers between devices with their start and end apart: 20 -> 20, of which waited for: 10 -> 7; matrix products, arithmetic and copies ran while one was open for 0% -> 0% of each run, Pallas kernels for 16% -> 15%
where the time goes in v11:
time: 140 us; the launch traced here: 138 us
  waiting for transfers between devices  52.3 us (37%)
  starting transfers between devices  41.3 us (30%)
  Pallas kernels  26.8 us (19%)
  between operations  13.6 us (10%)
  local copies, waits for them, and re-layouts  3.94 us (3%)
    all_to_all x1, waiting for transfers between devices, per_device(): sent = lax.all_to_all(sent, 'ccol', split_axis=0, concat_axis=0, tiled=True)  26 us
    ppermute x8, waiting for transfers between devices, both_ways(): lax.ppermute(up, 'ccol', ring(along_x, 1))  20.7 us
    ppermute x8, starting transfers between devices, both_ways(): lax.ppermute(down, 'ccol', ring(along_x, -1))  17.7 us
    ppermute x8, starting transfers between devices, both_ways(): lax.ppermute(up, 'ccol', ring(along_x, 1))  10.4 us
    pallas_call x1, Pallas kernels, far_field(): pl.pallas_call(functools.partial(far_kernel, slots, rows), in_specs=[whol...  8.94 us
    all_to_all x1, starting transfers between devices, per_device(): sent = lax.all_to_all(sent, 'ccol', split_axis=0, concat_axis=0, tiled=True)  8.01 us
    pallas_call x1, Pallas kernels, near_field(): pl.pallas_call(near_kernel, grid=(panels // CS,), in_specs=[pl.BlockSpec(...  7.99 us
    unnamed x15, local copies, waits for them, and re-layouts  3.94 us
  transfers between devices with their start and end apart: 20, of which 7 were waited for; matrix products, arithmetic and copies ran while one was open for 0% of the time, Pallas kernels for 15%

profile of v11, /device:TPU:0, one launch (start us, length us, event | category | flops | bytes accessed | tf_op | source)
XLA Modules:
  0.0 137.9 jit_solution(6813349751506853128)
XLA Ops:
  6.6 3.2 %compress.1 = (bf16[8,64,512]{2,1,0:T(8,128)(2,1)}, bf16[1024,512]{1,0:T(8,128)(2,1)}, bf16[1024,512]{1,0:T(8,128)(2,1)}) custom-call(bf16[64,2048]{1,0:T(8,128)(2,1)} %basis_ref.2, bf16[2048,512]{1,0:T(8,128)(2,1)} %modes_ref.3), custom_call_target="tpu_custom_call" | custom-call | flops 134217728 | bytes 3145728 | tf_op jit(solution)/shard_map/compress/pallas_call | solution.py:49
  10.1 3.1 %dispatch.1 = bf16[16,528,128]{2,1,0:T(8,128)(2,1)} custom-call(s32[128]{0:T(128)S(1)} %copy-done.1, s32[128]{0:T(128)S(1)} %bitcast.4, s32[128]{0:T(128)S(1)} %copy-done.3, bf16[128,32,128]{2,1,0:T(8,128)(2,1)S(1)} %bitcast.3), custom_call_target="tpu_custom_call" | custom-call | flops 4194304 | bytes 3145728 | tf_op jit(solution)/shard_map/dispatch/pallas_call | solution.py:108
  13.2 8.0 %all-to-all-start = ((bf16[16,528,128]{2,1,0:T(8,128)(2,1)}), bf16[16,528,128]{2,1,0:T(8,128)(2,1)}, u32[]{:S(2)}, u32[]{:S(2)}) async-start(bf16[16,528,128]{2,1,0:T(8,128)(2,1)} %dispatch.1), calls=%async_computation | async-start | bytes 4325376 | tf_op jit(solution)/shard_map/all_to_all | solution.py:415
  21.2 3.8 %collective-permute-start = (bf16[1024,512]{1,0:T(8,128)(2,1)}, bf16[1024,512]{1,0:T(8,128)(2,1)S(1)}, u32[]{:S(2)}, u32[]{:S(2)}) collective-permute-start(bf16[1024,512]{1,0:T(8,128)(2,1)} %get-tuple-element.42), channel_id=1, source_target_pairs={{0,1},{1,2},{2,3},{3,4},{4,5},{5,6},{6,7},{7,8},{8,9},{9,10},{10,1... | collective-permute-start | bytes 3145736 | tf_op jit(solution)/shard_map/ppermute | solution.py:419
  26.5 26.0 %all-to-all-done.sent_ref = bf16[16,528,128]{2,1,0:T(8,128)(2,1)} async-done(((bf16[16,528,128]{2,1,0:T(8,128)(2,1)}), bf16[16,528,128]{2,1,0:T(8,128)(2,1)}, u32[]{:S(2)}, u32[]{:S(2)}) %all-to-all-start) | async-done | bytes 2162720 | tf_op jit(solution)/shard_map/all_to_all | solution.py:415
  52.5 8.9 %far_field.1 = (bf16[16,64,512]{2,1,0:T(8,128)(2,1)S(1)}, bf16[16,64,512]{2,1,0:T(8,128)(2,1)S(1)}, f32[8,64,512]{2,1,0:T(8,128)S(1)}, f32[8,64,512]{2,1,0:T(8,1...) custom-call(bf16[64,64,512]{2,1,0:T(8,128)(2,1)} %all-gather.2.clone, ...), custom_call_target="tpu_custom_call" | custom-call | flops 4294967296 | bytes 25165824 | tf_op jit(solution)/shard_map/far_field/pallas_call | solution.py:203
  62.9 1.9 %collective-permute-start.11 = (bf16[16,64,512]{2,1,0:T(8,128)(2,1)S(1)}, bf16[16,64,512]{2,1,0:T(8,128)(2,1)S(1)}, u32[]{:S(2)}, u32[]{:S(2)}) collective-permute-start(bf16[16,64,512]{2,1,0:T(8,128)(2,1)S(1)} %get-tuple-element.67), channel_id=1, source_target_pairs={{0,3},{1,0},{2,1},{3,2},{4,7},{5,4},{6,5},{7,6},{8,11},{9,8},{10,9... | collective-permute-start | bytes 3145736 | tf_op jit(solution)/shard_map/ppermute | solution.py:237
  65.3 2.9 %collective-permute-done.before_ref = bf16[1024,512]{1,0:T(8,128)(2,1)S(1)} collective-permute-done((bf16[1024,512]{1,0:T(8,128)(2,1)}, bf16[1024,512]{1,0:T(8,128)(2,1)S(1)}, u32[]{:S(2)}, u32[]{:S(2)}) %collective-permute-start) | collective-permute-done | bytes 1048608 | tf_op jit(solution)/shard_map/ppermute | solution.py:419
  68.2 3.9 %collective-permute-start.2 = (bf16[16,64,512]{2,1,0:T(8,128)(2,1)S(1)}, bf16[16,64,512]{2,1,0:T(8,128)(2,1)S(1)}, u32[]{:S(2)}, u32[]{:S(2)}) collective-permute-start(bf16[16,64,512]{2,1,0:T(8,128)(2,1)S(1)} %get-tuple-element.45), channel_id=1, source_target_pairs={{0,4},{1,5},{2,6},{3,7},{4,8},{5,9},{6,10},{7,11},{8,12},{9,13},{1... | collective-permute-start | bytes 3145736 | tf_op jit(solution)/shard_map/ppermute | solution.py:237
  72.1 3.7 %copy-done.4 = bf16[2048,2304]{1,0:T(8,128)(2,1)S(1)} copy-done((bf16[2048,2304]{1,0:T(8,128)(2,1)S(1)}, bf16[2048,2304]{1,0:T(8,128)(2,1)}, u32[]{:S(2)}) %copy-start.4) | copy-done | bytes 9437208
  75.7 8.0 %near_field.1 = (f32[2048,512]{1,0:T(8,128)S(1)}, bf16[2048,64]{1,0:T(8,128)(2,1)S(1)}) custom-call(bf16[2048,2304]{1,0:T(8,128)(2,1)S(1)} %copy-done.4, bf16[1024,512]{1,0:T(8,128)(2,1)S(1)} %collective-permute-done.before_ref, bf16[2048,512]{1,0:T(8,128)(2,1)S(1)} %copy-done, bf16[1024,512]{1,0:T(8,128)(2,1)} %collective-permute-done.1.after_ref, ...), custom_call_target="tpu_custom_call" | custom-call | flops 4831838208 | bytes 2097152 | tf_op jit(solution)/shard_map/near_field/pallas_call | solution.py:331
  83.7 6.9 %collective-permute-done.10.up_ref.up_in_ref = bf16[16,64,512]{2,1,0:T(8,128)(2,1)S(1)} collective-permute-done((bf16[16,64,512]{2,1,0:T(8,128)(2,1)S(1)}, bf16[16,64,512]{2,1,0:T(8,128)(2,1)S(1)}, u32[]{:S(2)}, u32[]{:S(2)}) %collective-permute-start.10) | collective-permute-done | bytes 1048608 | tf_op jit(solution)/shard_map/ppermute | solution.py:237
  90.7 2.7 %collective-permute-done.11.down_ref.down_in_ref = bf16[16,64,512]{2,1,0:T(8,128)(2,1)S(1)} collective-permute-done((bf16[16,64,512]{2,1,0:T(8,128)(2,1)S(1)}, bf16[16,64,512]{2,1,0:T(8,128)(2,1)S(1)}, u32[]{:S(2)}, u32[]{:S(2)}) %collective-permute-start.11) | collective-permute-done | bytes 1048608 | tf_op jit(solution)/shard_map/ppermute | solution.py:237
  93.6 3.8 %collective-permute-start.13 = (bf16[8,64,512]{2,1,0:T(8,128)(2,1)S(1)}, bf16[8,64,512]{2,1,0:T(8,128)(2,1)S(1)}, u32[]{:S(2)}, u32[]{:S(2)}) collective-permute-start(bf16[8,64,512]{2,1,0:T(8,128)(2,1)S(1)} %get-tuple-element.71), channel_id=1, source_target_pairs={{0,3},{1,0},{2,1},{3,2},{4,7},{5,4},{6,5},{7,6},{8,11},{9,8},{10,9... | collective-permute-start | bytes 1572872 | tf_op jit(solution)/shard_map/ppermute | solution.py:237
  98.2 2.6 %collective-permute-start.5 = (bf16[8,64,512]{2,1,0:T(8,128)(2,1)S(1)}, bf16[8,64,512]{2,1,0:T(8,128)(2,1)S(1)}, u32[]{:S(2)}, u32[]{:S(2)}) collective-permute-start(bf16[8,64,512]{2,1,0:T(8,128)(2,1)S(1)} %get-tuple-element.57), channel_id=1, source_target_pairs={{0,12},{1,13},{2,14},{3,15},{4,0},{5,1},{6,2},{7,3},{8,4},{9,5},{1... | collective-permute-start | bytes 1572872 | tf_op jit(solution)/shard_map/ppermute | solution.py:237
  100.8 8.6 %collective-permute-done.12.up_rest_ref = bf16[8,64,512]{2,1,0:T(8,128)(2,1)S(1)} collective-permute-done((bf16[8,64,512]{2,1,0:T(8,128)(2,1)S(1)}, bf16[8,64,512]{2,1,0:T(8,128)(2,1)S(1)}, u32[]{:S(2)}, u32[]{:S(2)}) %collective-permute-start.12) | collective-permute-done | bytes 524320 | tf_op jit(solution)/shard_map/ppermute | solution.py:237
  110.3 2.8 %collective-permute-start.15 = (bf16[8,64,256]{2,1,0:T(8,128)(2,1)S(1)}, bf16[8,64,256]{2,1,0:T(8,128)(2,1)S(1)}, u32[]{:S(2)}, u32[]{:S(2)}) collective-permute-start(bf16[8,64,256]{2,1,0:T(8,128)(2,1)S(1)} %get-tuple-element.74), channel_id=1, source_target_pairs={{0,12},{1,13},{2,14},{3,15},{4,0},{5,1},{6,2},{7,3},{8,4},{9,5},{1... | collective-permute-start | bytes 786440 | tf_op jit(solution)/shard_map/ppermute | solution.py:237
  114.6 2.1 %collective-permute-start.7 = (bf16[8,64,256]{2,1,0:T(8,128)(2,1)S(1)}, bf16[8,64,256]{2,1,0:T(8,128)(2,1)S(1)}, u32[]{:S(2)}, u32[]{:S(2)}) collective-permute-start(bf16[8,64,256]{2,1,0:T(8,128)(2,1)S(1)} %get-tuple-element.60), channel_id=1, source_target_pairs={{0,3},{1,0},{2,1},{3,2},{4,7},{5,4},{6,5},{7,6},{8,11},{9,8},{10,9... | collective-permute-start | bytes 786440 | tf_op jit(solution)/shard_map/ppermute | solution.py:237
  116.7 2.2 %collective-permute-done.14.up_ref.refs_6_ = bf16[8,64,256]{2,1,0:T(8,128)(2,1)S(1)} collective-permute-done((bf16[8,64,256]{2,1,0:T(8,128)(2,1)S(1)}, bf16[8,64,256]{2,1,0:T(8,128)(2,1)S(1)}, u32[]{:S(2)}, u32[]{:S(2)}) %collective-permute-start.14) | collective-permute-done | bytes 262176 | tf_op jit(solution)/shard_map/ppermute | solution.py:237
  118.9 1.6 %collective-permute-start.16 = (bf16[4,64,256]{2,1,0:T(8,128)(2,1)S(1)}, bf16[4,64,256]{2,1,0:T(8,128)(2,1)S(1)}, u32[]{:S(2)}, u32[]{:S(2)}) collective-permute-start(bf16[4,64,256]{2,1,0:T(8,128)(2,1)S(1)} %get-tuple-element.77), channel_id=1, source_target_pairs={{0,4},{1,5},{2,6},{3,7},{4,8},{5,9},{6,10},{7,11},{8,12},{9,13},{1... | collective-permute-start | bytes 393224 | tf_op jit(solution)/shard_map/ppermute | solution.py:237
  120.6 1.7 %collective-permute-start.17 = (bf16[4,64,256]{2,1,0:T(8,128)(2,1)S(1)}, bf16[4,64,256]{2,1,0:T(8,128)(2,1)S(1)}, u32[]{:S(2)}, u32[]{:S(2)}) collective-permute-start(bf16[4,64,256]{2,1,0:T(8,128)(2,1)S(1)} %get-tuple-element.78), channel_id=1, source_target_pairs={{0,12},{1,13},{2,14},{3,15},{4,0},{5,1},{6,2},{7,3},{8,4},{9,5},{1... | collective-permute-start | bytes 393224 | tf_op jit(solution)/shard_map/ppermute | solution.py:237
  123.2 2.4 %collective-permute-start.9 = (bf16[4,64,256]{2,1,0:T(8,128)(2,1)S(1)}, bf16[4,64,256]{2,1,0:T(8,128)(2,1)S(1)}, u32[]{:S(2)}, u32[]{:S(2)}) collective-permute-start(bf16[4,64,256]{2,1,0:T(8,128)(2,1)S(1)} %get-tuple-element.64), channel_id=1, source_target_pairs={{0,3},{1,0},{2,1},{3,2},{4,7},{5,4},{6,5},{7,6},{8,11},{9,8},{10,9... | collective-permute-start | bytes 393224 | tf_op jit(solution)/shard_map/ppermute | solution.py:237
  125.6 2.9 %collective-permute-done.8.refs_3_ = bf16[4,64,256]{2,1,0:T(8,128)(2,1)S(1)} collective-permute-done((bf16[4,64,256]{2,1,0:T(8,128)(2,1)S(1)}, bf16[4,64,256]{2,1,0:T(8,128)(2,1)S(1)}, u32[]{:S(2)}, u32[]{:S(2)}) %collective-permute-start.8) | collective-permute-done | bytes 131104 | tf_op jit(solution)/shard_map/ppermute | solution.py:237
  128.5 2.5 %expand.1 = bf16[2048,512]{1,0:T(8,128)(2,1)} custom-call(f32[2048,512]{1,0:T(8,128)S(1)} %get-tuple-element.48.near_ref, bf16[2048,64]{1,0:T(8,128)(2,1)S(1)} %get-tuple-element.49.basis_ref, f32[4,64,512]{2,1,0:T(8,128)S(1)} %get-tuple-element.58.refs_0_, bf16[8,64,256]{2,1,0:T(8,128)(2,1)S(1)} %collective-permute-done.6.up_ref.refs_1_, ...), custom_call_target="tpu_custom_call" | custom-call | flops 134217728 | bytes 7340032 | tf_op jit(solution)/shard_map/expand/pallas_call | solution.py:381
  (43 shorter events, 8.1 us)
Async XLA Ops:
  6.5 3.6 %copy-start.1 = (s32[128]{0:T(128)S(1)}, s32[128]{0:T(128)}, u32[]{:S(2)}) copy-start(s32[128]{0:T(128)} %rows_ref.1) | copy-start | bytes 1540
  6.5 46.0 %all-gather.2.cloned.1.call-start = ((), (), s32[]{:S(2)}) async-start(), calls=%async_computation.1 | async-start | bytes 4718592 | tf_op jit(solution)/shard_map/all_gather | solution.py:408
  13.2 39.3 %all-to-all-start = ((bf16[16,528,128]{2,1,0:T(8,128)(2,1)}), bf16[16,528,128]{2,1,0:T(8,128)(2,1)}, u32[]{:S(2)}, u32[]{:S(2)}) async-start(bf16[16,528,128]{2,1,0:T(8,128)(2,1)} %dispatch.1), calls=%async_computation | async-start | bytes 4325376 | tf_op jit(solution)/shard_map/all_to_all | solution.py:415
  21.2 47.0 %collective-permute-start = (bf16[1024,512]{1,0:T(8,128)(2,1)}, bf16[1024,512]{1,0:T(8,128)(2,1)S(1)}, u32[]{:S(2)}, u32[]{:S(2)}) collective-permute-start(bf16[1024,512]{1,0:T(8,128)(2,1)} %get-tuple-element.42), channel_id=1, source_target_pairs={{0,1},{1,2},{2,3},{3,4},{4,5},{5,6},{6,7},{7,8},{8,9},{9,10},{10,1... | collective-permute-start | bytes 3145736 | tf_op jit(solution)/shard_map/ppermute | solution.py:419
  25.1 47.0 %copy-start = (bf16[2048,512]{1,0:T(8,128)(2,1)S(1)}, bf16[2048,512]{1,0:T(8,128)(2,1)}, u32[]{:S(2)}) copy-start(bf16[2048,512]{1,0:T(8,128)(2,1)} %modes_ref.3) | copy-start | bytes 6291460
  25.1 47.0 %copy-start.5 = (bf16[64,2048]{1,0:T(8,128)(2,1)S(1)}, bf16[64,2048]{1,0:T(8,128)(2,1)}, u32[]{:S(2)}) copy-start(bf16[64,2048]{1,0:T(8,128)(2,1)} %basis_ref.3) | copy-start | bytes 786436
  25.1 47.0 %collective-permute-start.1 = (bf16[1024,512]{1,0:T(8,128)(2,1)}, bf16[1024,512]{1,0:T(8,128)(2,1)}, u32[]{:S(2)}, u32[]{:S(2)}) collective-permute-start(bf16[1024,512]{1,0:T(8,128)(2,1)} %get-tuple-element.43), channel_id=1, source_target_pairs={{1,0},{2,1},{3,2},{4,3},{5,4},{6,5},{7,6},{8,7},{9,8},{10,9},{11,1... | collective-permute-start | bytes 3145736 | tf_op jit(solution)/shard_map/ppermute | solution.py:420
  61.5 29.2 %collective-permute-start.10 = (bf16[16,64,512]{2,1,0:T(8,128)(2,1)S(1)}, bf16[16,64,512]{2,1,0:T(8,128)(2,1)S(1)}, u32[]{:S(2)}, u32[]{:S(2)}) collective-permute-start(bf16[16,64,512]{2,1,0:T(8,128)(2,1)S(1)} %get-tuple-element.66), channel_id=1, source_target_pairs={{0,1},{1,2},{2,3},{3,0},{4,5},{5,6},{6,7},{7,4},{8,9},{9,10},{10,1... | collective-permute-start | bytes 3145736 | tf_op jit(solution)/shard_map/ppermute | solution.py:237
  62.9 30.4 %collective-permute-start.11 = (bf16[16,64,512]{2,1,0:T(8,128)(2,1)S(1)}, bf16[16,64,512]{2,1,0:T(8,128)(2,1)S(1)}, u32[]{:S(2)}, u32[]{:S(2)}) collective-permute-start(bf16[16,64,512]{2,1,0:T(8,128)(2,1)S(1)} %get-tuple-element.67), channel_id=1, source_target_pairs={{0,3},{1,0},{2,1},{3,2},{4,7},{5,4},{6,5},{7,6},{8,11},{9,8},{10,9... | collective-permute-start | bytes 3145736 | tf_op jit(solution)/shard_map/ppermute | solution.py:237
  64.8 32.6 %collective-permute-start.3 = (bf16[16,64,512]{2,1,0:T(8,128)(2,1)S(1)}, bf16[16,64,512]{2,1,0:T(8,128)(2,1)S(1)}, u32[]{:S(2)}, u32[]{:S(2)}) collective-permute-start(bf16[16,64,512]{2,1,0:T(8,128)(2,1)S(1)} %get-tuple-element.51), channel_id=1, source_target_pairs={{0,12},{1,13},{2,14},{3,15},{4,0},{5,1},{6,2},{7,3},{8,4},{9,5},{1... | collective-permute-start | bytes 3145736 | tf_op jit(solution)/shard_map/ppermute | solution.py:237
  68.2 29.2 %collective-permute-start.2 = (bf16[16,64,512]{2,1,0:T(8,128)(2,1)S(1)}, bf16[16,64,512]{2,1,0:T(8,128)(2,1)S(1)}, u32[]{:S(2)}, u32[]{:S(2)}) collective-permute-start(bf16[16,64,512]{2,1,0:T(8,128)(2,1)S(1)} %get-tuple-element.45), channel_id=1, source_target_pairs={{0,4},{1,5},{2,6},{3,7},{4,8},{5,9},{6,10},{7,11},{8,12},{9,13},{1... | collective-permute-start | bytes 3145736 | tf_op jit(solution)/shard_map/ppermute | solution.py:237
  72.1 3.7 %copy-start.4 = (bf16[2048,2304]{1,0:T(8,128)(2,1)S(1)}, bf16[2048,2304]{1,0:T(8,128)(2,1)}, u32[]{:S(2)}) copy-start(bf16[2048,2304]{1,0:T(8,128)(2,1)} %near_ref.1) | copy-start | bytes 28311556
  93.5 16.0 %collective-permute-start.12 = (bf16[8,64,512]{2,1,0:T(8,128)(2,1)S(1)}, bf16[8,64,512]{2,1,0:T(8,128)(2,1)S(1)}, u32[]{:S(2)}, u32[]{:S(2)}) collective-permute-start(bf16[8,64,512]{2,1,0:T(8,128)(2,1)S(1)} %get-tuple-element.70), channel_id=1, source_target_pairs={{0,1},{1,2},{2,3},{3,0},{4,5},{5,6},{6,7},{7,4},{8,9},{9,10},{10,1... | collective-permute-start | bytes 1572872 | tf_op jit(solution)/shard_map/ppermute | solution.py:237
  93.6 15.9 %collective-permute-start.13 = (bf16[8,64,512]{2,1,0:T(8,128)(2,1)S(1)}, bf16[8,64,512]{2,1,0:T(8,128)(2,1)S(1)}, u32[]{:S(2)}, u32[]{:S(2)}) collective-permute-start(bf16[8,64,512]{2,1,0:T(8,128)(2,1)S(1)} %get-tuple-element.71), channel_id=1, source_target_pairs={{0,3},{1,0},{2,1},{3,2},{4,7},{5,4},{6,5},{7,6},{8,11},{9,8},{10,9... | collective-permute-start | bytes 1572872 | tf_op jit(solution)/shard_map/ppermute | solution.py:237
  97.5 15.6 %collective-permute-start.4 = (bf16[8,64,512]{2,1,0:T(8,128)(2,1)S(1)}, bf16[8,64,512]{2,1,0:T(8,128)(2,1)S(1)}, u32[]{:S(2)}, u32[]{:S(2)}) collective-permute-start(bf16[8,64,512]{2,1,0:T(8,128)(2,1)S(1)} %get-tuple-element.56), channel_id=1, source_target_pairs={{0,4},{1,5},{2,6},{3,7},{4,8},{5,9},{6,10},{7,11},{8,12},{9,13},{1... | collective-permute-start | bytes 1572872 | tf_op jit(solution)/shard_map/ppermute | solution.py:237
  98.2 14.8 %collective-permute-start.5 = (bf16[8,64,512]{2,1,0:T(8,128)(2,1)S(1)}, bf16[8,64,512]{2,1,0:T(8,128)(2,1)S(1)}, u32[]{:S(2)}, u32[]{:S(2)}) collective-permute-start(bf16[8,64,512]{2,1,0:T(8,128)(2,1)S(1)} %get-tuple-element.57), channel_id=1, source_target_pairs={{0,12},{1,13},{2,14},{3,15},{4,0},{5,1},{6,2},{7,3},{8,4},{9,5},{1... | collective-permute-start | bytes 1572872 | tf_op jit(solution)/shard_map/ppermute | solution.py:237
  109.8 9.1 %collective-permute-start.14 = (bf16[8,64,256]{2,1,0:T(8,128)(2,1)S(1)}, bf16[8,64,256]{2,1,0:T(8,128)(2,1)S(1)}, u32[]{:S(2)}, u32[]{:S(2)}) collective-permute-start(bf16[8,64,256]{2,1,0:T(8,128)(2,1)S(1)} %get-tuple-element.73), channel_id=1, source_target_pairs={{0,4},{1,5},{2,6},{3,7},{4,8},{5,9},{6,10},{7,11},{8,12},{9,13},{1... | collective-permute-start | bytes 786440 | tf_op jit(solution)/shard_map/ppermute | solution.py:237
  110.3 8.5 %collective-permute-start.15 = (bf16[8,64,256]{2,1,0:T(8,128)(2,1)S(1)}, bf16[8,64,256]{2,1,0:T(8,128)(2,1)S(1)}, u32[]{:S(2)}, u32[]{:S(2)}) collective-permute-start(bf16[8,64,256]{2,1,0:T(8,128)(2,1)S(1)} %get-tuple-element.74), channel_id=1, source_target_pairs={{0,12},{1,13},{2,14},{3,15},{4,0},{5,1},{6,2},{7,3},{8,4},{9,5},{1... | collective-permute-start | bytes 786440 | tf_op jit(solution)/shard_map/ppermute | solution.py:237
  113.4 8.9 %collective-permute-start.6 = (bf16[8,64,256]{2,1,0:T(8,128)(2,1)S(1)}, bf16[8,64,256]{2,1,0:T(8,128)(2,1)S(1)}, u32[]{:S(2)}, u32[]{:S(2)}) collective-permute-start(bf16[8,64,256]{2,1,0:T(8,128)(2,1)S(1)} %get-tuple-element.59), channel_id=1, source_target_pairs={{0,1},{1,2},{2,3},{3,0},{4,5},{5,6},{6,7},{7,4},{8,9},{9,10},{10,1... | collective-permute-start | bytes 786440 | tf_op jit(solution)/shard_map/ppermute | solution.py:237
  114.6 7.7 %collective-permute-start.7 = (bf16[8,64,256]{2,1,0:T(8,128)(2,1)S(1)}, bf16[8,64,256]{2,1,0:T(8,128)(2,1)S(1)}, u32[]{:S(2)}, u32[]{:S(2)}) collective-permute-start(bf16[8,64,256]{2,1,0:T(8,128)(2,1)S(1)} %get-tuple-element.60), channel_id=1, source_target_pairs={{0,3},{1,0},{2,1},{3,2},{4,7},{5,4},{6,5},{7,6},{8,11},{9,8},{10,9... | collective-permute-start | bytes 786440 | tf_op jit(solution)/shard_map/ppermute | solution.py:237
  118.9 6.7 %collective-permute-start.16 = (bf16[4,64,256]{2,1,0:T(8,128)(2,1)S(1)}, bf16[4,64,256]{2,1,0:T(8,128)(2,1)S(1)}, u32[]{:S(2)}, u32[]{:S(2)}) collective-permute-start(bf16[4,64,256]{2,1,0:T(8,128)(2,1)S(1)} %get-tuple-element.77), channel_id=1, source_target_pairs={{0,4},{1,5},{2,6},{3,7},{4,8},{5,9},{6,10},{7,11},{8,12},{9,13},{1... | collective-permute-start | bytes 393224 | tf_op jit(solution)/shard_map/ppermute | solution.py:237
  120.6 5.0 %collective-permute-start.17 = (bf16[4,64,256]{2,1,0:T(8,128)(2,1)S(1)}, bf16[4,64,256]{2,1,0:T(8,128)(2,1)S(1)}, u32[]{:S(2)}, u32[]{:S(2)}) collective-permute-start(bf16[4,64,256]{2,1,0:T(8,128)(2,1)S(1)} %get-tuple-element.78), channel_id=1, source_target_pairs={{0,12},{1,13},{2,14},{3,15},{4,0},{5,1},{6,2},{7,3},{8,4},{9,5},{1... | collective-permute-start | bytes 393224 | tf_op jit(solution)/shard_map/ppermute | solution.py:237
  122.3 6.2 %collective-permute-start.8 = (bf16[4,64,256]{2,1,0:T(8,128)(2,1)S(1)}, bf16[4,64,256]{2,1,0:T(8,128)(2,1)S(1)}, u32[]{:S(2)}, u32[]{:S(2)}) collective-permute-start(bf16[4,64,256]{2,1,0:T(8,128)(2,1)S(1)} %get-tuple-element.63), channel_id=1, source_target_pairs={{0,1},{1,2},{2,3},{3,0},{4,5},{5,6},{6,7},{7,4},{8,9},{9,10},{10,1... | collective-permute-start | bytes 393224 | tf_op jit(solution)/shard_map/ppermute | solution.py:237
  123.2 5.4 %collective-permute-start.9 = (bf16[4,64,256]{2,1,0:T(8,128)(2,1)S(1)}, bf16[4,64,256]{2,1,0:T(8,128)(2,1)S(1)}, u32[]{:S(2)}, u32[]{:S(2)}) collective-permute-start(bf16[4,64,256]{2,1,0:T(8,128)(2,1)S(1)} %get-tuple-element.64), channel_id=1, source_target_pairs={{0,3},{1,0},{2,1},{3,2},{4,7},{5,4},{6,5},{7,6},{8,11},{9,8},{10,9... | collective-permute-start | bytes 393224 | tf_op jit(solution)/shard_map/ppermute | solution.py:237
  (3 other events, 10.5 us)
Sparse Core Ops, SparseCore 0:
  10.0 34.5 all-gather.1

commit v12 on v11

--- a/solution.py
+++ b/solution.py
@@ -121,8 +121,10 @@
 X_ROWS = 4
 
 
-def far_kernel(slots, rows, comp_ref, sent_ref, *refs):
-    outs, (acc_ref, meta_ref, smem_ref, list_ref, sem) = (refs[:5], refs[5:10]), refs[10:]
+def far_kernel(slots, rows, gathered_ref, sent_ref, *refs):
+    outs, (comp_ref, acc_ref, meta_ref, smem_ref, list_ref, sem, comp_sem) = (refs[:5], refs[5:10]), refs[10:]
+    comp_copy = pltpu.make_async_copy(gathered_ref, comp_ref, comp_sem)
+    comp_copy.start()
     sources = sent_ref.shape[0]
     group_rows = acc_ref.shape[0]
     part = group_rows // 4
@@ -157,6 +159,8 @@
     for i in range(UNROLL):
         list_ref[total + i] = 0
 
+    comp_copy.wait()
+
     def group(g, carry):
         for i in range(UNROLL):
             at = g * UNROLL + i
@@ -202,14 +206,16 @@
     ]
     parts = pl.pallas_call(
         functools.partial(far_kernel, slots, rows),
-        in_specs=[whole()] * 2,
+        in_specs=[whole(pl.ANY), whole()],
         out_specs=[whole()] * len(kinds),
         out_shape=[jax.ShapeDtypeStruct((n, rank, cols), kind) for n, kind in kinds],
         scratch_shapes=[
+            VMEM(comp.shape, comp.dtype),
             VMEM((group_rows, rank, cols), jnp.float32),
             VMEM((sources, 128), jnp.int32),
             SMEM((sources, 128), jnp.int32),
             SMEM((sources * slots + UNROLL + slots,), jnp.int32),
+            pltpu.SemaphoreType.DMA,
             pltpu.SemaphoreType.DMA,
         ],
         compiler_params=pltpu.CompilerParams(vmem_limit_bytes=40 * MIB),

time: 140 us -> 140 us (level)
  no operation moved by 1% of the time
where the time goes in v12:
time: 140 us; the launch traced here: 138 us
  waiting for transfers between devices  53.1 us (38%)
  starting transfers between devices  40.9 us (29%)
  Pallas kernels  26.4 us (19%)
  between operations  13.6 us (10%)
  local copies, waits for them, and re-layouts  3.94 us (3%)
    all_to_all x1, waiting for transfers between devices, per_device(): sent = lax.all_to_all(sent, 'ccol', split_axis=0, concat_axis=0, tiled=True)  26 us
    ppermute x8, waiting for transfers between devices, both_ways(): lax.ppermute(up, 'ccol', ring(along_x, 1))  20.5 us
    ppermute x8, starting transfers between devices, both_ways(): lax.ppermute(down, 'ccol', ring(along_x, -1))  17.9 us
    ppermute x8, starting transfers between devices, both_ways(): lax.ppermute(up, 'ccol', ring(along_x, 1))  9.62 us
    pallas_call x1, Pallas kernels, far_field(): pl.pallas_call(functools.partial(far_kernel, slots, rows), in_specs=[whol...  8.59 us
    all_to_all x1, starting transfers between devices, per_device(): sent = lax.all_to_all(sent, 'ccol', split_axis=0, concat_axis=0, tiled=True)  8.01 us
    pallas_call x1, Pallas kernels, near_field(): pl.pallas_call(near_kernel, grid=(panels // CS,), in_specs=[pl.BlockSpec(...  8 us
    unnamed x15, local copies, waits for them, and re-layouts  3.94 us
  transfers between devices with their start and end apart: 20, of which 7 were waited for; matrix products, arithmetic and copies ran while one was open for 0% of the time, Pallas kernels for 15%

profile of v12, /device:TPU:0, one launch (start us, length us, event | category | flops | bytes accessed | tf_op | source)
XLA Modules:
  0.0 137.9 jit_solution(16699326984954625427)
XLA Ops:
  6.6 3.2 %compress.1 = (bf16[8,64,512]{2,1,0:T(8,128)(2,1)}, bf16[1024,512]{1,0:T(8,128)(2,1)}, bf16[1024,512]{1,0:T(8,128)(2,1)}) custom-call(bf16[64,2048]{1,0:T(8,128)(2,1)} %basis_ref.2, bf16[2048,512]{1,0:T(8,128)(2,1)} %modes_ref.3), custom_call_target="tpu_custom_call" | custom-call | flops 134217728 | bytes 3145728 | tf_op jit(solution)/shard_map/compress/pallas_call | solution.py:49
  10.1 3.0 %dispatch.1 = bf16[16,528,128]{2,1,0:T(8,128)(2,1)} custom-call(s32[128]{0:T(128)S(1)} %copy-done.1, s32[128]{0:T(128)S(1)} %bitcast.4, s32[128]{0:T(128)S(1)} %copy-done.3, bf16[128,32,128]{2,1,0:T(8,128)(2,1)S(1)} %bitcast.3), custom_call_target="tpu_custom_call" | custom-call | flops 4194304 | bytes 3145728 | tf_op jit(solution)/shard_map/dispatch/pallas_call | solution.py:108
  13.2 8.0 %all-to-all-start = ((bf16[16,528,128]{2,1,0:T(8,128)(2,1)}), bf16[16,528,128]{2,1,0:T(8,128)(2,1)}, u32[]{:S(2)}, u32[]{:S(2)}) async-start(bf16[16,528,128]{2,1,0:T(8,128)(2,1)} %dispatch.1), calls=%async_computation | async-start | bytes 4325376 | tf_op jit(solution)/shard_map/all_to_all | solution.py:421
  21.2 3.8 %collective-permute-start = (bf16[1024,512]{1,0:T(8,128)(2,1)}, bf16[1024,512]{1,0:T(8,128)(2,1)S(1)}, u32[]{:S(2)}, u32[]{:S(2)}) collective-permute-start(bf16[1024,512]{1,0:T(8,128)(2,1)} %get-tuple-element.42), channel_id=1, source_target_pairs={{0,1},{1,2},{2,3},{3,4},{4,5},{5,6},{6,7},{7,8},{8,9},{9,10},{10,1... | collective-permute-start | bytes 3145736 | tf_op jit(solution)/shard_map/ppermute | solution.py:425
  26.5 26.0 %all-to-all-done.sent_ref = bf16[16,528,128]{2,1,0:T(8,128)(2,1)} async-done(((bf16[16,528,128]{2,1,0:T(8,128)(2,1)}), bf16[16,528,128]{2,1,0:T(8,128)(2,1)}, u32[]{:S(2)}, u32[]{:S(2)}) %all-to-all-start) | async-done | bytes 2162720 | tf_op jit(solution)/shard_map/all_to_all | solution.py:421
  52.5 8.6 %far_field.1 = (bf16[16,64,512]{2,1,0:T(8,128)(2,1)S(1)}, bf16[16,64,512]{2,1,0:T(8,128)(2,1)S(1)}, f32[8,64,512]{2,1,0:T(8,128)S(1)}, f32[8,64,512]{2,1,0:T(8,1...) custom-call(bf16[64,64,512]{2,1,0:T(8,128)(2,1)} %all-gather.2.clone, ...), custom_call_target="tpu_custom_call" | custom-call | flops 4294967296 | bytes 25165824 | tf_op jit(solution)/shard_map/far_field/pallas_call | solution.py:207
  61.8 2.7 %collective-permute-start.11 = (bf16[16,64,512]{2,1,0:T(8,128)(2,1)S(1)}, bf16[16,64,512]{2,1,0:T(8,128)(2,1)S(1)}, u32[]{:S(2)}, u32[]{:S(2)}) collective-permute-start(bf16[16,64,512]{2,1,0:T(8,128)(2,1)S(1)} %get-tuple-element.67), channel_id=1, source_target_pairs={{0,3},{1,0},{2,1},{3,2},{4,7},{5,4},{6,5},{7,6},{8,11},{9,8},{10,9... | collective-permute-start | bytes 3145736 | tf_op jit(solution)/shard_map/ppermute | solution.py:243
  64.4 3.7 %collective-permute-done.before_ref = bf16[1024,512]{1,0:T(8,128)(2,1)S(1)} collective-permute-done((bf16[1024,512]{1,0:T(8,128)(2,1)}, bf16[1024,512]{1,0:T(8,128)(2,1)S(1)}, u32[]{:S(2)}, u32[]{:S(2)}) %collective-permute-start) | collective-permute-done | bytes 1048608 | tf_op jit(solution)/shard_map/ppermute | solution.py:425
  68.2 3.9 %collective-permute-start.2 = (bf16[16,64,512]{2,1,0:T(8,128)(2,1)S(1)}, bf16[16,64,512]{2,1,0:T(8,128)(2,1)S(1)}, u32[]{:S(2)}, u32[]{:S(2)}) collective-permute-start(bf16[16,64,512]{2,1,0:T(8,128)(2,1)S(1)} %get-tuple-element.45), channel_id=1, source_target_pairs={{0,4},{1,5},{2,6},{3,7},{4,8},{5,9},{6,10},{7,11},{8,12},{9,13},{1... | collective-permute-start | bytes 3145736 | tf_op jit(solution)/shard_map/ppermute | solution.py:243
  72.1 3.7 %copy-done.4 = bf16[2048,2304]{1,0:T(8,128)(2,1)S(1)} copy-done((bf16[2048,2304]{1,0:T(8,128)(2,1)S(1)}, bf16[2048,2304]{1,0:T(8,128)(2,1)}, u32[]{:S(2)}) %copy-start.4) | copy-done | bytes 9437208
  75.7 8.0 %near_field.1 = (f32[2048,512]{1,0:T(8,128)S(1)}, bf16[2048,64]{1,0:T(8,128)(2,1)S(1)}) custom-call(bf16[2048,2304]{1,0:T(8,128)(2,1)S(1)} %copy-done.4, bf16[1024,512]{1,0:T(8,128)(2,1)S(1)} %collective-permute-done.before_ref, bf16[2048,512]{1,0:T(8,128)(2,1)S(1)} %copy-done, bf16[1024,512]{1,0:T(8,128)(2,1)} %collective-permute-done.1.after_ref, ...), custom_call_target="tpu_custom_call" | custom-call | flops 4831838208 | bytes 2097152 | tf_op jit(solution)/shard_map/near_field/pallas_call | solution.py:337
  83.8 6.7 %collective-permute-done.10.up_ref.up_in_ref = bf16[16,64,512]{2,1,0:T(8,128)(2,1)S(1)} collective-permute-done((bf16[16,64,512]{2,1,0:T(8,128)(2,1)S(1)}, bf16[16,64,512]{2,1,0:T(8,128)(2,1)S(1)}, u32[]{:S(2)}, u32[]{:S(2)}) %collective-permute-start.10) | collective-permute-done | bytes 1048608 | tf_op jit(solution)/shard_map/ppermute | solution.py:243
  90.5 2.8 %collective-permute-done.11.down_ref.down_in_ref = bf16[16,64,512]{2,1,0:T(8,128)(2,1)S(1)} collective-permute-done((bf16[16,64,512]{2,1,0:T(8,128)(2,1)S(1)}, bf16[16,64,512]{2,1,0:T(8,128)(2,1)S(1)}, u32[]{:S(2)}, u32[]{:S(2)}) %collective-permute-start.11) | collective-permute-done | bytes 1048608 | tf_op jit(solution)/shard_map/ppermute | solution.py:243
  93.6 3.8 %collective-permute-start.13 = (bf16[8,64,512]{2,1,0:T(8,128)(2,1)S(1)}, bf16[8,64,512]{2,1,0:T(8,128)(2,1)S(1)}, u32[]{:S(2)}, u32[]{:S(2)}) collective-permute-start(bf16[8,64,512]{2,1,0:T(8,128)(2,1)S(1)} %get-tuple-element.71), channel_id=1, source_target_pairs={{0,3},{1,0},{2,1},{3,2},{4,7},{5,4},{6,5},{7,6},{8,11},{9,8},{10,9... | collective-permute-start | bytes 1572872 | tf_op jit(solution)/shard_map/ppermute | solution.py:243
  98.3 2.6 %collective-permute-start.5 = (bf16[8,64,512]{2,1,0:T(8,128)(2,1)S(1)}, bf16[8,64,512]{2,1,0:T(8,128)(2,1)S(1)}, u32[]{:S(2)}, u32[]{:S(2)}) collective-permute-start(bf16[8,64,512]{2,1,0:T(8,128)(2,1)S(1)} %get-tuple-element.57), channel_id=1, source_target_pairs={{0,12},{1,13},{2,14},{3,15},{4,0},{5,1},{6,2},{7,3},{8,4},{9,5},{1... | collective-permute-start | bytes 1572872 | tf_op jit(solution)/shard_map/ppermute | solution.py:243
  100.8 8.6 %collective-permute-done.12.up_rest_ref = bf16[8,64,512]{2,1,0:T(8,128)(2,1)S(1)} collective-permute-done((bf16[8,64,512]{2,1,0:T(8,128)(2,1)S(1)}, bf16[8,64,512]{2,1,0:T(8,128)(2,1)S(1)}, u32[]{:S(2)}, u32[]{:S(2)}) %collective-permute-start.12) | collective-permute-done | bytes 524320 | tf_op jit(solution)/shard_map/ppermute | solution.py:243
  110.3 2.8 %collective-permute-start.15 = (bf16[8,64,256]{2,1,0:T(8,128)(2,1)S(1)}, bf16[8,64,256]{2,1,0:T(8,128)(2,1)S(1)}, u32[]{:S(2)}, u32[]{:S(2)}) collective-permute-start(bf16[8,64,256]{2,1,0:T(8,128)(2,1)S(1)} %get-tuple-element.74), channel_id=1, source_target_pairs={{0,12},{1,13},{2,14},{3,15},{4,0},{5,1},{6,2},{7,3},{8,4},{9,5},{1... | collective-permute-start | bytes 786440 | tf_op jit(solution)/shard_map/ppermute | solution.py:243
  114.6 2.1 %collective-permute-start.7 = (bf16[8,64,256]{2,1,0:T(8,128)(2,1)S(1)}, bf16[8,64,256]{2,1,0:T(8,128)(2,1)S(1)}, u32[]{:S(2)}, u32[]{:S(2)}) collective-permute-start(bf16[8,64,256]{2,1,0:T(8,128)(2,1)S(1)} %get-tuple-element.60), channel_id=1, source_target_pairs={{0,3},{1,0},{2,1},{3,2},{4,7},{5,4},{6,5},{7,6},{8,11},{9,8},{10,9... | collective-permute-start | bytes 786440 | tf_op jit(solution)/shard_map/ppermute | solution.py:243
  116.7 2.2 %collective-permute-done.14.up_ref.refs_6_ = bf16[8,64,256]{2,1,0:T(8,128)(2,1)S(1)} collective-permute-done((bf16[8,64,256]{2,1,0:T(8,128)(2,1)S(1)}, bf16[8,64,256]{2,1,0:T(8,128)(2,1)S(1)}, u32[]{:S(2)}, u32[]{:S(2)}) %collective-permute-start.14) | collective-permute-done | bytes 262176 | tf_op jit(solution)/shard_map/ppermute | solution.py:243
  118.9 1.6 %collective-permute-start.16 = (bf16[4,64,256]{2,1,0:T(8,128)(2,1)S(1)}, bf16[4,64,256]{2,1,0:T(8,128)(2,1)S(1)}, u32[]{:S(2)}, u32[]{:S(2)}) collective-permute-start(bf16[4,64,256]{2,1,0:T(8,128)(2,1)S(1)} %get-tuple-element.77), channel_id=1, source_target_pairs={{0,4},{1,5},{2,6},{3,7},{4,8},{5,9},{6,10},{7,11},{8,12},{9,13},{1... | collective-permute-start | bytes 393224 | tf_op jit(solution)/shard_map/ppermute | solution.py:243
  120.6 1.7 %collective-permute-start.17 = (bf16[4,64,256]{2,1,0:T(8,128)(2,1)S(1)}, bf16[4,64,256]{2,1,0:T(8,128)(2,1)S(1)}, u32[]{:S(2)}, u32[]{:S(2)}) collective-permute-start(bf16[4,64,256]{2,1,0:T(8,128)(2,1)S(1)} %get-tuple-element.78), channel_id=1, source_target_pairs={{0,12},{1,13},{2,14},{3,15},{4,0},{5,1},{6,2},{7,3},{8,4},{9,5},{1... | collective-permute-start | bytes 393224 | tf_op jit(solution)/shard_map/ppermute | solution.py:243
  123.2 2.4 %collective-permute-start.9 = (bf16[4,64,256]{2,1,0:T(8,128)(2,1)S(1)}, bf16[4,64,256]{2,1,0:T(8,128)(2,1)S(1)}, u32[]{:S(2)}, u32[]{:S(2)}) collective-permute-start(bf16[4,64,256]{2,1,0:T(8,128)(2,1)S(1)} %get-tuple-element.64), channel_id=1, source_target_pairs={{0,3},{1,0},{2,1},{3,2},{4,7},{5,4},{6,5},{7,6},{8,11},{9,8},{10,9... | collective-permute-start | bytes 393224 | tf_op jit(solution)/shard_map/ppermute | solution.py:243
  125.6 2.9 %collective-permute-done.8.refs_3_ = bf16[4,64,256]{2,1,0:T(8,128)(2,1)S(1)} collective-permute-done((bf16[4,64,256]{2,1,0:T(8,128)(2,1)S(1)}, bf16[4,64,256]{2,1,0:T(8,128)(2,1)S(1)}, u32[]{:S(2)}, u32[]{:S(2)}) %collective-permute-start.8) | collective-permute-done | bytes 131104 | tf_op jit(solution)/shard_map/ppermute | solution.py:243
  128.5 2.5 %expand.1 = bf16[2048,512]{1,0:T(8,128)(2,1)} custom-call(f32[2048,512]{1,0:T(8,128)S(1)} %get-tuple-element.48.near_ref, bf16[2048,64]{1,0:T(8,128)(2,1)S(1)} %get-tuple-element.49.basis_ref, f32[4,64,512]{2,1,0:T(8,128)S(1)} %get-tuple-element.58.refs_0_, bf16[8,64,256]{2,1,0:T(8,128)(2,1)S(1)} %collective-permute-done.6.up_ref.refs_1_, ...), custom_call_target="tpu_custom_call" | custom-call | flops 134217728 | bytes 7340032 | tf_op jit(solution)/shard_map/expand/pallas_call | solution.py:387
  (43 shorter events, 6.9 us)
Async XLA Ops:
  6.5 3.6 %copy-start.1 = (s32[128]{0:T(128)S(1)}, s32[128]{0:T(128)}, u32[]{:S(2)}) copy-start(s32[128]{0:T(128)} %rows_ref.1) | copy-start | bytes 1540
  6.5 46.0 %all-gather.2.cloned.1.call-start = ((), (), s32[]{:S(2)}) async-start(), calls=%async_computation.1 | async-start | bytes 4718592 | tf_op jit(solution)/shard_map/all_gather | solution.py:414
  13.2 39.3 %all-to-all-start = ((bf16[16,528,128]{2,1,0:T(8,128)(2,1)}), bf16[16,528,128]{2,1,0:T(8,128)(2,1)}, u32[]{:S(2)}, u32[]{:S(2)}) async-start(bf16[16,528,128]{2,1,0:T(8,128)(2,1)} %dispatch.1), calls=%async_computation | async-start | bytes 4325376 | tf_op jit(solution)/shard_map/all_to_all | solution.py:421
  21.2 47.0 %collective-permute-start = (bf16[1024,512]{1,0:T(8,128)(2,1)}, bf16[1024,512]{1,0:T(8,128)(2,1)S(1)}, u32[]{:S(2)}, u32[]{:S(2)}) collective-permute-start(bf16[1024,512]{1,0:T(8,128)(2,1)} %get-tuple-element.42), channel_id=1, source_target_pairs={{0,1},{1,2},{2,3},{3,4},{4,5},{5,6},{6,7},{7,8},{8,9},{9,10},{10,1... | collective-permute-start | bytes 3145736 | tf_op jit(solution)/shard_map/ppermute | solution.py:425
  25.1 47.0 %copy-start = (bf16[2048,512]{1,0:T(8,128)(2,1)S(1)}, bf16[2048,512]{1,0:T(8,128)(2,1)}, u32[]{:S(2)}) copy-start(bf16[2048,512]{1,0:T(8,128)(2,1)} %modes_ref.3) | copy-start | bytes 6291460
  25.1 47.0 %copy-start.5 = (bf16[64,2048]{1,0:T(8,128)(2,1)S(1)}, bf16[64,2048]{1,0:T(8,128)(2,1)}, u32[]{:S(2)}) copy-start(bf16[64,2048]{1,0:T(8,128)(2,1)} %basis_ref.3) | copy-start | bytes 786436
  25.1 47.0 %collective-permute-start.1 = (bf16[1024,512]{1,0:T(8,128)(2,1)}, bf16[1024,512]{1,0:T(8,128)(2,1)}, u32[]{:S(2)}, u32[]{:S(2)}) collective-permute-start(bf16[1024,512]{1,0:T(8,128)(2,1)} %get-tuple-element.43), channel_id=1, source_target_pairs={{1,0},{2,1},{3,2},{4,3},{5,4},{6,5},{7,6},{8,7},{9,8},{10,9},{11,1... | collective-permute-start | bytes 3145736 | tf_op jit(solution)/shard_map/ppermute | solution.py:426
  61.1 29.4 %collective-permute-start.10 = (bf16[16,64,512]{2,1,0:T(8,128)(2,1)S(1)}, bf16[16,64,512]{2,1,0:T(8,128)(2,1)S(1)}, u32[]{:S(2)}, u32[]{:S(2)}) collective-permute-start(bf16[16,64,512]{2,1,0:T(8,128)(2,1)S(1)} %get-tuple-element.66), channel_id=1, source_target_pairs={{0,1},{1,2},{2,3},{3,0},{4,5},{5,6},{6,7},{7,4},{8,9},{9,10},{10,1... | collective-permute-start | bytes 3145736 | tf_op jit(solution)/shard_map/ppermute | solution.py:243
  61.8 31.6 %collective-permute-start.11 = (bf16[16,64,512]{2,1,0:T(8,128)(2,1)S(1)}, bf16[16,64,512]{2,1,0:T(8,128)(2,1)S(1)}, u32[]{:S(2)}, u32[]{:S(2)}) collective-permute-start(bf16[16,64,512]{2,1,0:T(8,128)(2,1)S(1)} %get-tuple-element.67), channel_id=1, source_target_pairs={{0,3},{1,0},{2,1},{3,2},{4,7},{5,4},{6,5},{7,6},{8,11},{9,8},{10,9... | collective-permute-start | bytes 3145736 | tf_op jit(solution)/shard_map/ppermute | solution.py:243
  64.4 32.9 %collective-permute-start.3 = (bf16[16,64,512]{2,1,0:T(8,128)(2,1)S(1)}, bf16[16,64,512]{2,1,0:T(8,128)(2,1)S(1)}, u32[]{:S(2)}, u32[]{:S(2)}) collective-permute-start(bf16[16,64,512]{2,1,0:T(8,128)(2,1)S(1)} %get-tuple-element.51), channel_id=1, source_target_pairs={{0,12},{1,13},{2,14},{3,15},{4,0},{5,1},{6,2},{7,3},{8,4},{9,5},{1... | collective-permute-start | bytes 3145736 | tf_op jit(solution)/shard_map/ppermute | solution.py:243
  68.2 29.2 %collective-permute-start.2 = (bf16[16,64,512]{2,1,0:T(8,128)(2,1)S(1)}, bf16[16,64,512]{2,1,0:T(8,128)(2,1)S(1)}, u32[]{:S(2)}, u32[]{:S(2)}) collective-permute-start(bf16[16,64,512]{2,1,0:T(8,128)(2,1)S(1)} %get-tuple-element.45), channel_id=1, source_target_pairs={{0,4},{1,5},{2,6},{3,7},{4,8},{5,9},{6,10},{7,11},{8,12},{9,13},{1... | collective-permute-start | bytes 3145736 | tf_op jit(solution)/shard_map/ppermute | solution.py:243
  72.1 3.7 %copy-start.4 = (bf16[2048,2304]{1,0:T(8,128)(2,1)S(1)}, bf16[2048,2304]{1,0:T(8,128)(2,1)}, u32[]{:S(2)}) copy-start(bf16[2048,2304]{1,0:T(8,128)(2,1)} %near_ref.1) | copy-start | bytes 28311556
  93.5 16.0 %collective-permute-start.12 = (bf16[8,64,512]{2,1,0:T(8,128)(2,1)S(1)}, bf16[8,64,512]{2,1,0:T(8,128)(2,1)S(1)}, u32[]{:S(2)}, u32[]{:S(2)}) collective-permute-start(bf16[8,64,512]{2,1,0:T(8,128)(2,1)S(1)} %get-tuple-element.70), channel_id=1, source_target_pairs={{0,1},{1,2},{2,3},{3,0},{4,5},{5,6},{6,7},{7,4},{8,9},{9,10},{10,1... | collective-permute-start | bytes 1572872 | tf_op jit(solution)/shard_map/ppermute | solution.py:243
  93.6 15.9 %collective-permute-start.13 = (bf16[8,64,512]{2,1,0:T(8,128)(2,1)S(1)}, bf16[8,64,512]{2,1,0:T(8,128)(2,1)S(1)}, u32[]{:S(2)}, u32[]{:S(2)}) collective-permute-start(bf16[8,64,512]{2,1,0:T(8,128)(2,1)S(1)} %get-tuple-element.71), channel_id=1, source_target_pairs={{0,3},{1,0},{2,1},{3,2},{4,7},{5,4},{6,5},{7,6},{8,11},{9,8},{10,9... | collective-permute-start | bytes 1572872 | tf_op jit(solution)/shard_map/ppermute | solution.py:243
  97.5 15.6 %collective-permute-start.4 = (bf16[8,64,512]{2,1,0:T(8,128)(2,1)S(1)}, bf16[8,64,512]{2,1,0:T(8,128)(2,1)S(1)}, u32[]{:S(2)}, u32[]{:S(2)}) collective-permute-start(bf16[8,64,512]{2,1,0:T(8,128)(2,1)S(1)} %get-tuple-element.56), channel_id=1, source_target_pairs={{0,4},{1,5},{2,6},{3,7},{4,8},{5,9},{6,10},{7,11},{8,12},{9,13},{1... | collective-permute-start | bytes 1572872 | tf_op jit(solution)/shard_map/ppermute | solution.py:243
  98.3 14.8 %collective-permute-start.5 = (bf16[8,64,512]{2,1,0:T(8,128)(2,1)S(1)}, bf16[8,64,512]{2,1,0:T(8,128)(2,1)S(1)}, u32[]{:S(2)}, u32[]{:S(2)}) collective-permute-start(bf16[8,64,512]{2,1,0:T(8,128)(2,1)S(1)} %get-tuple-element.57), channel_id=1, source_target_pairs={{0,12},{1,13},{2,14},{3,15},{4,0},{5,1},{6,2},{7,3},{8,4},{9,5},{1... | collective-permute-start | bytes 1572872 | tf_op jit(solution)/shard_map/ppermute | solution.py:243
  109.8 9.1 %collective-permute-start.14 = (bf16[8,64,256]{2,1,0:T(8,128)(2,1)S(1)}, bf16[8,64,256]{2,1,0:T(8,128)(2,1)S(1)}, u32[]{:S(2)}, u32[]{:S(2)}) collective-permute-start(bf16[8,64,256]{2,1,0:T(8,128)(2,1)S(1)} %get-tuple-element.73), channel_id=1, source_target_pairs={{0,4},{1,5},{2,6},{3,7},{4,8},{5,9},{6,10},{7,11},{8,12},{9,13},{1... | collective-permute-start | bytes 786440 | tf_op jit(solution)/shard_map/ppermute | solution.py:243
  110.3 8.5 %collective-permute-start.15 = (bf16[8,64,256]{2,1,0:T(8,128)(2,1)S(1)}, bf16[8,64,256]{2,1,0:T(8,128)(2,1)S(1)}, u32[]{:S(2)}, u32[]{:S(2)}) collective-permute-start(bf16[8,64,256]{2,1,0:T(8,128)(2,1)S(1)} %get-tuple-element.74), channel_id=1, source_target_pairs={{0,12},{1,13},{2,14},{3,15},{4,0},{5,1},{6,2},{7,3},{8,4},{9,5},{1... | collective-permute-start | bytes 786440 | tf_op jit(solution)/shard_map/ppermute | solution.py:243
  113.4 8.9 %collective-permute-start.6 = (bf16[8,64,256]{2,1,0:T(8,128)(2,1)S(1)}, bf16[8,64,256]{2,1,0:T(8,128)(2,1)S(1)}, u32[]{:S(2)}, u32[]{:S(2)}) collective-permute-start(bf16[8,64,256]{2,1,0:T(8,128)(2,1)S(1)} %get-tuple-element.59), channel_id=1, source_target_pairs={{0,1},{1,2},{2,3},{3,0},{4,5},{5,6},{6,7},{7,4},{8,9},{9,10},{10,1... | collective-permute-start | bytes 786440 | tf_op jit(solution)/shard_map/ppermute | solution.py:243
  114.6 7.7 %collective-permute-start.7 = (bf16[8,64,256]{2,1,0:T(8,128)(2,1)S(1)}, bf16[8,64,256]{2,1,0:T(8,128)(2,1)S(1)}, u32[]{:S(2)}, u32[]{:S(2)}) collective-permute-start(bf16[8,64,256]{2,1,0:T(8,128)(2,1)S(1)} %get-tuple-element.60), channel_id=1, source_target_pairs={{0,3},{1,0},{2,1},{3,2},{4,7},{5,4},{6,5},{7,6},{8,11},{9,8},{10,9... | collective-permute-start | bytes 786440 | tf_op jit(solution)/shard_map/ppermute | solution.py:243
  118.9 6.7 %collective-permute-start.16 = (bf16[4,64,256]{2,1,0:T(8,128)(2,1)S(1)}, bf16[4,64,256]{2,1,0:T(8,128)(2,1)S(1)}, u32[]{:S(2)}, u32[]{:S(2)}) collective-permute-start(bf16[4,64,256]{2,1,0:T(8,128)(2,1)S(1)} %get-tuple-element.77), channel_id=1, source_target_pairs={{0,4},{1,5},{2,6},{3,7},{4,8},{5,9},{6,10},{7,11},{8,12},{9,13},{1... | collective-permute-start | bytes 393224 | tf_op jit(solution)/shard_map/ppermute | solution.py:243
  120.6 5.0 %collective-permute-start.17 = (bf16[4,64,256]{2,1,0:T(8,128)(2,1)S(1)}, bf16[4,64,256]{2,1,0:T(8,128)(2,1)S(1)}, u32[]{:S(2)}, u32[]{:S(2)}) collective-permute-start(bf16[4,64,256]{2,1,0:T(8,128)(2,1)S(1)} %get-tuple-element.78), channel_id=1, source_target_pairs={{0,12},{1,13},{2,14},{3,15},{4,0},{5,1},{6,2},{7,3},{8,4},{9,5},{1... | collective-permute-start | bytes 393224 | tf_op jit(solution)/shard_map/ppermute | solution.py:243
  122.3 6.2 %collective-permute-start.8 = (bf16[4,64,256]{2,1,0:T(8,128)(2,1)S(1)}, bf16[4,64,256]{2,1,0:T(8,128)(2,1)S(1)}, u32[]{:S(2)}, u32[]{:S(2)}) collective-permute-start(bf16[4,64,256]{2,1,0:T(8,128)(2,1)S(1)} %get-tuple-element.63), channel_id=1, source_target_pairs={{0,1},{1,2},{2,3},{3,0},{4,5},{5,6},{6,7},{7,4},{8,9},{9,10},{10,1... | collective-permute-start | bytes 393224 | tf_op jit(solution)/shard_map/ppermute | solution.py:243
  123.2 5.4 %collective-permute-start.9 = (bf16[4,64,256]{2,1,0:T(8,128)(2,1)S(1)}, bf16[4,64,256]{2,1,0:T(8,128)(2,1)S(1)}, u32[]{:S(2)}, u32[]{:S(2)}) collective-permute-start(bf16[4,64,256]{2,1,0:T(8,128)(2,1)S(1)} %get-tuple-element.64), channel_id=1, source_target_pairs={{0,3},{1,0},{2,1},{3,2},{4,7},{5,4},{6,5},{7,6},{8,11},{9,8},{10,9... | collective-permute-start | bytes 393224 | tf_op jit(solution)/shard_map/ppermute | solution.py:243
  (3 other events, 10.5 us)
Sparse Core Ops, SparseCore 0:
  10.0 34.5 all-gather.1
